TPU v7x, 32 devices: a whole 2x2x4 slice. The times are simulated.
32 devices in a mesh: row: 4 (over z), col: 8 (over y, x, core).
Axes of the slice: x: 2, y: 2, z: 4, core: 2. Of those that a mesh axis runs over, the one named last changes fastest.
Arguments:
- hamiltonian: float32 [3072, 3072], P('row', 'col'), may hold values from -40 to 40, as said below
- panel: float32 [3072, 256], P('row'), may hold values from -180 to 180
Outputs:
- updated: float32 [3072, 3072], P('row', 'col')
- band_block: float32 [256, 256], replicated
Inputs may be any that keep to these rules, and one draw needn't show every extreme that they name: hamiltonian is exactly symmetric.
All inputs are finite; a program needn't handle non-finite values.
Results may differ from a plain program's by a relative error of at most 0.0003.
Values sent between devices are 32-bit elements; how exact they have to be, the bound alone decides.
No kernel may reach another device: no remote copies, remote signals or barrier semaphores. Data moves between devices by JAX's collectives and lax.ppermute only.
A program may use at most 64 MiB of HBM per device.

v0:
```python
import jax
import jax.numpy as jnp
from jax import lax
from jax.sharding import PartitionSpec as P


def from_root(shard, axis, root):
    mine = lax.axis_index(axis) == root
    return lax.psum(jnp.where(mine, shard, jnp.zeros_like(shard)), axis)


def mult(left, right):
    return jnp.dot(left, right, precision=lax.Precision.HIGHEST, preferred_element_type=jnp.float32)


def lower_solve(low, rows):
    return jax.scipy.linalg.solve_triangular(low, rows.T, lower=True).T


def shards(hamiltonian, panel):
    rows_dev = panel.shape[0]
    width = panel.shape[1]
    cols_dev = hamiltonian.shape[1]
    row_place = lax.axis_index("row")
    col_place = lax.axis_index("col")
    global_rows = row_place * rows_dev + jnp.arange(rows_dev, dtype=jnp.int32)
    picker = (jnp.arange(width, dtype=jnp.int32)[:, None] == global_rows[None, :]).astype(
        jnp.float32
    )
    top_part = mult(picker, panel)
    gram, top_rows = lax.psum((mult(panel.T, panel), top_part), "row")
    first_low = jnp.linalg.cholesky(gram)
    half = lower_solve(first_low, panel)
    second_low = jnp.linalg.cholesky(lax.psum(mult(half.T, half), "row"))
    ortho = lower_solve(second_low, half)
    ortho_top = lower_solve(second_low, lower_solve(first_low, top_rows))
    ident = jnp.eye(width, dtype=jnp.float32)
    lead = ortho_top + ident
    factor = jax.scipy.linalg.cho_solve((jnp.linalg.cholesky(mult(lead, lead.T)), True), lead)
    reflectors = ortho + picker.T
    owner = col_place * cols_dev // rows_dev
    offset = col_place * cols_dev - owner * rows_dev
    reflect_slab = lax.dynamic_slice_in_dim(reflectors, offset, cols_dev, 0)
    reflect_cols = from_root(reflect_slab, "row", owner)
    partial_rows = mult(hamiltonian, reflect_cols)
    products = lax.psum(partial_rows, "col")
    images = mult(products, factor)
    coupling = lax.psum(mult(reflectors.T, images), "row")
    turned = mult(factor.T, coupling)
    correction = images - 0.5 * mult(reflectors, turned)
    correct_slab = lax.dynamic_slice_in_dim(correction, offset, cols_dev, 0)
    correct_cols = from_root(correct_slab, "row", owner)
    left_side = jnp.concatenate([reflectors, correction], axis=1)
    right_side = jnp.concatenate([correct_cols, reflect_cols], axis=1)
    updated = hamiltonian - mult(left_side, right_side.T)
    band_block = -mult(second_low.T, first_low.T)
    return (updated, band_block)


def solution(mesh):
    in_specs = (P("row", "col"), P("row", None))
    out_specs = (P("row", "col"), P())
    return jax.shard_map(shards, mesh=mesh, in_specs=in_specs, out_specs=out_specs, check_vma=False)
```

profile of v0, /device:TPU:0, one launch (start us, length us, event | category | flops | bytes accessed | tf_op | source)
XLA Modules:
  0.0 480.5 jit_solution(11626904846821870595)
XLA Ops:
  7.2 3.5 fusion.78
  10.8 38.1 %all-reduce.9.cloned.1.call-done = f32[256,256]{0,1:T(8,128)} async-done(((f32[256,256]{0,1:T(8,128)}), f32[256,256]{0,1:T(8,128)}) %all-reduce.9.cloned.1.call-update) | async-done | bytes 262160 | tf_op jit(solution)/shard_map/psum | solution.py:31
  48.9 1.1 copy.5
  50.0 1.0 fusion.22
  51.0 11.7 %cholesky.172 = f32[128,128]{1,0:T(8,128)S(1)} custom-call(f32[128,128]{1,0:T(8,128)S(1)} %cholesky.270), custom_call_target="Cholesky" | custom-call | tf_op jit(solution)/shard_map/jit(cholesky)/cholesky | solution.py:32
  62.8 9.8 %custom-call.24 = f32[1,128,128]{1,2,0:T(8,128)S(1)} custom-call(f32[1,128,128]{2,1,0:T(8,128)S(1)} %get-tuple-element.95), custom_call_target="InvertDiagBlocksLowerTriangular" | custom-call | tf_op jit(solution)/shard_map/jit(cholesky)/cholesky | solution.py:32
  73.1 11.7 %cholesky.189 = f32[128,128]{1,0:T(8,128)S(1)} custom-call(f32[128,128]{1,0:T(8,128)S(1)} %convolution_subtract_fusion.8), custom_call_target="Cholesky" | custom-call | tf_op jit(solution)/shard_map/jit(cholesky)/cholesky | solution.py:32
  84.9 0.7 compare_reduce_fusion.4
  87.1 4.4 while.12
  87.9 1.4 bitcast_dynamic-update-slice_fusion.7
  90.0 1.4 bitcast_dynamic-update-slice_fusion.7
  91.4 19.7 %custom-call.25 = f32[2,128,128]{1,2,0:T(8,128)S(1)} custom-call(f32[2,128,128]{2,1,0:T(8,128)S(1)} %get-tuple-element.47), custom_call_target="InvertDiagBlocksLowerTriangular" | custom-call | tf_op jit(solution)/shard_map/jit(_solve_triangular)/triangular_solve | solution.py:17
  111.7 0.8 convolution_subtract_fusion.1
  113.0 1.5 fusion.8
  114.6 1.3 convolution_bitcast_fusion.1
  116.0 33.8 %all-reduce.11.cloned.1.call-done = f32[256,256]{0,1:T(8,128)} async-done(((f32[256,256]{0,1:T(8,128)}), f32[256,256]{0,1:T(8,128)}) %all-reduce.11.cloned.1.call-update) | async-done | bytes 262160 | tf_op jit(solution)/shard_map/psum | solution.py:34
  149.8 1.1 copy.7
  150.8 1.0 fusion.21
  151.9 11.7 %cholesky.206 = f32[128,128]{1,0:T(8,128)S(1)} custom-call(f32[128,128]{1,0:T(8,128)S(1)} %cholesky.273), custom_call_target="Cholesky" | custom-call | tf_op jit(solution)/shard_map/jit(cholesky)/cholesky | solution.py:34
  164.2 9.8 %custom-call.26 = f32[1,128,128]{1,2,0:T(8,128)S(1)} custom-call(f32[1,128,128]{2,1,0:T(8,128)S(1)} %get-tuple-element.91), custom_call_target="InvertDiagBlocksLowerTriangular" | custom-call | tf_op jit(solution)/shard_map/jit(cholesky)/cholesky | solution.py:34
  174.6 11.7 %cholesky.223 = f32[128,128]{1,0:T(8,128)S(1)} custom-call(f32[128,128]{1,0:T(8,128)S(1)} %convolution_subtract_fusion.7), custom_call_target="Cholesky" | custom-call | tf_op jit(solution)/shard_map/jit(cholesky)/cholesky | solution.py:34
  186.3 0.7 compare_reduce_fusion.2
  188.3 15.1 %while.13 = (s32[]{:T(128)}, f32[256,256]{1,0:T(8,128)S(1)}, s32[2,2]{1,0:T(2,128)S(1)}, f32[2,128,128]{2,1,0:T(8,128)S(1)}, s32[]{:T(128)}) while((s32[]{:T(128)}, f32[256,256]{1,0:T(8,128)S(1)}, s32[2,2]{1,0:T(2,128)S(1)}, f32[2,128,128]{2,1,0:T(8,128)S(1)}, s32[]{:T(128)}) %tuple.97), condition=%wide.while_cond.clone, body=%wide.while_body.clone.sunk | while | flops 2 | bytes 131189 | solution.py:17
  200.1 1.4 bitcast_dynamic-update-slice_fusion.8
  202.0 1.4 bitcast_dynamic-update-slice_fusion.8
  203.4 19.7 %custom-call.27 = f32[2,128,128]{1,2,0:T(8,128)S(1)} custom-call(f32[2,128,128]{2,1,0:T(8,128)S(1)} %get-tuple-element.48), custom_call_target="InvertDiagBlocksLowerTriangular" | custom-call | tf_op jit(solution)/shard_map/jit(_solve_triangular)/triangular_solve | solution.py:17
  224.7 0.8 dynamic-slice_select_fusion.1
  225.6 40.6 %all-reduce.19.cloned.1.call-done = (f32[384,256]{0,1:T(8,128)}, f32[256,256]{0,1:T(8,128)}) async-done(((f32[384,256]{0,1:T(8,128)}, f32[256,256]{0,1:T(8,128)}), (f32[384,256]{0,1:T(8,128)}, f32[256,256]{0,1:T(8,128)})) %all-reduce.19.cloned.1.call-update) | async-done | bytes 655376 | tf_op jit(solution)/shard_map/psum | solution.py:9
  266.2 1.2 fusion.33
  267.4 1.3 convolution_subtract_fusion.5
  270.7 11.7 %cholesky.240 = f32[128,128]{1,0:T(8,128)S(1)} custom-call(f32[128,128]{1,0:T(8,128)S(1)} %cholesky.276), custom_call_target="Cholesky" | custom-call | tf_op jit(solution)/shard_map/jit(cholesky)/cholesky | solution.py:39
  283.1 9.8 %custom-call.30 = f32[1,128,128]{1,2,0:T(8,128)S(1)} custom-call(f32[1,128,128]{2,1,0:T(8,128)S(1)} %get-tuple-element.87), custom_call_target="InvertDiagBlocksLowerTriangular" | custom-call | tf_op jit(solution)/shard_map/jit(cholesky)/cholesky | solution.py:39
  293.4 11.9 %cholesky.257 = f32[128,128]{1,0:T(8,128)S(1)} custom-call(f32[128,128]{1,0:T(8,128)S(1)} %convolution_subtract_fusion.6), custom_call_target="Cholesky" | custom-call | tf_op jit(solution)/shard_map/jit(cholesky)/cholesky | solution.py:39
  307.4 4.0 while.11
  308.0 1.4 bitcast_dynamic-update-slice_fusion.6
  310.0 1.4 bitcast_dynamic-update-slice_fusion.6
  311.4 19.7 %custom-call.18 = f32[2,128,128]{1,2,0:T(8,128)S(1)} custom-call(f32[2,128,128]{2,1,0:T(8,128)S(1)} %get-tuple-element.28), custom_call_target="InvertDiagBlocksLowerTriangular" | custom-call | tf_op jit(solution)/shard_map/jit(_cho_solve)/triangular_solve | solution.py:39
  332.4 2.3 convolution_bitcast_fusion
  335.4 54.5 %all-reduce.13.cloned.1.call-done = f32[768,256]{0,1:T(8,128)} async-done(((f32[768,256]{0,1:T(8,128)}), f32[768,256]{0,1:T(8,128)}) %all-reduce.13.cloned.1.call-update) | async-done | bytes 786448 | tf_op jit(solution)/shard_map/psum | solution.py:46
  389.9 2.0 fusion.30
  391.9 1.5 fusion.79
  393.8 34.4 %all-reduce.15.cloned.1.call-done = f32[256,256]{1,0:T(8,128)} async-done(((f32[256,256]{1,0:T(8,128)}), f32[256,256]{1,0:T(8,128)}) %all-reduce.15.cloned.1.call-update) | async-done | bytes 262160 | tf_op jit(solution)/shard_map/psum | solution.py:48
  428.2 1.5 fusion.29
  429.8 0.9 fusion.7
  430.7 0.8 dynamic-slice_select_fusion
  431.8 1.2 convolution_negate_fusion
  433.0 35.4 %all-reduce.17.cloned.1.call-done = f32[384,256]{0,1:T(8,128)} async-done(((f32[384,256]{0,1:T(8,128)}), f32[384,256]{0,1:T(8,128)}) %all-reduce.17.cloned.1.call-update) | async-done | bytes 393232 | tf_op jit(solution)/shard_map/psum | solution.py:9
  468.4 4.8 fusion.4
  (88 shorter events, 14.8 us)
Async XLA Ops:
  7.2 41.8 %all-reduce.9.cloned.1.call-start = ((), (), s32[]{:S(2)}) async-start(), calls=%async_computation | async-start | bytes 524288 | tf_op jit(solution)/shard_map/psum | solution.py:31
  10.8 139.0 %all-reduce.11.cloned.1.call-start = ((), (), s32[]{:S(2)}) async-start(), calls=%async_computation.1 | async-start | bytes 524288 | tf_op jit(solution)/shard_map/psum | solution.py:34
  72.6 38.5 %copy-start = (f32[768,256]{1,0:T(8,128)S(1)}, f32[768,256]{1,0:T(8,128)}, u32[]{:S(2)}) copy-start(f32[768,256]{1,0:T(8,128)} %param.8) | copy-start | bytes 2359300
  84.9 26.2 %copy-start.2 = (f32[256,256]{1,0:T(8,128)}, f32[256,256]{1,0:T(8,128)S(1)}, u32[]{:S(2)}) copy-start(f32[256,256]{1,0:T(8,128)S(1)} %get-tuple-element.93) | copy-start | bytes 786436
  114.5 151.6 %all-reduce.19.cloned.1.call-start = ((), (), s32[]{:S(2)}) async-start(), calls=%async_computation.5 | async-start | bytes 1310720 | tf_op jit(solution)/shard_map/psum | solution.py:9
  186.3 37.3 %copy-start.4 = (f32[256,256]{1,0:T(8,128)}, f32[256,256]{1,0:T(8,128)S(1)}, u32[]{:S(2)}) copy-start(f32[256,256]{1,0:T(8,128)S(1)} %get-tuple-element.89) | copy-start | bytes 786436
  225.5 164.4 %all-reduce.13.cloned.1.call-start = ((), (), s32[]{:S(2)}) async-start(), calls=%async_computation.2 | async-start | bytes 1572864 | tf_op jit(solution)/shard_map/psum | solution.py:46
  307.4 25.0 %copy-start.1 = (f32[768,384]{1,0:T(8,128)S(1)}, f32[768,384]{1,0:T(8,128)}, u32[]{:S(2)}) copy-start(f32[768,384]{1,0:T(8,128)} %param.7) | copy-start | bytes 3538948
  307.4 25.0 %copy-start.6 = (f32[384,256]{0,1:T(8,128)S(1)}, f32[384,256]{0,1:T(8,128)}, u32[]{:S(2)}) copy-start(f32[384,256]{0,1:T(8,128)} %get-tuple-element.76) | copy-start | bytes 1179652
  334.8 93.4 %all-reduce.15.cloned.1.call-start = ((), (), s32[]{:S(2)}) async-start(), calls=%async_computation.3 | async-start | bytes 524288 | tf_op jit(solution)/shard_map/psum | solution.py:48
  393.5 74.9 %all-reduce.17.cloned.1.call-start = ((), (), s32[]{:S(2)}) async-start(), calls=%async_computation.4 | async-start | bytes 786432 | tf_op jit(solution)/shard_map/psum | solution.py:9
  430.6 1.0 copy-start.3
  430.6 1.2 copy-start.5
Sparse Core Ops, SparseCore 0:
  10.9 37.9 all-reduce.8
  114.7 35.0 all-reduce.10
  225.7 40.4 all-reduce.18
  334.9 54.9 all-reduce.12
  393.6 34.5 all-reduce.14
  431.6 36.7 all-reduce.16
where the time goes:
time: 489 us; the launch traced here: 480 us
  waiting for transfers between devices  237 us (48%)
  other arithmetic  166 us (34%)
  matrix products  31.5 us (6%)
  between operations  19 us (4%)
  local copies, waits for them, and re-layouts  14.7 us (3%)
  loops' own time  11.5 us (2%)
    psum x2, waiting for transfers between devices, from_root(): return lax.psum(jnp.where(mine, shard, jnp.zeros_like(shard)), axis)  76 us
    psum x1, waiting for transfers between devices, shards(): products = lax.psum(partial_rows, 'col')  54.5 us
    another operation x5, other arithmetic, lower_solve(): return jax.scipy.linalg.solve_triangular(low, rows.T, lower=True).T  39.4 us
    psum x1, waiting for transfers between devices, shards(): gram, top_rows = lax.psum((mult(panel.T, panel), top_part), 'row')  38.1 us
    another operation x7, other arithmetic, shards(): jnp.linalg.cholesky(mult(lead, lead.T))  34.8 us
    another operation x7, other arithmetic, shards(): second_low = jnp.linalg.cholesky(lax.psum(mult(half.T, half), 'row'))  34.6 us
    psum x1, waiting for transfers between devices, shards(): coupling = lax.psum(mult(reflectors.T, images), 'row')  34.4 us
    another operation x6, other arithmetic, shards(): first_low = jnp.linalg.cholesky(gram)  34 us
  transfers between devices with their start and end apart: 6, of which 6 were waited for; matrix products, arithmetic and copies ran while one was open for 1% of the time, Pallas kernels for 0%

commit v1 on v0

v1 whole, which is shorter than its diff:
```python
import functools

import jax
import jax.numpy as jnp
from jax import lax
from jax.experimental import pallas as pl
from jax.experimental.pallas import tpu as pltpu
from jax.sharding import PartitionSpec as P

SUB = 8
LANE = 128
BLOCK = 32
HIGHEST = lax.Precision.HIGHEST
HIGH = lax.Precision.HIGH


def mult(left, right, dims=((1,), (0,)), precision=HIGHEST):
    return lax.dot_general(
        left, right, (dims, ((), ())), precision=precision, preferred_element_type=jnp.float32
    )


def chol_kernel(gram_ref, upper_ref, inv_ref, work_ref):
    size = gram_ref.shape[0]
    tiles = size // LANE
    groups = BLOCK // SUB
    lanes = lax.broadcasted_iota(jnp.int32, (SUB, LANE), 1)
    work_ref[...] = gram_ref[...]

    def spread(row):
        return jnp.broadcast_to(row, (SUB, LANE))

    for first in range(0, size, BLOCK):
        rows = [
            [
                work_ref[first + SUB * g : first + SUB * (g + 1), LANE * t : LANE * (t + 1)]
                for t in range(tiles)
            ]
            for g in range(groups)
        ]
        for g in range(groups):
            col = first + SUB * g
            home, low = divmod(col, LANE)
            in_block = (lanes >= low) & (lanes < low + SUB)
            flat = [[spread(rows[g][t][k : k + 1, :]) for t in range(tiles)] for k in range(SUB)]
            diag = [
                [spread(flat[k][home][:, low + i : low + i + 1]) for i in range(k + 1)]
                for k in range(SUB)
            ]
            unit = [jnp.where(lanes == low + k, 1.0, 0.0) for k in range(SUB)]
            later = range(g + 1, groups)
            cols = {
                q: [spread(rows[q][home][:, low + i : low + i + 1]) for i in range(SUB)]
                for q in later
            }
            for q in later:
                rows[q][home] = jnp.where(in_block, 0.0, rows[q][home])
            for i in range(SUB):
                recip = 1.0 / diag[i][i]
                steps = [None] * SUB
                for k in range(i + 1, SUB):
                    steps[k] = diag[k][i] * recip
                for k in range(i + 1, SUB):
                    for j in range(i + 1, k + 1):
                        diag[k][j] = diag[k][j] - steps[k] * diag[j][i]
                for k in range(i + 1, SUB):
                    for t in range(tiles):
                        flat[k][t] = flat[k][t] - steps[k] * flat[i][t]
                    unit[k] = unit[k] - steps[k] * unit[i]
                for q in later:
                    step = cols[q][i] * recip
                    for j in range(i + 1, SUB):
                        cols[q][j] = cols[q][j] - step * diag[j][i]
                    for t in range(tiles):
                        source = flat[i][t]
                        if t == home:
                            source = jnp.where(in_block, unit[i], source)
                        rows[q][t] = rows[q][t] - step * source
            for k in range(SUB):
                scale = lax.rsqrt(diag[k][k])
                for t in range(tiles):
                    scaled = flat[k][t] * scale
                    if t < home:
                        up, inv = jnp.zeros_like(scaled), scaled
                    elif t > home:
                        up, inv = scaled, jnp.zeros_like(scaled)
                    else:
                        up = jnp.where(lanes >= low + k, scaled, 0.0)
                        inv = jnp.where(in_block, unit[k] * scale, scaled)
                        inv = jnp.where(lanes < low + SUB, inv, 0.0)
                    upper_ref[col + k : col + k + 1, LANE * t : LANE * (t + 1)] = up[0:1]
                    inv_ref[col + k : col + k + 1, LANE * t : LANE * (t + 1)] = inv[0:1]
        rest = first + BLOCK
        if rest == size:
            break
        start = rest // LANE * LANE
        left = upper_ref[first:rest, start:size]
        wide = lax.broadcasted_iota(jnp.int32, (BLOCK, size), 1)
        right = jnp.where(wide < rest, inv_ref[first:rest, :], upper_ref[first:rest, :])
        change = mult(left, right, ((0,), (0,)))
        below = lax.broadcasted_iota(jnp.int32, (size - rest, size), 1)
        old = jnp.where((below >= first) & (below < rest), 0.0, work_ref[rest:size, :])
        work_ref[rest:size, :] = old - change[rest - start :, :]


def cholesky(gram):
    size = gram.shape[0]
    shape = jax.ShapeDtypeStruct((size, size), jnp.float32)
    return pl.pallas_call(
        chol_kernel,
        out_shape=(shape, shape),
        scratch_shapes=[pltpu.VMEM((size, size), jnp.float32)],
        compiler_params=pltpu.CompilerParams(vmem_limit_bytes=32 * 2**20),
        name="cholesky_inverse",
    )(gram)


def inverse_kernel(mat_ref, out_ref):
    size = mat_ref.shape[0]
    row = lax.broadcasted_iota(jnp.int32, (size, size), 0)
    col = lax.broadcasted_iota(jnp.int32, (size, size), 1)
    ident = jnp.where(row == col, 1.0, 0.0)
    mat = mat_ref[...]

    def residual(guess):
        return ident - mult(mat, guess)

    def step(state):
        count, guess, rest, _ = state
        guess = guess + mult(guess, rest)
        rest = residual(guess)
        return count + 1, guess, rest, jnp.max(jnp.abs(rest))

    def more(state):
        count, _, _, worst = state
        return (worst > 3e-6) & (count < 40)

    guess = 0.5 * ident
    rest = ident - 0.5 * mat
    for _ in range(4):
        guess = guess + mult(guess, rest)
        rest = mult(rest, rest)
    guess = guess + mult(guess, rest)
    rest = residual(guess)
    state = (jnp.int32(0), guess, rest, jnp.max(jnp.abs(rest)))
    out_ref[...] = lax.while_loop(more, step, state)[1]


def inverse(mat):
    return pl.pallas_call(
        inverse_kernel,
        out_shape=jax.ShapeDtypeStruct(mat.shape, jnp.float32),
        compiler_params=pltpu.CompilerParams(vmem_limit_bytes=32 * 2**20),
        name="wy_inverse",
    )(mat)


def pair_sum(value, axis, size):
    terms = [value]
    for hop in range(1, size):
        terms.append(lax.ppermute(value, axis, [(i, i ^ hop) for i in range(size)]))
    while len(terms) > 1:
        terms = [terms[i] + terms[i + 1] for i in range(0, len(terms), 2)]
    return terms[0]


def scatter_sum(value, axis, size):
    place = lax.axis_index(axis)
    piece = value.shape[0] // size
    terms = []
    for hop in range(size):
        part = lax.dynamic_slice_in_dim(value, (place ^ hop) * piece, piece, 0)
        if hop:
            part = lax.ppermute(part, axis, [(i, i ^ hop) for i in range(size)])
        terms.append(part)
    while len(terms) > 1:
        terms = [terms[i] + terms[i + 1] for i in range(0, len(terms), 2)]
    return terms[0]


def swap_gather(piece, axis, size):
    place = lax.axis_index(axis)
    whole = jnp.zeros((size * piece.shape[0], piece.shape[1]), piece.dtype)
    for hop in range(size):
        part = piece
        if hop:
            part = lax.ppermute(piece, axis, [(i, i ^ hop) for i in range(size)])
        whole = lax.dynamic_update_slice_in_dim(whole, part, (place ^ hop) * piece.shape[0], 0)
    return whole


def gather_cols(piece, size):
    return lax.all_to_all(jnp.concatenate([piece] * size, axis=0), "col", 0, 0, tiled=True)


def spread_rows(value, owners, rows, cols):
    row_place = lax.axis_index("row")
    col_place = lax.axis_index("col")
    owner = jnp.asarray(owners, jnp.int32)[col_place]
    value = jnp.where(row_place == owner, value, 0.0)
    hop = rows // 2
    done = [0]
    while hop:
        pairs = []
        for c in range(cols):
            for d in done:
                source = owners[c] ^ d
                pairs.append((source * cols + c, (source ^ hop) * cols + c))
        value = value + lax.ppermute(value, ("row", "col"), pairs)
        done = done + [d ^ hop for d in done]
        hop //= 2
    return value


def shards(rows, cols, hamiltonian, panel):
    rows_dev, width = panel.shape
    cols_dev = hamiltonian.shape[1]
    row_place = lax.axis_index("row")
    col_place = lax.axis_index("col")
    strip = width // cols

    def sum_strips(strip_value):
        return gather_cols(pair_sum(strip_value, "row", rows), cols)

    def strip_of(array):
        return lax.dynamic_slice_in_dim(array, col_place * strip, strip, 1)

    gram = sum_strips(mult(strip_of(panel), panel, ((0,), (0,))))

    owners = [c * cols_dev // rows_dev for c in range(cols)]
    owner = col_place * cols_dev // rows_dev
    offset = col_place * cols_dev - owner * rows_dev
    slab = lax.dynamic_slice_in_dim(panel, offset, cols_dev, 0)
    top_strip = lax.dynamic_slice_in_dim(panel[:width], col_place * strip, strip, 0)
    gram, slab, top_strip = lax.optimization_barrier((gram, slab, top_strip))
    panel_cols = spread_rows(slab, owners, rows, cols)
    panel_top = gather_cols(spread_rows(top_strip, [0] * cols, rows, cols), cols)

    first_upper, first_inv = cholesky(gram)
    half = mult(panel, first_inv, ((1,), (1,)))
    half_cols = mult(panel_cols, first_inv, ((1,), (1,)))
    half_top = mult(panel_top, first_inv, ((1,), (1,)))

    gram2 = sum_strips(mult(strip_of(half), half, ((0,), (0,))))
    second_upper, _ = cholesky(gram2)
    band_block = -mult(second_upper, first_upper)

    def with_upper(block, first_row):
        lead_rows = block[:width] + jnp.where(first_row == 0, second_upper, 0.0)
        return jnp.concatenate([lead_rows, block[width:]], axis=0)

    left = with_upper(half, row_place)
    right = with_upper(half_cols, col_place)
    factor = inverse(gram2 + mult(half_top, second_upper, ((0,), (0,))))

    part = mult(hamiltonian, right, precision=HIGH)
    part_cols = mult(hamiltonian, left, ((0,), (0,)), precision=HIGH)
    part_coupling = mult(left, part, ((0,), (0,)), precision=HIGH)
    piece = rows_dev // cols
    packed = jnp.concatenate(
        [part.reshape(cols, piece, width), part_coupling.reshape(cols, strip, width)], axis=1
    ).reshape(cols * (piece + strip), width)
    packed = lax.all_to_all(packed, "col", 0, 0, tiled=True)
    packed = packed.reshape(cols, piece + strip, width).sum(axis=0)
    products = gather_cols(packed[:piece], cols)
    coupling = sum_strips_from(packed[piece:], rows, cols)
    products_cols = swap_gather(scatter_sum(part_cols, "row", rows), "row", rows)

    middle = mult(factor, mult(coupling, factor), ((0,), (0,)), precision=HIGH)
    near = mult(products_cols, factor, precision=HIGH) - mult(right, middle, precision=HIGH)
    far = mult(right, factor, ((1,), (1,)), precision=HIGH)
    updated = hamiltonian - mult(
        jnp.concatenate([left, products], axis=1),
        jnp.concatenate([near, far], axis=1),
        ((1,), (1,)),
        precision=HIGH,
    )
    return (updated, band_block)


def sum_strips_from(strip_value, rows, cols):
    return gather_cols(pair_sum(strip_value, "row", rows), cols)


def solution(mesh):
    in_specs = (P("row", "col"), P("row", None))
    out_specs = (P("row", "col"), P())
    body = functools.partial(shards, mesh.shape["row"], mesh.shape["col"])
    return jax.shard_map(body, mesh=mesh, in_specs=in_specs, out_specs=out_specs, check_vma=False)
```

time: 489 us -> 188 us (0.38); the launches traced: 480 us -> 187 us
  waiting for transfers between devices: 237 us -> 51.6 us
  other arithmetic: 166 us -> 8.34 us
  starting transfers between devices: 0.5 us -> 58.7 us
  Pallas kernels: 0 us -> 23.8 us
  between operations: 19 us -> 1.87 us
  matrix products: 31.5 us -> 18.7 us
  loops' own time: 11.5 us -> 0 us
  local copies, waits for them, and re-layouts: 14.7 us -> 23.9 us
    psum x6 -> x0, waiting for transfers between devices: 237 us -> none  [the longest x2 76 us: from_root(): return lax.psum(jnp.where(mine, shard, jnp.zeros_like(shard)), axis)]
    another operation x27 -> x0, other arithmetic: 163 us -> none  [the longest x5 39.4 us: lower_solve(): return jax.scipy.linalg.solve_triangular(low, rows.T, lower=True).T]
    ppermute x0 -> x19, starting transfers between devices: none -> 34 us  [the longest x9 14.1 us: pair_sum(): terms.append(lax.ppermute(value, axis, [(i, i ^ hop) for i in range(size)]))]
    ppermute x0 -> x19, waiting for transfers between devices: none -> 27.9 us  [the longest x3 8.8 us: swap_gather(): part = lax.ppermute(piece, axis, [(i, i ^ hop) for i in range(size)])]
    all_to_all x0 -> x6, starting transfers between devices: none -> 24.8 us  [the longest x5 17.8 us: gather_cols(): lax.all_to_all(jnp.concatenate([piece] * size, axis=0), 'col', 0, 0, tile...]
    pallas_call x0 -> x3, Pallas kernels: none -> 23.8 us  [the longest x2 20.1 us: cholesky(): pl.pallas_call(chol_kernel, out_shape=(shape, shape), scratch_shapes=[plt...]
    all_to_all x0 -> x6, waiting for transfers between devices: none -> 23.8 us  [the longest x5 23.8 us: gather_cols(): lax.all_to_all(jnp.concatenate([piece] * size, axis=0), 'col', 0, 0, tile...]
    unnamed x14 -> x57, local copies, waits for them, and re-layouts: 0.38 us -> 16.1 us
  transfers between devices with their start and end apart: 6 -> 25, of which waited for: 6 -> 12; matrix products, arithmetic and copies ran while one was open for 1% -> 12% of each run, Pallas kernels for 0% -> 8%
where the time goes in v1:
time: 188 us; the launch traced here: 187 us
  starting transfers between devices  58.7 us (31%)
  waiting for transfers between devices  51.6 us (27%)
  local copies, waits for them, and re-layouts  23.9 us (13%)
  Pallas kernels  23.8 us (13%)
  matrix products  18.7 us (10%)
  other arithmetic  8.34 us (4%)
    all_to_all x5, waiting for transfers between devices, gather_cols(): lax.all_to_all(jnp.concatenate([piece] * size, axis=0), 'col', 0, 0, tile...  23.8 us
    pallas_call x2, Pallas kernels, cholesky(): pl.pallas_call(chol_kernel, out_shape=(shape, shape), scratch_shapes=[plt...  20.1 us
    dot_general x16, matrix products, mult(): lax.dot_general(left, right, (dims, ((), ())), precision=precision, prefe...  18.7 us
    all_to_all x5, starting transfers between devices, gather_cols(): lax.all_to_all(jnp.concatenate([piece] * size, axis=0), 'col', 0, 0, tile...  17.8 us
    unnamed x57, local copies, waits for them, and re-layouts  16.1 us
    ppermute x9, starting transfers between devices, pair_sum(): terms.append(lax.ppermute(value, axis, [(i, i ^ hop) for i in range(size)]))  14.1 us
    ppermute x4, starting transfers between devices, spread_rows(): value = value + lax.ppermute(value, ('row', 'col'), pairs)  9.42 us
    ppermute x3, waiting for transfers between devices, swap_gather(): part = lax.ppermute(piece, axis, [(i, i ^ hop) for i in range(size)])  8.8 us
  transfers between devices with their start and end apart: 25, of which 12 were waited for; matrix products, arithmetic and copies ran while one was open for 12% of the time, Pallas kernels for 8%

profile of v1, /device:TPU:0, one launch (start us, length us, event | category | flops | bytes accessed | tf_op | source)
XLA Modules:
  0.0 187.0 jit_solution(16906899492259337829)
XLA Ops:
  0.7 2.2 %fusion.16 = f32[32,256]{1,0:T(8,128)S(1)} fusion(f32[768,256]{1,0:T(8,128)} %param.5, s32[]{:T(128)S(6)} %select_n.63), kind=kOutput, calls=%fused_computation.20 | convolution fusion | flops 75497472 | bytes 1212420 | tf_op jit(solution)/shard_map/dot_general | solution.py:18
  2.9 4.1 %collective-permute-start.1 = (f32[32,256]{1,0:T(8,128)S(1)}, f32[32,256]{1,0:T(8,128)S(1)}, u32[]{:S(2)}, u32[]{:S(2)}) collective-permute-start(f32[32,256]{1,0:T(8,128)S(1)} %fusion.16), channel_id=1, source_target_pairs={{0,16},{8,24},{16,0},{24,8},{1,17},{9,25},{17,1},{25,9},{2,18},{10... | collective-permute-start | bytes 98312 | tf_op jit(solution)/shard_map/ppermute | solution.py:161
  7.0 1.3 collective-permute-start.2
  9.9 2.9 %collective-permute-done.2 = f32[32,256]{1,0:T(8,128)S(1)} collective-permute-done((f32[32,256]{1,0:T(8,128)S(1)}, f32[32,256]{1,0:T(8,128)S(1)}, u32[]{:S(2)}, u32[]{:S(2)}) %collective-permute-start.2) | collective-permute-done | bytes 32800 | tf_op jit(solution)/shard_map/ppermute | solution.py:161
  17.7 3.7 %all-to-all-start = ((f32[8,32,256]{2,1,0:T(8,128)}), f32[8,32,256]{2,1,0:T(8,128)S(1)}, u32[]{:S(2)}, u32[]{:S(2)}) async-start(f32[8,32,256]{2,1,0:T(8,128)} %bitcast), calls=%async_computation | async-start | bytes 524288 | tf_op jit(solution)/shard_map/all_to_all | solution.py:193
  21.5 6.9 %all-to-all-done = f32[8,32,256]{2,1,0:T(8,128)S(1)} async-done(((f32[8,32,256]{2,1,0:T(8,128)}), f32[8,32,256]{2,1,0:T(8,128)S(1)}, u32[]{:S(2)}, u32[]{:S(2)}) %all-to-all-start) | async-done | bytes 262176 | tf_op jit(solution)/shard_map/all_to_all | solution.py:193
  28.3 9.7 %cholesky_inverse.2 = (f32[256,256]{1,0:T(8,128)S(1)}, f32[256,256]{1,0:T(8,128)S(1)}) custom-call(f32[256,256]{1,0:T(8,128)S(1)} %bitcast.49), custom_call_target="tpu_custom_call" | custom-call | tf_op jit(solution)/shard_map/cholesky_inverse/pallas_call | solution.py:109
  39.7 1.3 collective-permute-start.4
  42.0 1.2 collective-permute-start.3
  43.2 4.8 %collective-permute-start.6 = (f32[384,256]{1,0:T(8,128)S(1)}, f32[384,256]{1,0:T(8,128)}, u32[]{:S(2)}, u32[]{:S(2)}) collective-permute-start(f32[384,256]{1,0:T(8,128)S(1)} %broadcast_select_fusion), channel_id=1, source_target_pairs={{0,16},{1,17},{10,26},{11,27},{20,4},{21,5},{30,14},{31,15}} | collective-permute-start | bytes 1179656 | tf_op jit(solution)/shard_map/ppermute | solution.py:209
  48.0 1.1 copy.12
  50.3 1.3 collective-permute-start.14
  55.9 1.3 collective-permute-start.15
  57.9 3.4 %all-to-all-start.1 = ((f32[8,32,256]{2,1,0:T(8,128)}), f32[8,32,256]{2,1,0:T(8,128)S(1)}, u32[]{:S(2)}, u32[]{:S(2)}) async-start(f32[8,32,256]{2,1,0:T(8,128)} %bitcast.3), calls=%async_computation.1 | async-start | bytes 524288 | tf_op jit(solution)/shard_map/all_to_all | solution.py:193
  66.1 2.0 %all-to-all-done.1 = f32[8,32,256]{2,1,0:T(8,128)S(1)} async-done(((f32[8,32,256]{2,1,0:T(8,128)}), f32[8,32,256]{2,1,0:T(8,128)S(1)}, u32[]{:S(2)}, u32[]{:S(2)}) %all-to-all-start.1) | async-done | bytes 262176 | tf_op jit(solution)/shard_map/all_to_all | solution.py:193
  68.2 3.6 %all-to-all-start.4 = ((f32[8,32,256]{2,1,0:T(8,128)}), f32[8,32,256]{2,1,0:T(8,128)S(1)}, u32[]{:S(2)}, u32[]{:S(2)}) async-start(f32[8,32,256]{2,1,0:T(8,128)} %bitcast.15), calls=%async_computation.4 | async-start | bytes 524288 | tf_op jit(solution)/shard_map/all_to_all | solution.py:193
  71.8 10.4 %cholesky_inverse.3 = (f32[256,256]{1,0:T(8,128)S(1)}, f32[256,256]{1,0:T(8,128)}) custom-call(f32[256,256]{1,0:T(8,128)S(1)} %bitcast.47), custom_call_target="tpu_custom_call" | custom-call | tf_op jit(solution)/shard_map/cholesky_inverse/pallas_call | solution.py:109
  82.1 1.1 convolution_negate_fusion
  84.3 2.0 %collective-permute-start.7 = (f32[384,256]{1,0:T(8,128)S(1)}, f32[384,256]{1,0:T(8,128)}, u32[]{:S(2)}, u32[]{:S(2)}) collective-permute-start(f32[384,256]{1,0:T(8,128)S(1)} %fusion.59), channel_id=1, source_target_pairs={{0,8},{16,24},{1,9},{17,25},{10,2},{26,18},{11,3},{27,19},{20,28},... | collective-permute-start | bytes 1179656 | tf_op jit(solution)/shard_map/ppermute | solution.py:209
  87.4 3.8 %wy_inverse.1 = f32[256,256]{1,0:T(8,128)S(1)} custom-call(f32[256,256]{1,0:T(8,128)S(1)} %convolution_add_fusion.mat_ref), custom_call_target="tpu_custom_call" | custom-call | tf_op jit(solution)/shard_map/wy_inverse/pallas_call | solution.py:150
  91.1 3.5 %collective-permute-done.7 = f32[384,256]{1,0:T(8,128)} collective-permute-done((f32[384,256]{1,0:T(8,128)S(1)}, f32[384,256]{1,0:T(8,128)}, u32[]{:S(2)}, u32[]{:S(2)}) %collective-permute-start.7) | collective-permute-done | bytes 393248 | tf_op jit(solution)/shard_map/ppermute | solution.py:209
  94.6 1.5 fusion.14
  97.2 1.2 fusion.20
  98.4 1.6 fusion.12
  100.8 1.2 copy.13
  102.0 2.2 %pad_maximum_fusion = f32[8,128,256]{2,1,0:T(8,128)} fusion(f32[8,32,256]{2,1,0:T(8,128)S(1)} %bitcast.57, f32[8,96,256]{2,1,0:T(8,128)} %bitcast.54), kind=kLoop, calls=%fused_computation.10 | loop fusion | flops 262144 | bytes 2097152 | tf_op jit(solution)/shard_map/concatenate | solution.py:260
  104.2 6.9 %all-to-all-start.2 = ((f32[8,128,256]{2,1,0:T(8,128)}), f32[8,128,256]{2,1,0:T(8,128)}, u32[]{:S(2)}, u32[]{:S(2)}) async-start(f32[8,128,256]{2,1,0:T(8,128)} %pad_maximum_fusion), calls=%async_computation.2 | async-start | bytes 2097152 | tf_op jit(solution)/shard_map/all_to_all | solution.py:263
  111.4 2.3 %collective-permute-start.9 = (f32[96,256]{0,1:T(8,128)S(1)}, f32[96,256]{0,1:T(8,128)S(1)}, u32[]{:S(2)}, u32[]{:S(2)}) collective-permute-start(f32[96,256]{0,1:T(8,128)S(1)} %get-tuple-element.23), channel_id=1, source_target_pairs={{0,16},{8,24},{16,0},{24,8},{1,17},{9,25},{17,1},{25,9},{2,18},{10... | collective-permute-start | bytes 294920 | tf_op jit(solution)/shard_map/ppermute | solution.py:174
  113.7 2.0 %collective-permute-start.10 = (f32[96,256]{0,1:T(8,128)S(1)}, f32[96,256]{0,1:T(8,128)S(1)}, u32[]{:S(2)}, u32[]{:S(2)}) collective-permute-start(f32[96,256]{0,1:T(8,128)S(1)} %get-tuple-element.22), channel_id=1, source_target_pairs={{0,24},{8,16},{16,8},{24,0},{1,25},{9,17},{17,9},{25,1},{2,26},{10... | collective-permute-start | bytes 294920 | tf_op jit(solution)/shard_map/ppermute | solution.py:174
  115.7 1.1 fusion.18
  116.9 3.2 %collective-permute-done.8 = f32[96,256]{0,1:T(8,128)S(1)} collective-permute-done((f32[96,256]{0,1:T(8,128)S(1)}, f32[96,256]{0,1:T(8,128)S(1)}, u32[]{:S(2)}, u32[]{:S(2)}) %collective-permute-start.8) | collective-permute-done | bytes 98336 | tf_op jit(solution)/shard_map/ppermute | solution.py:174
  120.1 4.6 %collective-permute-done.10 = f32[96,256]{0,1:T(8,128)S(1)} collective-permute-done((f32[96,256]{0,1:T(8,128)S(1)}, f32[96,256]{0,1:T(8,128)S(1)}, u32[]{:S(2)}, u32[]{:S(2)}) %collective-permute-start.10) | collective-permute-done | bytes 98336 | tf_op jit(solution)/shard_map/ppermute | solution.py:174
  124.9 2.6 %collective-permute-start.11 = (f32[96,256]{0,1:T(8,128)S(1)}, f32[96,256]{0,1:T(8,128)S(1)}, u32[]{:S(2)}, u32[]{:S(2)}) collective-permute-start(f32[96,256]{0,1:T(8,128)S(1)} %fusion.21), channel_id=1, source_target_pairs={{0,8},{8,0},{16,24},{24,16},{1,9},{9,1},{17,25},{25,17},{2,10},{10... | collective-permute-start | bytes 294920 | tf_op jit(solution)/shard_map/ppermute | solution.py:187
  127.5 2.0 %collective-permute-start.12 = (f32[96,256]{0,1:T(8,128)S(1)}, f32[96,256]{0,1:T(8,128)S(1)}, u32[]{:S(2)}, u32[]{:S(2)}) collective-permute-start(f32[96,256]{0,1:T(8,128)S(1)} %fusion.21), channel_id=1, source_target_pairs={{0,16},{8,24},{16,0},{24,8},{1,17},{9,25},{17,1},{25,9},{2,18},{10... | collective-permute-start | bytes 294920 | tf_op jit(solution)/shard_map/ppermute | solution.py:187
  129.5 1.4 collective-permute-start.13
  130.9 2.1 %collective-permute-done.11 = f32[96,256]{0,1:T(8,128)S(1)} collective-permute-done((f32[96,256]{0,1:T(8,128)S(1)}, f32[96,256]{0,1:T(8,128)S(1)}, u32[]{:S(2)}, u32[]{:S(2)}) %collective-permute-start.11) | collective-permute-done | bytes 98336 | tf_op jit(solution)/shard_map/ppermute | solution.py:187
  133.2 6.7 %collective-permute-done.12 = f32[96,256]{0,1:T(8,128)S(1)} collective-permute-done((f32[96,256]{0,1:T(8,128)S(1)}, f32[96,256]{0,1:T(8,128)S(1)}, u32[]{:S(2)}, u32[]{:S(2)}) %collective-permute-start.12) | collective-permute-done | bytes 98336 | tf_op jit(solution)/shard_map/ppermute | solution.py:187
  140.1 1.4 reduce_sum.9
  141.6 4.2 %collective-permute-start.17 = (f32[32,256]{1,0:T(8,128)S(1)}, f32[32,256]{1,0:T(8,128)S(1)}, u32[]{:S(2)}, u32[]{:S(2)}) collective-permute-start(f32[32,256]{1,0:T(8,128)S(1)} %slice.33), channel_id=1, source_target_pairs={{0,16},{8,24},{16,0},{24,8},{1,17},{9,25},{17,1},{25,9},{2,18},{10... | collective-permute-start | bytes 98312 | tf_op jit(solution)/shard_map/ppermute | solution.py:161
  146.6 1.1 collective-permute-done.17
  147.7 3.8 %collective-permute-done.18 = f32[32,256]{1,0:T(8,128)S(1)} collective-permute-done((f32[32,256]{1,0:T(8,128)S(1)}, f32[32,256]{1,0:T(8,128)S(1)}, u32[]{:S(2)}, u32[]{:S(2)}) %collective-permute-start.18) | collective-permute-done | bytes 32800 | tf_op jit(solution)/shard_map/ppermute | solution.py:161
  156.3 3.6 %all-to-all-start.5 = ((f32[8,32,256]{2,1,0:T(8,128)}), f32[8,32,256]{2,1,0:T(8,128)S(1)}, u32[]{:S(2)}, u32[]{:S(2)}) async-start(f32[8,32,256]{2,1,0:T(8,128)} %bitcast.17), calls=%async_computation.5 | async-start | bytes 524288 | tf_op jit(solution)/shard_map/all_to_all | solution.py:193
  161.2 5.6 %all-to-all-done.5 = f32[8,32,256]{2,1,0:T(8,128)S(1)} async-done(((f32[8,32,256]{2,1,0:T(8,128)}), f32[8,32,256]{2,1,0:T(8,128)S(1)}, u32[]{:S(2)}, u32[]{:S(2)}) %all-to-all-start.5) | async-done | bytes 262176 | tf_op jit(solution)/shard_map/all_to_all | solution.py:193
  167.5 3.5 %all-to-all-start.3 = ((f32[8,96,256]{2,1,0:T(8,128)}), f32[8,96,256]{2,1,0:T(8,128)S(1)}, u32[]{:S(2)}, u32[]{:S(2)}) async-start(f32[8,96,256]{2,1,0:T(8,128)} %bitcast.58), calls=%async_computation.3 | async-start | bytes 1572864 | tf_op jit(solution)/shard_map/all_to_all | solution.py:193
  171.1 1.4 fusion.34
  173.3 1.1 convolution_subtract_fusion
  174.4 9.3 %all-to-all-done.3 = f32[8,96,256]{2,1,0:T(8,128)S(1)} async-done(((f32[8,96,256]{2,1,0:T(8,128)}), f32[8,96,256]{2,1,0:T(8,128)S(1)}, u32[]{:S(2)}, u32[]{:S(2)}) %all-to-all-start.3) | async-done | bytes 786464 | tf_op jit(solution)/shard_map/all_to_all | solution.py:193
  183.6 3.4 %fusion.6 = f32[768,384]{1,0:T(8,128)} fusion(f32[768,384]{1,0:T(8,128)S(1)} %copy-done, f32[768,256]{1,0:T(8,128)S(1)} %bitcast.51, f32[512,256]{1,0:T(8,128)S(1)} %slice.29, f32[256,256]{1,0:T(8,128)S(1)} %get-tuple-element.25, f32[384,256]{1,0:T(8,128)S(1)} %copy-done.7, f32[384,256]{1,0:T(8,128)} %convolution_subtract_fusion), kind=kOutput, calls=%fused_computation.6 | convolution fusion | flops 907247616 | bytes 4718592 | tf_op jit(solution)/shard_map/dot_general | solution.py:18
  (115 shorter events, 32.5 us)
Async XLA Ops:
  0.6 8.0 %copy-start.12 = (s32[8]{0:T(128)S(1)}, s32[8]{0:T(128)}, u32[]{:S(2)}) copy-start(s32[8]{0:T(128)} %constant.42.clone) | copy-start | bytes 100
  0.6 20.8 %slice-start = ((f32[768,256]{1,0:T(8,128)}), f32[256,256]{1,0:T(8,128)S(1)}, s32[]{:S(2)}) async-start(f32[768,256]{1,0:T(8,128)} %param.5), calls=%async_computation.6 | async-start | bytes 524288 | tf_op jit(solution)/shard_map/slice | solution.py:234
  0.7 20.8 %copy-start.1 = (f32[768,256]{1,0:T(8,128)S(1)}, f32[768,256]{1,0:T(8,128)}, u32[]{:S(2)}) copy-start(f32[768,256]{1,0:T(8,128)} %param.5) | copy-start | bytes 2359300
  2.9 6.9 %collective-permute-start.1 = (f32[32,256]{1,0:T(8,128)S(1)}, f32[32,256]{1,0:T(8,128)S(1)}, u32[]{:S(2)}, u32[]{:S(2)}) collective-permute-start(f32[32,256]{1,0:T(8,128)S(1)} %fusion.16), channel_id=1, source_target_pairs={{0,16},{8,24},{16,0},{24,8},{1,17},{9,25},{17,1},{25,9},{2,18},{10... | collective-permute-start | bytes 98312 | tf_op jit(solution)/shard_map/ppermute | solution.py:161
  7.0 5.7 %collective-permute-start.2 = (f32[32,256]{1,0:T(8,128)S(1)}, f32[32,256]{1,0:T(8,128)S(1)}, u32[]{:S(2)}, u32[]{:S(2)}) collective-permute-start(f32[32,256]{1,0:T(8,128)S(1)} %fusion.16), channel_id=1, source_target_pairs={{0,24},{8,16},{16,8},{24,0},{1,25},{9,17},{17,9},{25,1},{2,26},{10... | collective-permute-start | bytes 98312 | tf_op jit(solution)/shard_map/ppermute | solution.py:161
  8.4 4.4 %collective-permute-start = (f32[32,256]{1,0:T(8,128)S(1)}, f32[32,256]{1,0:T(8,128)S(1)}, u32[]{:S(2)}, u32[]{:S(2)}) collective-permute-start(f32[32,256]{1,0:T(8,128)S(1)} %fusion.16), channel_id=1, source_target_pairs={{0,8},{8,0},{16,24},{24,16},{1,9},{9,1},{17,25},{25,17},{2,10},{10... | collective-permute-start | bytes 98312 | tf_op jit(solution)/shard_map/ppermute | solution.py:161
  17.7 10.7 %all-to-all-start = ((f32[8,32,256]{2,1,0:T(8,128)}), f32[8,32,256]{2,1,0:T(8,128)S(1)}, u32[]{:S(2)}, u32[]{:S(2)}) async-start(f32[8,32,256]{2,1,0:T(8,128)} %bitcast), calls=%async_computation | async-start | bytes 524288 | tf_op jit(solution)/shard_map/all_to_all | solution.py:193
  39.7 11.9 %collective-permute-start.4 = (f32[32,256]{1,0:T(8,128)S(1)}, f32[32,256]{1,0:T(8,128)S(1)}, u32[]{:S(2)}, u32[]{:S(2)}) collective-permute-start(f32[32,256]{1,0:T(8,128)S(1)} %fusion.22), channel_id=1, source_target_pairs={{0,16},{8,24},{16,0},{24,8},{1,17},{9,25},{17,1},{25,9},{2,18},{10... | collective-permute-start | bytes 98312 | tf_op jit(solution)/shard_map/ppermute | solution.py:161
  41.0 10.6 %collective-permute-start.5 = (f32[32,256]{1,0:T(8,128)S(1)}, f32[32,256]{1,0:T(8,128)S(1)}, u32[]{:S(2)}, u32[]{:S(2)}) collective-permute-start(f32[32,256]{1,0:T(8,128)S(1)} %fusion.22), channel_id=1, source_target_pairs={{0,24},{8,16},{16,8},{24,0},{1,25},{9,17},{17,9},{25,1},{2,26},{10... | collective-permute-start | bytes 98312 | tf_op jit(solution)/shard_map/ppermute | solution.py:161
  42.0 9.6 %collective-permute-start.3 = (f32[32,256]{1,0:T(8,128)S(1)}, f32[32,256]{1,0:T(8,128)S(1)}, u32[]{:S(2)}, u32[]{:S(2)}) collective-permute-start(f32[32,256]{1,0:T(8,128)S(1)} %fusion.22), channel_id=1, source_target_pairs={{0,8},{8,0},{16,24},{24,16},{1,9},{9,1},{17,25},{25,17},{2,10},{10... | collective-permute-start | bytes 98312 | tf_op jit(solution)/shard_map/ppermute | solution.py:161
  43.2 40.0 %collective-permute-start.6 = (f32[384,256]{1,0:T(8,128)S(1)}, f32[384,256]{1,0:T(8,128)}, u32[]{:S(2)}, u32[]{:S(2)}) collective-permute-start(f32[384,256]{1,0:T(8,128)S(1)} %broadcast_select_fusion), channel_id=1, source_target_pairs={{0,16},{1,17},{10,26},{11,27},{20,4},{21,5},{30,14},{31,15}} | collective-permute-start | bytes 1179656 | tf_op jit(solution)/shard_map/ppermute | solution.py:209
  50.3 5.7 %collective-permute-start.14 = (f32[32,256]{1,0:T(8,128)S(1)}, f32[32,256]{1,0:T(8,128)S(1)}, u32[]{:S(2)}, u32[]{:S(2)}) collective-permute-start(f32[32,256]{1,0:T(8,128)S(1)} %broadcast_select_fusion.1), channel_id=1, source_target_pairs={{0,16},{1,17},{2,18},{3,19},{4,20},{5,21},{6,22},{7,23}} | collective-permute-start | bytes 98312 | tf_op jit(solution)/shard_map/ppermute | solution.py:209
  55.9 5.3 %collective-permute-start.15 = (f32[32,256]{1,0:T(8,128)S(1)}, f32[32,256]{1,0:T(8,128)S(1)}, u32[]{:S(2)}, u32[]{:S(2)}) collective-permute-start(f32[32,256]{1,0:T(8,128)S(1)} %fusion.58), channel_id=1, source_target_pairs={{0,8},{16,24},{1,9},{17,25},{2,10},{18,26},{3,11},{19,27},{4,12},{... | collective-permute-start | bytes 98312 | tf_op jit(solution)/shard_map/ppermute | solution.py:209
  57.9 10.3 %all-to-all-start.1 = ((f32[8,32,256]{2,1,0:T(8,128)}), f32[8,32,256]{2,1,0:T(8,128)S(1)}, u32[]{:S(2)}, u32[]{:S(2)}) async-start(f32[8,32,256]{2,1,0:T(8,128)} %bitcast.3), calls=%async_computation.1 | async-start | bytes 524288 | tf_op jit(solution)/shard_map/all_to_all | solution.py:193
  68.2 18.2 %all-to-all-start.4 = ((f32[8,32,256]{2,1,0:T(8,128)}), f32[8,32,256]{2,1,0:T(8,128)S(1)}, u32[]{:S(2)}, u32[]{:S(2)}) async-start(f32[8,32,256]{2,1,0:T(8,128)} %bitcast.15), calls=%async_computation.4 | async-start | bytes 524288 | tf_op jit(solution)/shard_map/all_to_all | solution.py:193
  84.3 10.3 %collective-permute-start.7 = (f32[384,256]{1,0:T(8,128)S(1)}, f32[384,256]{1,0:T(8,128)}, u32[]{:S(2)}, u32[]{:S(2)}) collective-permute-start(f32[384,256]{1,0:T(8,128)S(1)} %fusion.59), channel_id=1, source_target_pairs={{0,8},{16,24},{1,9},{17,25},{10,2},{26,18},{11,3},{27,19},{20,28},... | collective-permute-start | bytes 1179656 | tf_op jit(solution)/shard_map/ppermute | solution.py:209
  91.1 6.1 %copy-start = (f32[768,384]{1,0:T(8,128)S(1)}, f32[768,384]{1,0:T(8,128)}, u32[]{:S(2)}) copy-start(f32[768,384]{1,0:T(8,128)} %param.4) | copy-start | bytes 3538948
  96.1 2.3 %copy-start.5 = (f32[128,256]{1,0:T(8,128)}, f32[128,256]{1,0:T(8,128)S(1)}, u32[]{:S(2)}) copy-start(f32[128,256]{1,0:T(8,128)S(1)} %slice.31) | copy-start | bytes 393220
  97.2 18.5 %copy-start.2 = (f32[256,256]{1,0:T(8,128)}, f32[256,256]{1,0:T(8,128)S(1)}, u32[]{:S(2)}) copy-start(f32[256,256]{1,0:T(8,128)S(1)} %get-tuple-element.26) | copy-start | bytes 786436
  104.2 6.9 %copy-start.4 = (f32[256,384]{1,0:T(8,128)S(1)}, f32[256,384]{1,0:T(8,128)}, u32[]{:S(2)}) copy-start(f32[256,384]{1,0:T(8,128)} %fusion.12) | copy-start | bytes 1179652
  104.2 11.6 %copy-start.6 = (f32[128,256]{1,0:T(8,128)S(1)}, f32[128,256]{1,0:T(8,128)}, u32[]{:S(2)}) copy-start(f32[128,256]{1,0:T(8,128)} %copy-done.5) | copy-start | bytes 393220
  104.2 35.9 %all-to-all-start.2 = ((f32[8,128,256]{2,1,0:T(8,128)}), f32[8,128,256]{2,1,0:T(8,128)}, u32[]{:S(2)}, u32[]{:S(2)}) async-start(f32[8,128,256]{2,1,0:T(8,128)} %pad_maximum_fusion), calls=%async_computation.2 | async-start | bytes 2097152 | tf_op jit(solution)/shard_map/all_to_all | solution.py:263
  111.3 8.8 %collective-permute-start.8 = (f32[96,256]{0,1:T(8,128)S(1)}, f32[96,256]{0,1:T(8,128)S(1)}, u32[]{:S(2)}, u32[]{:S(2)}) collective-permute-start(f32[96,256]{0,1:T(8,128)S(1)} %get-tuple-element.24), channel_id=1, source_target_pairs={{0,8},{8,0},{16,24},{24,16},{1,9},{9,1},{17,25},{25,17},{2,10},{10... | collective-permute-start | bytes 294920 | tf_op jit(solution)/shard_map/ppermute | solution.py:174
  111.4 8.7 %collective-permute-start.9 = (f32[96,256]{0,1:T(8,128)S(1)}, f32[96,256]{0,1:T(8,128)S(1)}, u32[]{:S(2)}, u32[]{:S(2)}) collective-permute-start(f32[96,256]{0,1:T(8,128)S(1)} %get-tuple-element.23), channel_id=1, source_target_pairs={{0,16},{8,24},{16,0},{24,8},{1,17},{9,25},{17,1},{25,9},{2,18},{10... | collective-permute-start | bytes 294920 | tf_op jit(solution)/shard_map/ppermute | solution.py:174
  113.7 11.0 %collective-permute-start.10 = (f32[96,256]{0,1:T(8,128)S(1)}, f32[96,256]{0,1:T(8,128)S(1)}, u32[]{:S(2)}, u32[]{:S(2)}) collective-permute-start(f32[96,256]{0,1:T(8,128)S(1)} %get-tuple-element.22), channel_id=1, source_target_pairs={{0,24},{8,16},{16,8},{24,0},{1,25},{9,17},{17,9},{25,1},{2,26},{10... | collective-permute-start | bytes 294920 | tf_op jit(solution)/shard_map/ppermute | solution.py:174
  124.9 8.2 %collective-permute-start.11 = (f32[96,256]{0,1:T(8,128)S(1)}, f32[96,256]{0,1:T(8,128)S(1)}, u32[]{:S(2)}, u32[]{:S(2)}) collective-permute-start(f32[96,256]{0,1:T(8,128)S(1)} %fusion.21), channel_id=1, source_target_pairs={{0,8},{8,0},{16,24},{24,16},{1,9},{9,1},{17,25},{25,17},{2,10},{10... | collective-permute-start | bytes 294920 | tf_op jit(solution)/shard_map/ppermute | solution.py:187
  127.5 12.3 %collective-permute-start.12 = (f32[96,256]{0,1:T(8,128)S(1)}, f32[96,256]{0,1:T(8,128)S(1)}, u32[]{:S(2)}, u32[]{:S(2)}) collective-permute-start(f32[96,256]{0,1:T(8,128)S(1)} %fusion.21), channel_id=1, source_target_pairs={{0,16},{8,24},{16,0},{24,8},{1,17},{9,25},{17,1},{25,9},{2,18},{10... | collective-permute-start | bytes 294920 | tf_op jit(solution)/shard_map/ppermute | solution.py:187
  129.5 10.4 %collective-permute-start.13 = (f32[96,256]{0,1:T(8,128)S(1)}, f32[96,256]{0,1:T(8,128)S(1)}, u32[]{:S(2)}, u32[]{:S(2)}) collective-permute-start(f32[96,256]{0,1:T(8,128)S(1)} %fusion.21), channel_id=1, source_target_pairs={{0,24},{8,16},{16,8},{24,0},{1,25},{9,17},{17,9},{25,1},{2,26},{10... | collective-permute-start | bytes 294920 | tf_op jit(solution)/shard_map/ppermute | solution.py:187
  140.1 6.5 %copy-start.8 = (f32[384,256]{1,0:T(8,128)}, f32[384,256]{1,0:T(8,128)S(1)}, u32[]{:S(2)}) copy-start(f32[384,256]{1,0:T(8,128)S(1)} %constant_dynamic-update-slice_fusion.43) | copy-start | bytes 1179652
  141.6 6.1 %collective-permute-start.17 = (f32[32,256]{1,0:T(8,128)S(1)}, f32[32,256]{1,0:T(8,128)S(1)}, u32[]{:S(2)}, u32[]{:S(2)}) collective-permute-start(f32[32,256]{1,0:T(8,128)S(1)} %slice.33), channel_id=1, source_target_pairs={{0,16},{8,24},{16,0},{24,8},{1,17},{9,25},{17,1},{25,9},{2,18},{10... | collective-permute-start | bytes 98312 | tf_op jit(solution)/shard_map/ppermute | solution.py:161
  145.8 5.7 %collective-permute-start.18 = (f32[32,256]{1,0:T(8,128)S(1)}, f32[32,256]{1,0:T(8,128)S(1)}, u32[]{:S(2)}, u32[]{:S(2)}) collective-permute-start(f32[32,256]{1,0:T(8,128)S(1)} %slice.33), channel_id=1, source_target_pairs={{0,24},{8,16},{16,8},{24,0},{1,25},{9,17},{17,9},{25,1},{2,26},{10... | collective-permute-start | bytes 98312 | tf_op jit(solution)/shard_map/ppermute | solution.py:161
  146.5 5.0 %collective-permute-start.16 = (f32[32,256]{1,0:T(8,128)S(1)}, f32[32,256]{1,0:T(8,128)S(1)}, u32[]{:S(2)}, u32[]{:S(2)}) collective-permute-start(f32[32,256]{1,0:T(8,128)S(1)} %slice.33), channel_id=1, source_target_pairs={{0,8},{8,0},{16,24},{24,16},{1,9},{9,1},{17,25},{25,17},{2,10},{10... | collective-permute-start | bytes 98312 | tf_op jit(solution)/shard_map/ppermute | solution.py:161
  146.6 9.8 %copy-start.11 = (f32[768,256]{1,0:T(8,128)}, f32[768,256]{1,0:T(8,128)S(1)}, u32[]{:S(2)}) copy-start(f32[768,256]{1,0:T(8,128)S(1)} %constant_dynamic-update-slice_fusion.18) | copy-start | bytes 2359300
  156.3 10.5 %all-to-all-start.5 = ((f32[8,32,256]{2,1,0:T(8,128)}), f32[8,32,256]{2,1,0:T(8,128)S(1)}, u32[]{:S(2)}, u32[]{:S(2)}) async-start(f32[8,32,256]{2,1,0:T(8,128)} %bitcast.17), calls=%async_computation.5 | async-start | bytes 524288 | tf_op jit(solution)/shard_map/all_to_all | solution.py:193
  166.8 0.7 copy-start.10
  167.5 16.1 %all-to-all-start.3 = ((f32[8,96,256]{2,1,0:T(8,128)}), f32[8,96,256]{2,1,0:T(8,128)S(1)}, u32[]{:S(2)}, u32[]{:S(2)}) async-start(f32[8,96,256]{2,1,0:T(8,128)} %bitcast.58), calls=%async_computation.3 | async-start | bytes 1572864 | tf_op jit(solution)/shard_map/all_to_all | solution.py:193
  171.1 1.8 copy-start.3
  171.1 2.2 %copy-start.9 = (f32[384,256]{1,0:T(8,128)S(1)}, f32[384,256]{1,0:T(8,128)}, u32[]{:S(2)}) copy-start(f32[384,256]{1,0:T(8,128)} %copy-done.8) | copy-start | bytes 1179652
  173.3 10.4 %copy-start.7 = (f32[384,256]{1,0:T(8,128)S(1)}, f32[384,256]{1,0:T(8,128)}, u32[]{:S(2)}) copy-start(f32[384,256]{1,0:T(8,128)} %fusion.18) | copy-start | bytes 1179652

commit v2 on v1

--- a/solution.py
+++ b/solution.py
@@ -11,13 +11,28 @@
 LANE = 128
 BLOCK = 32
 HIGHEST = lax.Precision.HIGHEST
-HIGH = lax.Precision.HIGH
-
-
-def mult(left, right, dims=((1,), (0,)), precision=HIGHEST):
+PARAMS = pltpu.CompilerParams(vmem_limit_bytes=48 * 2**20)
+PLAIN = ((1,), (0,))
+TURNED = ((0,), (0,))
+ACROSS = ((1,), (1,))
+
+
+def mult(left, right, dims=PLAIN):
     return lax.dot_general(
-        left, right, (dims, ((), ())), precision=precision, preferred_element_type=jnp.float32
+        left, right, (dims, ((), ())), precision=HIGHEST, preferred_element_type=jnp.float32
     )
+
+
+def split(value):
+    high = value.astype(jnp.bfloat16)
+    return high, (value - high.astype(jnp.float32)).astype(jnp.bfloat16)
+
+
+def mult3(left, right, dims=PLAIN):
+    def one(a, b):
+        return lax.dot_general(a, b, (dims, ((), ())), preferred_element_type=jnp.float32)
+
+    return one(left[0], right[0]) + (one(left[0], right[1]) + one(left[1], right[0]))
 
 
 def chol_kernel(gram_ref, upper_ref, inv_ref, work_ref):
@@ -103,24 +118,86 @@
         work_ref[rest:size, :] = old - change[rest - start :, :]
 
 
+def estimate(micros):
+    return pl.CostEstimate(flops=int(micros * 1e9), bytes_accessed=int(micros * 3e6), transcendentals=0)
+
+
+def square(size):
+    return jax.ShapeDtypeStruct((size, size), jnp.float32)
+
+
 def cholesky(gram):
     size = gram.shape[0]
-    shape = jax.ShapeDtypeStruct((size, size), jnp.float32)
     return pl.pallas_call(
         chol_kernel,
-        out_shape=(shape, shape),
+        out_shape=(square(size), square(size)),
         scratch_shapes=[pltpu.VMEM((size, size), jnp.float32)],
-        compiler_params=pltpu.CompilerParams(vmem_limit_bytes=32 * 2**20),
+        compiler_params=PARAMS,
+        cost_estimate=estimate(10),
         name="cholesky_inverse",
     )(gram)
 
 
-def inverse_kernel(mat_ref, out_ref):
-    size = mat_ref.shape[0]
+def grids(size):
     row = lax.broadcasted_iota(jnp.int32, (size, size), 0)
     col = lax.broadcasted_iota(jnp.int32, (size, size), 1)
+    return row, col
+
+
+def near_kernel(gram_ref, first_ref, upper_ref, band_ref, inv_ref, work_ref):
+    size = gram_ref.shape[0]
+    row, col = grids(size)
     ident = jnp.where(row == col, 1.0, 0.0)
-    mat = mat_ref[...]
+    weight = jnp.where(row > col, 1.0, ident * 0.5)
+    gram = gram_ref[...]
+
+    def look(inv):
+        upper = mult(inv, gram)
+        low = weight * (mult(upper, inv, ACROSS) - ident)
+        return upper, low, jnp.max(jnp.abs(low))
+
+    def more(state):
+        count, _, _, _, worst = state
+        return jnp.logical_not(worst < 1e-4) & (count < 8)
+
+    def step(state):
+        count, inv, _, low, _ = state
+        turn = mult(low, inv)
+        inv = inv - turn + mult(low, turn)
+        return (count + 1, inv) + look(inv)
+
+    low = weight * (gram - ident)
+    inv = ident - low + mult(low, low)
+    state = lax.while_loop(more, step, (jnp.int32(0), inv) + look(inv))
+    _, _, upper, low, worst = state
+    upper = jnp.where(row <= col, upper + mult(low, upper, TURNED), 0.0)
+    upper_ref[...] = upper
+
+    @pl.when(jnp.logical_not(worst < 1e-4))
+    def _():
+        chol_kernel(gram_ref, upper_ref, inv_ref, work_ref)
+
+    band_ref[...] = -mult(upper_ref[...], first_ref[...])
+
+
+def near_cholesky(gram, first_upper):
+    size = gram.shape[0]
+    return pl.pallas_call(
+        near_kernel,
+        out_shape=(square(size), square(size)),
+        scratch_shapes=[pltpu.VMEM((size, size), jnp.float32)] * 2,
+        compiler_params=PARAMS,
+        cost_estimate=estimate(3),
+        name="near_cholesky",
+    )(gram, first_upper)
+
+
+def factor_kernel(gram_ref, top_ref, inv_ref, upper_ref, out_ref):
+    size = gram_ref.shape[0]
+    row, col = grids(size)
+    ident = jnp.where(row == col, 1.0, 0.0)
+    half_top = mult(top_ref[...], inv_ref[...], ACROSS)
+    mat = gram_ref[...] + mult(half_top, upper_ref[...], TURNED)
 
     def residual(guess):
         return ident - mult(mat, guess)
@@ -146,51 +223,90 @@
     out_ref[...] = lax.while_loop(more, step, state)[1]
 
 
-def inverse(mat):
-    return pl.pallas_call(
-        inverse_kernel,
-        out_shape=jax.ShapeDtypeStruct(mat.shape, jnp.float32),
-        compiler_params=pltpu.CompilerParams(vmem_limit_bytes=32 * 2**20),
-        name="wy_inverse",
-    )(mat)
-
-
-def pair_sum(value, axis, size):
-    terms = [value]
-    for hop in range(1, size):
-        terms.append(lax.ppermute(value, axis, [(i, i ^ hop) for i in range(size)]))
-    while len(terms) > 1:
-        terms = [terms[i] + terms[i + 1] for i in range(0, len(terms), 2)]
-    return terms[0]
-
-
-def scatter_sum(value, axis, size):
-    place = lax.axis_index(axis)
-    piece = value.shape[0] // size
-    terms = []
-    for hop in range(size):
-        part = lax.dynamic_slice_in_dim(value, (place ^ hop) * piece, piece, 0)
-        if hop:
-            part = lax.ppermute(part, axis, [(i, i ^ hop) for i in range(size)])
-        terms.append(part)
-    while len(terms) > 1:
-        terms = [terms[i] + terms[i + 1] for i in range(0, len(terms), 2)]
-    return terms[0]
-
-
-def swap_gather(piece, axis, size):
-    place = lax.axis_index(axis)
-    whole = jnp.zeros((size * piece.shape[0], piece.shape[1]), piece.dtype)
-    for hop in range(size):
-        part = piece
-        if hop:
-            part = lax.ppermute(piece, axis, [(i, i ^ hop) for i in range(size)])
-        whole = lax.dynamic_update_slice_in_dim(whole, part, (place ^ hop) * piece.shape[0], 0)
-    return whole
-
-
-def gather_cols(piece, size):
-    return lax.all_to_all(jnp.concatenate([piece] * size, axis=0), "col", 0, 0, tiled=True)
+def compact_factor(gram, top, inv, upper):
+    return pl.pallas_call(
+        factor_kernel,
+        out_shape=square(gram.shape[0]),
+        compiler_params=PARAMS,
+        cost_estimate=estimate(4),
+        name="compact_factor",
+    )(gram, top, inv, upper)
+
+
+def products_kernel(
+    place_ref, ham_ref, half_ref, near_ref, upper_ref, left_ref, right_ref, packed_ref, cols_ref
+):
+    width = upper_ref.shape[0]
+    cols = packed_ref.shape[0]
+    piece = ham_ref.shape[0] // cols
+    strip = width // cols
+    left_ref[...] = half_ref[...]
+    right_ref[...] = near_ref[...]
+    for axis, ref in enumerate((left_ref, right_ref)):
+
+        @pl.when(place_ref[axis] == 0)
+        def _():
+            ref[:width, :] = ref[:width, :] + upper_ref[...]
+
+    ham = split(ham_ref[...])
+    left = split(left_ref[...])
+    part = mult3(ham, split(right_ref[...]))
+    coupling = mult3(left, split(part), TURNED)
+    for c in range(cols):
+        packed_ref[c, :piece, :] = part[c * piece : (c + 1) * piece]
+        packed_ref[c, piece:, :] = coupling[c * strip : (c + 1) * strip]
+    cols_ref[...] = mult3(ham, left, TURNED)
+
+
+def products(place, hamiltonian, half, half_cols, upper, cols):
+    rows_dev, cols_dev = hamiltonian.shape
+    width = upper.shape[0]
+    share = (rows_dev + width) // cols
+
+    def shape(*dims):
+        return jax.ShapeDtypeStruct(dims, jnp.float32)
+
+    vmem = pl.BlockSpec(memory_space=pltpu.VMEM)
+    return pl.pallas_call(
+        products_kernel,
+        in_specs=[pl.BlockSpec(memory_space=pltpu.SMEM)] + [vmem] * 4,
+        out_shape=(
+            shape(rows_dev, width),
+            shape(cols_dev, width),
+            shape(cols, share, width),
+            shape(cols_dev, width),
+        ),
+        compiler_params=PARAMS,
+        cost_estimate=estimate(3),
+        name="products",
+    )(place, hamiltonian, half, half_cols, upper)
+
+
+def update_kernel(ham_ref, left_ref, prod_ref, right_ref, near_ref, factor_ref, coupling_ref, out_ref):
+    factor = split(factor_ref[...])
+    right = split(right_ref[...])
+    turn = mult3(split(coupling_ref[...]), factor)
+    middle = mult3(factor, split(turn), TURNED)
+    near = mult3(split(near_ref[...]), factor) - mult3(right, split(middle))
+    far = mult3(right, factor, ACROSS)
+    change = mult3(split(left_ref[...]), split(near), ACROSS)
+    change = change + mult3(split(prod_ref[...]), split(far), ACROSS)
+    out_ref[...] = ham_ref[...] - change
+
+
+def update(hamiltonian, *operands):
+    return pl.pallas_call(
+        update_kernel,
+        out_shape=jax.ShapeDtypeStruct(hamiltonian.shape, jnp.float32),
+        compiler_params=PARAMS,
+        cost_estimate=estimate(3),
+        name="two_sided_update",
+    )(hamiltonian, *operands)
+
+
+def gather(piece, axis, size):
+    copies = jnp.broadcast_to(piece[None], (size,) + piece.shape)
+    return lax.all_to_all(copies, axis, 0, 0, tiled=True)
 
 
 def spread_rows(value, owners, rows, cols):
@@ -218,68 +334,52 @@
     row_place = lax.axis_index("row")
     col_place = lax.axis_index("col")
     strip = width // cols
-
-    def sum_strips(strip_value):
-        return gather_cols(pair_sum(strip_value, "row", rows), cols)
+    piece = rows_dev // cols
 
     def strip_of(array):
         return lax.dynamic_slice_in_dim(array, col_place * strip, strip, 1)
 
-    gram = sum_strips(mult(strip_of(panel), panel, ((0,), (0,))))
+    def sum_rows(value):
+        return gather(value, "row", rows).sum(axis=0)
+
+    gram_strip = sum_rows(mult(strip_of(panel), panel, TURNED))
 
     owners = [c * cols_dev // rows_dev for c in range(cols)]
     owner = col_place * cols_dev // rows_dev
     offset = col_place * cols_dev - owner * rows_dev
     slab = lax.dynamic_slice_in_dim(panel, offset, cols_dev, 0)
     top_strip = lax.dynamic_slice_in_dim(panel[:width], col_place * strip, strip, 0)
-    gram, slab, top_strip = lax.optimization_barrier((gram, slab, top_strip))
+    gram_strip, slab, top_strip = lax.optimization_barrier((gram_strip, slab, top_strip))
     panel_cols = spread_rows(slab, owners, rows, cols)
-    panel_top = gather_cols(spread_rows(top_strip, [0] * cols, rows, cols), cols)
-
+    top_strip = spread_rows(top_strip, [0] * cols, rows, cols)
+
+    gram = gather(gram_strip, "col", cols).reshape(width, width)
     first_upper, first_inv = cholesky(gram)
-    half = mult(panel, first_inv, ((1,), (1,)))
-    half_cols = mult(panel_cols, first_inv, ((1,), (1,)))
-    half_top = mult(panel_top, first_inv, ((1,), (1,)))
-
-    gram2 = sum_strips(mult(strip_of(half), half, ((0,), (0,))))
-    second_upper, _ = cholesky(gram2)
-    band_block = -mult(second_upper, first_upper)
-
-    def with_upper(block, first_row):
-        lead_rows = block[:width] + jnp.where(first_row == 0, second_upper, 0.0)
-        return jnp.concatenate([lead_rows, block[width:]], axis=0)
-
-    left = with_upper(half, row_place)
-    right = with_upper(half_cols, col_place)
-    factor = inverse(gram2 + mult(half_top, second_upper, ((0,), (0,))))
-
-    part = mult(hamiltonian, right, precision=HIGH)
-    part_cols = mult(hamiltonian, left, ((0,), (0,)), precision=HIGH)
-    part_coupling = mult(left, part, ((0,), (0,)), precision=HIGH)
-    piece = rows_dev // cols
-    packed = jnp.concatenate(
-        [part.reshape(cols, piece, width), part_coupling.reshape(cols, strip, width)], axis=1
-    ).reshape(cols * (piece + strip), width)
-    packed = lax.all_to_all(packed, "col", 0, 0, tiled=True)
-    packed = packed.reshape(cols, piece + strip, width).sum(axis=0)
-    products = gather_cols(packed[:piece], cols)
-    coupling = sum_strips_from(packed[piece:], rows, cols)
-    products_cols = swap_gather(scatter_sum(part_cols, "row", rows), "row", rows)
-
-    middle = mult(factor, mult(coupling, factor), ((0,), (0,)), precision=HIGH)
-    near = mult(products_cols, factor, precision=HIGH) - mult(right, middle, precision=HIGH)
-    far = mult(right, factor, ((1,), (1,)), precision=HIGH)
-    updated = hamiltonian - mult(
-        jnp.concatenate([left, products], axis=1),
-        jnp.concatenate([near, far], axis=1),
-        ((1,), (1,)),
-        precision=HIGH,
+    half = mult(panel, first_inv, ACROSS)
+    half_cols = mult(panel_cols, first_inv, ACROSS)
+
+    gram2_strip = sum_rows(mult(strip_of(half), half, TURNED))
+    both = gather(jnp.concatenate([gram2_strip, top_strip], axis=0), "col", cols)
+    gram2 = both[:, :strip].reshape(width, width)
+    panel_top = both[:, strip:].reshape(width, width)
+    second_upper, band_block = near_cholesky(gram2, first_upper)
+
+    place = jnp.stack([row_place, col_place]).astype(jnp.int32)
+    left, right, packed, part_cols = products(
+        place, hamiltonian, half, half_cols, second_upper, cols
     )
+    gram2, panel_top, packed = lax.optimization_barrier((gram2, panel_top, packed))
+    factor = compact_factor(gram2, panel_top, first_inv, second_upper)
+    packed = lax.all_to_all(packed, "col", 0, 0, tiled=True).sum(axis=0)
+    part_cols = part_cols.reshape(rows, cols_dev // rows, width)
+    cols_piece = lax.all_to_all(part_cols, "row", 0, 0, tiled=True).sum(axis=0)
+    product_rows = gather(packed[:piece], "col", cols).reshape(rows_dev, width)
+    both = gather(jnp.concatenate([cols_piece, packed[piece:]], axis=0), "row", rows)
+    product_cols = both[:, : cols_dev // rows].reshape(cols_dev, width)
+    coupling_strip = both[:, cols_dev // rows :].sum(axis=0)
+    coupling = gather(coupling_strip, "col", cols).reshape(width, width)
+    updated = update(hamiltonian, left, product_rows, right, product_cols, factor, coupling)
     return (updated, band_block)
-
-
-def sum_strips_from(strip_value, rows, cols):
-    return gather_cols(pair_sum(strip_value, "row", rows), cols)
 
 
 def solution(mesh):

time: 188 us -> 172 us (0.915)
  waiting for transfers between devices: 51.6 us -> 75.4 us
  matrix products: 18.7 us -> 4.38 us
  starting transfers between devices: 58.7 us -> 47.9 us
  local copies, waits for them, and re-layouts: 23.9 us -> 13.8 us
  other arithmetic: 8.34 us -> 0.32 us
  Pallas kernels: 23.8 us -> 27.6 us
    all_to_all x6 -> x9, waiting for transfers between devices: 23.8 us -> 68.6 us  [the longest x7 43.9 us: gather(): return lax.all_to_all(copies, axis, 0, 0, tiled=True)]
    ppermute x15 -> x0, starting transfers between devices: 24.6 us -> none  [the longest x9 14.1 us: pair_sum(): terms.append(lax.ppermute(value, axis, [(i, i ^ hop) for i in range(size)]))]
    ppermute x15 -> x0, waiting for transfers between devices: 24.4 us -> none  [the longest x3 8.8 us: swap_gather(): part = lax.ppermute(piece, axis, [(i, i ^ hop) for i in range(size)])]
    dot_general x16 -> x4, matrix products: 18.7 us -> 4.38 us  [mult(): lax.dot_general(left, right, (dims, ((), ())), precision=HIGHEST, preferr...]
    all_to_all x6 -> x9, starting transfers between devices: 24.8 us -> 38.8 us  [the longest x7 28.8 us: gather(): return lax.all_to_all(copies, axis, 0, 0, tiled=True)]
    unnamed x57 -> x30, local copies, waits for them, and re-layouts: 16.1 us -> 7.33 us
    broadcast_in_dim x1 -> x7, local copies, waits for them, and re-layouts: 0.03 us -> 5.46 us  [gather(): copies = jnp.broadcast_to(piece[None], (size,) + piece.shape)]
    pallas_call x3 -> x5, Pallas kernels: 23.8 us -> 27.6 us  [the longest x1 9.68 us: cholesky(): pl.pallas_call(chol_kernel, out_shape=(square(size), square(size)), scrat...]
  transfers between devices with their start and end apart: 25 -> 13, of which waited for: 12 -> 9; matrix products, arithmetic and copies ran while one was open for 12% -> 3% of each run, Pallas kernels for 8% -> 8%
where the time goes in v2:
time: 172 us; the launch traced here: 171 us
  waiting for transfers between devices  75.4 us (44%)
  starting transfers between devices  47.9 us (28%)
  Pallas kernels  27.6 us (16%)
  local copies, waits for them, and re-layouts  13.8 us (8%)
  matrix products  4.38 us (3%)
    all_to_all x7, waiting for transfers between devices, gather(): return lax.all_to_all(copies, axis, 0, 0, tiled=True)  43.9 us
    all_to_all x7, starting transfers between devices, gather(): return lax.all_to_all(copies, axis, 0, 0, tiled=True)  28.8 us
    all_to_all x1, waiting for transfers between devices, shards(): packed = lax.all_to_all(packed, 'col', 0, 0, tiled=True).sum(axis=0)  15.4 us
    pallas_call x1, Pallas kernels, cholesky(): pl.pallas_call(chol_kernel, out_shape=(square(size), square(size)), scrat...  9.68 us
    all_to_all x1, waiting for transfers between devices, shards(): cols_piece = lax.all_to_all(part_cols, 'row', 0, 0, tiled=True).sum(axis=0)  9.32 us
    ppermute x4, starting transfers between devices, spread_rows(): value = value + lax.ppermute(value, ('row', 'col'), pairs)  9.17 us
    unnamed x30, local copies, waits for them, and re-layouts  7.33 us
    ppermute x4, waiting for transfers between devices, spread_rows(): value = value + lax.ppermute(value, ('row', 'col'), pairs)  6.78 us
  transfers between devices with their start and end apart: 13, of which 9 were waited for; matrix products, arithmetic and copies ran while one was open for 3% of the time, Pallas kernels for 8%

profile of v2, /device:TPU:0, one launch (start us, length us, event | category | flops | bytes accessed | tf_op | source)
XLA Modules:
  0.0 171.0 jit_solution(5605606464495455259)
XLA Ops:
  0.7 2.2 %fusion.2 = f32[32,256]{1,0:T(8,128)S(1)} fusion(f32[768,256]{1,0:T(8,128)} %param.5, s32[]{:T(128)S(6)} %select_n.33), kind=kOutput, calls=%fused_computation.2 | convolution fusion | flops 75497472 | bytes 1212420 | tf_op jit(solution)/shard_map/dot_general | solution.py:21
  2.9 0.7 broadcast_in_dim.22
  3.6 6.3 %all-to-all-start = ((f32[4,32,256]{2,1,0:T(8,128)}), f32[4,32,256]{2,1,0:T(8,128)S(1)}, u32[]{:S(2)}, u32[]{:S(2)}) async-start(f32[4,32,256]{2,1,0:T(8,128)} %broadcast_in_dim.22), calls=%async_computation | async-start | bytes 262144 | tf_op jit(solution)/shard_map/all_to_all | solution.py:309
  9.9 0.6 dynamic_slice.19
  11.2 4.7 %all-to-all-done = f32[4,32,256]{2,1,0:T(8,128)S(1)} async-done(((f32[4,32,256]{2,1,0:T(8,128)}), f32[4,32,256]{2,1,0:T(8,128)S(1)}, u32[]{:S(2)}, u32[]{:S(2)}) %all-to-all-start) | async-done | bytes 131104 | tf_op jit(solution)/shard_map/all_to_all | solution.py:309
  16.0 2.7 %collective-permute-start.2 = (f32[32,256]{1,0:T(8,128)S(1)}, f32[32,256]{1,0:T(8,128)S(1)}, u32[]{:S(2)}, u32[]{:S(2)}) collective-permute-start(f32[32,256]{1,0:T(8,128)S(1)} %broadcast_select_fusion.1), channel_id=1, source_target_pairs={{0,16},{1,17},{2,18},{3,19},{4,20},{5,21},{6,22},{7,23}} | collective-permute-start | bytes 98312 | tf_op jit(solution)/shard_map/ppermute | solution.py:325
  18.7 0.7 broadcast_in_dim.23
  19.4 3.7 %all-to-all-start.1 = ((f32[8,32,256]{2,1,0:T(8,128)}), f32[8,32,256]{2,1,0:T(8,128)S(1)}, u32[]{:S(2)}, u32[]{:S(2)}) async-start(f32[8,32,256]{2,1,0:T(8,128)} %broadcast_in_dim.23), calls=%async_computation.1 | async-start | bytes 524288 | tf_op jit(solution)/shard_map/all_to_all | solution.py:309
  23.2 1.3 collective-permute-start
  24.5 5.6 %all-to-all-done.1 = f32[8,32,256]{2,1,0:T(8,128)S(1)} async-done(((f32[8,32,256]{2,1,0:T(8,128)}), f32[8,32,256]{2,1,0:T(8,128)S(1)}, u32[]{:S(2)}, u32[]{:S(2)}) %all-to-all-start.1) | async-done | bytes 262176 | tf_op jit(solution)/shard_map/all_to_all | solution.py:309
  30.1 9.7 %cholesky_inverse.1 = (f32[256,256]{1,0:T(8,128)S(1)}, f32[256,256]{1,0:T(8,128)S(1)}) custom-call(f32[256,256]{1,0:T(8,128)S(1)} %bitcast.20), custom_call_target="tpu_custom_call" | custom-call | flops 10000000000 | bytes 30000000 | tf_op jit(solution)/shard_map/cholesky_inverse/pallas_call | solution.py:131
  39.8 0.8 fusion.9
  40.6 0.8 fusion.4
  41.4 0.7 broadcast_in_dim.25
  42.1 3.3 %all-to-all-start.2 = ((f32[4,32,256]{2,1,0:T(8,128)}), f32[4,32,256]{2,1,0:T(8,128)S(1)}, u32[]{:S(2)}, u32[]{:S(2)}) async-start(f32[4,32,256]{2,1,0:T(8,128)} %broadcast_in_dim.25), calls=%async_computation.2 | async-start | bytes 262144 | tf_op jit(solution)/shard_map/all_to_all | solution.py:309
  45.5 3.9 %collective-permute-start.1 = (f32[384,256]{1,0:T(8,128)S(1)}, f32[384,256]{1,0:T(8,128)S(1)}, u32[]{:S(2)}, u32[]{:S(2)}) collective-permute-start(f32[384,256]{1,0:T(8,128)S(1)} %fusion.16), channel_id=1, source_target_pairs={{0,8},{16,24},{1,9},{17,25},{10,2},{26,18},{11,3},{27,19},{20,28},... | collective-permute-start | bytes 1179656 | tf_op jit(solution)/shard_map/ppermute | solution.py:325
  49.4 1.3 collective-permute-start.3
  50.7 6.8 %collective-permute-done.3 = f32[32,256]{1,0:T(8,128)S(1)} collective-permute-done((f32[32,256]{1,0:T(8,128)S(1)}, f32[32,256]{1,0:T(8,128)S(1)}, u32[]{:S(2)}, u32[]{:S(2)}) %collective-permute-start.3) | collective-permute-done | bytes 32800 | tf_op jit(solution)/shard_map/ppermute | solution.py:325
  57.5 0.8 broadcast_in_dim.27
  58.4 3.5 %all-to-all-start.3 = ((f32[8,64,256]{2,1,0:T(8,128)}), f32[8,64,256]{2,1,0:T(8,128)S(1)}, u32[]{:S(2)}, u32[]{:S(2)}) async-start(f32[8,64,256]{2,1,0:T(8,128)} %broadcast_in_dim.27), calls=%async_computation.3 | async-start | bytes 1048576 | tf_op jit(solution)/shard_map/all_to_all | solution.py:309
  62.0 0.3 copy.7
  62.2 0.5 fusion.near_ref
  62.8 8.8 %all-to-all-done.3 = f32[8,64,256]{2,1,0:T(8,128)S(1)} async-done(((f32[8,64,256]{2,1,0:T(8,128)}), f32[8,64,256]{2,1,0:T(8,128)S(1)}, u32[]{:S(2)}, u32[]{:S(2)}) %all-to-all-start.3) | async-done | bytes 524320 | tf_op jit(solution)/shard_map/all_to_all | solution.py:309
  71.6 0.9 copy-done.10
  72.5 5.4 %near_cholesky.1 = (f32[256,256]{1,0:T(8,128)S(1)}, f32[256,256]{1,0:T(8,128)}) custom-call(f32[256,256]{1,0:T(8,128)S(1)} %bitcast.22, f32[256,256]{1,0:T(8,128)S(1)} %copy-done.10), custom_call_target="tpu_custom_call" | custom-call | flops 3000000000 | bytes 9000000 | tf_op jit(solution)/shard_map/near_cholesky/pallas_call | solution.py:185
  78.0 4.2 %products.1 = (f32[768,256]{1,0:T(8,128)S(1)}, f32[384,256]{1,0:T(8,128)S(1)}, f32[8,128,256]{2,1,0:T(8,128)}, f32[384,256]{1,0:T(8,128)}) custom-call(s32[2]{0:T(128)S(1)} %pad_add_fusion.place_ref, f32[768,384]{1,0:T(8,128)S(1)} %copy-done, f32[768,256]{1,0:T(8,128)S(1)} %bitcast.17, f32[384,256]{1,0:T(8,128)S(1)} %fusion.near_ref, ...), custom_call_target="tpu_custom_call" | custom-call | flops 3000000000 | bytes 9000000 | tf_op jit(solution)/shard_map/products/pallas_call | solution.py:270
  82.2 0.9 copy-done.1
  83.1 0.7 copy-done.3
  83.8 5.6 %all-to-all-start.6 = ((f32[4,96,256]{2,1,0:T(8,128)}), f32[4,96,256]{2,1,0:T(8,128)S(1)}, u32[]{:S(2)}, u32[]{:S(2)}) async-start(f32[4,96,256]{2,1,0:T(8,128)} %bitcast.8), calls=%async_computation.6 | async-start | bytes 786432 | tf_op jit(solution)/shard_map/all_to_all | solution.py:375
  89.4 9.3 %all-to-all-done.6 = f32[4,96,256]{2,1,0:T(8,128)S(1)} async-done(((f32[4,96,256]{2,1,0:T(8,128)}), f32[4,96,256]{2,1,0:T(8,128)S(1)}, u32[]{:S(2)}, u32[]{:S(2)}) %all-to-all-start.6) | async-done | bytes 393248 | tf_op jit(solution)/shard_map/all_to_all | solution.py:375
  98.7 4.4 %all-to-all-start.4 = ((f32[8,128,256]{2,1,0:T(8,128)}), f32[8,128,256]{2,1,0:T(8,128)S(1)}, u32[]{:S(2)}, u32[]{:S(2)}) async-start(f32[8,128,256]{2,1,0:T(8,128)} %get-tuple-element.24), calls=%async_computation.4 | async-start | bytes 2097152 | tf_op jit(solution)/shard_map/all_to_all | solution.py:373
  103.1 15.4 %all-to-all-done.4 = f32[8,128,256]{2,1,0:T(8,128)S(1)} async-done(((f32[8,128,256]{2,1,0:T(8,128)}), f32[8,128,256]{2,1,0:T(8,128)S(1)}, u32[]{:S(2)}, u32[]{:S(2)}) %all-to-all-start.4) | async-done | bytes 1048608 | tf_op jit(solution)/shard_map/all_to_all | solution.py:373
  118.6 0.8 broadcast_in_dim.29
  119.5 3.5 %all-to-all-start.7 = ((f32[4,128,256]{2,1,0:T(8,128)}), f32[4,128,256]{2,1,0:T(8,128)S(1)}, u32[]{:S(2)}, u32[]{:S(2)}) async-start(f32[4,128,256]{2,1,0:T(8,128)} %broadcast_in_dim.29), calls=%async_computation.7 | async-start | bytes 1048576 | tf_op jit(solution)/shard_map/all_to_all | solution.py:309
  123.0 11.9 %all-to-all-done.7 = f32[4,128,256]{2,1,0:T(8,128)S(1)} async-done(((f32[4,128,256]{2,1,0:T(8,128)}), f32[4,128,256]{2,1,0:T(8,128)S(1)}, u32[]{:S(2)}, u32[]{:S(2)}) %all-to-all-start.7) | async-done | bytes 524320 | tf_op jit(solution)/shard_map/all_to_all | solution.py:309
  134.9 1.0 broadcast_in_dim.28
  135.9 4.8 %all-to-all-start.5 = ((f32[8,96,256]{2,1,0:T(8,128)}), f32[8,96,256]{2,1,0:T(8,128)S(1)}, u32[]{:S(2)}, u32[]{:S(2)}) async-start(f32[8,96,256]{2,1,0:T(8,128)} %broadcast_in_dim.28), calls=%async_computation.5 | async-start | bytes 1572864 | tf_op jit(solution)/shard_map/all_to_all | solution.py:309
  140.7 12.6 %all-to-all-done.5 = f32[8,96,256]{2,1,0:T(8,128)S(1)} async-done(((f32[8,96,256]{2,1,0:T(8,128)}), f32[8,96,256]{2,1,0:T(8,128)S(1)}, u32[]{:S(2)}, u32[]{:S(2)}) %all-to-all-start.5) | async-done | bytes 786464 | tf_op jit(solution)/shard_map/all_to_all | solution.py:309
  153.3 0.7 broadcast_in_dim.30
  154.0 3.6 %all-to-all-start.8 = ((f32[8,32,256]{2,1,0:T(8,128)}), f32[8,32,256]{2,1,0:T(8,128)S(1)}, u32[]{:S(2)}, u32[]{:S(2)}) async-start(f32[8,32,256]{2,1,0:T(8,128)} %broadcast_in_dim.30), calls=%async_computation.8 | async-start | bytes 524288 | tf_op jit(solution)/shard_map/all_to_all | solution.py:309
  157.7 0.9 copy-done.8
  158.6 4.7 %compact_factor.1.factor_ref = f32[256,256]{1,0:T(8,128)S(1)} custom-call(f32[256,256]{1,0:T(8,128)S(1)} %bitcast.23, f32[256,256]{1,0:T(8,128)S(1)} %bitcast.21, f32[256,256]{1,0:T(8,128)S(1)} %get-tuple-element.17.inv_ref, f32[256,256]{1,0:T(8,128)S(1)} %copy-done.8), custom_call_target="tpu_custom_call" | custom-call | flops 4000000000 | bytes 12000000 | tf_op jit(solution)/shard_map/compact_factor/pallas_call | solution.py:227
  163.3 0.7 copy-done.5
  164.0 0.3 all-to-all-done.8
  164.3 1.1 copy-done.2
  165.5 1.0 copy-done.4
  166.4 0.9 copy-done.6
  167.4 3.6 %two_sided_update.1 = f32[768,384]{1,0:T(8,128)} custom-call(f32[768,384]{1,0:T(8,128)S(1)} %copy-done, f32[768,256]{1,0:T(8,128)S(1)} %copy-done.2, f32[768,256]{1,0:T(8,128)S(1)} %bitcast.16, f32[384,256]{1,0:T(8,128)S(1)} %copy-done.4, f32[384,256]{1,0:T(8,128)S(1)} %bitcast.18, f32[256,256]{1,0:T(8,128)S(1)} %copy-done.6, f32[256,256]{1,0:T(8,128)S(1)} %bitcast.19), custom_call_target="tpu_custom_call" | custom-call | flops 3000000000 | bytes 9000000 | tf_op jit(solution)/shard_map/two_sided_update/pallas_call | solution.py:298
  (47 shorter events, 0.5 us)
Async XLA Ops:
  0.6 9.3 %copy-start.14 = (s32[8]{0:T(128)S(1)}, s32[8]{0:T(128)}, u32[]{:S(2)}) copy-start(s32[8]{0:T(128)} %constant.34.clone) | copy-start | bytes 100
  0.6 10.5 %slice-start = ((f32[768,256]{1,0:T(8,128)}), f32[256,256]{1,0:T(8,128)S(1)}, s32[]{:S(2)}) async-start(f32[768,256]{1,0:T(8,128)} %param.5), calls=%async_computation.9 | async-start | bytes 524288 | tf_op jit(solution)/shard_map/slice | solution.py:351
  0.7 10.5 %copy-start.11 = (f32[768,256]{1,0:T(8,128)S(1)}, f32[768,256]{1,0:T(8,128)}, u32[]{:S(2)}) copy-start(f32[768,256]{1,0:T(8,128)} %param.5) | copy-start | bytes 2359300
  3.6 12.4 %all-to-all-start = ((f32[4,32,256]{2,1,0:T(8,128)}), f32[4,32,256]{2,1,0:T(8,128)S(1)}, u32[]{:S(2)}, u32[]{:S(2)}) async-start(f32[4,32,256]{2,1,0:T(8,128)} %broadcast_in_dim.22), calls=%async_computation | async-start | bytes 262144 | tf_op jit(solution)/shard_map/all_to_all | solution.py:309
  16.0 33.4 %collective-permute-start.2 = (f32[32,256]{1,0:T(8,128)S(1)}, f32[32,256]{1,0:T(8,128)S(1)}, u32[]{:S(2)}, u32[]{:S(2)}) collective-permute-start(f32[32,256]{1,0:T(8,128)S(1)} %broadcast_select_fusion.1), channel_id=1, source_target_pairs={{0,16},{1,17},{2,18},{3,19},{4,20},{5,21},{6,22},{7,23}} | collective-permute-start | bytes 98312 | tf_op jit(solution)/shard_map/ppermute | solution.py:325
  19.4 10.7 %all-to-all-start.1 = ((f32[8,32,256]{2,1,0:T(8,128)}), f32[8,32,256]{2,1,0:T(8,128)S(1)}, u32[]{:S(2)}, u32[]{:S(2)}) async-start(f32[8,32,256]{2,1,0:T(8,128)} %broadcast_in_dim.23), calls=%async_computation.1 | async-start | bytes 524288 | tf_op jit(solution)/shard_map/all_to_all | solution.py:309
  23.2 22.3 %collective-permute-start = (f32[384,256]{1,0:T(8,128)S(1)}, f32[384,256]{1,0:T(8,128)S(1)}, u32[]{:S(2)}, u32[]{:S(2)}) collective-permute-start(f32[384,256]{1,0:T(8,128)S(1)} %broadcast_select_fusion), channel_id=1, source_target_pairs={{0,16},{1,17},{10,26},{11,27},{20,4},{21,5},{30,14},{31,15}} | collective-permute-start | bytes 1179656 | tf_op jit(solution)/shard_map/ppermute | solution.py:325
  39.7 1.7 copy-start.9
  42.1 15.4 %all-to-all-start.2 = ((f32[4,32,256]{2,1,0:T(8,128)}), f32[4,32,256]{2,1,0:T(8,128)S(1)}, u32[]{:S(2)}, u32[]{:S(2)}) async-start(f32[4,32,256]{2,1,0:T(8,128)} %broadcast_in_dim.25), calls=%async_computation.2 | async-start | bytes 262144 | tf_op jit(solution)/shard_map/all_to_all | solution.py:309
  45.5 16.7 %collective-permute-start.1 = (f32[384,256]{1,0:T(8,128)S(1)}, f32[384,256]{1,0:T(8,128)S(1)}, u32[]{:S(2)}, u32[]{:S(2)}) collective-permute-start(f32[384,256]{1,0:T(8,128)S(1)} %fusion.16), channel_id=1, source_target_pairs={{0,8},{16,24},{1,9},{17,25},{10,2},{26,18},{11,3},{27,19},{20,28},... | collective-permute-start | bytes 1179656 | tf_op jit(solution)/shard_map/ppermute | solution.py:325
  49.4 8.1 %collective-permute-start.3 = (f32[32,256]{1,0:T(8,128)S(1)}, f32[32,256]{1,0:T(8,128)S(1)}, u32[]{:S(2)}, u32[]{:S(2)}) collective-permute-start(f32[32,256]{1,0:T(8,128)S(1)} %fusion.15), channel_id=1, source_target_pairs={{0,8},{16,24},{1,9},{17,25},{2,10},{18,26},{3,11},{19,27},{4,12},{... | collective-permute-start | bytes 98312 | tf_op jit(solution)/shard_map/ppermute | solution.py:325
  58.4 13.2 %all-to-all-start.3 = ((f32[8,64,256]{2,1,0:T(8,128)}), f32[8,64,256]{2,1,0:T(8,128)S(1)}, u32[]{:S(2)}, u32[]{:S(2)}) async-start(f32[8,64,256]{2,1,0:T(8,128)} %broadcast_in_dim.27), calls=%async_computation.3 | async-start | bytes 1048576 | tf_op jit(solution)/shard_map/all_to_all | solution.py:309
  71.6 1.0 copy-start.10
  72.5 5.4 %copy-start = (f32[768,384]{1,0:T(8,128)S(1)}, f32[768,384]{1,0:T(8,128)}, u32[]{:S(2)}) copy-start(f32[768,384]{1,0:T(8,128)} %ham_ref.3) | copy-start | bytes 3538948
  78.0 4.2 %copy-start.7 = (f32[256,256]{1,0:T(8,128)}, f32[256,256]{1,0:T(8,128)S(1)}, u32[]{:S(2)}) copy-start(f32[256,256]{1,0:T(8,128)S(1)} %get-tuple-element.21.upper_ref) | copy-start | bytes 786436
  82.2 0.9 copy-start.1
  83.1 0.7 copy-start.3
  83.8 14.9 %all-to-all-start.6 = ((f32[4,96,256]{2,1,0:T(8,128)}), f32[4,96,256]{2,1,0:T(8,128)S(1)}, u32[]{:S(2)}, u32[]{:S(2)}) async-start(f32[4,96,256]{2,1,0:T(8,128)} %bitcast.8), calls=%async_computation.6 | async-start | bytes 786432 | tf_op jit(solution)/shard_map/all_to_all | solution.py:375
  98.7 19.8 %all-to-all-start.4 = ((f32[8,128,256]{2,1,0:T(8,128)}), f32[8,128,256]{2,1,0:T(8,128)S(1)}, u32[]{:S(2)}, u32[]{:S(2)}) async-start(f32[8,128,256]{2,1,0:T(8,128)} %get-tuple-element.24), calls=%async_computation.4 | async-start | bytes 2097152 | tf_op jit(solution)/shard_map/all_to_all | solution.py:373
  119.5 15.4 %all-to-all-start.7 = ((f32[4,128,256]{2,1,0:T(8,128)}), f32[4,128,256]{2,1,0:T(8,128)S(1)}, u32[]{:S(2)}, u32[]{:S(2)}) async-start(f32[4,128,256]{2,1,0:T(8,128)} %broadcast_in_dim.29), calls=%async_computation.7 | async-start | bytes 1048576 | tf_op jit(solution)/shard_map/all_to_all | solution.py:309
  134.9 5.8 %copy-start.12 = (f32[4,128,256]{2,1,0:T(8,128)}, f32[4,128,256]{2,1,0:T(8,128)S(1)}, u32[]{:S(2)}) copy-start(f32[4,128,256]{2,1,0:T(8,128)S(1)} %all-to-all-done.7) | copy-start | bytes 1572868
  135.9 17.4 %all-to-all-start.5 = ((f32[8,96,256]{2,1,0:T(8,128)}), f32[8,96,256]{2,1,0:T(8,128)S(1)}, u32[]{:S(2)}, u32[]{:S(2)}) async-start(f32[8,96,256]{2,1,0:T(8,128)} %broadcast_in_dim.28), calls=%async_computation.5 | async-start | bytes 1572864 | tf_op jit(solution)/shard_map/all_to_all | solution.py:309
  154.0 10.3 %all-to-all-start.8 = ((f32[8,32,256]{2,1,0:T(8,128)}), f32[8,32,256]{2,1,0:T(8,128)S(1)}, u32[]{:S(2)}, u32[]{:S(2)}) async-start(f32[8,32,256]{2,1,0:T(8,128)} %broadcast_in_dim.30), calls=%async_computation.8 | async-start | bytes 524288 | tf_op jit(solution)/shard_map/all_to_all | solution.py:309
  157.7 1.0 copy-start.8
  158.6 5.4 %copy-start.13 = (f32[4,128,256]{2,1,0:T(8,128)S(1)}, f32[4,128,256]{2,1,0:T(8,128)}, u32[]{:S(2)}) copy-start(f32[4,128,256]{2,1,0:T(8,128)} %copy-done.12) | copy-start | bytes 1572868
  163.3 0.7 copy-start.5
  164.3 1.1 copy-start.2
  165.5 1.0 copy-start.4
  166.4 0.9 copy-start.6

commit v3 on v2

--- a/solution.py
+++ b/solution.py
@@ -144,16 +144,17 @@
     return row, col
 
 
-def near_kernel(gram_ref, first_ref, upper_ref, band_ref, inv_ref, work_ref):
+def near_kernel(gram_ref, upper_ref, inv_ref, work_ref):
     size = gram_ref.shape[0]
     row, col = grids(size)
     ident = jnp.where(row == col, 1.0, 0.0)
     weight = jnp.where(row > col, 1.0, ident * 0.5)
-    gram = gram_ref[...]
+    gram = split(gram_ref[...])
 
     def look(inv):
-        upper = mult(inv, gram)
-        low = weight * (mult(upper, inv, ACROSS) - ident)
+        halves = split(inv)
+        upper = mult3(halves, gram)
+        low = weight * (mult3(split(upper), halves, ACROSS) - ident)
         return upper, low, jnp.max(jnp.abs(low))
 
     def more(state):
@@ -162,151 +163,192 @@
 
     def step(state):
         count, inv, _, low, _ = state
-        turn = mult(low, inv)
-        inv = inv - turn + mult(low, turn)
+        low = split(low)
+        turn = mult3(low, split(inv))
+        inv = inv - turn + mult3(low, split(turn))
         return (count + 1, inv) + look(inv)
 
-    low = weight * (gram - ident)
-    inv = ident - low + mult(low, low)
+    low = weight * (gram_ref[...] - ident)
+    halves = split(low)
+    inv = ident - low + mult3(halves, halves)
     state = lax.while_loop(more, step, (jnp.int32(0), inv) + look(inv))
     _, _, upper, low, worst = state
-    upper = jnp.where(row <= col, upper + mult(low, upper, TURNED), 0.0)
-    upper_ref[...] = upper
+    upper = upper + mult3(split(low), split(upper), TURNED)
+    upper_ref[...] = jnp.where(row <= col, upper, 0.0)
 
     @pl.when(jnp.logical_not(worst < 1e-4))
     def _():
         chol_kernel(gram_ref, upper_ref, inv_ref, work_ref)
 
-    band_ref[...] = -mult(upper_ref[...], first_ref[...])
-
-
-def near_cholesky(gram, first_upper):
+
+def near_cholesky(gram):
     size = gram.shape[0]
     return pl.pallas_call(
         near_kernel,
-        out_shape=(square(size), square(size)),
+        out_shape=square(size),
         scratch_shapes=[pltpu.VMEM((size, size), jnp.float32)] * 2,
         compiler_params=PARAMS,
         cost_estimate=estimate(3),
         name="near_cholesky",
-    )(gram, first_upper)
-
-
-def factor_kernel(gram_ref, top_ref, inv_ref, upper_ref, out_ref):
+    )(gram)
+
+
+def factor_kernel(gram_ref, top_ref, inv_ref, upper_ref, first_ref, out_ref, band_ref):
     size = gram_ref.shape[0]
     row, col = grids(size)
     ident = jnp.where(row == col, 1.0, 0.0)
+    band_ref[...] = -mult(upper_ref[...], first_ref[...])
     half_top = mult(top_ref[...], inv_ref[...], ACROSS)
     mat = gram_ref[...] + mult(half_top, upper_ref[...], TURNED)
+    halves = split(mat)
 
     def residual(guess):
-        return ident - mult(mat, guess)
+        return ident - mult3(halves, split(guess))
 
     def step(state):
         count, guess, rest, _ = state
-        guess = guess + mult(guess, rest)
+        guess = guess + mult3(split(guess), split(rest))
         rest = residual(guess)
         return count + 1, guess, rest, jnp.max(jnp.abs(rest))
 
     def more(state):
         count, _, _, worst = state
-        return (worst > 3e-6) & (count < 40)
+        return (worst > 2e-5) & (count < 40)
 
     guess = 0.5 * ident
     rest = ident - 0.5 * mat
     for _ in range(4):
-        guess = guess + mult(guess, rest)
-        rest = mult(rest, rest)
-    guess = guess + mult(guess, rest)
+        parts = split(rest)
+        guess = guess + mult3(split(guess), parts)
+        rest = mult3(parts, parts)
+    guess = guess + mult3(split(guess), split(rest))
     rest = residual(guess)
     state = (jnp.int32(0), guess, rest, jnp.max(jnp.abs(rest)))
     out_ref[...] = lax.while_loop(more, step, state)[1]
 
 
-def compact_factor(gram, top, inv, upper):
+def compact_factor(gram, top, inv, upper, first):
     return pl.pallas_call(
         factor_kernel,
-        out_shape=square(gram.shape[0]),
+        out_shape=(square(gram.shape[0]), square(gram.shape[0])),
         compiler_params=PARAMS,
         cost_estimate=estimate(4),
         name="compact_factor",
-    )(gram, top, inv, upper)
+    )(gram, top, inv, upper, first)
 
 
 def products_kernel(
-    place_ref, ham_ref, half_ref, near_ref, upper_ref, left_ref, right_ref, packed_ref, cols_ref
+    place_ref, ham_ref, wide_ref, half_ref, near_ref, next_ref, upper_ref,
+    left_ref, right_ref, packed_ref, *rest_refs
 ):
+    piece_refs, cols_ref = rest_refs[:-1], rest_refs[-1]
     width = upper_ref.shape[0]
-    cols = packed_ref.shape[0]
-    piece = ham_ref.shape[0] // cols
-    strip = width // cols
+    chips = packed_ref.shape[0]
+    deep = wide_ref.shape[0]
+    piece, strip = deep // chips, width // chips
+    share = piece_refs[0].shape[0]
+    row_place, col_place = place_ref[0], place_ref[1]
+    mine = pl.ds(pl.multiple_of((col_place & 1) * deep, deep), deep)
+    row_lead = jnp.where(row_place == 0, 1.0, 0.0)
     left_ref[...] = half_ref[...]
+    left_ref[:width, :] = half_ref[:width, :] + row_lead * upper_ref[...]
+    col_lead = jnp.where(col_place == 0, 1.0, 0.0)
     right_ref[...] = near_ref[...]
-    for axis, ref in enumerate((left_ref, right_ref)):
-
-        @pl.when(place_ref[axis] == 0)
-        def _():
-            ref[:width, :] = ref[:width, :] + upper_ref[...]
-
-    ham = split(ham_ref[...])
-    left = split(left_ref[...])
-    part = mult3(ham, split(right_ref[...]))
-    coupling = mult3(left, split(part), TURNED)
-    for c in range(cols):
+    right_ref[:width, :] = near_ref[:width, :] + col_lead * upper_ref[...]
+    next_lead = jnp.where(col_place == 1, 1.0, 0.0)
+    beside = jnp.concatenate(
+        [next_ref[:width, :] + next_lead * upper_ref[...], next_ref[width:, :]], axis=0
+    )
+    part = mult3(split(ham_ref[mine, :]), split(right_ref[...]))
+    part = part + mult3(split(wide_ref[...]), split(beside))
+    coupling = mult3(split(left_ref[mine, :]), split(part), TURNED)
+    for c in range(chips):
         packed_ref[c, :piece, :] = part[c * piece : (c + 1) * piece]
         packed_ref[c, piece:, :] = coupling[c * strip : (c + 1) * strip]
-    cols_ref[...] = mult3(ham, left, TURNED)
-
-
-def products(place, hamiltonian, half, half_cols, upper, cols):
+    cols_ref[...] = mult3(split(ham_ref[...]), split(left_ref[...]), TURNED)
+    for hop, ref in enumerate(piece_refs):
+        start = pl.multiple_of((row_place ^ hop) * share, share)
+        ref[...] = cols_ref[pl.ds(start, share), :]
+
+
+def products(place, hamiltonian, wide, half, half_cols, half_next, upper, rows, cols):
     rows_dev, cols_dev = hamiltonian.shape
     width = upper.shape[0]
-    share = (rows_dev + width) // cols
+    chips = cols // 2
+    share = (rows_dev // 2 + width) // chips
 
     def shape(*dims):
         return jax.ShapeDtypeStruct(dims, jnp.float32)
 
     vmem = pl.BlockSpec(memory_space=pltpu.VMEM)
-    return pl.pallas_call(
+    out = pl.pallas_call(
         products_kernel,
-        in_specs=[pl.BlockSpec(memory_space=pltpu.SMEM)] + [vmem] * 4,
+        in_specs=[pl.BlockSpec(memory_space=pltpu.SMEM)] + [vmem] * 6,
         out_shape=(
             shape(rows_dev, width),
             shape(cols_dev, width),
-            shape(cols, share, width),
-            shape(cols_dev, width),
-        ),
+            shape(chips, share, width),
+        )
+        + (shape(cols_dev // rows, width),) * rows,
+        scratch_shapes=[pltpu.VMEM((cols_dev, width), jnp.float32)],
         compiler_params=PARAMS,
         cost_estimate=estimate(3),
         name="products",
-    )(place, hamiltonian, half, half_cols, upper)
-
-
-def update_kernel(ham_ref, left_ref, prod_ref, right_ref, near_ref, factor_ref, coupling_ref, out_ref):
+    )(place, hamiltonian, wide, half, half_cols, half_next, upper)
+    return out[0], out[1], out[2], out[3:]
+
+
+def update_kernel(place_ref, ham_ref, left_ref, mine_ref, other_ref, right_ref, factor_ref,
+                  coupling_ref, *rest_refs):
+    piece_refs, out_ref, near_ref = rest_refs[:-2], rest_refs[-2], rest_refs[-1]
+    deep = mine_ref.shape[0]
+    share = near_ref.shape[0] // len(piece_refs)
+    row_place, core = place_ref[0], place_ref[1] & 1
+    for hop, ref in enumerate(piece_refs):
+        start = pl.multiple_of((row_place ^ hop) * share, share)
+        near_ref[pl.ds(start, share), :] = ref[:share, :]
     factor = split(factor_ref[...])
     right = split(right_ref[...])
     turn = mult3(split(coupling_ref[...]), factor)
     middle = mult3(factor, split(turn), TURNED)
-    near = mult3(split(near_ref[...]), factor) - mult3(right, split(middle))
-    far = mult3(right, factor, ACROSS)
-    change = mult3(split(left_ref[...]), split(near), ACROSS)
-    change = change + mult3(split(prod_ref[...]), split(far), ACROSS)
-    out_ref[...] = ham_ref[...] - change
-
-
-def update(hamiltonian, *operands):
+    near = split(mult3(split(near_ref[...]), factor) - mult3(right, split(middle)))
+    far = split(mult3(right, factor, ACROSS))
+    for place, prod_ref in ((core, mine_ref), (1 - core, other_ref)):
+        block = pl.ds(pl.multiple_of(place * deep, deep), deep)
+        change = mult3(split(left_ref[block, :]), near, ACROSS)
+        change = change + mult3(split(prod_ref[...]), far, ACROSS)
+        out_ref[block, :] = ham_ref[block, :] - change
+
+
+def update(place, hamiltonian, left, mine, other, right, factor, coupling, pieces):
+    vmem = pl.BlockSpec(memory_space=pltpu.VMEM)
     return pl.pallas_call(
         update_kernel,
+        in_specs=[pl.BlockSpec(memory_space=pltpu.SMEM)] + [vmem] * (7 + len(pieces)),
         out_shape=jax.ShapeDtypeStruct(hamiltonian.shape, jnp.float32),
+        scratch_shapes=[pltpu.VMEM(right.shape, jnp.float32)],
         compiler_params=PARAMS,
         cost_estimate=estimate(3),
         name="two_sided_update",
-    )(hamiltonian, *operands)
+    )(place, hamiltonian, left, mine, other, right, factor, coupling, *pieces)
 
 
 def gather(piece, axis, size):
     copies = jnp.broadcast_to(piece[None], (size,) + piece.shape)
     return lax.all_to_all(copies, axis, 0, 0, tiled=True)
+
+
+def hops(values, size):
+    got = [values[0]]
+    for hop in range(1, size):
+        got.append(lax.ppermute(values[hop], "row", [(i, i ^ hop) for i in range(size)]))
+    return got
+
+
+def tree_sum(terms):
+    while len(terms) > 1:
+        terms = [terms[i] + terms[i + 1] for i in range(0, len(terms), 2)]
+    return terms[0]
 
 
 def spread_rows(value, owners, rows, cols):
@@ -333,52 +375,69 @@
     cols_dev = hamiltonian.shape[1]
     row_place = lax.axis_index("row")
     col_place = lax.axis_index("col")
+    core = col_place % 2
+    chips = cols // 2
     strip = width // cols
-    piece = rows_dev // cols
+    deep = rows_dev // 2
+    piece = deep // chips
+    share = cols_dev // rows
+    pair = [(i, i ^ 1) for i in range(cols)]
+    groups = [[2 * k + e for k in range(chips)] for e in range(2)]
+    place = jnp.stack([row_place, col_place]).astype(jnp.int32)
 
     def strip_of(array):
         return lax.dynamic_slice_in_dim(array, col_place * strip, strip, 1)
 
-    def sum_rows(value):
-        return gather(value, "row", rows).sum(axis=0)
-
-    gram_strip = sum_rows(mult(strip_of(panel), panel, TURNED))
+    wide = lax.dynamic_slice_in_dim(hamiltonian, (1 - core) * deep, deep, 0)
+    wide = lax.ppermute(wide, "col", pair)
+
+    gram_strip = mult(strip_of(panel), panel, TURNED)
+    top_strip = lax.dynamic_slice_in_dim(panel[:width], col_place * strip, strip, 0)
+    top_strip = jnp.where(row_place == 0, top_strip, 0.0)
+    strips = gather(jnp.concatenate([gram_strip, top_strip], axis=0), "row", rows).sum(axis=0)
 
     owners = [c * cols_dev // rows_dev for c in range(cols)]
     owner = col_place * cols_dev // rows_dev
     offset = col_place * cols_dev - owner * rows_dev
     slab = lax.dynamic_slice_in_dim(panel, offset, cols_dev, 0)
-    top_strip = lax.dynamic_slice_in_dim(panel[:width], col_place * strip, strip, 0)
-    gram_strip, slab, top_strip = lax.optimization_barrier((gram_strip, slab, top_strip))
+    strips, slab = lax.optimization_barrier((strips, slab))
     panel_cols = spread_rows(slab, owners, rows, cols)
-    top_strip = spread_rows(top_strip, [0] * cols, rows, cols)
-
-    gram = gather(gram_strip, "col", cols).reshape(width, width)
+    panel_next = lax.ppermute(panel_cols, "col", pair)
+
+    strips = gather(strips, "col", cols)
+    gram = strips[:, :strip].reshape(width, width)
+    panel_top = strips[:, strip:].reshape(width, width)
     first_upper, first_inv = cholesky(gram)
     half = mult(panel, first_inv, ACROSS)
     half_cols = mult(panel_cols, first_inv, ACROSS)
-
-    gram2_strip = sum_rows(mult(strip_of(half), half, TURNED))
-    both = gather(jnp.concatenate([gram2_strip, top_strip], axis=0), "col", cols)
-    gram2 = both[:, :strip].reshape(width, width)
-    panel_top = both[:, strip:].reshape(width, width)
-    second_upper, band_block = near_cholesky(gram2, first_upper)
-
-    place = jnp.stack([row_place, col_place]).astype(jnp.int32)
-    left, right, packed, part_cols = products(
-        place, hamiltonian, half, half_cols, second_upper, cols
+    half, half_cols = lax.optimization_barrier((half, half_cols))
+    half_next = mult(panel_next, first_inv, ACROSS)
+
+    gram2_strip = gather(mult(strip_of(half), half, TURNED), "row", rows).sum(axis=0)
+    gram2 = gather(gram2_strip, "col", cols).reshape(width, width)
+    second_upper = near_cholesky(gram2)
+
+    left, right, packed, pieces = products(
+        place, hamiltonian, wide, half, half_cols, half_next, second_upper, rows, cols
     )
     gram2, panel_top, packed = lax.optimization_barrier((gram2, panel_top, packed))
-    factor = compact_factor(gram2, panel_top, first_inv, second_upper)
-    packed = lax.all_to_all(packed, "col", 0, 0, tiled=True).sum(axis=0)
-    part_cols = part_cols.reshape(rows, cols_dev // rows, width)
-    cols_piece = lax.all_to_all(part_cols, "row", 0, 0, tiled=True).sum(axis=0)
-    product_rows = gather(packed[:piece], "col", cols).reshape(rows_dev, width)
-    both = gather(jnp.concatenate([cols_piece, packed[piece:]], axis=0), "row", rows)
-    product_cols = both[:, : cols_dev // rows].reshape(cols_dev, width)
-    coupling_strip = both[:, cols_dev // rows :].sum(axis=0)
-    coupling = gather(coupling_strip, "col", cols).reshape(width, width)
-    updated = update(hamiltonian, left, product_rows, right, product_cols, factor, coupling)
+    factor, band_block = compact_factor(
+        gram2, panel_top, first_inv, second_upper, first_upper
+    )
+    packed = lax.all_to_all(packed, "col", 0, 0, axis_index_groups=groups, tiled=True)
+    packed = packed.sum(axis=0)
+    near_piece = tree_sum(hops(pieces, rows))
+    mine = jnp.broadcast_to(packed[:piece][None], (chips, piece, width))
+    mine = lax.all_to_all(mine, "col", 0, 0, axis_index_groups=groups, tiled=True)
+    mine = mine.reshape(deep, width)
+    other = lax.ppermute(mine, "col", pair)
+    both = jnp.concatenate([near_piece, packed[piece:]], axis=0)
+    both = hops([both] * rows, rows)
+    coupling_strip = tree_sum([value[share:] for value in both])
+    coupling = gather(coupling_strip, "col", cols)
+    coupling = coupling.reshape(chips, 2, width // chips, width).sum(axis=1)
+    coupling = coupling.reshape(width, width)
+    updated = update(place, hamiltonian, left, mine, other, right, factor, coupling, both)
     return (updated, band_block)
 
 

time: 172 us -> 137 us (0.80)
  waiting for transfers between devices: 75.4 us -> 41 us
  starting transfers between devices: 47.9 us -> 42.4 us
  other arithmetic: 0.32 us -> 3.3 us
  Pallas kernels: 27.6 us -> 25.1 us
  local copies, waits for them, and re-layouts: 13.8 us -> 16 us
    all_to_all x2, waiting for transfers between devices: 24.7 us -> 0.01 us  [the longest x1 0.01 us: shards(): lax.all_to_all(packed, 'col', 0, 0, axis_index_groups=groups, tiled=True)]
    all_to_all x7 -> x5, waiting for transfers between devices: 43.9 us -> 26.1 us  [gather(): return lax.all_to_all(copies, axis, 0, 0, tiled=True)]
    ppermute x0 -> x9, waiting for transfers between devices: none -> 12.7 us  [the longest x6 12.7 us: hops(): lax.ppermute(values[hop], 'row', [(i, i ^ hop) for i in range(size)])]
    ppermute x0 -> x9, starting transfers between devices: none -> 9.35 us  [the longest x6 8.9 us: hops(): lax.ppermute(values[hop], 'row', [(i, i ^ hop) for i in range(size)])]
    all_to_all x7 -> x5, starting transfers between devices: 28.8 us -> 21.9 us  [gather(): return lax.all_to_all(copies, axis, 0, 0, tiled=True)]
    ppermute x4 -> x2, starting transfers between devices: 9.17 us -> 3.79 us  [spread_rows(): value = value + lax.ppermute(value, ('row', 'col'), pairs)]
    ppermute x4 -> x2, waiting for transfers between devices: 6.78 us -> 2.2 us  [spread_rows(): value = value + lax.ppermute(value, ('row', 'col'), pairs)]
    pallas_call x3, Pallas kernels: 13.7 us -> 11.1 us  [the longest x1 4.23 us: compact_factor(): pl.pallas_call(factor_kernel, out_shape=(square(gram.shape[0]), square(gr...]
  transfers between devices with their start and end apart: 13 -> 18, of which waited for: 9 -> 9; matrix products, arithmetic and copies ran while one was open for 3% -> 8% of each run, Pallas kernels for 8% -> 12%
where the time goes in v3:
time: 137 us; the launch traced here: 136 us
  starting transfers between devices  42.4 us (31%)
  waiting for transfers between devices  41 us (30%)
  Pallas kernels  25.1 us (18%)
  local copies, waits for them, and re-layouts  16 us (12%)
  matrix products  5.97 us (4%)
  other arithmetic  3.3 us (2%)
  between operations  1.67 us (1%)
    all_to_all x5, waiting for transfers between devices, gather(): return lax.all_to_all(copies, axis, 0, 0, tiled=True)  26.1 us
    all_to_all x5, starting transfers between devices, gather(): return lax.all_to_all(copies, axis, 0, 0, tiled=True)  21.9 us
    ppermute x6, waiting for transfers between devices, hops(): lax.ppermute(values[hop], 'row', [(i, i ^ hop) for i in range(size)])  12.7 us
    unnamed x44, local copies, waits for them, and re-layouts  9.92 us
    pallas_call x1, Pallas kernels, cholesky(): pl.pallas_call(chol_kernel, out_shape=(square(size), square(size)), scrat...  9.68 us
    ppermute x6, starting transfers between devices, hops(): lax.ppermute(values[hop], 'row', [(i, i ^ hop) for i in range(size)])  8.9 us
    dot_general x5, matrix products, mult(): lax.dot_general(left, right, (dims, ((), ())), precision=HIGHEST, preferr...  5.97 us
    pallas_call x1, Pallas kernels, products(): pl.pallas_call(products_kernel, in_specs=[pl.BlockSpec(memory_space=pltpu...  4.33 us
  transfers between devices with their start and end apart: 18, of which 9 were waited for; matrix products, arithmetic and copies ran while one was open for 8% of the time, Pallas kernels for 12%

profile of v3, /device:TPU:0, one launch (start us, length us, event | category | flops | bytes accessed | tf_op | source)
XLA Modules:
  0.0 135.6 jit_solution(12098928285482648634)
XLA Ops:
  0.7 2.2 %fusion.2 = f32[32,256]{1,0:T(8,128)S(1)} fusion(f32[768,256]{1,0:T(8,128)} %param.4, s32[]{:T(128)S(6)} %select_n.43), kind=kOutput, calls=%fused_computation.4 | convolution fusion | flops 75497472 | bytes 1212420 | tf_op jit(solution)/shard_map/dot_general | solution.py:21
  3.7 6.3 %all-to-all-start = ((f32[4,64,256]{2,1,0:T(8,128)}), f32[4,64,256]{2,1,0:T(8,128)S(1)}, u32[]{:S(2)}, u32[]{:S(2)}) async-start(f32[4,64,256]{2,1,0:T(8,128)} %broadcast_in_dim.21), calls=%async_computation | async-start | bytes 524288 | tf_op jit(solution)/shard_map/all_to_all | solution.py:338
  11.3 7.6 %all-to-all-done = f32[4,64,256]{2,1,0:T(8,128)S(1)} async-done(((f32[4,64,256]{2,1,0:T(8,128)}), f32[4,64,256]{2,1,0:T(8,128)S(1)}, u32[]{:S(2)}, u32[]{:S(2)}) %all-to-all-start) | async-done | bytes 262176 | tf_op jit(solution)/shard_map/all_to_all | solution.py:338
  19.0 1.7 %collective-permute-start.1 = (f32[384,256]{1,0:T(8,128)S(1)}, f32[384,256]{1,0:T(8,128)S(1)}, u32[]{:S(2)}, u32[]{:S(2)}) collective-permute-start(f32[384,256]{1,0:T(8,128)S(1)} %broadcast_select_fusion), channel_id=1, source_target_pairs={{0,16},{1,17},{10,26},{11,27},{20,4},{21,5},{30,14},{31,15}} | collective-permute-start | bytes 1179656 | tf_op jit(solution)/shard_map/ppermute | solution.py:367
  20.7 0.8 broadcast_in_dim.22
  21.6 3.5 %all-to-all-start.1 = ((f32[8,64,256]{2,1,0:T(8,128)}), f32[8,64,256]{2,1,0:T(8,128)S(1)}, u32[]{:S(2)}, u32[]{:S(2)}) async-start(f32[8,64,256]{2,1,0:T(8,128)} %broadcast_in_dim.22), calls=%async_computation.1 | async-start | bytes 1048576 | tf_op jit(solution)/shard_map/all_to_all | solution.py:338
  25.1 2.2 %collective-permute-done.1 = f32[384,256]{1,0:T(8,128)S(1)} collective-permute-done((f32[384,256]{1,0:T(8,128)S(1)}, f32[384,256]{1,0:T(8,128)S(1)}, u32[]{:S(2)}, u32[]{:S(2)}) %collective-permute-start.1) | collective-permute-done | bytes 393248 | tf_op jit(solution)/shard_map/ppermute | solution.py:367
  27.3 2.0 %collective-permute-start.2 = (f32[384,256]{1,0:T(8,128)S(1)}, f32[384,256]{1,0:T(8,128)}, u32[]{:S(2)}, u32[]{:S(2)}) collective-permute-start(f32[384,256]{1,0:T(8,128)S(1)} %fusion.18), channel_id=1, source_target_pairs={{0,8},{16,24},{1,9},{17,25},{10,2},{26,18},{11,3},{27,19},{20,28},... | collective-permute-start | bytes 1179656 | tf_op jit(solution)/shard_map/ppermute | solution.py:367
  29.4 5.4 %all-to-all-done.1 = f32[8,64,256]{2,1,0:T(8,128)S(1)} async-done(((f32[8,64,256]{2,1,0:T(8,128)}), f32[8,64,256]{2,1,0:T(8,128)S(1)}, u32[]{:S(2)}, u32[]{:S(2)}) %all-to-all-start.1) | async-done | bytes 524320 | tf_op jit(solution)/shard_map/all_to_all | solution.py:338
  34.8 9.7 %cholesky_inverse.1 = (f32[256,256]{1,0:T(8,128)S(1)}, f32[256,256]{1,0:T(8,128)S(1)}) custom-call(f32[256,256]{1,0:T(8,128)S(1)} %bitcast.26), custom_call_target="tpu_custom_call" | custom-call | flops 10000000000 | bytes 30000000 | tf_op jit(solution)/shard_map/cholesky_inverse/pallas_call | solution.py:131
  44.5 0.8 convolution_bitcast_fusion.half_ref
  45.3 1.0 add.49
  47.0 0.9 fusion
  48.6 4.3 %all-to-all-start.2 = ((f32[4,32,256]{2,1,0:T(8,128)}), f32[4,32,256]{2,1,0:T(8,128)S(1)}, u32[]{:S(2)}, u32[]{:S(2)}) async-start(f32[4,32,256]{2,1,0:T(8,128)} %broadcast_in_dim.24), calls=%async_computation.2 | async-start | bytes 262144 | tf_op jit(solution)/shard_map/all_to_all | solution.py:338
  52.8 0.9 constant_dynamic-slice_fusion.1
  54.0 5.3 %all-to-all-done.2 = f32[4,32,256]{2,1,0:T(8,128)S(1)} async-done(((f32[4,32,256]{2,1,0:T(8,128)}), f32[4,32,256]{2,1,0:T(8,128)S(1)}, u32[]{:S(2)}, u32[]{:S(2)}) %all-to-all-start.2) | async-done | bytes 131104 | tf_op jit(solution)/shard_map/all_to_all | solution.py:338
  60.0 3.4 %all-to-all-start.3 = ((f32[8,32,256]{2,1,0:T(8,128)}), f32[8,32,256]{2,1,0:T(8,128)S(1)}, u32[]{:S(2)}, u32[]{:S(2)}) async-start(f32[8,32,256]{2,1,0:T(8,128)} %broadcast_in_dim.25), calls=%async_computation.3 | async-start | bytes 524288 | tf_op jit(solution)/shard_map/all_to_all | solution.py:338
  63.4 1.5 %fusion.9.next_ref = f32[384,256]{1,0:T(8,128)S(1)} fusion(f32[384,256]{1,0:T(8,128)} %collective-permute-done.3, f32[256,256]{1,0:T(8,128)S(1)} %get-tuple-element.21.inv_ref), kind=kOutput, calls=%fused_computation.21 | convolution fusion | flops 301989888 | bytes 1048576 | tf_op jit(solution)/shard_map/dot_general | solution.py:21
  64.9 5.3 %all-to-all-done.3 = f32[8,32,256]{2,1,0:T(8,128)S(1)} async-done(((f32[8,32,256]{2,1,0:T(8,128)}), f32[8,32,256]{2,1,0:T(8,128)S(1)}, u32[]{:S(2)}, u32[]{:S(2)}) %all-to-all-start.3) | async-done | bytes 262176 | tf_op jit(solution)/shard_map/all_to_all | solution.py:338
  70.3 2.9 %near_cholesky.1.upper_ref = f32[256,256]{1,0:T(8,128)S(1)} custom-call(f32[256,256]{1,0:T(8,128)S(1)} %bitcast.23), custom_call_target="tpu_custom_call" | custom-call | flops 3000000000 | bytes 9000000 | tf_op jit(solution)/shard_map/near_cholesky/pallas_call | solution.py:186
  73.2 4.3 %products.1 = (f32[768,256]{1,0:T(8,128)S(1)}, f32[384,256]{1,0:T(8,128)S(1)}, f32[4,160,256]{2,1,0:T(8,128)}, f32[96,256]{1,0:T(8,128)S(1)}, f32[96,256]{1,0:T(...) custom-call(s32[2]{0:T(128)S(1)} %pad_add_fusion.place_ref, f32[768,384]{1,0:T(8,128)S(1)} %copy-done, ...), custom_call_target="tpu_custom_call" | custom-call | flops 3000000000 | bytes 9000000 | tf_op jit(solution)/shard_map/products/pallas_call | solution.py:284
  80.1 0.9 copy-done.9
  81.0 0.7 copy-done.11
  81.7 3.6 %all-to-all-start.4 = ((f32[4,160,256]{2,1,0:T(8,128)}), f32[4,160,256]{2,1,0:T(8,128)S(1)}, u32[]{:S(2)}, u32[]{:S(2)}) async-start(f32[4,160,256]{2,1,0:T(8,128)} %get-tuple-element.27), calls=%async_computation.4 | async-start | bytes 1310720 | tf_op jit(solution)/shard_map/all_to_all | solution.py:427
  85.3 1.1 collective-permute-start.5
  86.5 1.3 collective-permute-start.6
  87.7 2.1 %collective-permute-start.7 = (f32[96,256]{1,0:T(8,128)S(1)}, f32[96,256]{1,0:T(8,128)S(1)}, u32[]{:S(2)}, u32[]{:S(2)}) collective-permute-start(f32[96,256]{1,0:T(8,128)S(1)} %copy-done.4), channel_id=1, source_target_pairs={{0,24},{8,16},{16,8},{24,0},{1,25},{9,17},{17,9},{25,1},{2,26},{10... | collective-permute-start | bytes 294920 | tf_op jit(solution)/shard_map/ppermute | solution.py:344
  89.8 1.2 collective-permute-done.5
  91.0 5.3 %collective-permute-done.6 = f32[96,256]{1,0:T(8,128)S(1)} collective-permute-done((f32[96,256]{1,0:T(8,128)S(1)}, f32[96,256]{1,0:T(8,128)S(1)}, u32[]{:S(2)}, u32[]{:S(2)}) %collective-permute-start.6) | collective-permute-done | bytes 98336 | tf_op jit(solution)/shard_map/ppermute | solution.py:344
  96.4 1.2 collective-permute-start.10
  97.6 1.9 %collective-permute-start.9 = (f32[160,256]{1,0:T(8,128)S(1)}, f32[160,256]{1,0:T(8,128)S(1)}, u32[]{:S(2)}, u32[]{:S(2)}) collective-permute-start(f32[160,256]{1,0:T(8,128)S(1)} %pad_maximum_fusion.rest_refs_0_), channel_id=1, source_target_pairs={{0,16},{8,24},{16,0},{24,8},{1,17},{9,25},{17,1},{25,9},{2,18},{10... | collective-permute-start | bytes 491528 | tf_op jit(solution)/shard_map/ppermute | solution.py:344
  99.5 1.3 collective-permute-start.8
  100.8 0.8 broadcast_in_dim.26
  101.6 3.8 %all-to-all-start.5 = ((f32[4,96,256]{2,1,0:T(8,128)}), f32[4,96,256]{2,1,0:T(8,128)S(1)}, u32[]{:S(2)}, u32[]{:S(2)}) async-start(f32[4,96,256]{2,1,0:T(8,128)} %broadcast_in_dim.26), calls=%async_computation.5 | async-start | bytes 786432 | tf_op jit(solution)/shard_map/all_to_all | solution.py:431
  105.4 6.3 %collective-permute-done.9.rest_refs_2_ = f32[160,256]{1,0:T(8,128)S(1)} collective-permute-done((f32[160,256]{1,0:T(8,128)S(1)}, f32[160,256]{1,0:T(8,128)S(1)}, u32[]{:S(2)}, u32[]{:S(2)}) %collective-permute-start.9) | collective-permute-done | bytes 163872 | tf_op jit(solution)/shard_map/ppermute | solution.py:344
  111.7 0.9 fusion.4
  112.6 0.9 broadcast_in_dim.27
  113.4 4.4 %all-to-all-start.6 = ((f32[8,64,256]{2,1,0:T(8,128)}), f32[8,64,256]{2,1,0:T(8,128)}, u32[]{:S(2)}, u32[]{:S(2)}) async-start(f32[8,64,256]{2,1,0:T(8,128)} %broadcast_in_dim.27), calls=%async_computation.6 | async-start | bytes 1048576 | tf_op jit(solution)/shard_map/all_to_all | solution.py:338
  118.0 0.9 copy-done.16
  118.9 0.9 copy-done.18
  119.9 4.2 %compact_factor.1 = (f32[256,256]{1,0:T(8,128)S(1)}, f32[256,256]{1,0:T(8,128)}) custom-call(f32[256,256]{1,0:T(8,128)S(1)} %bitcast.24, f32[256,256]{1,0:T(8,128)S(1)} %bitcast.25, f32[256,256]{1,0:T(8,128)S(1)} %get-tuple-element.21.inv_ref, f32[256,256]{1,0:T(8,128)S(1)} %copy-done.16, f32[256,256]{1,0:T(8,128)S(1)} %copy-done.18), custom_call_target="tpu_custom_call" | custom-call | flops 4000000000 | bytes 12000000 | tf_op jit(solution)/shard_map/compact_factor/pallas_call | solution.py:231
  124.1 0.7 copy-done.13
  124.8 2.5 %all-to-all-done.6 = f32[8,64,256]{2,1,0:T(8,128)} async-done(((f32[8,64,256]{2,1,0:T(8,128)}), f32[8,64,256]{2,1,0:T(8,128)}, u32[]{:S(2)}, u32[]{:S(2)}) %all-to-all-start.6) | async-done | bytes 524320 | tf_op jit(solution)/shard_map/all_to_all | solution.py:338
  127.4 1.1 bitcast_reduce_fusion
  128.5 1.1 copy-done.10
  129.6 1.0 copy-done.12
  130.6 0.9 copy-done.14
  131.6 4.0 %two_sided_update.1 = f32[768,384]{1,0:T(8,128)} custom-call(s32[2]{0:T(128)S(1)} %pad_add_fusion.place_ref, f32[768,384]{1,0:T(8,128)S(1)} %copy-done, f32[768,256]{1,0:T(8,128)S(1)} %copy-done.10, f32[384,256]{1,0:T(8,128)S(1)} %bitcast.21, f32[384,256]{1,0:T(8,128)S(1)} %collective-permute-done.4.other_ref, f32[384,256]{1,0:T(8,128)S(1)} %copy-done.12, ...), custom_call_target="tpu_custom_call" | custom-call | flops 3000000000 | bytes 9000000 | tf_op jit(solution)/shard_map/two_sided_update/pallas_call | solution.py:325
  (69 shorter events, 6.7 us)
Async XLA Ops:
  0.6 2.3 %slice-start = ((f32[768,256]{1,0:T(8,128)}), f32[256,256]{1,0:T(8,128)S(1)}, s32[]{:S(2)}) async-start(f32[768,256]{1,0:T(8,128)} %param.4), calls=%async_computation.7 | async-start | bytes 524288 | tf_op jit(solution)/shard_map/slice | solution.py:395
  0.6 9.4 %copy-start.21 = (s32[8]{0:T(128)S(1)}, s32[8]{0:T(128)}, u32[]{:S(2)}) copy-start(s32[8]{0:T(128)} %constant.44.clone) | copy-start | bytes 100
  0.7 10.6 %copy-start.19 = (f32[768,256]{1,0:T(8,128)S(1)}, f32[768,256]{1,0:T(8,128)}, u32[]{:S(2)}) copy-start(f32[768,256]{1,0:T(8,128)} %param.4) | copy-start | bytes 2359300
  3.7 15.2 %all-to-all-start = ((f32[4,64,256]{2,1,0:T(8,128)}), f32[4,64,256]{2,1,0:T(8,128)S(1)}, u32[]{:S(2)}, u32[]{:S(2)}) async-start(f32[4,64,256]{2,1,0:T(8,128)} %broadcast_in_dim.21), calls=%async_computation | async-start | bytes 524288 | tf_op jit(solution)/shard_map/all_to_all | solution.py:338
  19.0 8.3 %collective-permute-start.1 = (f32[384,256]{1,0:T(8,128)S(1)}, f32[384,256]{1,0:T(8,128)S(1)}, u32[]{:S(2)}, u32[]{:S(2)}) collective-permute-start(f32[384,256]{1,0:T(8,128)S(1)} %broadcast_select_fusion), channel_id=1, source_target_pairs={{0,16},{1,17},{10,26},{11,27},{20,4},{21,5},{30,14},{31,15}} | collective-permute-start | bytes 1179656 | tf_op jit(solution)/shard_map/ppermute | solution.py:367
  21.6 13.2 %all-to-all-start.1 = ((f32[8,64,256]{2,1,0:T(8,128)}), f32[8,64,256]{2,1,0:T(8,128)S(1)}, u32[]{:S(2)}, u32[]{:S(2)}) async-start(f32[8,64,256]{2,1,0:T(8,128)} %broadcast_in_dim.22), calls=%async_computation.1 | async-start | bytes 1048576 | tf_op jit(solution)/shard_map/all_to_all | solution.py:338
  27.3 18.0 %collective-permute-start.2 = (f32[384,256]{1,0:T(8,128)S(1)}, f32[384,256]{1,0:T(8,128)}, u32[]{:S(2)}, u32[]{:S(2)}) collective-permute-start(f32[384,256]{1,0:T(8,128)S(1)} %fusion.18), channel_id=1, source_target_pairs={{0,8},{16,24},{1,9},{17,25},{10,2},{26,18},{11,3},{27,19},{20,28},... | collective-permute-start | bytes 1179656 | tf_op jit(solution)/shard_map/ppermute | solution.py:367
  44.5 1.9 %copy-start.17 = (f32[256,256]{1,0:T(8,128)}, f32[256,256]{1,0:T(8,128)S(1)}, u32[]{:S(2)}) copy-start(f32[256,256]{1,0:T(8,128)S(1)} %get-tuple-element.31.first_ref) | copy-start | bytes 786436
  46.4 6.5 %copy-start = (f32[768,384]{1,0:T(8,128)S(1)}, f32[768,384]{1,0:T(8,128)}, u32[]{:S(2)}) copy-start(f32[768,384]{1,0:T(8,128)} %ham_ref.3) | copy-start | bytes 3538948
  46.4 17.0 %collective-permute-start.3 = (f32[384,256]{1,0:T(8,128)S(1)}, f32[384,256]{1,0:T(8,128)}, u32[]{:S(2)}, u32[]{:S(2)}) collective-permute-start(f32[384,256]{1,0:T(8,128)S(1)} %add.49), channel_id=1, source_target_pairs={{0,1},{1,0},{2,3},{3,2},{4,5},{5,4},{6,7},{7,6},{8,9},{9,8},{10,11... | collective-permute-start | bytes 1179656 | tf_op jit(solution)/shard_map/ppermute | solution.py:405
  48.6 10.7 %all-to-all-start.2 = ((f32[4,32,256]{2,1,0:T(8,128)}), f32[4,32,256]{2,1,0:T(8,128)S(1)}, u32[]{:S(2)}, u32[]{:S(2)}) async-start(f32[4,32,256]{2,1,0:T(8,128)} %broadcast_in_dim.24), calls=%async_computation.2 | async-start | bytes 262144 | tf_op jit(solution)/shard_map/all_to_all | solution.py:338
  53.7 19.5 %collective-permute-start = (f32[384,384]{1,0:T(8,128)}, f32[384,384]{1,0:T(8,128)}, u32[]{:S(2)}, u32[]{:S(2)}) collective-permute-start(f32[384,384]{1,0:T(8,128)} %constant_dynamic-slice_fusion.1), channel_id=1, source_target_pairs={{0,1},{1,0},{2,3},{3,2},{4,5},{5,4},{6,7},{7,6},{8,9},{9,8},{10,11... | collective-permute-start | bytes 1769480 | tf_op jit(solution)/shard_map/ppermute | solution.py:392
  60.0 10.3 %all-to-all-start.3 = ((f32[8,32,256]{2,1,0:T(8,128)}), f32[8,32,256]{2,1,0:T(8,128)S(1)}, u32[]{:S(2)}, u32[]{:S(2)}) async-start(f32[8,32,256]{2,1,0:T(8,128)} %broadcast_in_dim.25), calls=%async_computation.3 | async-start | bytes 524288 | tf_op jit(solution)/shard_map/all_to_all | solution.py:338
  73.2 4.4 %copy-start.15 = (f32[256,256]{1,0:T(8,128)}, f32[256,256]{1,0:T(8,128)S(1)}, u32[]{:S(2)}) copy-start(f32[256,256]{1,0:T(8,128)S(1)} %near_cholesky.1.upper_ref) | copy-start | bytes 786436
  77.5 0.6 copy-start.1
  78.2 0.6 copy-start.3
  78.8 0.6 copy-start.5
  79.4 0.6 copy-start.7
  80.1 0.9 copy-start.9
  80.9 0.7 copy-start.11
  81.7 3.6 %copy-start.8 = (f32[96,256]{1,0:T(8,128)S(1)}, f32[96,256]{1,0:T(8,128)}, u32[]{:S(2)}) copy-start(f32[96,256]{1,0:T(8,128)} %copy-done.7) | copy-start | bytes 294916
  81.7 4.8 %copy-start.6 = (f32[96,256]{1,0:T(8,128)S(1)}, f32[96,256]{1,0:T(8,128)}, u32[]{:S(2)}) copy-start(f32[96,256]{1,0:T(8,128)} %copy-done.5) | copy-start | bytes 294916
  81.7 6.0 %copy-start.4 = (f32[96,256]{1,0:T(8,128)S(1)}, f32[96,256]{1,0:T(8,128)}, u32[]{:S(2)}) copy-start(f32[96,256]{1,0:T(8,128)} %copy-done.3) | copy-start | bytes 294916
  81.7 14.5 %copy-start.2 = (f32[96,256]{1,0:T(8,128)S(1)}, f32[96,256]{1,0:T(8,128)}, u32[]{:S(2)}) copy-start(f32[96,256]{1,0:T(8,128)} %copy-done.1) | copy-start | bytes 294916
  81.7 14.6 %all-to-all-start.4 = ((f32[4,160,256]{2,1,0:T(8,128)}), f32[4,160,256]{2,1,0:T(8,128)S(1)}, u32[]{:S(2)}, u32[]{:S(2)}) async-start(f32[4,160,256]{2,1,0:T(8,128)} %get-tuple-element.27), calls=%async_computation.4 | async-start | bytes 1310720 | tf_op jit(solution)/shard_map/all_to_all | solution.py:427
  85.3 5.6 %collective-permute-start.5 = (f32[96,256]{1,0:T(8,128)S(1)}, f32[96,256]{1,0:T(8,128)S(1)}, u32[]{:S(2)}, u32[]{:S(2)}) collective-permute-start(f32[96,256]{1,0:T(8,128)S(1)} %copy-done.8), channel_id=1, source_target_pairs={{0,8},{8,0},{16,24},{24,16},{1,9},{9,1},{17,25},{25,17},{2,10},{10... | collective-permute-start | bytes 294920 | tf_op jit(solution)/shard_map/ppermute | solution.py:344
  86.5 9.8 %collective-permute-start.6 = (f32[96,256]{1,0:T(8,128)S(1)}, f32[96,256]{1,0:T(8,128)S(1)}, u32[]{:S(2)}, u32[]{:S(2)}) collective-permute-start(f32[96,256]{1,0:T(8,128)S(1)} %copy-done.6), channel_id=1, source_target_pairs={{0,16},{8,24},{16,0},{24,8},{1,17},{9,25},{17,1},{25,9},{2,18},{10... | collective-permute-start | bytes 294920 | tf_op jit(solution)/shard_map/ppermute | solution.py:344
  87.7 8.5 %collective-permute-start.7 = (f32[96,256]{1,0:T(8,128)S(1)}, f32[96,256]{1,0:T(8,128)S(1)}, u32[]{:S(2)}, u32[]{:S(2)}) collective-permute-start(f32[96,256]{1,0:T(8,128)S(1)} %copy-done.4), channel_id=1, source_target_pairs={{0,24},{8,16},{16,8},{24,0},{1,25},{9,17},{17,9},{25,1},{2,26},{10... | collective-permute-start | bytes 294920 | tf_op jit(solution)/shard_map/ppermute | solution.py:344
  96.3 5.3 %copy-start.20 = (f32[160,256]{1,0:T(8,128)}, f32[160,256]{1,0:T(8,128)S(1)}, u32[]{:S(2)}) copy-start(f32[160,256]{1,0:T(8,128)S(1)} %reduce_sum.38) | copy-start | bytes 491524
  96.4 9.1 %collective-permute-start.10 = (f32[160,256]{1,0:T(8,128)S(1)}, f32[160,256]{1,0:T(8,128)S(1)}, u32[]{:S(2)}, u32[]{:S(2)}) collective-permute-start(f32[160,256]{1,0:T(8,128)S(1)} %pad_maximum_fusion.rest_refs_0_), channel_id=1, source_target_pairs={{0,24},{8,16},{16,8},{24,0},{1,25},{9,17},{17,9},{25,1},{2,26},{10... | collective-permute-start | bytes 491528 | tf_op jit(solution)/shard_map/ppermute | solution.py:344
  97.6 14.1 %collective-permute-start.9 = (f32[160,256]{1,0:T(8,128)S(1)}, f32[160,256]{1,0:T(8,128)S(1)}, u32[]{:S(2)}, u32[]{:S(2)}) collective-permute-start(f32[160,256]{1,0:T(8,128)S(1)} %pad_maximum_fusion.rest_refs_0_), channel_id=1, source_target_pairs={{0,16},{8,24},{16,0},{24,8},{1,17},{9,25},{17,1},{25,9},{2,18},{10... | collective-permute-start | bytes 491528 | tf_op jit(solution)/shard_map/ppermute | solution.py:344
  99.5 12.2 %collective-permute-start.8 = (f32[160,256]{1,0:T(8,128)S(1)}, f32[160,256]{1,0:T(8,128)S(1)}, u32[]{:S(2)}, u32[]{:S(2)}) collective-permute-start(f32[160,256]{1,0:T(8,128)S(1)} %pad_maximum_fusion.rest_refs_0_), channel_id=1, source_target_pairs={{0,8},{8,0},{16,24},{24,16},{1,9},{9,1},{17,25},{25,17},{2,10},{10... | collective-permute-start | bytes 491528 | tf_op jit(solution)/shard_map/ppermute | solution.py:344
  101.6 11.0 %all-to-all-start.5 = ((f32[4,96,256]{2,1,0:T(8,128)}), f32[4,96,256]{2,1,0:T(8,128)S(1)}, u32[]{:S(2)}, u32[]{:S(2)}) async-start(f32[4,96,256]{2,1,0:T(8,128)} %broadcast_in_dim.26), calls=%async_computation.5 | async-start | bytes 786432 | tf_op jit(solution)/shard_map/all_to_all | solution.py:431
  113.4 13.9 %all-to-all-start.6 = ((f32[8,64,256]{2,1,0:T(8,128)}), f32[8,64,256]{2,1,0:T(8,128)}, u32[]{:S(2)}, u32[]{:S(2)}) async-start(f32[8,64,256]{2,1,0:T(8,128)} %broadcast_in_dim.27), calls=%async_computation.6 | async-start | bytes 1048576 | tf_op jit(solution)/shard_map/all_to_all | solution.py:338
  117.8 10.6 %collective-permute-start.4 = (f32[384,256]{1,0:T(8,128)S(1)}, f32[384,256]{1,0:T(8,128)S(1)}, u32[]{:S(2)}, u32[]{:S(2)}) collective-permute-start(f32[384,256]{1,0:T(8,128)S(1)} %bitcast.20), channel_id=1, source_target_pairs={{0,1},{1,0},{2,3},{3,2},{4,5},{5,4},{6,7},{7,6},{8,9},{9,8},{10,11... | collective-permute-start | bytes 1179656 | tf_op jit(solution)/shard_map/ppermute | solution.py:433
  118.0 0.9 copy-start.16
  118.9 0.9 copy-start.18
  124.1 0.7 copy-start.13
  128.5 1.1 copy-start.10
  129.6 1.0 copy-start.12
  130.6 0.9 copy-start.14

commit v4 on v3

--- a/solution.py
+++ b/solution.py
@@ -11,7 +11,10 @@
 LANE = 128
 BLOCK = 32
 HIGHEST = lax.Precision.HIGHEST
-PARAMS = pltpu.CompilerParams(vmem_limit_bytes=48 * 2**20)
+SMALL = pltpu.CompilerParams(vmem_limit_bytes=10 * 2**20)
+LARGE = pltpu.CompilerParams(vmem_limit_bytes=24 * 2**20)
+VMEM = pl.BlockSpec(memory_space=pltpu.VMEM)
+SMEM = pl.BlockSpec(memory_space=pltpu.SMEM)
 PLAIN = ((1,), (0,))
 TURNED = ((0,), (0,))
 ACROSS = ((1,), (1,))
@@ -132,7 +135,7 @@
         chol_kernel,
         out_shape=(square(size), square(size)),
         scratch_shapes=[pltpu.VMEM((size, size), jnp.float32)],
-        compiler_params=PARAMS,
+        compiler_params=SMALL,
         cost_estimate=estimate(10),
         name="cholesky_inverse",
     )(gram)
@@ -155,11 +158,11 @@
         halves = split(inv)
         upper = mult3(halves, gram)
         low = weight * (mult3(split(upper), halves, ACROSS) - ident)
-        return upper, low, jnp.max(jnp.abs(low))
+        return upper, low, jnp.sum(low * low)
 
     def more(state):
         count, _, _, _, worst = state
-        return jnp.logical_not(worst < 1e-4) & (count < 8)
+        return jnp.logical_not(worst < 1e-5) & (count < 8)
 
     def step(state):
         count, inv, _, low, _ = state
@@ -176,7 +179,7 @@
     upper = upper + mult3(split(low), split(upper), TURNED)
     upper_ref[...] = jnp.where(row <= col, upper, 0.0)
 
-    @pl.when(jnp.logical_not(worst < 1e-4))
+    @pl.when(jnp.logical_not(worst < 1e-5))
     def _():
         chol_kernel(gram_ref, upper_ref, inv_ref, work_ref)
 
@@ -187,7 +190,7 @@
         near_kernel,
         out_shape=square(size),
         scratch_shapes=[pltpu.VMEM((size, size), jnp.float32)] * 2,
-        compiler_params=PARAMS,
+        compiler_params=SMALL,
         cost_estimate=estimate(3),
         name="near_cholesky",
     )(gram)
@@ -231,7 +234,7 @@
     return pl.pallas_call(
         factor_kernel,
         out_shape=(square(gram.shape[0]), square(gram.shape[0])),
-        compiler_params=PARAMS,
+        compiler_params=SMALL,
         cost_estimate=estimate(4),
         name="compact_factor",
     )(gram, top, inv, upper, first)
@@ -244,7 +247,7 @@
     piece_refs, cols_ref = rest_refs[:-1], rest_refs[-1]
     width = upper_ref.shape[0]
     chips = packed_ref.shape[0]
-    deep = wide_ref.shape[0]
+    deep = wide_ref.shape[0] // 2
     piece, strip = deep // chips, width // chips
     share = piece_refs[0].shape[0]
     row_place, col_place = place_ref[0], place_ref[1]
@@ -260,7 +263,7 @@
         [next_ref[:width, :] + next_lead * upper_ref[...], next_ref[width:, :]], axis=0
     )
     part = mult3(split(ham_ref[mine, :]), split(right_ref[...]))
-    part = part + mult3(split(wide_ref[...]), split(beside))
+    part = part + mult3(split(wide_ref[mine, :]), split(beside))
     coupling = mult3(split(left_ref[mine, :]), split(part), TURNED)
     for c in range(chips):
         packed_ref[c, :piece, :] = part[c * piece : (c + 1) * piece]
@@ -276,30 +279,82 @@
     width = upper.shape[0]
     chips = cols // 2
     share = (rows_dev // 2 + width) // chips
-
-    def shape(*dims):
-        return jax.ShapeDtypeStruct(dims, jnp.float32)
-
-    vmem = pl.BlockSpec(memory_space=pltpu.VMEM)
     out = pl.pallas_call(
         products_kernel,
-        in_specs=[pl.BlockSpec(memory_space=pltpu.SMEM)] + [vmem] * 6,
+        in_specs=[SMEM] + [VMEM] * 6,
         out_shape=(
-            shape(rows_dev, width),
-            shape(cols_dev, width),
-            shape(chips, share, width),
+            array(rows_dev, width),
+            array(cols_dev, width),
+            array(chips, share, width),
         )
-        + (shape(cols_dev // rows, width),) * rows,
+        + (array(cols_dev // rows, width),) * rows,
         scratch_shapes=[pltpu.VMEM((cols_dev, width), jnp.float32)],
-        compiler_params=PARAMS,
-        cost_estimate=estimate(3),
+        compiler_params=LARGE,
+        cost_estimate=estimate(4),
         name="products",
     )(place, hamiltonian, wide, half, half_cols, half_next, upper)
     return out[0], out[1], out[2], out[3:]
 
 
-def update_kernel(place_ref, ham_ref, left_ref, mine_ref, other_ref, right_ref, factor_ref,
-                  coupling_ref, *rest_refs):
+def array(*dims):
+    return jax.ShapeDtypeStruct(dims, jnp.float32)
+
+
+def gram_kernel(place_ref, panel_ref, out_ref, gram_ref):
+    strip = out_ref.shape[1] // 2
+    mine = pl.ds(pl.multiple_of(place_ref[1] * strip, strip), strip)
+    gram_ref[...] = mult(panel_ref[...], panel_ref[...], TURNED)
+    top = panel_ref[mine, :] * jnp.where(place_ref[0] == 0, 1.0, 0.0)
+    for r in range(out_ref.shape[0]):
+        out_ref[r, :strip, :] = gram_ref[mine, :]
+        out_ref[r, strip:, :] = top
+
+
+def gram_strips(place, panel, rows, cols):
+    width = panel.shape[1]
+    return pl.pallas_call(
+        gram_kernel,
+        in_specs=[SMEM, VMEM],
+        out_shape=array(rows, 2 * width // cols, width),
+        scratch_shapes=[pltpu.VMEM((width, width), jnp.float32)],
+        compiler_params=LARGE,
+        cost_estimate=estimate(2),
+        name="gram_strips",
+    )(place, panel)
+
+
+def half_kernel(place_ref, panel_ref, slab_ref, got_ref, inv_ref, half_ref, cols_ref, out_ref,
+                gram_ref):
+    strip = out_ref.shape[1]
+    mine = pl.ds(pl.multiple_of(place_ref[1] * strip, strip), strip)
+    half = mult(panel_ref[...], inv_ref[...], ACROSS)
+    half_ref[...] = half
+    cols_ref[...] = mult(slab_ref[...] + got_ref[...], inv_ref[...], ACROSS)
+    parts = split(half)
+    gram_ref[...] = mult3(parts, parts, TURNED)
+    for r in range(out_ref.shape[0]):
+        out_ref[r] = gram_ref[mine, :]
+
+
+def half_stage(place, panel, slab, got, inv, rows, cols):
+    width = panel.shape[1]
+    return pl.pallas_call(
+        half_kernel,
+        in_specs=[SMEM] + [VMEM] * 4,
+        out_shape=(
+            array(*panel.shape),
+            array(*slab.shape),
+            array(rows, width // cols, width),
+        ),
+        scratch_shapes=[pltpu.VMEM((width, width), jnp.float32)],
+        compiler_params=LARGE,
+        cost_estimate=estimate(3),
+        name="half_stage",
+    )(place, panel, slab, got, inv)
+
+
+def base_kernel(place_ref, ham_ref, left_ref, mine_ref, other_ref, right_ref, factor_ref,
+                *rest_refs):
     piece_refs, out_ref, near_ref = rest_refs[:-2], rest_refs[-2], rest_refs[-1]
     deep = mine_ref.shape[0]
     share = near_ref.shape[0] // len(piece_refs)
@@ -308,11 +363,8 @@
         start = pl.multiple_of((row_place ^ hop) * share, share)
         near_ref[pl.ds(start, share), :] = ref[:share, :]
     factor = split(factor_ref[...])
-    right = split(right_ref[...])
-    turn = mult3(split(coupling_ref[...]), factor)
-    middle = mult3(factor, split(turn), TURNED)
-    near = split(mult3(split(near_ref[...]), factor) - mult3(right, split(middle)))
-    far = split(mult3(right, factor, ACROSS))
+    near = split(mult3(split(near_ref[...]), factor))
+    far = split(mult3(split(right_ref[...]), factor, ACROSS))
     for place, prod_ref in ((core, mine_ref), (1 - core, other_ref)):
         block = pl.ds(pl.multiple_of(place * deep, deep), deep)
         change = mult3(split(left_ref[block, :]), near, ACROSS)
@@ -320,17 +372,39 @@
         out_ref[block, :] = ham_ref[block, :] - change
 
 
-def update(place, hamiltonian, left, mine, other, right, factor, coupling, pieces):
-    vmem = pl.BlockSpec(memory_space=pltpu.VMEM)
-    return pl.pallas_call(
-        update_kernel,
-        in_specs=[pl.BlockSpec(memory_space=pltpu.SMEM)] + [vmem] * (7 + len(pieces)),
-        out_shape=jax.ShapeDtypeStruct(hamiltonian.shape, jnp.float32),
+def base_update(place, hamiltonian, left, mine, other, right, factor, pieces):
+    return pl.pallas_call(
+        base_kernel,
+        in_specs=[SMEM] + [VMEM] * (6 + len(pieces)),
+        out_shape=array(*hamiltonian.shape),
         scratch_shapes=[pltpu.VMEM(right.shape, jnp.float32)],
-        compiler_params=PARAMS,
+        compiler_params=LARGE,
         cost_estimate=estimate(3),
-        name="two_sided_update",
-    )(place, hamiltonian, left, mine, other, right, factor, coupling, *pieces)
+        name="base_update",
+    )(place, hamiltonian, left, mine, other, right, factor, *pieces)
+
+
+def coupling_kernel(base_ref, left_ref, right_ref, factor_ref, parts_ref, out_ref, sum_ref):
+    strip = parts_ref.shape[1]
+    for k in range(parts_ref.shape[0] // 2):
+        sum_ref[k * strip : (k + 1) * strip, :] = parts_ref[2 * k] + parts_ref[2 * k + 1]
+    factor = split(factor_ref[...])
+    turn = mult3(split(sum_ref[...]), factor)
+    middle = mult3(factor, split(turn), TURNED)
+    near = mult3(split(right_ref[...]), split(middle))
+    out_ref[...] = base_ref[...] + mult3(split(left_ref[...]), split(near), ACROSS)
+
+
+def coupling_update(base, left, right, factor, parts):
+    return pl.pallas_call(
+        coupling_kernel,
+        in_specs=[VMEM] * 5,
+        out_shape=array(*base.shape),
+        scratch_shapes=[pltpu.VMEM(factor.shape, jnp.float32)],
+        compiler_params=LARGE,
+        cost_estimate=estimate(2),
+        name="coupling_update",
+    )(base, left, right, factor, parts)
 
 
 def gather(piece, axis, size):
@@ -351,31 +425,11 @@
     return terms[0]
 
 
-def spread_rows(value, owners, rows, cols):
-    row_place = lax.axis_index("row")
-    col_place = lax.axis_index("col")
-    owner = jnp.asarray(owners, jnp.int32)[col_place]
-    value = jnp.where(row_place == owner, value, 0.0)
-    hop = rows // 2
-    done = [0]
-    while hop:
-        pairs = []
-        for c in range(cols):
-            for d in done:
-                source = owners[c] ^ d
-                pairs.append((source * cols + c, (source ^ hop) * cols + c))
-        value = value + lax.ppermute(value, ("row", "col"), pairs)
-        done = done + [d ^ hop for d in done]
-        hop //= 2
-    return value
-
-
 def shards(rows, cols, hamiltonian, panel):
     rows_dev, width = panel.shape
     cols_dev = hamiltonian.shape[1]
     row_place = lax.axis_index("row")
     col_place = lax.axis_index("col")
-    core = col_place % 2
     chips = cols // 2
     strip = width // cols
     deep = rows_dev // 2
@@ -385,35 +439,39 @@
     groups = [[2 * k + e for k in range(chips)] for e in range(2)]
     place = jnp.stack([row_place, col_place]).astype(jnp.int32)
 
-    def strip_of(array):
-        return lax.dynamic_slice_in_dim(array, col_place * strip, strip, 1)
-
-    wide = lax.dynamic_slice_in_dim(hamiltonian, (1 - core) * deep, deep, 0)
-    wide = lax.ppermute(wide, "col", pair)
-
-    gram_strip = mult(strip_of(panel), panel, TURNED)
-    top_strip = lax.dynamic_slice_in_dim(panel[:width], col_place * strip, strip, 0)
-    top_strip = jnp.where(row_place == 0, top_strip, 0.0)
-    strips = gather(jnp.concatenate([gram_strip, top_strip], axis=0), "row", rows).sum(axis=0)
+    wide = lax.ppermute(hamiltonian, "col", pair)
 
     owners = [c * cols_dev // rows_dev for c in range(cols)]
     owner = col_place * cols_dev // rows_dev
     offset = col_place * cols_dev - owner * rows_dev
     slab = lax.dynamic_slice_in_dim(panel, offset, cols_dev, 0)
-    strips, slab = lax.optimization_barrier((strips, slab))
-    panel_cols = spread_rows(slab, owners, rows, cols)
-    panel_next = lax.ppermute(panel_cols, "col", pair)
+    slab = jnp.where(row_place == owner, slab, 0.0)
+    hop, having = rows // 2, [0]
+    got = jnp.zeros_like(slab)
+    strips = None
+    while hop:
+        if having != [0]:
+            slab = slab + got
+        if strips is None and (having != [0] or hop == 1):
+            strips = gram_strips(place, panel, rows, cols)
+            strips = lax.all_to_all(strips, "row", 0, 0, tiled=True).sum(axis=0)
+            strips, slab = lax.optimization_barrier((strips, slab))
+        pairs = [
+            ((owners[c] ^ d) * cols + c, (owners[c] ^ d ^ hop) * cols + c)
+            for c in range(cols)
+            for d in having
+        ]
+        got = lax.ppermute(slab, ("row", "col"), pairs)
+        having = having + [d ^ hop for d in having]
+        hop //= 2
 
     strips = gather(strips, "col", cols)
     gram = strips[:, :strip].reshape(width, width)
     panel_top = strips[:, strip:].reshape(width, width)
     first_upper, first_inv = cholesky(gram)
-    half = mult(panel, first_inv, ACROSS)
-    half_cols = mult(panel_cols, first_inv, ACROSS)
-    half, half_cols = lax.optimization_barrier((half, half_cols))
-    half_next = mult(panel_next, first_inv, ACROSS)
-
-    gram2_strip = gather(mult(strip_of(half), half, TURNED), "row", rows).sum(axis=0)
+    half, half_cols, gram2_strips = half_stage(place, panel, slab, got, first_inv, rows, cols)
+    gram2_strip = lax.all_to_all(gram2_strips, "row", 0, 0, tiled=True).sum(axis=0)
+    half_next = lax.ppermute(half_cols, "col", pair)
     gram2 = gather(gram2_strip, "col", cols).reshape(width, width)
     second_upper = near_cholesky(gram2)
 
@@ -434,10 +492,10 @@
     both = jnp.concatenate([near_piece, packed[piece:]], axis=0)
     both = hops([both] * rows, rows)
     coupling_strip = tree_sum([value[share:] for value in both])
+    coupling_strip, factor = lax.optimization_barrier((coupling_strip, factor))
     coupling = gather(coupling_strip, "col", cols)
-    coupling = coupling.reshape(chips, 2, width // chips, width).sum(axis=1)
-    coupling = coupling.reshape(width, width)
-    updated = update(place, hamiltonian, left, mine, other, right, factor, coupling, both)
+    base = base_update(place, hamiltonian, left, mine, other, right, factor, both)
+    updated = coupling_update(base, left, right, factor, coupling)
     return (updated, band_block)
 
 

time: 137 us -> 138 us (level)
  blocking collectives: 0 us -> 9.53 us
  waiting for transfers between devices: 41 us -> 33.5 us
  Pallas kernels: 25.1 us -> 32.4 us
  matrix products: 5.97 us -> 0 us
  starting transfers between devices: 42.4 us -> 41 us
    all_to_all x5 -> x3, starting transfers between devices: 21.9 us -> 11.9 us  [gather(): return lax.all_to_all(copies, axis, 0, 0, tiled=True)]
    all_to_all x0 -> x1, blocking collectives: none -> 9.53 us  [shards(): lax.all_to_all(gram2_strips, 'row', 0, 0, tiled=True).sum(axis=0)]
    all_to_all x5 -> x3, waiting for transfers between devices: 26.1 us -> 18 us  [gather(): return lax.all_to_all(copies, axis, 0, 0, tiled=True)]
    pallas_call x2 -> x5, Pallas kernels: 8.36 us -> 14.6 us  [the longest x1 4.44 us: products(): pl.pallas_call(products_kernel, in_specs=[SMEM] + [VMEM] * 6, out_shape=(...]
    all_to_all x0 -> x1, waiting for transfers between devices: none -> 6.14 us  [shards(): strips = lax.all_to_all(strips, 'row', 0, 0, tiled=True).sum(axis=0)]
    ppermute x6, waiting for transfers between devices: 12.7 us -> 6.65 us  [hops(): lax.ppermute(values[hop], 'row', [(i, i ^ hop) for i in range(size)])]
    dot_general x5 -> x0, matrix products: 5.97 us -> none  [mult(): lax.dot_general(left, right, (dims, ((), ())), precision=HIGHEST, preferr...]
    ppermute x4, starting transfers between devices: 4.08 us -> 8.81 us  [the longest x2 8.04 us: shards(): got = lax.ppermute(slab, ('row', 'col'), pairs)]
  transfers between devices with their start and end apart: 18 -> 17, of which waited for: 9 -> 7; matrix products, arithmetic and copies ran while one was open for 8% -> 3% of each run, Pallas kernels for 12% -> 18%
where the time goes in v4:
time: 138 us; the launch traced here: 137 us
  starting transfers between devices  41 us (30%)
  waiting for transfers between devices  33.5 us (24%)
  Pallas kernels  32.4 us (23%)
  local copies, waits for them, and re-layouts  16.8 us (12%)
  blocking collectives  9.53 us (7%)
  other arithmetic  2.43 us (2%)
    all_to_all x3, waiting for transfers between devices, gather(): return lax.all_to_all(copies, axis, 0, 0, tiled=True)  18 us
    unnamed x38, local copies, waits for them, and re-layouts  12.6 us
    all_to_all x3, starting transfers between devices, gather(): return lax.all_to_all(copies, axis, 0, 0, tiled=True)  11.9 us
    pallas_call x1, Pallas kernels, cholesky(): pl.pallas_call(chol_kernel, out_shape=(square(size), square(size)), scrat...  9.69 us
    all_to_all x1, blocking collectives, shards(): lax.all_to_all(gram2_strips, 'row', 0, 0, tiled=True).sum(axis=0)  9.53 us
    ppermute x6, starting transfers between devices, hops(): lax.ppermute(values[hop], 'row', [(i, i ^ hop) for i in range(size)])  8.9 us
    ppermute x2, starting transfers between devices, shards(): got = lax.ppermute(slab, ('row', 'col'), pairs)  8.04 us
    ppermute x6, waiting for transfers between devices, hops(): lax.ppermute(values[hop], 'row', [(i, i ^ hop) for i in range(size)])  6.65 us
  transfers between devices with their start and end apart: 17, of which 7 were waited for; matrix products, arithmetic and copies ran while one was open for 3% of the time, Pallas kernels for 18%

profile of v4, /device:TPU:0, one launch (start us, length us, event | category | flops | bytes accessed | tf_op | source)
XLA Modules:
  0.0 136.6 jit_solution(2485610636489125627)
XLA Ops:
  0.7 1.0 dynamic-slice_select_fusion
  1.7 6.0 %collective-permute-start.1 = (f32[384,256]{1,0:T(8,128)S(1)}, f32[384,256]{1,0:T(8,128)S(1)}, u32[]{:S(2)}, u32[]{:S(2)}) collective-permute-start(f32[384,256]{1,0:T(8,128)S(1)} %dynamic-slice_select_fusion), channel_id=1, source_target_pairs={{0,16},{1,17},{10,26},{11,27},{20,4},{21,5},{30,14},{31,15}} | collective-permute-start | bytes 1179656 | tf_op jit(solution)/shard_map/ppermute | solution.py:464
  7.7 1.1 copy-done
  8.9 2.2 %gram_strips.1 = f32[4,64,256]{2,1,0:T(8,128)} custom-call(s32[2]{0:T(128)S(1)} %pad_add_fusion.place_ref, f32[768,256]{1,0:T(8,128)S(1)} %copy-done), custom_call_target="tpu_custom_call" | custom-call | flops 2000000000 | bytes 6000000 | tf_op jit(solution)/shard_map/gram_strips/pallas_call | solution.py:315
  11.1 3.4 %all-to-all-start = ((f32[4,64,256]{2,1,0:T(8,128)}), f32[4,64,256]{2,1,0:T(8,128)S(1)}, u32[]{:S(2)}, u32[]{:S(2)}) async-start(f32[4,64,256]{2,1,0:T(8,128)} %gram_strips.1), calls=%async_computation | async-start | bytes 524288 | tf_op jit(solution)/shard_map/all_to_all | solution.py:457
  14.5 2.7 %collective-permute-done.1 = f32[384,256]{1,0:T(8,128)S(1)} collective-permute-done((f32[384,256]{1,0:T(8,128)S(1)}, f32[384,256]{1,0:T(8,128)S(1)}, u32[]{:S(2)}, u32[]{:S(2)}) %collective-permute-start.1) | collective-permute-done | bytes 393248 | tf_op jit(solution)/shard_map/ppermute | solution.py:464
  17.2 6.1 %all-to-all-done = f32[4,64,256]{2,1,0:T(8,128)S(1)} async-done(((f32[4,64,256]{2,1,0:T(8,128)}), f32[4,64,256]{2,1,0:T(8,128)S(1)}, u32[]{:S(2)}, u32[]{:S(2)}) %all-to-all-start) | async-done | bytes 262176 | tf_op jit(solution)/shard_map/all_to_all | solution.py:457
  23.4 0.8 broadcast_in_dim.13
  24.2 4.2 %all-to-all-start.1 = ((f32[8,64,256]{2,1,0:T(8,128)}), f32[8,64,256]{2,1,0:T(8,128)}, u32[]{:S(2)}, u32[]{:S(2)}) async-start(f32[8,64,256]{2,1,0:T(8,128)} %broadcast_in_dim.13), calls=%async_computation.1 | async-start | bytes 1048576 | tf_op jit(solution)/shard_map/all_to_all | solution.py:412
  28.8 2.1 %collective-permute-start.2 = (f32[384,256]{1,0:T(8,128)S(1)}, f32[384,256]{1,0:T(8,128)S(1)}, u32[]{:S(2)}, u32[]{:S(2)}) collective-permute-start(f32[384,256]{1,0:T(8,128)S(1)} %fusion.2.slab_ref), channel_id=1, source_target_pairs={{0,8},{16,24},{1,9},{17,25},{10,2},{26,18},{11,3},{27,19},{20,28},... | collective-permute-start | bytes 1179656 | tf_op jit(solution)/shard_map/ppermute | solution.py:464
  30.8 7.3 %all-to-all-done.1 = f32[8,64,256]{2,1,0:T(8,128)} async-done(((f32[8,64,256]{2,1,0:T(8,128)}), f32[8,64,256]{2,1,0:T(8,128)}, u32[]{:S(2)}, u32[]{:S(2)}) %all-to-all-start.1) | async-done | bytes 524320 | tf_op jit(solution)/shard_map/all_to_all | solution.py:412
  38.1 1.1 fusion.1
  39.2 9.7 %cholesky_inverse.1 = (f32[256,256]{1,0:T(8,128)S(1)}, f32[256,256]{1,0:T(8,128)S(1)}) custom-call(f32[256,256]{1,0:T(8,128)S(1)} %bitcast.11), custom_call_target="tpu_custom_call" | custom-call | flops 10000000000 | bytes 30000000 | tf_op jit(solution)/shard_map/cholesky_inverse/pallas_call | solution.py:134
  49.6 2.6 %half_stage.1 = (f32[768,256]{1,0:T(8,128)S(1)}, f32[384,256]{1,0:T(8,128)S(1)}, f32[4,32,256]{2,1,0:T(8,128)S(1)}) custom-call(s32[2]{0:T(128)S(1)} %pad_add_fusion.place_ref, f32[768,256]{1,0:T(8,128)S(1)} %copy-done.1, f32[384,256]{1,0:T(8,128)S(1)} %fusion.2.slab_ref, f32[384,256]{1,0:T(8,128)S(1)} %collective-permute-done.2.got_ref, ...), custom_call_target="tpu_custom_call" | custom-call | flops 3000000000 | bytes 9000000 | tf_op jit(solution)/shard_map/half_stage/pallas_call | solution.py:341
  52.3 0.9 copy-done.13
  53.1 9.5 %all_to_all.35 = f32[4,32,256]{2,1,0:T(8,128)S(1)} all-to-all(f32[4,32,256]{2,1,0:T(8,128)S(1)} %get-tuple-element.28), channel_id=1, replica_groups=mesh['row'=4,'col'=8] {'row'}, dimensions={0} | all-to-all | bytes 262144 | tf_op jit(solution)/shard_map/all_to_all | solution.py:473
  62.7 0.7 broadcast_in_dim.14
  63.4 3.4 %all-to-all-start.3 = ((f32[8,32,256]{2,1,0:T(8,128)}), f32[8,32,256]{2,1,0:T(8,128)S(1)}, u32[]{:S(2)}, u32[]{:S(2)}) async-start(f32[8,32,256]{2,1,0:T(8,128)} %broadcast_in_dim.14), calls=%async_computation.3 | async-start | bytes 524288 | tf_op jit(solution)/shard_map/all_to_all | solution.py:412
  67.2 6.5 %all-to-all-done.3 = f32[8,32,256]{2,1,0:T(8,128)S(1)} async-done(((f32[8,32,256]{2,1,0:T(8,128)}), f32[8,32,256]{2,1,0:T(8,128)S(1)}, u32[]{:S(2)}, u32[]{:S(2)}) %all-to-all-start.3) | async-done | bytes 262176 | tf_op jit(solution)/shard_map/all_to_all | solution.py:412
  73.7 2.9 %near_cholesky.1.upper_ref = f32[256,256]{1,0:T(8,128)S(1)} custom-call(f32[256,256]{1,0:T(8,128)S(1)} %bitcast.8), custom_call_target="tpu_custom_call" | custom-call | flops 3000000000 | bytes 9000000 | tf_op jit(solution)/shard_map/near_cholesky/pallas_call | solution.py:189
  76.6 4.4 %products.1 = (f32[768,256]{1,0:T(8,128)S(1)}, f32[384,256]{1,0:T(8,128)S(1)}, f32[4,160,256]{2,1,0:T(8,128)}, f32[96,256]{1,0:T(8,128)S(1)}, f32[96,256]{1,0:T(...) custom-call(s32[2]{0:T(128)S(1)} %pad_add_fusion.place_ref, f32[768,384]{1,0:T(8,128)S(1)} %copy-done.2, ...), custom_call_target="tpu_custom_call" | custom-call | flops 4000000000 | bytes 12000000 | tf_op jit(solution)/shard_map/products/pallas_call | solution.py:282
  81.0 0.9 copy-done.5
  81.9 0.8 copy-done.8
  82.7 4.2 %all-to-all-start.4 = ((f32[4,160,256]{2,1,0:T(8,128)}), f32[4,160,256]{2,1,0:T(8,128)}, u32[]{:S(2)}, u32[]{:S(2)}) async-start(f32[4,160,256]{2,1,0:T(8,128)} %get-tuple-element.31), calls=%async_computation.4 | async-start | bytes 1310720 | tf_op jit(solution)/shard_map/all_to_all | solution.py:485
  86.9 1.3 collective-permute-start.5
  88.9 2.4 %collective-permute-start.7 = (f32[96,256]{1,0:T(8,128)S(1)}, f32[96,256]{1,0:T(8,128)S(1)}, u32[]{:S(2)}, u32[]{:S(2)}) collective-permute-start(f32[96,256]{1,0:T(8,128)S(1)} %get-tuple-element.36), channel_id=1, source_target_pairs={{0,24},{8,16},{16,8},{24,0},{1,25},{9,17},{17,9},{25,1},{2,26},{10... | collective-permute-start | bytes 294920 | tf_op jit(solution)/shard_map/ppermute | solution.py:418
  91.3 1.3 collective-permute-done.5
  92.6 5.4 %collective-permute-done.6 = f32[96,256]{1,0:T(8,128)S(1)} collective-permute-done((f32[96,256]{1,0:T(8,128)S(1)}, f32[96,256]{1,0:T(8,128)S(1)}, u32[]{:S(2)}, u32[]{:S(2)}) %collective-permute-start.6) | collective-permute-done | bytes 98336 | tf_op jit(solution)/shard_map/ppermute | solution.py:418
  98.0 1.2 reduce_sum.29
  99.3 1.2 collective-permute-start.10
  100.5 1.9 %collective-permute-start.9 = (f32[160,256]{1,0:T(8,128)S(1)}, f32[160,256]{1,0:T(8,128)S(1)}, u32[]{:S(2)}, u32[]{:S(2)}) collective-permute-start(f32[160,256]{1,0:T(8,128)S(1)} %pad_maximum_fusion.rest_refs_0_), channel_id=1, source_target_pairs={{0,16},{8,24},{16,0},{24,8},{1,17},{9,25},{17,1},{25,9},{2,18},{10... | collective-permute-start | bytes 491528 | tf_op jit(solution)/shard_map/ppermute | solution.py:418
  102.4 1.3 collective-permute-start.8
  103.7 0.8 broadcast_in_dim.15
  104.5 3.8 %all-to-all-start.5 = ((f32[4,96,256]{2,1,0:T(8,128)}), f32[4,96,256]{2,1,0:T(8,128)S(1)}, u32[]{:S(2)}, u32[]{:S(2)}) async-start(f32[4,96,256]{2,1,0:T(8,128)} %broadcast_in_dim.15), calls=%async_computation.5 | async-start | bytes 786432 | tf_op jit(solution)/shard_map/all_to_all | solution.py:489
  108.3 0.9 copy-done.18
  109.3 5.3 %compact_factor.1 = (f32[256,256]{1,0:T(8,128)S(1)}, f32[256,256]{1,0:T(8,128)}) custom-call(f32[256,256]{1,0:T(8,128)S(1)} %bitcast.9, f32[256,256]{1,0:T(8,128)S(1)} %bitcast.10, f32[256,256]{1,0:T(8,128)S(1)} %copy-done.16, f32[256,256]{1,0:T(8,128)S(1)} %near_cholesky.1.upper_ref, f32[256,256]{1,0:T(8,128)S(1)} %copy-done.18), custom_call_target="tpu_custom_call" | custom-call | flops 4000000000 | bytes 12000000 | tf_op jit(solution)/shard_map/compact_factor/pallas_call | solution.py:234
  114.6 0.7 copy-done.11
  115.4 0.8 broadcast_in_dim.16
  116.2 4.3 %all-to-all-start.6 = ((f32[8,64,256]{2,1,0:T(8,128)}), f32[8,64,256]{2,1,0:T(8,128)S(1)}, u32[]{:S(2)}, u32[]{:S(2)}) async-start(f32[8,64,256]{2,1,0:T(8,128)} %broadcast_in_dim.16), calls=%async_computation.6 | async-start | bytes 1048576 | tf_op jit(solution)/shard_map/all_to_all | solution.py:412
  120.5 1.1 copy-done.6
  121.6 1.0 copy-done.9
  122.6 2.4 %base_update.1.base_ref = f32[768,384]{1,0:T(8,128)S(1)} custom-call(s32[2]{0:T(128)S(1)} %pad_add_fusion.place_ref, f32[768,384]{1,0:T(8,128)S(1)} %copy-done.2, f32[768,256]{1,0:T(8,128)S(1)} %copy-done.6, f32[384,256]{1,0:T(8,128)S(1)} %bitcast.7, f32[384,256]{1,0:T(8,128)S(1)} %collective-permute-done.4.other_ref, f32[384,256]{1,0:T(8,128)S(1)} %copy-done.9, ...), custom_call_target="tpu_custom_call" | custom-call | flops 3000000000 | bytes 9000000 | tf_op jit(solution)/shard_map/base_update/pallas_call | solution.py:376
  125.0 1.0 copy-done.3
  126.0 4.2 %all-to-all-done.6.parts_ref = f32[8,64,256]{2,1,0:T(8,128)S(1)} async-done(((f32[8,64,256]{2,1,0:T(8,128)}), f32[8,64,256]{2,1,0:T(8,128)S(1)}, u32[]{:S(2)}, u32[]{:S(2)}) %all-to-all-start.6) | async-done | bytes 524320 | tf_op jit(solution)/shard_map/all_to_all | solution.py:412
  130.2 1.3 copy-done.4
  131.5 1.1 copy-done.7
  132.6 1.0 copy-done.10
  133.6 3.0 %coupling_update.1 = f32[768,384]{1,0:T(8,128)} custom-call(f32[768,384]{1,0:T(8,128)S(1)} %copy-done.4, f32[768,256]{1,0:T(8,128)S(1)} %copy-done.7, f32[384,256]{1,0:T(8,128)S(1)} %copy-done.10, f32[256,256]{1,0:T(8,128)S(1)} %copy-done.12, f32[8,64,256]{2,1,0:T(8,128)S(1)} %all-to-all-done.6.parts_ref), custom_call_target="tpu_custom_call" | custom-call | flops 2000000000 | bytes 6000000 | tf_op jit(solution)/shard_map/coupling_update/pallas_call | solution.py:399
  (49 shorter events, 2.5 us)
Async XLA Ops:
  1.7 15.4 %collective-permute-start.1 = (f32[384,256]{1,0:T(8,128)S(1)}, f32[384,256]{1,0:T(8,128)S(1)}, u32[]{:S(2)}, u32[]{:S(2)}) collective-permute-start(f32[384,256]{1,0:T(8,128)S(1)} %dynamic-slice_select_fusion), channel_id=1, source_target_pairs={{0,16},{1,17},{10,26},{11,27},{20,4},{21,5},{30,14},{31,15}} | collective-permute-start | bytes 1179656 | tf_op jit(solution)/shard_map/ppermute | solution.py:464
  7.7 1.1 copy-start
  8.9 8.3 %copy-start.1 = (f32[768,256]{1,0:T(8,128)S(1)}, f32[768,256]{1,0:T(8,128)}, u32[]{:S(2)}) copy-start(f32[768,256]{1,0:T(8,128)} %panel_ref.3) | copy-start | bytes 2359300
  11.1 12.3 %all-to-all-start = ((f32[4,64,256]{2,1,0:T(8,128)}), f32[4,64,256]{2,1,0:T(8,128)S(1)}, u32[]{:S(2)}, u32[]{:S(2)}) async-start(f32[4,64,256]{2,1,0:T(8,128)} %gram_strips.1), calls=%async_computation | async-start | bytes 524288 | tf_op jit(solution)/shard_map/all_to_all | solution.py:457
  17.2 11.2 %copy-start.2 = (f32[768,384]{1,0:T(8,128)S(1)}, f32[768,384]{1,0:T(8,128)}, u32[]{:S(2)}) copy-start(f32[768,384]{1,0:T(8,128)} %ham_ref.3) | copy-start | bytes 3538948
  24.2 13.9 %all-to-all-start.1 = ((f32[8,64,256]{2,1,0:T(8,128)}), f32[8,64,256]{2,1,0:T(8,128)}, u32[]{:S(2)}, u32[]{:S(2)}) async-start(f32[8,64,256]{2,1,0:T(8,128)} %broadcast_in_dim.13), calls=%async_computation.1 | async-start | bytes 1048576 | tf_op jit(solution)/shard_map/all_to_all | solution.py:412
  28.4 48.2 %collective-permute-start = (f32[768,384]{1,0:T(8,128)S(1)}, f32[768,384]{1,0:T(8,128)}, u32[]{:S(2)}, u32[]{:S(2)}) collective-permute-start(f32[768,384]{1,0:T(8,128)S(1)} %copy-done.2), channel_id=1, source_target_pairs={{0,1},{1,0},{2,3},{3,2},{4,5},{5,4},{6,7},{7,6},{8,9},{9,8},{10,11... | collective-permute-start | bytes 3538952 | tf_op jit(solution)/shard_map/ppermute | solution.py:442
  28.8 20.9 %collective-permute-start.2 = (f32[384,256]{1,0:T(8,128)S(1)}, f32[384,256]{1,0:T(8,128)S(1)}, u32[]{:S(2)}, u32[]{:S(2)}) collective-permute-start(f32[384,256]{1,0:T(8,128)S(1)} %fusion.2.slab_ref), channel_id=1, source_target_pairs={{0,8},{16,24},{1,9},{17,25},{10,2},{26,18},{11,3},{27,19},{20,28},... | collective-permute-start | bytes 1179656 | tf_op jit(solution)/shard_map/ppermute | solution.py:464
  48.9 0.7 copy-start.17
  49.6 2.6 %copy-start.15 = (f32[256,256]{1,0:T(8,128)}, f32[256,256]{1,0:T(8,128)S(1)}, u32[]{:S(2)}) copy-start(f32[256,256]{1,0:T(8,128)S(1)} %get-tuple-element.25.inv_ref) | copy-start | bytes 786436
  52.2 0.9 copy-start.13
  63.4 10.3 %all-to-all-start.3 = ((f32[8,32,256]{2,1,0:T(8,128)}), f32[8,32,256]{2,1,0:T(8,128)S(1)}, u32[]{:S(2)}, u32[]{:S(2)}) async-start(f32[8,32,256]{2,1,0:T(8,128)} %broadcast_in_dim.14), calls=%async_computation.3 | async-start | bytes 524288 | tf_op jit(solution)/shard_map/all_to_all | solution.py:412
  66.8 9.8 %collective-permute-start.3 = (f32[384,256]{1,0:T(8,128)S(1)}, f32[384,256]{1,0:T(8,128)S(1)}, u32[]{:S(2)}, u32[]{:S(2)}) collective-permute-start(f32[384,256]{1,0:T(8,128)S(1)} %get-tuple-element.27.near_ref), channel_id=1, source_target_pairs={{0,1},{1,0},{2,3},{3,2},{4,5},{5,4},{6,7},{7,6},{8,9},{9,8},{10,11... | collective-permute-start | bytes 1179656 | tf_op jit(solution)/shard_map/ppermute | solution.py:474
  73.7 2.9 %copy-start.14 = (f32[768,256]{1,0:T(8,128)S(1)}, f32[768,256]{1,0:T(8,128)}, u32[]{:S(2)}) copy-start(f32[768,256]{1,0:T(8,128)} %copy-done.13) | copy-start | bytes 2359300
  81.0 0.9 copy-start.5
  81.9 0.8 copy-start.8
  82.7 15.3 %all-to-all-start.4 = ((f32[4,160,256]{2,1,0:T(8,128)}), f32[4,160,256]{2,1,0:T(8,128)}, u32[]{:S(2)}, u32[]{:S(2)}) async-start(f32[4,160,256]{2,1,0:T(8,128)} %get-tuple-element.31), calls=%async_computation.4 | async-start | bytes 1310720 | tf_op jit(solution)/shard_map/all_to_all | solution.py:485
  86.9 5.7 %collective-permute-start.5 = (f32[96,256]{1,0:T(8,128)S(1)}, f32[96,256]{1,0:T(8,128)S(1)}, u32[]{:S(2)}, u32[]{:S(2)}) collective-permute-start(f32[96,256]{1,0:T(8,128)S(1)} %get-tuple-element.34), channel_id=1, source_target_pairs={{0,8},{8,0},{16,24},{24,16},{1,9},{9,1},{17,25},{25,17},{2,10},{10... | collective-permute-start | bytes 294920 | tf_op jit(solution)/shard_map/ppermute | solution.py:418
  88.2 9.8 %collective-permute-start.6 = (f32[96,256]{1,0:T(8,128)S(1)}, f32[96,256]{1,0:T(8,128)S(1)}, u32[]{:S(2)}, u32[]{:S(2)}) collective-permute-start(f32[96,256]{1,0:T(8,128)S(1)} %get-tuple-element.35), channel_id=1, source_target_pairs={{0,16},{8,24},{16,0},{24,8},{1,17},{9,25},{17,1},{25,9},{2,18},{10... | collective-permute-start | bytes 294920 | tf_op jit(solution)/shard_map/ppermute | solution.py:418
  88.9 9.1 %collective-permute-start.7 = (f32[96,256]{1,0:T(8,128)S(1)}, f32[96,256]{1,0:T(8,128)S(1)}, u32[]{:S(2)}, u32[]{:S(2)}) collective-permute-start(f32[96,256]{1,0:T(8,128)S(1)} %get-tuple-element.36), channel_id=1, source_target_pairs={{0,24},{8,16},{16,8},{24,0},{1,25},{9,17},{17,9},{25,1},{2,26},{10... | collective-permute-start | bytes 294920 | tf_op jit(solution)/shard_map/ppermute | solution.py:418
  98.0 10.3 %copy-start.16 = (f32[256,256]{1,0:T(8,128)S(1)}, f32[256,256]{1,0:T(8,128)}, u32[]{:S(2)}) copy-start(f32[256,256]{1,0:T(8,128)} %copy-done.15) | copy-start | bytes 786436
  99.3 16.0 %collective-permute-start.10 = (f32[160,256]{1,0:T(8,128)S(1)}, f32[160,256]{1,0:T(8,128)S(1)}, u32[]{:S(2)}, u32[]{:S(2)}) collective-permute-start(f32[160,256]{1,0:T(8,128)S(1)} %pad_maximum_fusion.rest_refs_0_), channel_id=1, source_target_pairs={{0,24},{8,16},{16,8},{24,0},{1,25},{9,17},{17,9},{25,1},{2,26},{10... | collective-permute-start | bytes 491528 | tf_op jit(solution)/shard_map/ppermute | solution.py:418
  100.5 14.8 %collective-permute-start.9 = (f32[160,256]{1,0:T(8,128)S(1)}, f32[160,256]{1,0:T(8,128)S(1)}, u32[]{:S(2)}, u32[]{:S(2)}) collective-permute-start(f32[160,256]{1,0:T(8,128)S(1)} %pad_maximum_fusion.rest_refs_0_), channel_id=1, source_target_pairs={{0,16},{8,24},{16,0},{24,8},{1,17},{9,25},{17,1},{25,9},{2,18},{10... | collective-permute-start | bytes 491528 | tf_op jit(solution)/shard_map/ppermute | solution.py:418
  102.4 12.9 %collective-permute-start.8 = (f32[160,256]{1,0:T(8,128)S(1)}, f32[160,256]{1,0:T(8,128)S(1)}, u32[]{:S(2)}, u32[]{:S(2)}) collective-permute-start(f32[160,256]{1,0:T(8,128)S(1)} %pad_maximum_fusion.rest_refs_0_), channel_id=1, source_target_pairs={{0,8},{8,0},{16,24},{24,16},{1,9},{9,1},{17,25},{25,17},{2,10},{10... | collective-permute-start | bytes 491528 | tf_op jit(solution)/shard_map/ppermute | solution.py:418
  104.5 10.8 %all-to-all-start.5 = ((f32[4,96,256]{2,1,0:T(8,128)}), f32[4,96,256]{2,1,0:T(8,128)S(1)}, u32[]{:S(2)}, u32[]{:S(2)}) async-start(f32[4,96,256]{2,1,0:T(8,128)} %broadcast_in_dim.15), calls=%async_computation.5 | async-start | bytes 786432 | tf_op jit(solution)/shard_map/all_to_all | solution.py:489
  108.3 1.0 copy-start.18
  114.6 0.7 copy-start.11
  115.3 5.2 %copy-start.12 = (f32[256,256]{1,0:T(8,128)S(1)}, f32[256,256]{1,0:T(8,128)}, u32[]{:S(2)}) copy-start(f32[256,256]{1,0:T(8,128)} %copy-done.11) | copy-start | bytes 786436
  115.3 5.2 %collective-permute-start.4 = (f32[384,256]{1,0:T(8,128)S(1)}, f32[384,256]{1,0:T(8,128)S(1)}, u32[]{:S(2)}, u32[]{:S(2)}) collective-permute-start(f32[384,256]{1,0:T(8,128)S(1)} %bitcast.6), channel_id=1, source_target_pairs={{0,1},{1,0},{2,3},{3,2},{4,5},{5,4},{6,7},{7,6},{8,9},{9,8},{10,11... | collective-permute-start | bytes 1179656 | tf_op jit(solution)/shard_map/ppermute | solution.py:491
  116.2 14.0 %all-to-all-start.6 = ((f32[8,64,256]{2,1,0:T(8,128)}), f32[8,64,256]{2,1,0:T(8,128)S(1)}, u32[]{:S(2)}, u32[]{:S(2)}) async-start(f32[8,64,256]{2,1,0:T(8,128)} %broadcast_in_dim.16), calls=%async_computation.6 | async-start | bytes 1048576 | tf_op jit(solution)/shard_map/all_to_all | solution.py:412
  120.5 1.1 copy-start.6
  121.6 1.0 copy-start.9
  125.0 1.0 copy-start.3
  130.2 1.3 copy-start.4
  131.5 1.1 copy-start.7
  132.6 1.0 copy-start.10

commit v5 on v4

v5 whole, which is shorter than its diff:
```python
import functools

import jax
import jax.numpy as jnp
from jax import lax
from jax.experimental import pallas as pl
from jax.experimental.pallas import tpu as pltpu
from jax.sharding import PartitionSpec as P

SUB = 8
LANE = 128
BLOCK = 32
HIGHEST = lax.Precision.HIGHEST
SMALL = pltpu.CompilerParams(vmem_limit_bytes=10 * 2**20)
LARGE = pltpu.CompilerParams(vmem_limit_bytes=24 * 2**20)
VMEM = pl.BlockSpec(memory_space=pltpu.VMEM)
SMEM = pl.BlockSpec(memory_space=pltpu.SMEM)
HBM = pl.BlockSpec(memory_space=pltpu.HBM)
PLAIN = ((1,), (0,))
TURNED = ((0,), (0,))
ACROSS = ((1,), (1,))


def mult(left, right, dims=PLAIN):
    return lax.dot_general(
        left, right, (dims, ((), ())), precision=HIGHEST, preferred_element_type=jnp.float32
    )


def move(pairs, sems):
    copies = [pltpu.make_async_copy(src, dst, sems.at[i]) for i, (src, dst) in enumerate(pairs)]
    for copy in copies:
        copy.start()
    return copies


def wait(copies):
    for copy in copies:
        copy.wait()


def split(value):
    high = value.astype(jnp.bfloat16)
    return high, (value - high.astype(jnp.float32)).astype(jnp.bfloat16)


def mult3(left, right, dims=PLAIN):
    def one(a, b):
        return lax.dot_general(a, b, (dims, ((), ())), preferred_element_type=jnp.float32)

    return one(left[0], right[0]) + (one(left[0], right[1]) + one(left[1], right[0]))


def chol_kernel(gram_ref, upper_ref, inv_ref, work_ref):
    size = gram_ref.shape[0]
    tiles = size // LANE
    groups = BLOCK // SUB
    lanes = lax.broadcasted_iota(jnp.int32, (SUB, LANE), 1)
    work_ref[...] = gram_ref[...]

    def spread(row):
        return jnp.broadcast_to(row, (SUB, LANE))

    for first in range(0, size, BLOCK):
        rows = [
            [
                work_ref[first + SUB * g : first + SUB * (g + 1), LANE * t : LANE * (t + 1)]
                for t in range(tiles)
            ]
            for g in range(groups)
        ]
        for g in range(groups):
            col = first + SUB * g
            home, low = divmod(col, LANE)
            in_block = (lanes >= low) & (lanes < low + SUB)
            flat = [[spread(rows[g][t][k : k + 1, :]) for t in range(tiles)] for k in range(SUB)]
            diag = [
                [spread(flat[k][home][:, low + i : low + i + 1]) for i in range(k + 1)]
                for k in range(SUB)
            ]
            unit = [jnp.where(lanes == low + k, 1.0, 0.0) for k in range(SUB)]
            later = range(g + 1, groups)
            cols = {
                q: [spread(rows[q][home][:, low + i : low + i + 1]) for i in range(SUB)]
                for q in later
            }
            for q in later:
                rows[q][home] = jnp.where(in_block, 0.0, rows[q][home])
            for i in range(SUB):
                recip = 1.0 / diag[i][i]
                steps = [None] * SUB
                for k in range(i + 1, SUB):
                    steps[k] = diag[k][i] * recip
                for k in range(i + 1, SUB):
                    for j in range(i + 1, k + 1):
                        diag[k][j] = diag[k][j] - steps[k] * diag[j][i]
                for k in range(i + 1, SUB):
                    for t in range(tiles):
                        flat[k][t] = flat[k][t] - steps[k] * flat[i][t]
                    unit[k] = unit[k] - steps[k] * unit[i]
                for q in later:
                    step = cols[q][i] * recip
                    for j in range(i + 1, SUB):
                        cols[q][j] = cols[q][j] - step * diag[j][i]
                    for t in range(tiles):
                        source = flat[i][t]
                        if t == home:
                            source = jnp.where(in_block, unit[i], source)
                        rows[q][t] = rows[q][t] - step * source
            for k in range(SUB):
                scale = lax.rsqrt(diag[k][k])
                for t in range(tiles):
                    scaled = flat[k][t] * scale
                    if t < home:
                        up, inv = jnp.zeros_like(scaled), scaled
                    elif t > home:
                        up, inv = scaled, jnp.zeros_like(scaled)
                    else:
                        up = jnp.where(lanes >= low + k, scaled, 0.0)
                        inv = jnp.where(in_block, unit[k] * scale, scaled)
                        inv = jnp.where(lanes < low + SUB, inv, 0.0)
                    upper_ref[col + k : col + k + 1, LANE * t : LANE * (t + 1)] = up[0:1]
                    inv_ref[col + k : col + k + 1, LANE * t : LANE * (t + 1)] = inv[0:1]
        rest = first + BLOCK
        if rest == size:
            break
        start = rest // LANE * LANE
        left = upper_ref[first:rest, start:size]
        wide = lax.broadcasted_iota(jnp.int32, (BLOCK, size), 1)
        right = jnp.where(wide < rest, inv_ref[first:rest, :], upper_ref[first:rest, :])
        change = mult(left, right, ((0,), (0,)))
        below = lax.broadcasted_iota(jnp.int32, (size - rest, size), 1)
        old = jnp.where((below >= first) & (below < rest), 0.0, work_ref[rest:size, :])
        work_ref[rest:size, :] = old - change[rest - start :, :]


def estimate(micros):
    return pl.CostEstimate(flops=int(micros * 1e9), bytes_accessed=int(micros * 3e6), transcendentals=0)


def square(size):
    return jax.ShapeDtypeStruct((size, size), jnp.float32)


def first_kernel(parts_ref, upper_out, inv_ref, gram_ref, upper_ref, work_ref, sems):
    strip = parts_ref.shape[1]
    for c in range(parts_ref.shape[0]):
        gram_ref[c * strip : (c + 1) * strip, :] = parts_ref[c]
    chol_kernel(gram_ref, upper_ref, inv_ref, work_ref)
    wait(move([(upper_ref, upper_out)], sems))


def cholesky(parts):
    size = parts.shape[2]
    return pl.pallas_call(
        first_kernel,
        in_specs=[VMEM],
        out_specs=(HBM, VMEM),
        out_shape=(square(size), square(size)),
        scratch_shapes=[pltpu.VMEM((size, size), jnp.float32)] * 3 + [pltpu.SemaphoreType.DMA((1,))],
        compiler_params=SMALL,
        cost_estimate=estimate(10),
        name="cholesky_inverse",
    )(parts)


def grids(size):
    row = lax.broadcasted_iota(jnp.int32, (size, size), 0)
    col = lax.broadcasted_iota(jnp.int32, (size, size), 1)
    return row, col


def near_kernel(gram_ref, upper_ref, inv_ref, work_ref):
    size = gram_ref.shape[0]
    row, col = grids(size)
    ident = jnp.where(row == col, 1.0, 0.0)
    weight = jnp.where(row > col, 1.0, ident * 0.5)
    gram = split(gram_ref[...])

    def look(inv):
        halves = split(inv)
        upper = mult3(halves, gram)
        low = weight * (mult3(split(upper), halves, ACROSS) - ident)
        return upper, low, jnp.sum(low * low)

    def more(state):
        count, _, _, _, worst = state
        return jnp.logical_not(worst < 1e-5) & (count < 8)

    def step(state):
        count, inv, _, low, _ = state
        low = split(low)
        turn = mult3(low, split(inv))
        inv = inv - turn + mult3(low, split(turn))
        return (count + 1, inv) + look(inv)

    low = weight * (gram_ref[...] - ident)
    halves = split(low)
    inv = ident - low + mult3(halves, halves)
    state = lax.while_loop(more, step, (jnp.int32(0), inv) + look(inv))
    _, _, upper, low, worst = state
    upper = upper + mult3(split(low), split(upper), TURNED)
    upper_ref[...] = jnp.where(row <= col, upper, 0.0)

    @pl.when(jnp.logical_not(worst < 1e-5))
    def _():
        chol_kernel(gram_ref, upper_ref, inv_ref, work_ref)


def near_cholesky(gram):
    size = gram.shape[0]
    return pl.pallas_call(
        near_kernel,
        out_shape=square(size),
        scratch_shapes=[pltpu.VMEM((size, size), jnp.float32)] * 2,
        compiler_params=SMALL,
        cost_estimate=estimate(3),
        name="near_cholesky",
    )(gram)


def factor_kernel(parts_ref, inv_ref, upper_ref, first_ref, out_ref, band_ref,
                  first, out, band, sems):
    fetch = move([(first_ref, first)], sems)
    size = inv_ref.shape[0]
    strip = size // parts_ref.shape[0]
    row, col = grids(size)
    ident = jnp.where(row == col, 1.0, 0.0)
    pieces = range(parts_ref.shape[0])
    gram = jnp.concatenate([parts_ref[c, :strip, :] for c in pieces], axis=0)
    top = jnp.concatenate([parts_ref[c, strip:, :] for c in pieces], axis=0)
    half_top = mult(top, inv_ref[...], ACROSS)
    mat = gram + mult(half_top, upper_ref[...], TURNED)
    halves = split(mat)
    wait(fetch)
    band[...] = -mult(upper_ref[...], first[...])
    store = move([(band, band_ref)], sems)

    def residual(guess):
        return ident - mult3(halves, split(guess))

    def step(state):
        count, guess, rest, _ = state
        guess = guess + mult3(split(guess), split(rest))
        rest = residual(guess)
        return count + 1, guess, rest, jnp.max(jnp.abs(rest))

    def more(state):
        count, _, _, worst = state
        return (worst > 2e-5) & (count < 40)

    guess = 0.5 * ident
    rest = ident - 0.5 * mat
    for _ in range(4):
        parts = split(rest)
        guess = guess + mult3(split(guess), parts)
        rest = mult3(parts, parts)
    guess = guess + mult3(split(guess), split(rest))
    rest = residual(guess)
    state = (jnp.int32(0), guess, rest, jnp.max(jnp.abs(rest)))
    out[...] = lax.while_loop(more, step, state)[1]
    wait(store + move([(out, out_ref)], sems.at[pl.ds(1, 1)]))


def compact_factor(parts, inv, upper, first):
    size = inv.shape[0]
    return pl.pallas_call(
        factor_kernel,
        in_specs=[VMEM] * 3 + [HBM],
        out_specs=(HBM, HBM),
        out_shape=(square(size), square(size)),
        scratch_shapes=[pltpu.VMEM((size, size), jnp.float32)] * 3 + [pltpu.SemaphoreType.DMA((2,))],
        compiler_params=SMALL,
        cost_estimate=estimate(4),
        name="compact_factor",
    )(parts, inv, upper, first)


def array(*dims):
    return jax.ShapeDtypeStruct(dims, jnp.float32)


def scratch(*dims):
    return pltpu.VMEM(dims, jnp.float32)


def gram_kernel(place_ref, panel_ref, out_ref, gram_ref):
    strip = out_ref.shape[0] // 2
    mine = pl.ds(pl.multiple_of(place_ref[1] * strip, strip), strip)
    gram_ref[...] = mult(panel_ref[...], panel_ref[...], TURNED)
    out_ref[:strip, :] = gram_ref[mine, :]
    out_ref[strip:, :] = panel_ref[mine, :] * jnp.where(place_ref[0] == 0, 1.0, 0.0)


def gram_strips(place, panel, cols):
    width = panel.shape[1]
    return pl.pallas_call(
        gram_kernel,
        in_specs=[SMEM, VMEM],
        out_shape=array(2 * width // cols, width),
        scratch_shapes=[scratch(width, width)],
        compiler_params=LARGE,
        cost_estimate=estimate(2),
        name="gram_strips",
    )(place, panel)


def half_kernel(place_ref, panel_ref, slab_ref, got_ref, inv_ref, half_out, cols_out, out_ref,
                half_ref, cols_ref, gram_ref, sems):
    strip = out_ref.shape[0]
    mine = pl.ds(pl.multiple_of(place_ref[1] * strip, strip), strip)
    half = mult(panel_ref[...], inv_ref[...], ACROSS)
    half_ref[...] = half
    cols_ref[...] = mult(slab_ref[...] + got_ref[...], inv_ref[...], ACROSS)
    store = move([(half_ref, half_out), (cols_ref, cols_out)], sems)
    parts = split(half)
    gram_ref[...] = mult3(parts, parts, TURNED)
    out_ref[...] = gram_ref[mine, :]
    wait(store)


def half_stage(place, panel, slab, got, inv, cols):
    width = panel.shape[1]
    return pl.pallas_call(
        half_kernel,
        in_specs=[SMEM] + [VMEM] * 4,
        out_specs=(HBM, HBM, VMEM),
        out_shape=(array(*panel.shape), array(*slab.shape), array(width // cols, width)),
        scratch_shapes=[
            scratch(*panel.shape),
            scratch(*slab.shape),
            scratch(width, width),
            pltpu.SemaphoreType.DMA((2,)),
        ],
        compiler_params=LARGE,
        cost_estimate=estimate(3),
        name="half_stage",
    )(place, panel, slab, got, inv)


def products_kernel(place_ref, ham_ref, half_in, cols_in, upper_ref,
                    left_out, right_out, keep_ref, send_ref, *rest_refs):
    piece_refs = rest_refs[:-6]
    left_ref, right_ref, part_ref, coupling_ref, near_ref, sems = rest_refs[-6:]
    fetch = move([(cols_in, right_ref), (half_in, left_ref)], sems)
    width = upper_ref.shape[0]
    chips = keep_ref.shape[0]
    rows_dev = ham_ref.shape[0]
    piece, strip = rows_dev // 2 // chips, width // 2 // chips
    share = piece_refs[0].shape[0]
    row_place, col_place = place_ref[0], place_ref[1]
    core, chip = col_place & 1, col_place // 2
    ham = split(ham_ref[...])
    fetch[0].wait()
    lead = jnp.where(col_place == 0, 1.0, 0.0)
    right_ref[:width, :] = right_ref[:width, :] + lead * upper_ref[...]
    part = mult3(ham, split(right_ref[...]))
    part_ref[...] = part
    fetch[1].wait()
    lead = jnp.where(row_place == 0, 1.0, 0.0)
    left_ref[:width, :] = left_ref[:width, :] + lead * upper_ref[...]
    store = move([(right_ref, right_out), (left_ref, left_out)], sems)
    left = split(left_ref[...])
    coupling_ref[...] = mult3(left, split(part), TURNED)
    for ref, half in ((send_ref, 1 - core), (keep_ref, core)):
        for hop in range(chips):
            start = (half * chips + (chip ^ hop)) * piece
            ref[hop, :piece, :] = part_ref[pl.ds(pl.multiple_of(start, piece), piece), :]
            start = (half * chips + (chip ^ hop)) * strip
            ref[hop, piece:, :] = coupling_ref[pl.ds(pl.multiple_of(start, strip), strip), :]
    near_ref[...] = mult3(ham, left, TURNED)
    for hop, ref in enumerate(piece_refs):
        start = pl.multiple_of((row_place ^ hop) * share, share)
        ref[...] = near_ref[pl.ds(start, share), :]
    wait(store)


def products(place, hamiltonian, half, half_cols, upper, rows, cols):
    rows_dev, cols_dev = hamiltonian.shape
    width = upper.shape[0]
    chips = cols // 2
    share = (rows_dev + width) // cols
    out = pl.pallas_call(
        products_kernel,
        in_specs=[SMEM, VMEM, HBM, HBM, VMEM],
        out_specs=(HBM, HBM) + (VMEM,) * (2 + rows),
        out_shape=(
            array(rows_dev, width),
            array(cols_dev, width),
            array(chips, share, width),
            array(chips, share, width),
        )
        + (array(cols_dev // rows, width),) * rows,
        scratch_shapes=[
            scratch(rows_dev, width),
            scratch(cols_dev, width),
            scratch(rows_dev, width),
            scratch(width, width),
            scratch(cols_dev, width),
            pltpu.SemaphoreType.DMA((2,)),
        ],
        compiler_params=LARGE,
        cost_estimate=estimate(4),
        name="products",
    )(place, hamiltonian, half, half_cols, upper)
    return out[0], out[1], out[2], out[3], out[4:]


def pair_kernel(keep_ref, got_ref, *out_refs):
    for hop, ref in enumerate(out_refs):
        ref[...] = keep_ref[hop] + got_ref[hop]


def pair_add(keep, got):
    return pl.pallas_call(
        pair_kernel,
        in_specs=[VMEM] * 2,
        out_shape=(array(*keep.shape[1:]),) * keep.shape[0],
        compiler_params=LARGE,
        cost_estimate=estimate(0.5),
        name="pair_add",
    )(keep, got)


def tree_sum(terms):
    while len(terms) > 1:
        terms = [terms[i] + terms[i + 1] for i in range(0, len(terms), 2)]
    return terms[0]


def sums_kernel(count, *refs):
    total_refs, piece_refs = refs[:count], refs[count:-2]
    mine_ref, both_ref = refs[-2:]
    piece, share = mine_ref.shape[0], piece_refs[0].shape[0]
    total = tree_sum([ref[...] for ref in total_refs])
    mine_ref[...] = total[:piece]
    both_ref[:share, :] = tree_sum([ref[...] for ref in piece_refs])
    both_ref[share:, :] = total[piece:]


def sum_pieces(totals, pieces, piece):
    share, width = pieces[0].shape
    strip = totals[0].shape[0] - piece
    return pl.pallas_call(
        functools.partial(sums_kernel, len(totals)),
        in_specs=[VMEM] * (len(totals) + len(pieces)),
        out_shape=(array(piece, width), array(share + strip, width)),
        compiler_params=LARGE,
        cost_estimate=estimate(0.5),
        name="sum_pieces",
    )(*totals, *pieces)


def spread_kernel(groups, *refs):
    out_ref = refs[-1]
    start = 0
    for count, first, last in groups:
        total = tree_sum([ref[first:last, :] for ref in refs[:count]])
        refs = refs[count:]
        for c in range(out_ref.shape[0]):
            out_ref[c, start : start + last - first, :] = total
        start += last - first


def sum_gather(cols, *groups):
    terms = [term for group in groups for term in group[0]]
    bounds = [(len(group[0]), group[1], group[2]) for group in groups]
    height = sum(last - first for _, first, last in bounds)
    copies = pl.pallas_call(
        functools.partial(spread_kernel, bounds),
        in_specs=[VMEM] * len(terms),
        out_shape=array(cols, height, terms[0].shape[1]),
        compiler_params=LARGE,
        cost_estimate=estimate(0.5),
        name="sum_copies",
    )(*terms)
    return lax.all_to_all(copies, "col", 0, 0, tiled=True)


def merge_kernel(place_ref, *refs):
    out_ref = refs[-1]
    piece = refs[0].shape[0]
    chip = place_ref[1] // 2
    for hop, ref in enumerate(refs[:-1]):
        out_ref[pl.ds(pl.multiple_of((chip ^ hop) * piece, piece), piece), :] = ref[...]


def merge(place, pieces):
    piece, width = pieces[0].shape
    return pl.pallas_call(
        merge_kernel,
        in_specs=[SMEM] + [VMEM] * len(pieces),
        out_shape=array(len(pieces) * piece, width),
        compiler_params=LARGE,
        cost_estimate=estimate(0.5),
        name="merge_pieces",
    )(place, *pieces)


def base_kernel(place_ref, ham_ref, left_in, mine_ref, other_ref, right_in, factor_in, *rest_refs):
    piece_refs, out_hbm = rest_refs[:-7], rest_refs[-7]
    left_ref, right_ref, factor_ref, near_ref, out_ref, sems = rest_refs[-6:]
    fetch = move([(factor_in, factor_ref), (right_in, right_ref), (left_in, left_ref)], sems)
    deep = mine_ref.shape[0]
    share = near_ref.shape[0] // len(piece_refs)
    row_place, core = place_ref[0], place_ref[1] & 1
    for hop, ref in enumerate(piece_refs):
        start = pl.multiple_of((row_place ^ hop) * share, share)
        near_ref[pl.ds(start, share), :] = ref[:share, :]
    fetch[0].wait()
    factor = split(factor_ref[...])
    near = split(mult3(split(near_ref[...]), factor))
    fetch[1].wait()
    far = split(mult3(split(right_ref[...]), factor, ACROSS))
    fetch[2].wait()
    for place, prod_ref in ((core, mine_ref), (1 - core, other_ref)):
        block = pl.ds(pl.multiple_of(place * deep, deep), deep)
        change = mult3(split(left_ref[block, :]), near, ACROSS)
        change = change + mult3(split(prod_ref[...]), far, ACROSS)
        out_ref[block, :] = ham_ref[block, :] - change
    wait(move([(out_ref, out_hbm)], sems))


def base_update(place, hamiltonian, left, mine, other, right, factor, pieces):
    return pl.pallas_call(
        base_kernel,
        in_specs=[SMEM, VMEM, HBM, VMEM, VMEM, HBM, HBM] + [VMEM] * len(pieces),
        out_specs=HBM,
        out_shape=array(*hamiltonian.shape),
        scratch_shapes=[
            scratch(*left.shape),
            scratch(*right.shape),
            scratch(*factor.shape),
            scratch(*right.shape),
            scratch(*hamiltonian.shape),
            pltpu.SemaphoreType.DMA((3,)),
        ],
        compiler_params=LARGE,
        cost_estimate=estimate(4),
        name="base_update",
    )(place, hamiltonian, left, mine, other, right, factor, *pieces)


def coupling_kernel(base_in, left_in, right_in, factor_in, parts_ref, out_hbm,
                    base_ref, left_ref, right_ref, factor_ref, sum_ref, sems):
    fetch = move(
        [(factor_in, factor_ref), (right_in, right_ref), (left_in, left_ref), (base_in, base_ref)],
        sems,
    )
    strip = parts_ref.shape[1]
    chips = parts_ref.shape[0] // 2
    for c in range(parts_ref.shape[0]):
        start = ((c % 2) * chips + c // 2) * strip
        sum_ref[start : start + strip, :] = parts_ref[c]
    fetch[0].wait()
    factor = split(factor_ref[...])
    turn = mult3(split(sum_ref[...]), factor)
    middle = mult3(factor, split(turn), TURNED)
    fetch[1].wait()
    near = split(mult3(split(right_ref[...]), split(middle)))
    fetch[2].wait()
    fetch[3].wait()
    deep = base_ref.shape[0] // 2
    stores = []
    for half in range(2):
        block = pl.ds(half * deep, deep)
        base_ref[block, :] += mult3(split(left_ref[block, :]), near, ACROSS)
        copy = pltpu.make_async_copy(base_ref.at[block], out_hbm.at[block], sems.at[half])
        copy.start()
        stores.append(copy)
    wait(stores)


def coupling_update(base, left, right, factor, parts):
    return pl.pallas_call(
        coupling_kernel,
        in_specs=[HBM] * 4 + [VMEM],
        out_specs=HBM,
        out_shape=array(*base.shape),
        scratch_shapes=[
            scratch(*base.shape),
            scratch(*left.shape),
            scratch(*right.shape),
            scratch(*factor.shape),
            scratch(*factor.shape),
            pltpu.SemaphoreType.DMA((4,)),
        ],
        compiler_params=LARGE,
        cost_estimate=estimate(3),
        name="coupling_update",
    )(base, left, right, factor, parts)


def hops(values, axis, size, scale=1):
    got = [values[0]]
    for hop in range(1, len(values)):
        pairs = [(i, i ^ (hop * scale)) for i in range(size)]
        got.append(lax.ppermute(values[hop], axis, pairs))
    return got


def shards(rows, cols, hamiltonian, panel):
    rows_dev, width = panel.shape
    cols_dev = hamiltonian.shape[1]
    row_place = lax.axis_index("row")
    col_place = lax.axis_index("col")
    chips = cols // 2
    strip = width // cols
    piece = rows_dev // cols
    share = cols_dev // rows
    pair = [(i, i ^ 1) for i in range(cols)]
    place = jnp.stack([row_place, col_place]).astype(jnp.int32)

    strips = hops([gram_strips(place, panel, cols)] * rows, "row", rows)

    owners = [c * cols_dev // rows_dev for c in range(cols)]
    owner = col_place * cols_dev // rows_dev
    offset = col_place * cols_dev - owner * rows_dev
    slab = lax.dynamic_slice_in_dim(panel, offset, cols_dev, 0)
    slab = jnp.where(row_place == owner, slab, 0.0)
    strips, slab = lax.optimization_barrier((strips, slab))
    hop, having = rows // 2, [0]
    got = jnp.zeros_like(slab)
    while hop:
        if having != [0]:
            slab = slab + got
        pairs = [
            ((owners[c] ^ d) * cols + c, (owners[c] ^ d ^ hop) * cols + c)
            for c in range(cols)
            for d in having
        ]
        got = lax.ppermute(slab, ("row", "col"), pairs)
        having = having + [d ^ hop for d in having]
        hop //= 2

    gram = sum_gather(cols, (strips, 0, strip))
    first_upper, first_inv = cholesky(gram)
    half, half_cols, gram2_strip = half_stage(place, panel, slab, got, first_inv, cols)
    gram2_strips = hops([gram2_strip] * rows, "row", rows)
    parts = sum_gather(cols, (gram2_strips, 0, strip), (strips, strip, 2 * strip))
    gram2 = parts[:, :strip].reshape(width, width)
    second_upper = near_cholesky(gram2)

    left, right, keep, send, pieces = products(
        place, hamiltonian, half, half_cols, second_upper, rows, cols
    )
    parts, send = lax.optimization_barrier((parts, send))
    factor, band_block = compact_factor(parts, first_inv, second_upper, first_upper)
    totals = pair_add(keep, lax.ppermute(send, "col", pair))
    totals = hops(totals, "col", cols, 2)
    pieces = hops(pieces, "row", rows)
    mine, both = sum_pieces(totals, pieces, piece)
    both = hops([both] * rows, "row", rows)
    mine = merge(place, hops([mine] * chips, "col", cols, 2))
    other = lax.ppermute(mine, "col", pair)
    both, factor = lax.optimization_barrier((both, factor))
    coupling = sum_gather(cols, (both, share, share + strip))
    base = base_update(place, hamiltonian, left, mine, other, right, factor, both)
    updated = coupling_update(base, left, right, factor, coupling)
    return (updated, band_block)


def solution(mesh):
    in_specs = (P("row", "col"), P("row", None))
    out_specs = (P("row", "col"), P())
    body = functools.partial(shards, mesh.shape["row"], mesh.shape["col"])
    return jax.shard_map(body, mesh=mesh, in_specs=in_specs, out_specs=out_specs, check_vma=False)
```

time: 138 us -> 118 us (0.86)
  waiting for transfers between devices: 33.5 us -> 21.6 us
  local copies, waits for them, and re-layouts: 16.8 us -> 8.76 us
  blocking collectives: 9.53 us -> 12.2 us
  other arithmetic: 2.43 us -> 0.15 us
  Pallas kernels: 32.4 us -> 34.4 us
  starting transfers between devices: 41 us -> 39.6 us
    all_to_all x6 -> x2, waiting for transfers between devices: 24.1 us -> 3.12 us  [sum_gather(): return lax.all_to_all(copies, 'col', 0, 0, tiled=True)]
    ppermute x8 -> x19, starting transfers between devices: 9.68 us -> 27.9 us  [the longest x18 27.9 us: hops(): got.append(lax.ppermute(values[hop], axis, pairs))]
    all_to_all x6 -> x2, starting transfers between devices: 23.3 us -> 6.82 us  [sum_gather(): return lax.all_to_all(copies, 'col', 0, 0, tiled=True)]
    ppermute x8 -> x19, waiting for transfers between devices: 6.66 us -> 15.7 us  [the longest x18 15.7 us: hops(): got.append(lax.ppermute(values[hop], axis, pairs))]
    unnamed x38 -> x22, local copies, waits for them, and re-layouts: 12.6 us -> 8.74 us
    ppermute x2, starting transfers between devices: 8.04 us -> 4.82 us  [shards(): got = lax.ppermute(slab, ('row', 'col'), pairs)]
    broadcast_in_dim x4 -> x0, local copies, waits for them, and re-layouts: 3.17 us -> none  [the longest x3 2.4 us: gather(): copies = jnp.broadcast_to(piece[None], (size,) + piece.shape)]
    all_to_all x1, blocking collectives: 9.53 us -> 12.2 us  [sum_gather(): return lax.all_to_all(copies, 'col', 0, 0, tiled=True)]
  transfers between devices with their start and end apart: 17 -> 24, of which waited for: 7 -> 9; matrix products, arithmetic and copies ran while one was open for 3% -> 0% of each run, Pallas kernels for 18% -> 16%
where the time goes in v5:
time: 118 us
  starting transfers between devices  39.6 us (34%)
  Pallas kernels  34.4 us (29%)
  waiting for transfers between devices  21.6 us (18%)
  blocking collectives  12.2 us (10%)
  local copies, waits for them, and re-layouts  8.76 us (7%)
    ppermute x18, starting transfers between devices, hops(): got.append(lax.ppermute(values[hop], axis, pairs))  27.9 us
    ppermute x18, waiting for transfers between devices, hops(): got.append(lax.ppermute(values[hop], axis, pairs))  15.7 us
    all_to_all x1, blocking collectives, sum_gather(): return lax.all_to_all(copies, 'col', 0, 0, tiled=True)  12.2 us
    pallas_call x1, Pallas kernels, cholesky(): pl.pallas_call(first_kernel, in_specs=[VMEM], out_specs=(HBM, VMEM), out_...  9.72 us
    unnamed x22, local copies, waits for them, and re-layouts  8.74 us
    all_to_all x2, starting transfers between devices, sum_gather(): return lax.all_to_all(copies, 'col', 0, 0, tiled=True)  6.82 us
    ppermute x2, starting transfers between devices, shards(): got = lax.ppermute(slab, ('row', 'col'), pairs)  4.82 us
    pallas_call x1, Pallas kernels, products(): pl.pallas_call(products_kernel, in_specs=[SMEM, VMEM, HBM, HBM, VMEM], ou...  4.31 us
  transfers between devices with their start and end apart: 24, of which 9 were waited for; matrix products, arithmetic and copies ran while one was open for 0% of the time, Pallas kernels for 16%

profile of v5, /device:TPU:0, one launch (start us, length us, event | category | flops | bytes accessed | tf_op | source)
XLA Modules:
  0.0 117.7 jit_solution(12295367508345594082)
XLA Ops:
  0.7 1.1 copy-done
  1.8 1.5 %gram_strips.1.refs_0_.refs_4_ = f32[64,256]{1,0:T(8,128)S(1)} custom-call(s32[2]{0:T(128)S(1)} %pad_add_fusion.place_ref, f32[768,256]{1,0:T(8,128)S(1)} %copy-done), custom_call_target="tpu_custom_call" | custom-call | flops 2000000000 | bytes 6000000 | tf_op jit(solution)/shard_map/gram_strips/pallas_call | solution.py:297
  3.3 5.1 %collective-permute-start.2 = (f32[64,256]{1,0:T(8,128)S(1)}, f32[64,256]{1,0:T(8,128)S(1)}, u32[]{:S(2)}, u32[]{:S(2)}) collective-permute-start(f32[64,256]{1,0:T(8,128)S(1)} %gram_strips.1.refs_0_.refs_4_), channel_id=1, source_target_pairs={{0,24},{8,16},{16,8},{24,0},{1,25},{9,17},{17,9},{25,1},{2,26},{10... | collective-permute-start | bytes 196616 | tf_op jit(solution)/shard_map/ppermute | solution.py:598
  8.4 0.6 collective-permute-start
  9.1 1.9 %collective-permute-done.2.refs_3_.refs_7_ = f32[64,256]{1,0:T(8,128)S(1)} collective-permute-done((f32[64,256]{1,0:T(8,128)S(1)}, f32[64,256]{1,0:T(8,128)S(1)}, u32[]{:S(2)}, u32[]{:S(2)}) %collective-permute-start.2) | collective-permute-done | bytes 65568 | tf_op jit(solution)/shard_map/ppermute | solution.py:598
  11.0 3.0 %collective-permute-done.1.refs_2_.refs_6_ = f32[64,256]{1,0:T(8,128)S(1)} collective-permute-done((f32[64,256]{1,0:T(8,128)S(1)}, f32[64,256]{1,0:T(8,128)S(1)}, u32[]{:S(2)}, u32[]{:S(2)}) %collective-permute-start.1) | collective-permute-done | bytes 65568 | tf_op jit(solution)/shard_map/ppermute | solution.py:598
  14.0 3.5 %collective-permute-start.3 = (f32[384,256]{1,0:T(8,128)S(1)}, f32[384,256]{1,0:T(8,128)S(1)}, u32[]{:S(2)}, u32[]{:S(2)}) collective-permute-start(f32[384,256]{1,0:T(8,128)S(1)} %dynamic-slice_select_fusion), channel_id=1, source_target_pairs={{0,16},{1,17},{10,26},{11,27},{20,4},{21,5},{30,14},{31,15}} | collective-permute-start | bytes 1179656 | tf_op jit(solution)/shard_map/ppermute | solution.py:632
  17.5 0.7 sum_copies.3
  18.3 3.4 %all-to-all-start = ((f32[8,32,256]{2,1,0:T(8,128)}), f32[8,32,256]{2,1,0:T(8,128)S(1)}, u32[]{:S(2)}, u32[]{:S(2)}) async-start(f32[8,32,256]{2,1,0:T(8,128)} %sum_copies.3), calls=%async_computation | async-start | bytes 524288 | tf_op jit(solution)/shard_map/all_to_all | solution.py:477
  21.7 2.8 %collective-permute-done.3 = f32[384,256]{1,0:T(8,128)S(1)} collective-permute-done((f32[384,256]{1,0:T(8,128)S(1)}, f32[384,256]{1,0:T(8,128)S(1)}, u32[]{:S(2)}, u32[]{:S(2)}) %collective-permute-start.3) | collective-permute-done | bytes 393248 | tf_op jit(solution)/shard_map/ppermute | solution.py:632
  24.5 1.3 %collective-permute-start.4 = (f32[384,256]{1,0:T(8,128)S(1)}, f32[384,256]{1,0:T(8,128)S(1)}, u32[]{:S(2)}, u32[]{:S(2)}) collective-permute-start(f32[384,256]{1,0:T(8,128)S(1)} %add.8.slab_ref), channel_id=1, source_target_pairs={{0,8},{16,24},{1,9},{17,25},{10,2},{26,18},{11,3},{27,19},{20,28},... | collective-permute-start | bytes 1179656 | tf_op jit(solution)/shard_map/ppermute | solution.py:632
  25.8 2.7 %all-to-all-done.parts_ref = f32[8,32,256]{2,1,0:T(8,128)S(1)} async-done(((f32[8,32,256]{2,1,0:T(8,128)}), f32[8,32,256]{2,1,0:T(8,128)S(1)}, u32[]{:S(2)}, u32[]{:S(2)}) %all-to-all-start) | async-done | bytes 262176 | tf_op jit(solution)/shard_map/all_to_all | solution.py:477
  28.6 9.7 %cholesky_inverse.1 = (f32[256,256]{1,0:T(8,128)S(1)}, f32[256,256]{1,0:T(8,128)S(1)}) custom-call(f32[8,32,256]{2,1,0:T(8,128)S(1)} %all-to-all-done.parts_ref), custom_call_target="tpu_custom_call" | custom-call | flops 10000000000 | bytes 30000000 | tf_op jit(solution)/shard_map/cholesky_inverse/pallas_call | solution.py:155
  38.3 3.0 %half_stage.1 = (f32[768,256]{1,0:T(8,128)S(1)}, f32[384,256]{1,0:T(8,128)S(1)}, f32[32,256]{1,0:T(8,128)S(1)}) custom-call(s32[2]{0:T(128)S(1)} %pad_add_fusion.place_ref, f32[768,256]{1,0:T(8,128)S(1)} %copy-done.1, f32[384,256]{1,0:T(8,128)S(1)} %add.8.slab_ref, f32[384,256]{1,0:T(8,128)S(1)} %collective-permute-done.4.got_ref, ...), custom_call_target="tpu_custom_call" | custom-call | flops 3000000000 | bytes 9000000 | tf_op jit(solution)/shard_map/half_stage/pallas_call | solution.py:324
  41.3 2.3 %collective-permute-start.7 = (f32[32,256]{1,0:T(8,128)S(1)}, f32[32,256]{1,0:T(8,128)S(1)}, u32[]{:S(2)}, u32[]{:S(2)}) collective-permute-start(f32[32,256]{1,0:T(8,128)S(1)} %get-tuple-element.43.refs_0_), channel_id=1, source_target_pairs={{0,24},{8,16},{16,8},{24,0},{1,25},{9,17},{17,9},{25,1},{2,26},{10... | collective-permute-start | bytes 98312 | tf_op jit(solution)/shard_map/ppermute | solution.py:598
  44.0 1.8 %collective-permute-start.5 = (f32[32,256]{1,0:T(8,128)S(1)}, f32[32,256]{1,0:T(8,128)S(1)}, u32[]{:S(2)}, u32[]{:S(2)}) collective-permute-start(f32[32,256]{1,0:T(8,128)S(1)} %get-tuple-element.43.refs_0_), channel_id=1, source_target_pairs={{0,8},{8,0},{16,24},{24,16},{1,9},{9,1},{17,25},{25,17},{2,10},{10... | collective-permute-start | bytes 98312 | tf_op jit(solution)/shard_map/ppermute | solution.py:598
  45.8 1.3 %collective-permute-done.7.refs_3_ = f32[32,256]{1,0:T(8,128)S(1)} collective-permute-done((f32[32,256]{1,0:T(8,128)S(1)}, f32[32,256]{1,0:T(8,128)S(1)}, u32[]{:S(2)}, u32[]{:S(2)}) %collective-permute-start.7) | collective-permute-done | bytes 32800 | tf_op jit(solution)/shard_map/ppermute | solution.py:598
  47.1 1.3 %collective-permute-done.6.refs_2_ = f32[32,256]{1,0:T(8,128)S(1)} collective-permute-done((f32[32,256]{1,0:T(8,128)S(1)}, f32[32,256]{1,0:T(8,128)S(1)}, u32[]{:S(2)}, u32[]{:S(2)}) %collective-permute-start.6) | collective-permute-done | bytes 32800 | tf_op jit(solution)/shard_map/ppermute | solution.py:598
  48.5 12.2 %all_to_all.15.parts_ref = f32[8,64,256]{2,1,0:T(8,128)S(1)} all-to-all(f32[8,64,256]{2,1,0:T(8,128)S(1)} %sum_copies.4), channel_id=1, replica_groups=mesh['row'=4,'col'=8] {'col'}, dimensions={0} | all-to-all | bytes 1048576 | tf_op jit(solution)/shard_map/all_to_all | solution.py:477
  60.7 3.1 %near_cholesky.1.upper_ref = f32[256,256]{1,0:T(8,128)S(1)} custom-call(f32[256,256]{1,0:T(8,128)S(1)} %bitcast.3), custom_call_target="tpu_custom_call" | custom-call | flops 3000000000 | bytes 9000000 | tf_op jit(solution)/shard_map/near_cholesky/pallas_call | solution.py:212
  63.8 4.3 %products.1 = (f32[768,256]{1,0:T(8,128)S(1)}, f32[384,256]{1,0:T(8,128)S(1)}, f32[4,128,256]{2,1,0:T(8,128)S(1)}, f32[4,128,256]{2,1,0:T(8,128)S(1)}, f32[96,25...) custom-call(s32[2]{0:T(128)S(1)} %pad_add_fusion.place_ref, ...), custom_call_target="tpu_custom_call" | custom-call | flops 4000000000 | bytes 12000000 | tf_op jit(solution)/shard_map/products/pallas_call | solution.py:383
  68.2 0.7 copy-done.5
  68.9 1.9 %collective-permute-start.12 = (f32[96,256]{1,0:T(8,128)S(1)}, f32[96,256]{1,0:T(8,128)S(1)}, u32[]{:S(2)}, u32[]{:S(2)}) collective-permute-start(f32[96,256]{1,0:T(8,128)S(1)} %get-tuple-element.53), channel_id=1, source_target_pairs={{0,8},{8,0},{16,24},{24,16},{1,9},{9,1},{17,25},{25,17},{2,10},{10... | collective-permute-start | bytes 294920 | tf_op jit(solution)/shard_map/ppermute | solution.py:598
  70.9 0.6 collective-permute-start.9
  72.1 2.4 %collective-permute-start.11 = (f32[128,256]{1,0:T(8,128)S(1)}, f32[128,256]{1,0:T(8,128)S(1)}, u32[]{:S(2)}, u32[]{:S(2)}) collective-permute-start(f32[128,256]{1,0:T(8,128)S(1)} %get-tuple-element.51), channel_id=1, source_target_pairs={{0,6},{1,7},{2,4},{3,5},{4,2},{5,3},{6,0},{7,1},{8,14},{9,15},{10,... | collective-permute-start | bytes 393224 | tf_op jit(solution)/shard_map/ppermute | solution.py:598
  74.4 2.0 %collective-permute-start.13 = (f32[96,256]{1,0:T(8,128)S(1)}, f32[96,256]{1,0:T(8,128)S(1)}, u32[]{:S(2)}, u32[]{:S(2)}) collective-permute-start(f32[96,256]{1,0:T(8,128)S(1)} %get-tuple-element.54), channel_id=1, source_target_pairs={{0,16},{8,24},{16,0},{24,8},{1,17},{9,25},{17,1},{25,9},{2,18},{10... | collective-permute-start | bytes 294920 | tf_op jit(solution)/shard_map/ppermute | solution.py:598
  76.4 2.3 %collective-permute-start.14 = (f32[96,256]{1,0:T(8,128)S(1)}, f32[96,256]{1,0:T(8,128)S(1)}, u32[]{:S(2)}, u32[]{:S(2)}) collective-permute-start(f32[96,256]{1,0:T(8,128)S(1)} %get-tuple-element.55), channel_id=1, source_target_pairs={{0,24},{8,16},{16,8},{24,0},{1,25},{9,17},{17,9},{25,1},{2,26},{10... | collective-permute-start | bytes 294920 | tf_op jit(solution)/shard_map/ppermute | solution.py:598
  78.7 6.0 %collective-permute-done.13.refs_6_ = f32[96,256]{1,0:T(8,128)S(1)} collective-permute-done((f32[96,256]{1,0:T(8,128)S(1)}, f32[96,256]{1,0:T(8,128)S(1)}, u32[]{:S(2)}, u32[]{:S(2)}) %collective-permute-start.13) | collective-permute-done | bytes 98336 | tf_op jit(solution)/shard_map/ppermute | solution.py:598
  84.8 0.6 collective-permute-start.17
  85.4 1.5 %collective-permute-start.16 = (f32[96,256]{1,0:T(8,128)S(1)}, f32[96,256]{1,0:T(8,128)S(1)}, u32[]{:S(2)}, u32[]{:S(2)}) collective-permute-start(f32[96,256]{1,0:T(8,128)S(1)} %get-tuple-element.56.refs_0_), channel_id=1, source_target_pairs={{0,4},{1,5},{2,6},{3,7},{4,0},{5,1},{6,2},{7,3},{8,12},{9,13},{10,... | collective-permute-start | bytes 294920 | tf_op jit(solution)/shard_map/ppermute | solution.py:598
  86.9 1.5 %collective-permute-start.15 = (f32[96,256]{1,0:T(8,128)S(1)}, f32[96,256]{1,0:T(8,128)S(1)}, u32[]{:S(2)}, u32[]{:S(2)}) collective-permute-start(f32[96,256]{1,0:T(8,128)S(1)} %get-tuple-element.56.refs_0_), channel_id=1, source_target_pairs={{0,2},{1,3},{2,0},{3,1},{4,6},{5,7},{6,4},{7,5},{8,10},{9,11},{10,... | collective-permute-start | bytes 294920 | tf_op jit(solution)/shard_map/ppermute | solution.py:598
  88.3 1.9 %collective-permute-start.21 = (f32[128,256]{1,0:T(8,128)S(1)}, f32[128,256]{1,0:T(8,128)S(1)}, u32[]{:S(2)}, u32[]{:S(2)}) collective-permute-start(f32[128,256]{1,0:T(8,128)S(1)} %get-tuple-element.63.rest_refs_0_.refs_0_), channel_id=1, source_target_pairs={{0,24},{8,16},{16,8},{24,0},{1,25},{9,17},{17,9},{25,1},{2,26},{10... | collective-permute-start | bytes 393224 | tf_op jit(solution)/shard_map/ppermute | solution.py:598
  90.2 1.2 collective-permute-start.20
  91.4 1.3 %collective-permute-start.19 = (f32[128,256]{1,0:T(8,128)S(1)}, f32[128,256]{1,0:T(8,128)S(1)}, u32[]{:S(2)}, u32[]{:S(2)}) collective-permute-start(f32[128,256]{1,0:T(8,128)S(1)} %get-tuple-element.63.rest_refs_0_.refs_0_), channel_id=1, source_target_pairs={{0,8},{8,0},{16,24},{24,16},{1,9},{9,1},{17,25},{25,17},{2,10},{10... | collective-permute-start | bytes 393224 | tf_op jit(solution)/shard_map/ppermute | solution.py:598
  92.7 0.6 merge_pieces.1.mine_ref
  93.4 3.7 %compact_factor.1 = (f32[256,256]{1,0:T(8,128)S(1)}, f32[256,256]{1,0:T(8,128)}) custom-call(f32[8,64,256]{2,1,0:T(8,128)S(1)} %all_to_all.15.parts_ref, f32[256,256]{1,0:T(8,128)S(1)} %get-tuple-element.40.inv_ref, f32[256,256]{1,0:T(8,128)S(1)} %near_cholesky.1.upper_ref, f32[256,256]{1,0:T(8,128)S(1)} %get-tuple-element.60.first_ref), custom_call_target="tpu_custom_call" | custom-call | flops 4000000000 | bytes 12000000 | tf_op jit(solution)/shard_map/compact_factor/pallas_call | solution.py:267
  97.1 0.7 copy-done.8
  97.8 2.1 %collective-permute-done.20.rest_refs_2_.refs_2_ = f32[128,256]{1,0:T(8,128)S(1)} collective-permute-done((f32[128,256]{1,0:T(8,128)S(1)}, f32[128,256]{1,0:T(8,128)S(1)}, u32[]{:S(2)}, u32[]{:S(2)}) %collective-permute-start.20) | collective-permute-done | bytes 131104 | tf_op jit(solution)/shard_map/ppermute | solution.py:598
  99.8 0.7 sum_copies.5
  100.6 3.4 %all-to-all-start.2 = ((f32[8,32,256]{2,1,0:T(8,128)}), f32[8,32,256]{2,1,0:T(8,128)S(1)}, u32[]{:S(2)}, u32[]{:S(2)}) async-start(f32[8,32,256]{2,1,0:T(8,128)} %sum_copies.5), calls=%async_computation.2 | async-start | bytes 524288 | tf_op jit(solution)/shard_map/all_to_all | solution.py:477
  104.0 1.0 copy-done.6
  105.0 0.9 copy-done.9
  106.0 3.5 %base_update.1.base_in = f32[768,384]{1,0:T(8,128)S(1)} custom-call(s32[2]{0:T(128)S(1)} %pad_add_fusion.place_ref, f32[768,384]{1,0:T(8,128)S(1)} %copy-done.2, f32[768,256]{1,0:T(8,128)S(1)} %get-tuple-element.44.left_in, f32[384,256]{1,0:T(8,128)S(1)} %merge_pieces.1.mine_ref, f32[384,256]{1,0:T(8,128)S(1)} %collective-permute-done.18.other_ref, ...), custom_call_target="tpu_custom_call" | custom-call | flops 4000000000 | bytes 12000000 | tf_op jit(solution)/shard_map/base_update/pallas_call | solution.py:525
  109.5 1.0 copy-done.3
  110.9 1.3 %copy-done.4 = f32[768,384]{1,0:T(8,128)S(1)} copy-done((f32[768,384]{1,0:T(8,128)S(1)}, f32[768,384]{1,0:T(8,128)}, u32[]{:S(2)}) %copy-start.4) | copy-done | bytes 1179672
  112.1 1.0 copy-done.7
  113.1 0.9 copy-done.10
  114.1 3.5 %coupling_update.1 = f32[768,384]{1,0:T(8,128)} custom-call(f32[768,384]{1,0:T(8,128)S(1)} %copy-done.4, f32[768,256]{1,0:T(8,128)S(1)} %get-tuple-element.44.left_in, f32[384,256]{1,0:T(8,128)S(1)} %copy-done.7, f32[256,256]{1,0:T(8,128)S(1)} %copy-done.10, f32[8,32,256]{2,1,0:T(8,128)S(1)} %all-to-all-done.2.parts_ref), custom_call_target="tpu_custom_call" | custom-call | flops 3000000000 | bytes 9000000 | tf_op jit(solution)/shard_map/coupling_update/pallas_call | solution.py:575
  (41 shorter events, 1.8 us)
Async XLA Ops:
  0.7 1.1 copy-start
  1.8 7.2 %copy-start.1 = (f32[768,256]{1,0:T(8,128)S(1)}, f32[768,256]{1,0:T(8,128)}, u32[]{:S(2)}) copy-start(f32[768,256]{1,0:T(8,128)} %panel_ref.3) | copy-start | bytes 2359300
  3.3 7.7 %collective-permute-start.2 = (f32[64,256]{1,0:T(8,128)S(1)}, f32[64,256]{1,0:T(8,128)S(1)}, u32[]{:S(2)}, u32[]{:S(2)}) collective-permute-start(f32[64,256]{1,0:T(8,128)S(1)} %gram_strips.1.refs_0_.refs_4_), channel_id=1, source_target_pairs={{0,24},{8,16},{16,8},{24,0},{1,25},{9,17},{17,9},{25,1},{2,26},{10... | collective-permute-start | bytes 196616 | tf_op jit(solution)/shard_map/ppermute | solution.py:598
  8.4 5.6 %collective-permute-start.1 = (f32[64,256]{1,0:T(8,128)S(1)}, f32[64,256]{1,0:T(8,128)S(1)}, u32[]{:S(2)}, u32[]{:S(2)}) collective-permute-start(f32[64,256]{1,0:T(8,128)S(1)} %gram_strips.1.refs_0_.refs_4_), channel_id=1, source_target_pairs={{0,16},{8,24},{16,0},{24,8},{1,17},{9,25},{17,1},{25,9},{2,18},{10... | collective-permute-start | bytes 196616 | tf_op jit(solution)/shard_map/ppermute | solution.py:598
  8.4 5.6 %collective-permute-start = (f32[64,256]{1,0:T(8,128)S(1)}, f32[64,256]{1,0:T(8,128)S(1)}, u32[]{:S(2)}, u32[]{:S(2)}) collective-permute-start(f32[64,256]{1,0:T(8,128)S(1)} %gram_strips.1.refs_0_.refs_4_), channel_id=1, source_target_pairs={{0,8},{8,0},{16,24},{24,16},{1,9},{9,1},{17,25},{25,17},{2,10},{10... | collective-permute-start | bytes 196616 | tf_op jit(solution)/shard_map/ppermute | solution.py:598
  14.0 10.4 %collective-permute-start.3 = (f32[384,256]{1,0:T(8,128)S(1)}, f32[384,256]{1,0:T(8,128)S(1)}, u32[]{:S(2)}, u32[]{:S(2)}) collective-permute-start(f32[384,256]{1,0:T(8,128)S(1)} %dynamic-slice_select_fusion), channel_id=1, source_target_pairs={{0,16},{1,17},{10,26},{11,27},{20,4},{21,5},{30,14},{31,15}} | collective-permute-start | bytes 1179656 | tf_op jit(solution)/shard_map/ppermute | solution.py:632
  18.3 10.3 %all-to-all-start = ((f32[8,32,256]{2,1,0:T(8,128)}), f32[8,32,256]{2,1,0:T(8,128)S(1)}, u32[]{:S(2)}, u32[]{:S(2)}) async-start(f32[8,32,256]{2,1,0:T(8,128)} %sum_copies.3), calls=%async_computation | async-start | bytes 524288 | tf_op jit(solution)/shard_map/all_to_all | solution.py:477
  24.5 13.8 %collective-permute-start.4 = (f32[384,256]{1,0:T(8,128)S(1)}, f32[384,256]{1,0:T(8,128)S(1)}, u32[]{:S(2)}, u32[]{:S(2)}) collective-permute-start(f32[384,256]{1,0:T(8,128)S(1)} %add.8.slab_ref), channel_id=1, source_target_pairs={{0,8},{16,24},{1,9},{17,25},{10,2},{26,18},{11,3},{27,19},{20,28},... | collective-permute-start | bytes 1179656 | tf_op jit(solution)/shard_map/ppermute | solution.py:632
  41.3 5.8 %collective-permute-start.7 = (f32[32,256]{1,0:T(8,128)S(1)}, f32[32,256]{1,0:T(8,128)S(1)}, u32[]{:S(2)}, u32[]{:S(2)}) collective-permute-start(f32[32,256]{1,0:T(8,128)S(1)} %get-tuple-element.43.refs_0_), channel_id=1, source_target_pairs={{0,24},{8,16},{16,8},{24,0},{1,25},{9,17},{17,9},{25,1},{2,26},{10... | collective-permute-start | bytes 98312 | tf_op jit(solution)/shard_map/ppermute | solution.py:598
  43.6 4.8 %collective-permute-start.6 = (f32[32,256]{1,0:T(8,128)S(1)}, f32[32,256]{1,0:T(8,128)S(1)}, u32[]{:S(2)}, u32[]{:S(2)}) collective-permute-start(f32[32,256]{1,0:T(8,128)S(1)} %get-tuple-element.43.refs_0_), channel_id=1, source_target_pairs={{0,16},{8,24},{16,0},{24,8},{1,17},{9,25},{17,1},{25,9},{2,18},{10... | collective-permute-start | bytes 98312 | tf_op jit(solution)/shard_map/ppermute | solution.py:598
  44.0 4.5 %collective-permute-start.5 = (f32[32,256]{1,0:T(8,128)S(1)}, f32[32,256]{1,0:T(8,128)S(1)}, u32[]{:S(2)}, u32[]{:S(2)}) collective-permute-start(f32[32,256]{1,0:T(8,128)S(1)} %get-tuple-element.43.refs_0_), channel_id=1, source_target_pairs={{0,8},{8,0},{16,24},{24,16},{1,9},{9,1},{17,25},{25,17},{2,10},{10... | collective-permute-start | bytes 98312 | tf_op jit(solution)/shard_map/ppermute | solution.py:598
  60.7 3.1 %copy-start.2 = (f32[768,384]{1,0:T(8,128)S(1)}, f32[768,384]{1,0:T(8,128)}, u32[]{:S(2)}) copy-start(f32[768,384]{1,0:T(8,128)} %ham_ref.3) | copy-start | bytes 3538948
  68.2 0.7 copy-start.5
  68.9 1.9 %collective-permute-start.8 = (f32[4,128,256]{2,1,0:T(8,128)S(1)}, f32[4,128,256]{2,1,0:T(8,128)S(1)}, u32[]{:S(2)}, u32[]{:S(2)}) collective-permute-start(f32[4,128,256]{2,1,0:T(8,128)S(1)} %get-tuple-element.47), channel_id=1, source_target_pairs={{0,1},{1,0},{2,3},{3,2},{4,5},{5,4},{6,7},{7,6},{8,9},{9,8},{10,11... | collective-permute-start | bytes 1572872 | tf_op jit(solution)/shard_map/ppermute | solution.py:649
  68.9 7.5 %collective-permute-start.12 = (f32[96,256]{1,0:T(8,128)S(1)}, f32[96,256]{1,0:T(8,128)S(1)}, u32[]{:S(2)}, u32[]{:S(2)}) collective-permute-start(f32[96,256]{1,0:T(8,128)S(1)} %get-tuple-element.53), channel_id=1, source_target_pairs={{0,8},{8,0},{16,24},{24,16},{1,9},{9,1},{17,25},{25,17},{2,10},{10... | collective-permute-start | bytes 294920 | tf_op jit(solution)/shard_map/ppermute | solution.py:598
  70.9 13.8 %collective-permute-start.9 = (f32[128,256]{1,0:T(8,128)S(1)}, f32[128,256]{1,0:T(8,128)S(1)}, u32[]{:S(2)}, u32[]{:S(2)}) collective-permute-start(f32[128,256]{1,0:T(8,128)S(1)} %get-tuple-element.49), channel_id=1, source_target_pairs={{0,2},{1,3},{2,0},{3,1},{4,6},{5,7},{6,4},{7,5},{8,10},{9,11},{10,... | collective-permute-start | bytes 393224 | tf_op jit(solution)/shard_map/ppermute | solution.py:598
  71.5 13.2 %collective-permute-start.10 = (f32[128,256]{1,0:T(8,128)S(1)}, f32[128,256]{1,0:T(8,128)S(1)}, u32[]{:S(2)}, u32[]{:S(2)}) collective-permute-start(f32[128,256]{1,0:T(8,128)S(1)} %get-tuple-element.50), channel_id=1, source_target_pairs={{0,4},{1,5},{2,6},{3,7},{4,0},{5,1},{6,2},{7,3},{8,12},{9,13},{10,... | collective-permute-start | bytes 393224 | tf_op jit(solution)/shard_map/ppermute | solution.py:598
  72.1 12.6 %collective-permute-start.11 = (f32[128,256]{1,0:T(8,128)S(1)}, f32[128,256]{1,0:T(8,128)S(1)}, u32[]{:S(2)}, u32[]{:S(2)}) collective-permute-start(f32[128,256]{1,0:T(8,128)S(1)} %get-tuple-element.51), channel_id=1, source_target_pairs={{0,6},{1,7},{2,4},{3,5},{4,2},{5,3},{6,0},{7,1},{8,14},{9,15},{10,... | collective-permute-start | bytes 393224 | tf_op jit(solution)/shard_map/ppermute | solution.py:598
  74.4 10.3 %collective-permute-start.13 = (f32[96,256]{1,0:T(8,128)S(1)}, f32[96,256]{1,0:T(8,128)S(1)}, u32[]{:S(2)}, u32[]{:S(2)}) collective-permute-start(f32[96,256]{1,0:T(8,128)S(1)} %get-tuple-element.54), channel_id=1, source_target_pairs={{0,16},{8,24},{16,0},{24,8},{1,17},{9,25},{17,1},{25,9},{2,18},{10... | collective-permute-start | bytes 294920 | tf_op jit(solution)/shard_map/ppermute | solution.py:598
  76.4 8.3 %collective-permute-start.14 = (f32[96,256]{1,0:T(8,128)S(1)}, f32[96,256]{1,0:T(8,128)S(1)}, u32[]{:S(2)}, u32[]{:S(2)}) collective-permute-start(f32[96,256]{1,0:T(8,128)S(1)} %get-tuple-element.55), channel_id=1, source_target_pairs={{0,24},{8,16},{16,8},{24,0},{1,25},{9,17},{17,9},{25,1},{2,26},{10... | collective-permute-start | bytes 294920 | tf_op jit(solution)/shard_map/ppermute | solution.py:598
  84.8 6.6 %collective-permute-start.17 = (f32[96,256]{1,0:T(8,128)S(1)}, f32[96,256]{1,0:T(8,128)S(1)}, u32[]{:S(2)}, u32[]{:S(2)}) collective-permute-start(f32[96,256]{1,0:T(8,128)S(1)} %get-tuple-element.56.refs_0_), channel_id=1, source_target_pairs={{0,6},{1,7},{2,4},{3,5},{4,2},{5,3},{6,0},{7,1},{8,14},{9,15},{10,... | collective-permute-start | bytes 294920 | tf_op jit(solution)/shard_map/ppermute | solution.py:598
  85.4 7.3 %collective-permute-start.16 = (f32[96,256]{1,0:T(8,128)S(1)}, f32[96,256]{1,0:T(8,128)S(1)}, u32[]{:S(2)}, u32[]{:S(2)}) collective-permute-start(f32[96,256]{1,0:T(8,128)S(1)} %get-tuple-element.56.refs_0_), channel_id=1, source_target_pairs={{0,4},{1,5},{2,6},{3,7},{4,0},{5,1},{6,2},{7,3},{8,12},{9,13},{10,... | collective-permute-start | bytes 294920 | tf_op jit(solution)/shard_map/ppermute | solution.py:598
  86.9 5.9 %collective-permute-start.15 = (f32[96,256]{1,0:T(8,128)S(1)}, f32[96,256]{1,0:T(8,128)S(1)}, u32[]{:S(2)}, u32[]{:S(2)}) collective-permute-start(f32[96,256]{1,0:T(8,128)S(1)} %get-tuple-element.56.refs_0_), channel_id=1, source_target_pairs={{0,2},{1,3},{2,0},{3,1},{4,6},{5,7},{6,4},{7,5},{8,10},{9,11},{10,... | collective-permute-start | bytes 294920 | tf_op jit(solution)/shard_map/ppermute | solution.py:598
  88.3 9.5 %collective-permute-start.21 = (f32[128,256]{1,0:T(8,128)S(1)}, f32[128,256]{1,0:T(8,128)S(1)}, u32[]{:S(2)}, u32[]{:S(2)}) collective-permute-start(f32[128,256]{1,0:T(8,128)S(1)} %get-tuple-element.63.rest_refs_0_.refs_0_), channel_id=1, source_target_pairs={{0,24},{8,16},{16,8},{24,0},{1,25},{9,17},{17,9},{25,1},{2,26},{10... | collective-permute-start | bytes 393224 | tf_op jit(solution)/shard_map/ppermute | solution.py:598
  90.2 9.6 %collective-permute-start.20 = (f32[128,256]{1,0:T(8,128)S(1)}, f32[128,256]{1,0:T(8,128)S(1)}, u32[]{:S(2)}, u32[]{:S(2)}) collective-permute-start(f32[128,256]{1,0:T(8,128)S(1)} %get-tuple-element.63.rest_refs_0_.refs_0_), channel_id=1, source_target_pairs={{0,16},{8,24},{16,0},{24,8},{1,17},{9,25},{17,1},{25,9},{2,18},{10... | collective-permute-start | bytes 393224 | tf_op jit(solution)/shard_map/ppermute | solution.py:598
  91.4 8.5 %collective-permute-start.19 = (f32[128,256]{1,0:T(8,128)S(1)}, f32[128,256]{1,0:T(8,128)S(1)}, u32[]{:S(2)}, u32[]{:S(2)}) collective-permute-start(f32[128,256]{1,0:T(8,128)S(1)} %get-tuple-element.63.rest_refs_0_.refs_0_), channel_id=1, source_target_pairs={{0,8},{8,0},{16,24},{24,16},{1,9},{9,1},{17,25},{25,17},{2,10},{10... | collective-permute-start | bytes 393224 | tf_op jit(solution)/shard_map/ppermute | solution.py:598
  93.3 10.7 %collective-permute-start.18 = (f32[384,256]{1,0:T(8,128)S(1)}, f32[384,256]{1,0:T(8,128)S(1)}, u32[]{:S(2)}, u32[]{:S(2)}) collective-permute-start(f32[384,256]{1,0:T(8,128)S(1)} %merge_pieces.1.mine_ref), channel_id=1, source_target_pairs={{0,1},{1,0},{2,3},{3,2},{4,5},{5,4},{6,7},{7,6},{8,9},{9,8},{10,11... | collective-permute-start | bytes 1179656 | tf_op jit(solution)/shard_map/ppermute | solution.py:655
  97.1 0.7 copy-start.8
  100.6 10.3 %all-to-all-start.2 = ((f32[8,32,256]{2,1,0:T(8,128)}), f32[8,32,256]{2,1,0:T(8,128)S(1)}, u32[]{:S(2)}, u32[]{:S(2)}) async-start(f32[8,32,256]{2,1,0:T(8,128)} %sum_copies.5), calls=%async_computation.2 | async-start | bytes 524288 | tf_op jit(solution)/shard_map/all_to_all | solution.py:477
  104.0 1.0 copy-start.6
  105.0 0.9 copy-start.9
  109.5 1.0 copy-start.3
  110.9 1.3 %copy-start.4 = (f32[768,384]{1,0:T(8,128)S(1)}, f32[768,384]{1,0:T(8,128)}, u32[]{:S(2)}) copy-start(f32[768,384]{1,0:T(8,128)} %copy-done.3) | copy-start | bytes 3538948
  112.1 1.0 copy-start.7
  113.1 0.9 copy-start.10

commit v6 on v5

v6 whole, which is shorter than its diff:
```python
import functools

import jax
import jax.numpy as jnp
from jax import lax
from jax.experimental import pallas as pl
from jax.experimental.pallas import tpu as pltpu
from jax.sharding import PartitionSpec as P

SUB = 8
LANE = 128
BLOCK = 32
HIGHEST = lax.Precision.HIGHEST
SMALL = pltpu.CompilerParams(vmem_limit_bytes=10 * 2**20)
LARGE = pltpu.CompilerParams(vmem_limit_bytes=24 * 2**20)
VMEM = pl.BlockSpec(memory_space=pltpu.VMEM)
SMEM = pl.BlockSpec(memory_space=pltpu.SMEM)
PLAIN = ((1,), (0,))
TURNED = ((0,), (0,))
ACROSS = ((1,), (1,))


def mult(left, right, dims=PLAIN):
    return lax.dot_general(
        left, right, (dims, ((), ())), precision=HIGHEST, preferred_element_type=jnp.float32
    )


def split(value):
    high = value.astype(jnp.bfloat16)
    return high, (value - high.astype(jnp.float32)).astype(jnp.bfloat16)


def mult3(left, right, dims=PLAIN):
    def one(a, b):
        return lax.dot_general(a, b, (dims, ((), ())), preferred_element_type=jnp.float32)

    return one(left[0], right[0]) + (one(left[0], right[1]) + one(left[1], right[0]))


def chol_kernel(gram_ref, upper_ref, inv_ref, work_ref):
    size = gram_ref.shape[0]
    tiles = size // LANE
    groups = BLOCK // SUB
    lanes = lax.broadcasted_iota(jnp.int32, (SUB, LANE), 1)
    work_ref[...] = gram_ref[...]

    def spread(row):
        return jnp.broadcast_to(row, (SUB, LANE))

    for first in range(0, size, BLOCK):
        rows = [
            [
                work_ref[first + SUB * g : first + SUB * (g + 1), LANE * t : LANE * (t + 1)]
                for t in range(tiles)
            ]
            for g in range(groups)
        ]
        for g in range(groups):
            col = first + SUB * g
            home, low = divmod(col, LANE)
            in_block = (lanes >= low) & (lanes < low + SUB)
            flat = [[spread(rows[g][t][k : k + 1, :]) for t in range(tiles)] for k in range(SUB)]
            diag = [
                [spread(flat[k][home][:, low + i : low + i + 1]) for i in range(k + 1)]
                for k in range(SUB)
            ]
            unit = [jnp.where(lanes == low + k, 1.0, 0.0) for k in range(SUB)]
            later = range(g + 1, groups)
            cols = {
                q: [spread(rows[q][home][:, low + i : low + i + 1]) for i in range(SUB)]
                for q in later
            }
            for q in later:
                rows[q][home] = jnp.where(in_block, 0.0, rows[q][home])
            for i in range(SUB):
                recip = 1.0 / diag[i][i]
                steps = [None] * SUB
                for k in range(i + 1, SUB):
                    steps[k] = diag[k][i] * recip
                for k in range(i + 1, SUB):
                    for j in range(i + 1, k + 1):
                        diag[k][j] = diag[k][j] - steps[k] * diag[j][i]
                for k in range(i + 1, SUB):
                    for t in range(tiles):
                        flat[k][t] = flat[k][t] - steps[k] * flat[i][t]
                    unit[k] = unit[k] - steps[k] * unit[i]
                for q in later:
                    step = cols[q][i] * recip
                    for j in range(i + 1, SUB):
                        cols[q][j] = cols[q][j] - step * diag[j][i]
                    for t in range(tiles):
                        source = flat[i][t]
                        if t == home:
                            source = jnp.where(in_block, unit[i], source)
                        rows[q][t] = rows[q][t] - step * source
            for k in range(SUB):
                scale = lax.rsqrt(diag[k][k])
                for t in range(tiles):
                    scaled = flat[k][t] * scale
                    if t < home:
                        up, inv = jnp.zeros_like(scaled), scaled
                    elif t > home:
                        up, inv = scaled, jnp.zeros_like(scaled)
                    else:
                        up = jnp.where(lanes >= low + k, scaled, 0.0)
                        inv = jnp.where(in_block, unit[k] * scale, scaled)
                        inv = jnp.where(lanes < low + SUB, inv, 0.0)
                    upper_ref[col + k : col + k + 1, LANE * t : LANE * (t + 1)] = up[0:1]
                    inv_ref[col + k : col + k + 1, LANE * t : LANE * (t + 1)] = inv[0:1]
        rest = first + BLOCK
        if rest == size:
            break
        start = rest // LANE * LANE
        left = upper_ref[first:rest, start:size]
        wide = lax.broadcasted_iota(jnp.int32, (BLOCK, size), 1)
        right = jnp.where(wide < rest, inv_ref[first:rest, :], upper_ref[first:rest, :])
        change = mult(left, right, ((0,), (0,)))
        below = lax.broadcasted_iota(jnp.int32, (size - rest, size), 1)
        old = jnp.where((below >= first) & (below < rest), 0.0, work_ref[rest:size, :])
        work_ref[rest:size, :] = old - change[rest - start :, :]


def estimate(micros):
    return pl.CostEstimate(flops=int(micros * 1e7), bytes_accessed=int(micros * 3e4), transcendentals=0)


def square(size):
    return jax.ShapeDtypeStruct((size, size), jnp.float32)


def first_kernel(parts_ref, upper_ref, inv_ref, gram_ref, work_ref):
    strip = parts_ref.shape[1]
    for c in range(parts_ref.shape[0]):
        gram_ref[c * strip : (c + 1) * strip, :] = parts_ref[c]
    chol_kernel(gram_ref, upper_ref, inv_ref, work_ref)


def cholesky(parts):
    size = parts.shape[2]
    return pl.pallas_call(
        first_kernel,
        in_specs=[VMEM],
        out_shape=(square(size), square(size)),
        scratch_shapes=[pltpu.VMEM((size, size), jnp.float32)] * 2,
        compiler_params=SMALL,
        cost_estimate=estimate(10),
        name="cholesky_inverse",
    )(parts)


def grids(size):
    row = lax.broadcasted_iota(jnp.int32, (size, size), 0)
    col = lax.broadcasted_iota(jnp.int32, (size, size), 1)
    return row, col


def near_kernel(gram_ref, upper_ref, inv_ref, work_ref):
    size = gram_ref.shape[0]
    row, col = grids(size)
    ident = jnp.where(row == col, 1.0, 0.0)
    weight = jnp.where(row > col, 1.0, ident * 0.5)
    gram = split(gram_ref[...])

    def look(inv):
        halves = split(inv)
        upper = mult3(halves, gram)
        low = weight * (mult3(split(upper), halves, ACROSS) - ident)
        return upper, low, jnp.sum(low * low)

    def more(state):
        count, _, _, _, worst = state
        return jnp.logical_not(worst < 1e-5) & (count < 8)

    def step(state):
        count, inv, _, low, _ = state
        low = split(low)
        turn = mult3(low, split(inv))
        inv = inv - turn + mult3(low, split(turn))
        return (count + 1, inv) + look(inv)

    low = weight * (gram_ref[...] - ident)
    halves = split(low)
    inv = ident - low + mult3(halves, halves)
    state = lax.while_loop(more, step, (jnp.int32(0), inv) + look(inv))
    _, _, upper, low, worst = state
    upper = upper + mult3(split(low), split(upper), TURNED)
    upper_ref[...] = jnp.where(row <= col, upper, 0.0)

    @pl.when(jnp.logical_not(worst < 1e-5))
    def _():
        chol_kernel(gram_ref, upper_ref, inv_ref, work_ref)


def near_cholesky(gram):
    size = gram.shape[0]
    return pl.pallas_call(
        near_kernel,
        out_shape=square(size),
        scratch_shapes=[pltpu.VMEM((size, size), jnp.float32)] * 2,
        compiler_params=SMALL,
        cost_estimate=estimate(3),
        name="near_cholesky",
    )(gram)


def factor_kernel(gram_ref, top_ref, inv_ref, upper_ref, first_ref, out_ref, band_ref):
    size = inv_ref.shape[0]
    row, col = grids(size)
    ident = jnp.where(row == col, 1.0, 0.0)
    band_ref[...] = -mult(upper_ref[...], first_ref[...])
    top = top_ref[...].reshape(size, size)
    half_top = mult(top, inv_ref[...], ACROSS)
    mat = gram_ref[...].reshape(size, size) + mult3(split(half_top), split(upper_ref[...]), TURNED)
    halves = split(mat)

    def rough(left, right):
        return jnp.dot(
            left.astype(jnp.bfloat16),
            right.astype(jnp.bfloat16),
            preferred_element_type=jnp.float32,
        )

    def residual(guess):
        return ident - mult3(halves, split(guess))

    def step(state):
        count, guess, rest, _ = state
        guess = guess + mult3(split(guess), split(rest))
        rest = residual(guess)
        return count + 1, guess, rest, jnp.max(jnp.abs(rest))

    def more(state):
        count, _, _, worst = state
        return (worst > 2e-5) & (count < 40)

    guess = 0.5 * ident
    rest = ident - 0.5 * mat
    for _ in range(4):
        guess = guess + rough(guess, rest)
        rest = rough(rest, rest)
    guess = guess + rough(guess, rest)
    rest = residual(guess)
    state = (jnp.int32(0), guess, rest, jnp.max(jnp.abs(rest)))
    out_ref[...] = lax.while_loop(more, step, state)[1]


def compact_factor(gram, top, inv, upper, first):
    return pl.pallas_call(
        factor_kernel,
        out_shape=(square(inv.shape[0]), square(inv.shape[0])),
        compiler_params=SMALL,
        cost_estimate=estimate(4),
        name="compact_factor",
    )(gram, top, inv, upper, first)


def array(*dims):
    return jax.ShapeDtypeStruct(dims, jnp.float32)


def scratch(*dims):
    return pltpu.VMEM(dims, jnp.float32)


def gram_kernel(place_ref, panel_ref, out_ref, gram_ref):
    strip = out_ref.shape[0] // 2
    mine = pl.ds(pl.multiple_of(place_ref[1] * strip, strip), strip)
    gram_ref[...] = mult(panel_ref[...], panel_ref[...], TURNED)
    out_ref[:strip, :] = gram_ref[mine, :]
    out_ref[strip:, :] = panel_ref[mine, :] * jnp.where(place_ref[0] == 0, 1.0, 0.0)


def gram_strips(place, panel, cols):
    width = panel.shape[1]
    return pl.pallas_call(
        gram_kernel,
        in_specs=[SMEM, VMEM],
        out_shape=array(2 * width // cols, width),
        scratch_shapes=[scratch(width, width)],
        compiler_params=LARGE,
        cost_estimate=estimate(2),
        name="gram_strips",
    )(place, panel)


def half_kernel(place_ref, panel_ref, slab_ref, got_ref, inv_ref, half_ref, cols_ref, out_ref, gram_ref):
    strip = out_ref.shape[0]
    mine = pl.ds(pl.multiple_of(place_ref[1] * strip, strip), strip)
    half = mult(panel_ref[...], inv_ref[...], ACROSS)
    half_ref[...] = half
    parts = split(half)
    gram_ref[...] = mult3(parts, parts, TURNED)
    out_ref[...] = gram_ref[mine, :]
    cols_ref[...] = mult(slab_ref[...] + got_ref[...], inv_ref[...], ACROSS)


def half_stage(place, panel, slab, got, inv, cols):
    width = panel.shape[1]
    return pl.pallas_call(
        half_kernel,
        in_specs=[SMEM] + [VMEM] * 4,
        out_shape=(array(*panel.shape), array(*slab.shape), array(width // cols, width)),
        scratch_shapes=[scratch(width, width)],
        compiler_params=LARGE,
        cost_estimate=estimate(3),
        name="half_stage",
    )(place, panel, slab, got, inv)


def near_rows_kernel(place_ref, ham_ref, half_ref, top_ref, *rest_refs):
    piece_refs, near_ref = rest_refs[:-1], rest_refs[-1]
    share = piece_refs[0].shape[0]
    row_place = place_ref[0]
    near_ref[...] = mult3(split(ham_ref[...]), split(half_ref[...]), TURNED)
    for hop, ref in enumerate(piece_refs):
        start = pl.multiple_of((row_place ^ hop) * share, share)
        ref[...] = near_ref[pl.ds(start, share), :]
    top_ref[...] = ham_ref[: top_ref.shape[0], :] * jnp.where(row_place == 0, 1.0, 0.0)


def near_rows(place, hamiltonian, half, rows):
    cols_dev, width = hamiltonian.shape[1], half.shape[1]
    out = pl.pallas_call(
        near_rows_kernel,
        in_specs=[SMEM, VMEM, VMEM],
        out_shape=(array(width, cols_dev),) + (array(cols_dev // rows, width),) * rows,
        scratch_shapes=[scratch(cols_dev, width)],
        compiler_params=LARGE,
        cost_estimate=estimate(3),
        name="near_rows",
    )(place, hamiltonian, half)
    return out[0], out[1:]


def products_kernel(place_ref, ham_ref, half_ref, cols_ref, upper_ref,
                    left_ref, right_ref, keep_ref, send_ref, part_ref, coupling_ref):
    width = upper_ref.shape[0]
    chips = keep_ref.shape[0]
    rows_dev = ham_ref.shape[0]
    piece, strip = rows_dev // 2 // chips, width // 2 // chips
    row_place, col_place = place_ref[0], place_ref[1]
    core, chip = col_place & 1, col_place // 2
    lead = jnp.where(col_place == 0, 1.0, 0.0)
    right_ref[...] = cols_ref[...]
    right_ref[:width, :] = cols_ref[:width, :] + lead * upper_ref[...]
    part = mult3(split(ham_ref[...]), split(right_ref[...]))
    part_ref[...] = part
    lead = jnp.where(row_place == 0, 1.0, 0.0)
    left_ref[...] = half_ref[...]
    left_ref[:width, :] = half_ref[:width, :] + lead * upper_ref[...]
    coupling_ref[...] = mult3(split(left_ref[...]), split(part), TURNED)
    for ref, half in ((send_ref, 1 - core), (keep_ref, core)):
        for hop in range(chips):
            start = (half * chips + (chip ^ hop)) * piece
            ref[hop, :piece, :] = part_ref[pl.ds(pl.multiple_of(start, piece), piece), :]
            start = (half * chips + (chip ^ hop)) * strip
            ref[hop, piece:, :] = coupling_ref[pl.ds(pl.multiple_of(start, strip), strip), :]


def products(place, hamiltonian, half, half_cols, upper, cols):
    rows_dev, cols_dev = hamiltonian.shape
    width = upper.shape[0]
    chips = cols // 2
    share = (rows_dev + width) // cols
    return pl.pallas_call(
        products_kernel,
        in_specs=[SMEM] + [VMEM] * 4,
        out_shape=(
            array(rows_dev, width),
            array(cols_dev, width),
            array(chips, share, width),
            array(chips, share, width),
        ),
        scratch_shapes=[scratch(rows_dev, width), scratch(width, width)],
        compiler_params=LARGE,
        cost_estimate=estimate(4),
        name="products",
    )(place, hamiltonian, half, half_cols, upper)


def pair_kernel(keep_ref, got_ref, *out_refs):
    for hop, ref in enumerate(out_refs):
        ref[...] = keep_ref[hop] + got_ref[hop]


def pair_add(keep, got):
    return pl.pallas_call(
        pair_kernel,
        in_specs=[VMEM] * 2,
        out_shape=(array(*keep.shape[1:]),) * keep.shape[0],
        compiler_params=LARGE,
        cost_estimate=estimate(0.5),
        name="pair_add",
    )(keep, got)


def tree_sum(terms):
    while len(terms) > 1:
        terms = [terms[i] + terms[i + 1] for i in range(0, len(terms), 2)]
    return terms[0]


def sums_kernel(*refs):
    mine_ref, strip_ref = refs[-2:]
    piece = mine_ref.shape[0]
    total = tree_sum([ref[...] for ref in refs[:-2]])
    mine_ref[...] = total[:piece]
    strip_ref[...] = total[piece:]


def sum_pieces(totals, piece):
    height, width = totals[0].shape
    return pl.pallas_call(
        sums_kernel,
        out_shape=(array(piece, width), array(height - piece, width)),
        compiler_params=LARGE,
        cost_estimate=estimate(0.5),
        name="sum_pieces",
    )(*totals)


def spread_kernel(first, last, *refs):
    out_ref = refs[-1]
    total = tree_sum([ref[first:last, :] for ref in refs[:-1]])
    for c in range(out_ref.shape[0]):
        out_ref[c] = total


def sum_copies(cols, terms, first, last):
    return pl.pallas_call(
        functools.partial(spread_kernel, first, last),
        in_specs=[VMEM] * len(terms),
        out_shape=array(cols, last - first, terms[0].shape[1]),
        compiler_params=LARGE,
        cost_estimate=estimate(0.5),
        name="sum_copies",
    )(*terms)


def trade(copies):
    return lax.all_to_all(copies, "col", 0, 0, tiled=True)


def merge_kernel(place_ref, *refs):
    out_ref = refs[-1]
    piece = refs[0].shape[0]
    chip = place_ref[1] // 2
    for hop, ref in enumerate(refs[:-1]):
        out_ref[pl.ds(pl.multiple_of((chip ^ hop) * piece, piece), piece), :] = ref[...]


def merge(place, pieces):
    piece, width = pieces[0].shape
    return pl.pallas_call(
        merge_kernel,
        in_specs=[SMEM] + [VMEM] * len(pieces),
        out_shape=array(len(pieces) * piece, width),
        compiler_params=LARGE,
        cost_estimate=estimate(0.5),
        name="merge_pieces",
    )(place, *pieces)


def base_kernel(
    place_ref, ham_ref, left_ref, mine_ref, other_ref, right_ref, factor_ref,
    upper_ref, top_ref, got_ref, *rest_refs
):
    piece_refs, out_ref, near_ref = rest_refs[:-2], rest_refs[-2], rest_refs[-1]
    deep = mine_ref.shape[0]
    share = piece_refs[0].shape[0]
    row_place, core = place_ref[0], place_ref[1] & 1
    for hop, ref in enumerate(piece_refs):
        start = pl.multiple_of((row_place ^ hop) * share, share)
        near_ref[pl.ds(start, share), :] = ref[...]
    factor = split(factor_ref[...])
    top = split(top_ref[...] + got_ref[...])
    near = near_ref[...] + mult3(top, split(upper_ref[...]), TURNED)
    near = split(mult3(split(near), factor))
    far = split(mult3(split(right_ref[...]), factor, ACROSS))
    for place, prod_ref in ((core, mine_ref), (1 - core, other_ref)):
        block = pl.ds(pl.multiple_of(place * deep, deep), deep)
        change = mult3(split(left_ref[block, :]), near, ACROSS)
        change = change + mult3(split(prod_ref[...]), far, ACROSS)
        out_ref[block, :] = ham_ref[block, :] - change


def base_update(place, hamiltonian, left, mine, other, right, factor, upper, top, got, pieces):
    return pl.pallas_call(
        base_kernel,
        in_specs=[SMEM] + [VMEM] * (9 + len(pieces)),
        out_shape=array(*hamiltonian.shape),
        scratch_shapes=[scratch(*right.shape)],
        compiler_params=LARGE,
        cost_estimate=estimate(4),
        name="base_update",
    )(place, hamiltonian, left, mine, other, right, factor, upper, top, got, *pieces)


def coupling_kernel(base_ref, left_ref, right_ref, factor_ref, parts_ref, out_ref, sum_ref):
    strip = parts_ref.shape[1]
    chips = parts_ref.shape[0] // 2
    for c in range(parts_ref.shape[0]):
        start = ((c % 2) * chips + c // 2) * strip
        sum_ref[start : start + strip, :] = parts_ref[c]
    factor = split(factor_ref[...])
    turn = mult3(split(sum_ref[...]), factor)
    middle = mult3(factor, split(turn), TURNED)
    near = split(mult3(split(right_ref[...]), split(middle)))
    out_ref[...] = base_ref[...] + mult3(split(left_ref[...]), near, ACROSS)


def coupling_update(base, left, right, factor, parts):
    return pl.pallas_call(
        coupling_kernel,
        in_specs=[VMEM] * 5,
        out_shape=array(*base.shape),
        scratch_shapes=[scratch(*factor.shape)],
        compiler_params=LARGE,
        cost_estimate=estimate(3),
        name="coupling_update",
    )(base, left, right, factor, parts)


def hops(values, axis, size, scale=1):
    got = [values[0]]
    for hop in range(1, len(values)):
        pairs = [(i, i ^ (hop * scale)) for i in range(size)]
        got.append(lax.ppermute(values[hop], axis, pairs))
    return got


def pass_on(value, owners, rows, cols):
    hop, having = rows // 2, [0]
    got = jnp.zeros_like(value)
    while hop:
        if having != [0]:
            value = value + got
        pairs = [
            ((owners[c] ^ d) * cols + c, (owners[c] ^ d ^ hop) * cols + c)
            for c in range(cols)
            for d in having
        ]
        got = lax.ppermute(value, ("row", "col"), pairs)
        having = having + [d ^ hop for d in having]
        hop //= 2
    return value, got


def shards(rows, cols, hamiltonian, panel):
    rows_dev, width = panel.shape
    cols_dev = hamiltonian.shape[1]
    row_place = lax.axis_index("row")
    col_place = lax.axis_index("col")
    chips = cols // 2
    strip = width // cols
    piece = rows_dev // cols
    share = cols_dev // rows
    pair = [(i, i ^ 1) for i in range(cols)]
    place = jnp.stack([row_place, col_place]).astype(jnp.int32)

    strips = hops([gram_strips(place, panel, cols)] * rows, "row", rows)

    owners = [c * cols_dev // rows_dev for c in range(cols)]
    owner = col_place * cols_dev // rows_dev
    offset = col_place * cols_dev - owner * rows_dev
    slab = lax.dynamic_slice_in_dim(panel, offset, cols_dev, 0)
    slab = jnp.where(row_place == owner, slab, 0.0)
    strips, slab = lax.optimization_barrier((strips, slab))
    slab, got = pass_on(slab, owners, rows, cols)

    gram = trade(sum_copies(cols, strips, 0, strip))
    first_upper, first_inv = cholesky(gram)
    half, half_cols, gram2_strip = half_stage(place, panel, slab, got, first_inv, cols)
    gram2_strips = hops([gram2_strip] * rows, "row", rows)
    gram2 = trade(sum_copies(cols, gram2_strips, 0, strip))

    half, _ = lax.optimization_barrier((half, gram2_strips[-1]))
    ham_top, near_pieces = near_rows(place, hamiltonian, half, rows)
    gram2, near_pieces = lax.optimization_barrier((gram2, near_pieces))
    near_pieces = hops(near_pieces, "row", rows)
    second_upper = near_cholesky(gram2.reshape(width, width))
    second_upper, near_pieces = lax.optimization_barrier((second_upper, near_pieces))

    left, right, keep, send = products(place, hamiltonian, half, half_cols, second_upper, cols)
    got = lax.ppermute(send, "col", pair)
    near_pieces, _ = lax.optimization_barrier((near_pieces, left))
    near_piece = tree_sum(near_pieces)
    got, near_piece = lax.optimization_barrier((got, near_piece))
    near_pieces = hops([near_piece] * rows, "row", rows)
    totals = pair_add(keep, got)
    ham_top, _ = lax.optimization_barrier((ham_top, totals[0]))
    ham_top, top_got = pass_on(ham_top, [0] * cols, rows, cols)
    totals = hops(totals, "col", cols, 2)
    late = lax.optimization_barrier(tuple(strips) + (totals[0],))
    top = sum_copies(cols, late[:-1], strip, 2 * strip)
    totals, top, near_pieces = lax.optimization_barrier((totals, top, near_pieces))
    top = trade(top)
    mine, coupling_strip = sum_pieces(totals, piece)
    coupling_strips = hops([coupling_strip] * rows, "row", rows)
    mine = merge(place, hops([mine] * chips, "col", cols, 2))
    other = lax.ppermute(mine, "col", pair)
    factor, band_block = compact_factor(gram2, top, first_inv, second_upper, first_upper)
    coupling = trade(sum_copies(cols, coupling_strips, 0, strip))
    base = base_update(place, hamiltonian, left, mine, other, right, factor, second_upper,
                       ham_top, top_got, near_pieces)
    updated = coupling_update(base, left, right, factor, coupling)
    return (updated, band_block)


def solution(mesh):
    in_specs = (P("row", "col"), P("row", None))
    out_specs = (P("row", "col"), P())
    body = functools.partial(shards, mesh.shape["row"], mesh.shape["col"])
    return jax.shard_map(body, mesh=mesh, in_specs=in_specs, out_specs=out_specs, check_vma=False)
```

time: 118 us -> 164 us (1.39)
  waiting for transfers between devices: 21.6 us -> 41.2 us
  starting transfers between devices: 39.6 us -> 56.1 us
  local copies, waits for them, and re-layouts: 8.76 us -> 13.5 us
  other arithmetic: 0.15 us -> 2.33 us
  Pallas kernels: 34.4 us -> 36.2 us
    ppermute x18 -> x21, waiting for transfers between devices: 15.7 us -> 27.6 us  [hops(): got.append(lax.ppermute(values[hop], axis, pairs))]
    ppermute x3 -> x5, starting transfers between devices: 4.82 us -> 14.5 us  [the longest x4 14.5 us: pass_on(): got = lax.ppermute(value, ('row', 'col'), pairs)]
    ppermute x3 -> x5, waiting for transfers between devices: 2.77 us -> 9.48 us  [the longest x4 7.63 us: pass_on(): got = lax.ppermute(value, ('row', 'col'), pairs)]
    all_to_all x2 -> x3, starting transfers between devices: 6.82 us -> 11.9 us  [trade(): return lax.all_to_all(copies, 'col', 0, 0, tiled=True)]
    unnamed x22 -> x62, local copies, waits for them, and re-layouts: 8.74 us -> 13.5 us
    pallas_call x10 -> x12, Pallas kernels: 29.2 us -> 31.5 us  [the longest x1 9.68 us: cholesky(): pl.pallas_call(first_kernel, in_specs=[VMEM], out_shape=(square(size), sq...]
    ppermute x18 -> x21, starting transfers between devices: 27.9 us -> 29.2 us  [hops(): got.append(lax.ppermute(values[hop], axis, pairs))]
    all_to_all x2 -> x3, waiting for transfers between devices: 3.12 us -> 4.1 us  [trade(): return lax.all_to_all(copies, 'col', 0, 0, tiled=True)]
  transfers between devices with their start and end apart: 24 -> 30, of which waited for: 9 -> 14; matrix products, arithmetic and copies ran while one was open for 0% -> 1% of each run, Pallas kernels for 16% -> 15%
where the time goes in v6:
time: 164 us; the launch traced here: 162 us
  starting transfers between devices  56.1 us (34%)
  waiting for transfers between devices  41.2 us (25%)
  Pallas kernels  36.2 us (22%)
  local copies, waits for them, and re-layouts  13.5 us (8%)
  blocking collectives  12.1 us (7%)
  other arithmetic  2.33 us (1%)
    ppermute x21, starting transfers between devices, hops(): got.append(lax.ppermute(values[hop], axis, pairs))  29.2 us
    ppermute x21, waiting for transfers between devices, hops(): got.append(lax.ppermute(values[hop], axis, pairs))  27.6 us
    ppermute x4, starting transfers between devices, pass_on(): got = lax.ppermute(value, ('row', 'col'), pairs)  14.5 us
    unnamed x62, local copies, waits for them, and re-layouts  13.5 us
    all_to_all x1, blocking collectives, trade(): return lax.all_to_all(copies, 'col', 0, 0, tiled=True)  12.1 us
    all_to_all x3, starting transfers between devices, trade(): return lax.all_to_all(copies, 'col', 0, 0, tiled=True)  11.9 us
    pallas_call x1, Pallas kernels, cholesky(): pl.pallas_call(first_kernel, in_specs=[VMEM], out_shape=(square(size), sq...  9.68 us
    ppermute x4, waiting for transfers between devices, pass_on(): got = lax.ppermute(value, ('row', 'col'), pairs)  7.63 us
  transfers between devices with their start and end apart: 30, of which 14 were waited for; matrix products, arithmetic and copies ran while one was open for 1% of the time, Pallas kernels for 15%

profile of v6, /device:TPU:0, one launch (start us, length us, event | category | flops | bytes accessed | tf_op | source)
XLA Modules:
  0.0 162.5 jit_solution(14320576012673381903)
XLA Ops:
  0.7 1.1 copy-done.1
  1.8 1.4 gram_strips.1.refs_0_
  3.3 5.1 %collective-permute-start.2 = (f32[64,256]{1,0:T(8,128)S(1)}, f32[64,256]{1,0:T(8,128)S(1)}, u32[]{:S(2)}, u32[]{:S(2)}) collective-permute-start(f32[64,256]{1,0:T(8,128)S(1)} %gram_strips.1.refs_0_), channel_id=1, source_target_pairs={{0,24},{8,16},{16,8},{24,0},{1,25},{9,17},{17,9},{25,1},{2,26},{10... | collective-permute-start | bytes 196616 | tf_op jit(solution)/shard_map/ppermute | solution.py:529
  9.1 1.0 dynamic-slice_select_fusion
  11.0 3.0 %collective-permute-done.1.refs_2_ = f32[64,256]{1,0:T(8,128)S(1)} collective-permute-done((f32[64,256]{1,0:T(8,128)S(1)}, f32[64,256]{1,0:T(8,128)S(1)}, u32[]{:S(2)}, u32[]{:S(2)}) %collective-permute-start.1) | collective-permute-done | bytes 65568 | tf_op jit(solution)/shard_map/ppermute | solution.py:529
  14.0 3.5 %collective-permute-start.3 = (f32[384,256]{1,0:T(8,128)S(1)}, f32[384,256]{1,0:T(8,128)S(1)}, u32[]{:S(2)}, u32[]{:S(2)}) collective-permute-start(f32[384,256]{1,0:T(8,128)S(1)} %dynamic-slice_select_fusion), channel_id=1, source_target_pairs={{0,16},{1,17},{10,26},{11,27},{20,4},{21,5},{30,14},{31,15}} | collective-permute-start | bytes 1179656 | tf_op jit(solution)/shard_map/ppermute | solution.py:544
  17.5 7.6 %collective-permute-done.3 = f32[384,256]{1,0:T(8,128)S(1)} collective-permute-done((f32[384,256]{1,0:T(8,128)S(1)}, f32[384,256]{1,0:T(8,128)S(1)}, u32[]{:S(2)}, u32[]{:S(2)}) %collective-permute-start.3) | collective-permute-done | bytes 393248 | tf_op jit(solution)/shard_map/ppermute | solution.py:544
  25.2 1.3 collective-permute-start.4
  26.6 12.1 %all_to_all.20.parts_ref = f32[8,32,256]{2,1,0:T(8,128)S(1)} all-to-all(f32[8,32,256]{2,1,0:T(8,128)S(1)} %sum_copies.4), channel_id=1, replica_groups=mesh['row'=4,'col'=8] {'col'}, dimensions={0} | all-to-all | bytes 524288 | tf_op jit(solution)/shard_map/all_to_all | solution.py:442
  38.6 9.7 %cholesky_inverse.1 = (f32[256,256]{1,0:T(8,128)S(1)}, f32[256,256]{1,0:T(8,128)S(1)}) custom-call(f32[8,32,256]{2,1,0:T(8,128)S(1)} %all_to_all.20.parts_ref), custom_call_target="tpu_custom_call" | custom-call | flops 100000000 | bytes 300000 | tf_op jit(solution)/shard_map/cholesky_inverse/pallas_call | solution.py:141
  48.4 3.2 %half_stage.1 = (f32[768,256]{1,0:T(8,128)S(1)}, f32[384,256]{1,0:T(8,128)S(1)}, f32[32,256]{1,0:T(8,128)S(1)}) custom-call(s32[2]{0:T(128)S(1)} %pad_add_fusion.place_ref, f32[768,256]{1,0:T(8,128)S(1)} %copy-done.2, f32[384,256]{1,0:T(8,128)S(1)} %add.20.slab_ref, f32[384,256]{1,0:T(8,128)S(1)} %collective-permute-done.4.got_ref, ...), custom_call_target="tpu_custom_call" | custom-call | flops 30000000 | bytes 90000 | tf_op jit(solution)/shard_map/half_stage/pallas_call | solution.py:300
  53.0 1.3 collective-permute-start.6
  54.3 2.4 %collective-permute-start.5 = (f32[32,256]{1,0:T(8,128)S(1)}, f32[32,256]{1,0:T(8,128)S(1)}, u32[]{:S(2)}, u32[]{:S(2)}) collective-permute-start(f32[32,256]{1,0:T(8,128)S(1)} %get-tuple-element.67.refs_0_), channel_id=1, source_target_pairs={{0,24},{8,16},{16,8},{24,0},{1,25},{9,17},{17,9},{25,1},{2,26},{10... | collective-permute-start | bytes 98312 | tf_op jit(solution)/shard_map/ppermute | solution.py:529
  57.3 2.8 %collective-permute-done.5.refs_3_ = f32[32,256]{1,0:T(8,128)S(1)} collective-permute-done((f32[32,256]{1,0:T(8,128)S(1)}, f32[32,256]{1,0:T(8,128)S(1)}, u32[]{:S(2)}, u32[]{:S(2)}) %collective-permute-start.5) | collective-permute-done | bytes 32800 | tf_op jit(solution)/shard_map/ppermute | solution.py:529
  60.7 3.6 %all-to-all-start.1 = ((f32[8,32,256]{2,1,0:T(8,128)}), f32[8,32,256]{2,1,0:T(8,128)S(1)}, u32[]{:S(2)}, u32[]{:S(2)}) async-start(f32[8,32,256]{2,1,0:T(8,128)} %sum_copies.5), calls=%async_computation.1 | async-start | bytes 524288 | tf_op jit(solution)/shard_map/all_to_all | solution.py:442
  64.4 2.0 %near_rows.1 = (f32[256,384]{1,0:T(8,128)}, f32[96,256]{1,0:T(8,128)S(1)}, f32[96,256]{1,0:T(8,128)S(1)}, f32[96,256]{1,0:T(8,128)S(1)}, f32[96,256]{1,0:T(8,128)S(1)}) custom-call(s32[2]{0:T(128)S(1)} %pad_add_fusion.place_ref, f32[768,384]{1,0:T(8,128)S(1)} %copy-done, f32[768,256]{1,0:T(8,128)S(1)} %get-tuple-element.68.half_ref), custom_call_target="tpu_custom_call" | custom-call | flops 30000000 | bytes 90000 | tf_op jit(solution)/shard_map/near_rows/pallas_call | solution.py:324
  66.9 4.1 %all-to-all-done.1.gram_ref = f32[8,32,256]{2,1,0:T(8,128)S(1)} async-done(((f32[8,32,256]{2,1,0:T(8,128)}), f32[8,32,256]{2,1,0:T(8,128)S(1)}, u32[]{:S(2)}, u32[]{:S(2)}) %all-to-all-start.1) | async-done | bytes 262176 | tf_op jit(solution)/shard_map/all_to_all | solution.py:442
  71.0 3.0 %collective-permute-start.9 = (f32[96,256]{1,0:T(8,128)S(1)}, f32[96,256]{1,0:T(8,128)S(1)}, u32[]{:S(2)}, u32[]{:S(2)}) collective-permute-start(f32[96,256]{1,0:T(8,128)S(1)} %get-tuple-element.77), channel_id=1, source_target_pairs={{0,16},{8,24},{16,0},{24,8},{1,17},{9,25},{17,1},{25,9},{2,18},{10... | collective-permute-start | bytes 294920 | tf_op jit(solution)/shard_map/ppermute | solution.py:529
  74.0 1.4 collective-permute-start.10
  75.4 2.7 %near_cholesky.1.upper_ref = f32[256,256]{1,0:T(8,128)S(1)} custom-call(f32[256,256]{1,0:T(8,128)S(1)} %bitcast.3), custom_call_target="tpu_custom_call" | custom-call | flops 30000000 | bytes 90000 | tf_op jit(solution)/shard_map/near_cholesky/pallas_call | solution.py:197
  78.1 3.1 %collective-permute-done.9 = f32[96,256]{1,0:T(8,128)S(1)} collective-permute-done((f32[96,256]{1,0:T(8,128)S(1)}, f32[96,256]{1,0:T(8,128)S(1)}, u32[]{:S(2)}, u32[]{:S(2)}) %collective-permute-start.9) | collective-permute-done | bytes 98336 | tf_op jit(solution)/shard_map/ppermute | solution.py:529
  81.2 1.0 copy-done.16
  82.2 2.2 %products.1 = (f32[768,256]{1,0:T(8,128)S(1)}, f32[384,256]{1,0:T(8,128)S(1)}, f32[4,128,256]{2,1,0:T(8,128)S(1)}, f32[4,128,256]{2,1,0:T(8,128)S(1)}) custom-call(s32[2]{0:T(128)S(1)} %pad_add_fusion.place_ref, f32[768,384]{1,0:T(8,128)S(1)} %copy-done, f32[768,256]{1,0:T(8,128)S(1)} %get-tuple-element.68.half_ref, f32[384,256]{1,0:T(8,128)S(1)} %copy-done.16, ...), custom_call_target="tpu_custom_call" | custom-call | flops 40000000 | bytes 120000 | tf_op jit(solution)/shard_map/products/pallas_call | solution.py:366
  84.6 1.9 %collective-permute-done.11.got_ref = f32[4,128,256]{2,1,0:T(8,128)S(1)} collective-permute-done((f32[4,128,256]{2,1,0:T(8,128)S(1)}, f32[4,128,256]{2,1,0:T(8,128)S(1)}, u32[]{:S(2)}, u32[]{:S(2)}) %collective-permute-start.11) | collective-permute-done | bytes 524320 | tf_op jit(solution)/shard_map/ppermute | solution.py:586
  86.5 5.1 %collective-permute-start.22 = (f32[256,384]{1,0:T(8,128)}, f32[256,384]{1,0:T(8,128)}, u32[]{:S(2)}, u32[]{:S(2)}) collective-permute-start(f32[256,384]{1,0:T(8,128)} %get-tuple-element.111), channel_id=1, source_target_pairs={{0,16},{1,17},{2,18},{3,19},{4,20},{5,21},{6,22},{7,23}} | collective-permute-start | bytes 1179656 | tf_op jit(solution)/shard_map/ppermute | solution.py:544
  91.6 1.3 collective-permute-start.12
  93.3 9.4 %collective-permute-done.17.rest_refs_3_ = f32[96,256]{1,0:T(8,128)S(1)} collective-permute-done((f32[96,256]{1,0:T(8,128)S(1)}, f32[96,256]{1,0:T(8,128)S(1)}, u32[]{:S(2)}, u32[]{:S(2)}) %collective-permute-start.17) | collective-permute-done | bytes 98336 | tf_op jit(solution)/shard_map/ppermute | solution.py:529
  102.7 1.1 collective-permute-start.14
  104.0 4.0 %collective-permute-start.15 = (f32[96,256]{1,0:T(8,128)S(1)}, f32[96,256]{1,0:T(8,128)S(1)}, u32[]{:S(2)}, u32[]{:S(2)}) collective-permute-start(f32[96,256]{1,0:T(8,128)S(1)} %add_add_fusion.rest_refs_0_), channel_id=1, source_target_pairs={{0,8},{8,0},{16,24},{24,16},{1,9},{9,1},{17,25},{25,17},{2,10},{10... | collective-permute-start | bytes 294920 | tf_op jit(solution)/shard_map/ppermute | solution.py:529
  108.7 2.0 %collective-permute-done.15.rest_refs_1_ = f32[96,256]{1,0:T(8,128)S(1)} collective-permute-done((f32[96,256]{1,0:T(8,128)S(1)}, f32[96,256]{1,0:T(8,128)S(1)}, u32[]{:S(2)}, u32[]{:S(2)}) %collective-permute-start.15) | collective-permute-done | bytes 98336 | tf_op jit(solution)/shard_map/ppermute | solution.py:529
  110.8 1.1 collective-permute-start.20
  112.0 1.7 %collective-permute-start.19 = (f32[96,256]{1,0:T(8,128)S(1)}, f32[96,256]{1,0:T(8,128)S(1)}, u32[]{:S(2)}, u32[]{:S(2)}) collective-permute-start(f32[96,256]{1,0:T(8,128)S(1)} %get-tuple-element.105.refs_0_), channel_id=1, source_target_pairs={{0,4},{1,5},{2,6},{3,7},{4,0},{5,1},{6,2},{7,3},{8,12},{9,13},{10,... | collective-permute-start | bytes 294920 | tf_op jit(solution)/shard_map/ppermute | solution.py:529
  114.4 4.1 %all-to-all-start.2 = ((f32[8,32,256]{2,1,0:T(8,128)}), f32[8,32,256]{2,1,0:T(8,128)}, u32[]{:S(2)}, u32[]{:S(2)}) async-start(f32[8,32,256]{2,1,0:T(8,128)} %sum_copies.6), calls=%async_computation.2 | async-start | bytes 524288 | tf_op jit(solution)/shard_map/all_to_all | solution.py:442
  119.5 1.2 add.24.top_ref
  120.7 4.5 %collective-permute-start.23 = (f32[256,384]{1,0:T(8,128)S(1)}, f32[256,384]{1,0:T(8,128)}, u32[]{:S(2)}, u32[]{:S(2)}) collective-permute-start(f32[256,384]{1,0:T(8,128)S(1)} %add.24.top_ref), channel_id=1, source_target_pairs={{0,8},{16,24},{1,9},{17,25},{2,10},{18,26},{3,11},{19,27},{4,12},{... | collective-permute-start | bytes 1179656 | tf_op jit(solution)/shard_map/ppermute | solution.py:544
  125.2 1.5 collective-permute-start.26
  126.8 1.9 %collective-permute-start.25 = (f32[32,256]{1,0:T(8,128)S(1)}, f32[32,256]{1,0:T(8,128)S(1)}, u32[]{:S(2)}, u32[]{:S(2)}) collective-permute-start(f32[32,256]{1,0:T(8,128)S(1)} %get-tuple-element.116.refs_0_), channel_id=1, source_target_pairs={{0,16},{8,24},{16,0},{24,8},{1,17},{9,25},{17,1},{25,9},{2,18},{10... | collective-permute-start | bytes 98312 | tf_op jit(solution)/shard_map/ppermute | solution.py:529
  128.6 1.0 collective-permute-start.24
  129.6 4.9 %collective-permute-done.26.refs_3_ = f32[32,256]{1,0:T(8,128)S(1)} collective-permute-done((f32[32,256]{1,0:T(8,128)S(1)}, f32[32,256]{1,0:T(8,128)S(1)}, u32[]{:S(2)}, u32[]{:S(2)}) %collective-permute-start.26) | collective-permute-done | bytes 32800 | tf_op jit(solution)/shard_map/ppermute | solution.py:529
  136.0 4.3 %all-to-all-start.3 = ((f32[8,32,256]{2,1,0:T(8,128)}), f32[8,32,256]{2,1,0:T(8,128)}, u32[]{:S(2)}, u32[]{:S(2)}) async-start(f32[8,32,256]{2,1,0:T(8,128)} %copy-done.14), calls=%async_computation.3 | async-start | bytes 524288 | tf_op jit(solution)/shard_map/all_to_all | solution.py:442
  140.3 1.0 copy-done.13
  142.2 5.8 %compact_factor.1 = (f32[256,256]{1,0:T(8,128)S(1)}, f32[256,256]{1,0:T(8,128)}) custom-call(f32[8,32,256]{2,1,0:T(8,128)S(1)} %all-to-all-done.1.gram_ref, f32[8,32,256]{2,1,0:T(8,128)} %all-to-all-done.2.top_ref, f32[256,256]{1,0:T(8,128)S(1)} %copy-done.13, f32[256,256]{1,0:T(8,128)S(1)} %near_cholesky.1.upper_ref, f32[256,256]{1,0:T(8,128)S(1)} %copy-done.18), custom_call_target="tpu_custom_call" | custom-call | flops 40000000 | bytes 120000 | tf_op jit(solution)/shard_map/compact_factor/pallas_call | solution.py:249
  148.1 1.0 copy-done.4
  149.1 1.0 copy-done.6
  152.7 3.1 %base_update.1.base_ref = f32[768,384]{1,0:T(8,128)S(1)} custom-call(s32[2]{0:T(128)S(1)} %pad_add_fusion.place_ref, f32[768,384]{1,0:T(8,128)S(1)} %copy-done, f32[768,256]{1,0:T(8,128)S(1)} %get-tuple-element.80.left_ref, f32[384,256]{1,0:T(8,128)S(1)} %copy-done.4, f32[384,256]{1,0:T(8,128)} %collective-permute-done.21.other_ref, ...), custom_call_target="tpu_custom_call" | custom-call | flops 40000000 | bytes 120000 | tf_op jit(solution)/shard_map/base_update/pallas_call | solution.py:489
  156.6 1.0 copy-done.9
  157.6 0.9 copy-done.11
  158.5 3.9 %coupling_update.1 = f32[768,384]{1,0:T(8,128)} custom-call(f32[768,384]{1,0:T(8,128)S(1)} %base_update.1.base_ref, f32[768,256]{1,0:T(8,128)S(1)} %get-tuple-element.80.left_ref, f32[384,256]{1,0:T(8,128)S(1)} %copy-done.9, f32[256,256]{1,0:T(8,128)S(1)} %copy-done.11, f32[8,32,256]{2,1,0:T(8,128)} %all-to-all-done.3.parts_ref), custom_call_target="tpu_custom_call" | custom-call | flops 30000000 | bytes 90000 | tf_op jit(solution)/shard_map/coupling_update/pallas_call | solution.py:514
  (96 shorter events, 14.1 us)
Async XLA Ops:
  0.7 1.1 copy-start.1
  3.3 7.7 %collective-permute-start.2 = (f32[64,256]{1,0:T(8,128)S(1)}, f32[64,256]{1,0:T(8,128)S(1)}, u32[]{:S(2)}, u32[]{:S(2)}) collective-permute-start(f32[64,256]{1,0:T(8,128)S(1)} %gram_strips.1.refs_0_), channel_id=1, source_target_pairs={{0,24},{8,16},{16,8},{24,0},{1,25},{9,17},{17,9},{25,1},{2,26},{10... | collective-permute-start | bytes 196616 | tf_op jit(solution)/shard_map/ppermute | solution.py:529
  8.4 5.6 %collective-permute-start.1 = (f32[64,256]{1,0:T(8,128)S(1)}, f32[64,256]{1,0:T(8,128)S(1)}, u32[]{:S(2)}, u32[]{:S(2)}) collective-permute-start(f32[64,256]{1,0:T(8,128)S(1)} %gram_strips.1.refs_0_), channel_id=1, source_target_pairs={{0,16},{8,24},{16,0},{24,8},{1,17},{9,25},{17,1},{25,9},{2,18},{10... | collective-permute-start | bytes 196616 | tf_op jit(solution)/shard_map/ppermute | solution.py:529
  8.4 5.6 %collective-permute-start = (f32[64,256]{1,0:T(8,128)S(1)}, f32[64,256]{1,0:T(8,128)S(1)}, u32[]{:S(2)}, u32[]{:S(2)}) collective-permute-start(f32[64,256]{1,0:T(8,128)S(1)} %gram_strips.1.refs_0_), channel_id=1, source_target_pairs={{0,8},{8,0},{16,24},{24,16},{1,9},{9,1},{17,25},{25,17},{2,10},{10... | collective-permute-start | bytes 196616 | tf_op jit(solution)/shard_map/ppermute | solution.py:529
  10.1 38.3 %copy-start.2 = (f32[768,256]{1,0:T(8,128)S(1)}, f32[768,256]{1,0:T(8,128)}, u32[]{:S(2)}) copy-start(f32[768,256]{1,0:T(8,128)} %panel_ref.3) | copy-start | bytes 2359300
  14.0 34.3 %copy-start.19 = (f32[64,256]{1,0:T(8,128)}, f32[64,256]{1,0:T(8,128)S(1)}, u32[]{:S(2)}) copy-start(f32[64,256]{1,0:T(8,128)S(1)} %collective-permute-done.1.refs_2_) | copy-start | bytes 196612
  14.0 34.3 %copy-start.21 = (f32[64,256]{1,0:T(8,128)}, f32[64,256]{1,0:T(8,128)S(1)}, u32[]{:S(2)}) copy-start(f32[64,256]{1,0:T(8,128)S(1)} %collective-permute-done.refs_1_) | copy-start | bytes 196612
  14.0 11.1 %collective-permute-start.3 = (f32[384,256]{1,0:T(8,128)S(1)}, f32[384,256]{1,0:T(8,128)S(1)}, u32[]{:S(2)}, u32[]{:S(2)}) collective-permute-start(f32[384,256]{1,0:T(8,128)S(1)} %dynamic-slice_select_fusion), channel_id=1, source_target_pairs={{0,16},{1,17},{10,26},{11,27},{20,4},{21,5},{30,14},{31,15}} | collective-permute-start | bytes 1179656 | tf_op jit(solution)/shard_map/ppermute | solution.py:544
  25.2 23.1 %collective-permute-start.4 = (f32[384,256]{1,0:T(8,128)S(1)}, f32[384,256]{1,0:T(8,128)S(1)}, u32[]{:S(2)}, u32[]{:S(2)}) collective-permute-start(f32[384,256]{1,0:T(8,128)S(1)} %add.20.slab_ref), channel_id=1, source_target_pairs={{0,8},{16,24},{1,9},{17,25},{10,2},{26,18},{11,3},{27,19},{20,28},... | collective-permute-start | bytes 1179656 | tf_op jit(solution)/shard_map/ppermute | solution.py:544
  48.3 3.2 %copy-start.12 = (f32[256,256]{1,0:T(8,128)}, f32[256,256]{1,0:T(8,128)S(1)}, u32[]{:S(2)}) copy-start(f32[256,256]{1,0:T(8,128)S(1)} %get-tuple-element.65.inv_ref) | copy-start | bytes 786436
  48.3 4.0 %copy-start.17 = (f32[256,256]{1,0:T(8,128)}, f32[256,256]{1,0:T(8,128)S(1)}, u32[]{:S(2)}) copy-start(f32[256,256]{1,0:T(8,128)S(1)} %get-tuple-element.108.first_ref) | copy-start | bytes 786436
  48.4 16.0 %copy-start = (f32[768,384]{1,0:T(8,128)S(1)}, f32[768,384]{1,0:T(8,128)}, u32[]{:S(2)}) copy-start(f32[768,384]{1,0:T(8,128)} %ham_ref.5) | copy-start | bytes 3538948
  52.3 4.9 %collective-permute-start.7 = (f32[32,256]{1,0:T(8,128)S(1)}, f32[32,256]{1,0:T(8,128)S(1)}, u32[]{:S(2)}, u32[]{:S(2)}) collective-permute-start(f32[32,256]{1,0:T(8,128)S(1)} %get-tuple-element.67.refs_0_), channel_id=1, source_target_pairs={{0,16},{8,24},{16,0},{24,8},{1,17},{9,25},{17,1},{25,9},{2,18},{10... | collective-permute-start | bytes 98312 | tf_op jit(solution)/shard_map/ppermute | solution.py:529
  53.0 4.3 %collective-permute-start.6 = (f32[32,256]{1,0:T(8,128)S(1)}, f32[32,256]{1,0:T(8,128)S(1)}, u32[]{:S(2)}, u32[]{:S(2)}) collective-permute-start(f32[32,256]{1,0:T(8,128)S(1)} %get-tuple-element.67.refs_0_), channel_id=1, source_target_pairs={{0,8},{8,0},{16,24},{24,16},{1,9},{9,1},{17,25},{25,17},{2,10},{10... | collective-permute-start | bytes 98312 | tf_op jit(solution)/shard_map/ppermute | solution.py:529
  54.3 5.7 %collective-permute-start.5 = (f32[32,256]{1,0:T(8,128)S(1)}, f32[32,256]{1,0:T(8,128)S(1)}, u32[]{:S(2)}, u32[]{:S(2)}) collective-permute-start(f32[32,256]{1,0:T(8,128)S(1)} %get-tuple-element.67.refs_0_), channel_id=1, source_target_pairs={{0,24},{8,16},{16,8},{24,0},{1,25},{9,17},{17,9},{25,1},{2,26},{10... | collective-permute-start | bytes 98312 | tf_op jit(solution)/shard_map/ppermute | solution.py:529
  60.7 10.3 %all-to-all-start.1 = ((f32[8,32,256]{2,1,0:T(8,128)}), f32[8,32,256]{2,1,0:T(8,128)S(1)}, u32[]{:S(2)}, u32[]{:S(2)}) async-start(f32[8,32,256]{2,1,0:T(8,128)} %sum_copies.5), calls=%async_computation.1 | async-start | bytes 524288 | tf_op jit(solution)/shard_map/all_to_all | solution.py:442
  71.0 7.1 %collective-permute-start.8 = (f32[96,256]{1,0:T(8,128)S(1)}, f32[96,256]{1,0:T(8,128)S(1)}, u32[]{:S(2)}, u32[]{:S(2)}) collective-permute-start(f32[96,256]{1,0:T(8,128)S(1)} %get-tuple-element.76), channel_id=1, source_target_pairs={{0,8},{8,0},{16,24},{24,16},{1,9},{9,1},{17,25},{25,17},{2,10},{10... | collective-permute-start | bytes 294920 | tf_op jit(solution)/shard_map/ppermute | solution.py:529
  71.0 10.2 %collective-permute-start.9 = (f32[96,256]{1,0:T(8,128)S(1)}, f32[96,256]{1,0:T(8,128)S(1)}, u32[]{:S(2)}, u32[]{:S(2)}) collective-permute-start(f32[96,256]{1,0:T(8,128)S(1)} %get-tuple-element.77), channel_id=1, source_target_pairs={{0,16},{8,24},{16,0},{24,8},{1,17},{9,25},{17,1},{25,9},{2,18},{10... | collective-permute-start | bytes 294920 | tf_op jit(solution)/shard_map/ppermute | solution.py:529
  74.0 7.2 %collective-permute-start.10 = (f32[96,256]{1,0:T(8,128)S(1)}, f32[96,256]{1,0:T(8,128)S(1)}, u32[]{:S(2)}, u32[]{:S(2)}) collective-permute-start(f32[96,256]{1,0:T(8,128)S(1)} %get-tuple-element.78), channel_id=1, source_target_pairs={{0,24},{8,16},{16,8},{24,0},{1,25},{9,17},{17,9},{25,1},{2,26},{10... | collective-permute-start | bytes 294920 | tf_op jit(solution)/shard_map/ppermute | solution.py:529
  82.2 2.3 %copy-start.24 = (f32[96,256]{1,0:T(8,128)S(1)}, f32[96,256]{1,0:T(8,128)}, u32[]{:S(2)}) copy-start(f32[96,256]{1,0:T(8,128)} %copy-done.23) | copy-start | bytes 294916
  84.4 26.4 %copy-start.7 = (f32[384,256]{1,0:T(8,128)}, f32[384,256]{1,0:T(8,128)S(1)}, u32[]{:S(2)}) copy-start(f32[384,256]{1,0:T(8,128)S(1)} %get-tuple-element.106.right_ref) | copy-start | bytes 1179652
  84.4 23.6 %copy-start.20 = (f32[64,256]{1,0:T(8,128)S(1)}, f32[64,256]{1,0:T(8,128)}, u32[]{:S(2)}) copy-start(f32[64,256]{1,0:T(8,128)} %copy-done.19) | copy-start | bytes 196612
  84.4 23.6 %copy-start.22 = (f32[64,256]{1,0:T(8,128)S(1)}, f32[64,256]{1,0:T(8,128)}, u32[]{:S(2)}) copy-start(f32[64,256]{1,0:T(8,128)} %copy-done.21) | copy-start | bytes 196612
  84.5 2.0 %collective-permute-start.11 = (f32[4,128,256]{2,1,0:T(8,128)S(1)}, f32[4,128,256]{2,1,0:T(8,128)S(1)}, u32[]{:S(2)}, u32[]{:S(2)}) collective-permute-start(f32[4,128,256]{2,1,0:T(8,128)S(1)} %get-tuple-element.82), channel_id=1, source_target_pairs={{0,1},{1,0},{2,3},{3,2},{4,5},{5,4},{6,7},{7,6},{8,9},{9,8},{10,11... | collective-permute-start | bytes 1572872 | tf_op jit(solution)/shard_map/ppermute | solution.py:586
  86.5 33.0 %collective-permute-start.22 = (f32[256,384]{1,0:T(8,128)}, f32[256,384]{1,0:T(8,128)}, u32[]{:S(2)}, u32[]{:S(2)}) collective-permute-start(f32[256,384]{1,0:T(8,128)} %get-tuple-element.111), channel_id=1, source_target_pairs={{0,16},{1,17},{2,18},{3,19},{4,20},{5,21},{6,22},{7,23}} | collective-permute-start | bytes 1179656 | tf_op jit(solution)/shard_map/ppermute | solution.py:544
  91.6 11.1 %collective-permute-start.17 = (f32[96,256]{1,0:T(8,128)S(1)}, f32[96,256]{1,0:T(8,128)S(1)}, u32[]{:S(2)}, u32[]{:S(2)}) collective-permute-start(f32[96,256]{1,0:T(8,128)S(1)} %add_add_fusion.rest_refs_0_), channel_id=1, source_target_pairs={{0,24},{8,16},{16,8},{24,0},{1,25},{9,17},{17,9},{25,1},{2,26},{10... | collective-permute-start | bytes 294920 | tf_op jit(solution)/shard_map/ppermute | solution.py:529
  91.6 12.4 %collective-permute-start.16 = (f32[96,256]{1,0:T(8,128)S(1)}, f32[96,256]{1,0:T(8,128)S(1)}, u32[]{:S(2)}, u32[]{:S(2)}) collective-permute-start(f32[96,256]{1,0:T(8,128)S(1)} %add_add_fusion.rest_refs_0_), channel_id=1, source_target_pairs={{0,16},{8,24},{16,0},{24,8},{1,17},{9,25},{17,1},{25,9},{2,18},{10... | collective-permute-start | bytes 294920 | tf_op jit(solution)/shard_map/ppermute | solution.py:529
  91.6 19.1 %collective-permute-start.12 = (f32[128,256]{1,0:T(8,128)S(1)}, f32[128,256]{1,0:T(8,128)S(1)}, u32[]{:S(2)}, u32[]{:S(2)}) collective-permute-start(f32[128,256]{1,0:T(8,128)S(1)} %get-tuple-element.93), channel_id=1, source_target_pairs={{0,2},{1,3},{2,0},{3,1},{4,6},{5,7},{6,4},{7,5},{8,10},{9,11},{10,... | collective-permute-start | bytes 393224 | tf_op jit(solution)/shard_map/ppermute | solution.py:529
  92.9 17.8 %collective-permute-start.13 = (f32[128,256]{1,0:T(8,128)S(1)}, f32[128,256]{1,0:T(8,128)S(1)}, u32[]{:S(2)}, u32[]{:S(2)}) collective-permute-start(f32[128,256]{1,0:T(8,128)S(1)} %get-tuple-element.94), channel_id=1, source_target_pairs={{0,4},{1,5},{2,6},{3,7},{4,0},{5,1},{6,2},{7,3},{8,12},{9,13},{10,... | collective-permute-start | bytes 393224 | tf_op jit(solution)/shard_map/ppermute | solution.py:529
  102.7 15.8 %copy-start.25 = (f32[96,256]{1,0:T(8,128)}, f32[96,256]{1,0:T(8,128)S(1)}, u32[]{:S(2)}) copy-start(f32[96,256]{1,0:T(8,128)S(1)} %collective-permute-done.17.rest_refs_3_) | copy-start | bytes 294916
  102.7 8.1 %collective-permute-start.14 = (f32[128,256]{1,0:T(8,128)S(1)}, f32[128,256]{1,0:T(8,128)S(1)}, u32[]{:S(2)}, u32[]{:S(2)}) collective-permute-start(f32[128,256]{1,0:T(8,128)S(1)} %get-tuple-element.95), channel_id=1, source_target_pairs={{0,6},{1,7},{2,4},{3,5},{4,2},{5,3},{6,0},{7,1},{8,14},{9,15},{10,... | collective-permute-start | bytes 393224 | tf_op jit(solution)/shard_map/ppermute | solution.py:529
  104.0 6.8 %copy-start.27 = (f32[96,256]{1,0:T(8,128)}, f32[96,256]{1,0:T(8,128)S(1)}, u32[]{:S(2)}) copy-start(f32[96,256]{1,0:T(8,128)S(1)} %collective-permute-done.16.rest_refs_2_) | copy-start | bytes 294916
  104.0 6.8 %collective-permute-start.15 = (f32[96,256]{1,0:T(8,128)S(1)}, f32[96,256]{1,0:T(8,128)S(1)}, u32[]{:S(2)}, u32[]{:S(2)}) collective-permute-start(f32[96,256]{1,0:T(8,128)S(1)} %add_add_fusion.rest_refs_0_), channel_id=1, source_target_pairs={{0,8},{8,0},{16,24},{24,16},{1,9},{9,1},{17,25},{25,17},{2,10},{10... | collective-permute-start | bytes 294920 | tf_op jit(solution)/shard_map/ppermute | solution.py:529
  110.8 1.2 copy-start.29
  110.8 7.6 %collective-permute-start.20 = (f32[96,256]{1,0:T(8,128)S(1)}, f32[96,256]{1,0:T(8,128)S(1)}, u32[]{:S(2)}, u32[]{:S(2)}) collective-permute-start(f32[96,256]{1,0:T(8,128)S(1)} %get-tuple-element.105.refs_0_), channel_id=1, source_target_pairs={{0,6},{1,7},{2,4},{3,5},{4,2},{5,3},{6,0},{7,1},{8,14},{9,15},{10,... | collective-permute-start | bytes 294920 | tf_op jit(solution)/shard_map/ppermute | solution.py:529
  112.0 6.5 %collective-permute-start.19 = (f32[96,256]{1,0:T(8,128)S(1)}, f32[96,256]{1,0:T(8,128)S(1)}, u32[]{:S(2)}, u32[]{:S(2)}) collective-permute-start(f32[96,256]{1,0:T(8,128)S(1)} %get-tuple-element.105.refs_0_), channel_id=1, source_target_pairs={{0,4},{1,5},{2,6},{3,7},{4,0},{5,1},{6,2},{7,3},{8,12},{9,13},{10,... | collective-permute-start | bytes 294920 | tf_op jit(solution)/shard_map/ppermute | solution.py:529
  113.7 4.8 %collective-permute-start.18 = (f32[96,256]{1,0:T(8,128)S(1)}, f32[96,256]{1,0:T(8,128)S(1)}, u32[]{:S(2)}, u32[]{:S(2)}) collective-permute-start(f32[96,256]{1,0:T(8,128)S(1)} %get-tuple-element.105.refs_0_), channel_id=1, source_target_pairs={{0,2},{1,3},{2,0},{3,1},{4,6},{5,7},{6,4},{7,5},{8,10},{9,11},{10,... | collective-permute-start | bytes 294920 | tf_op jit(solution)/shard_map/ppermute | solution.py:529
  114.4 21.6 %all-to-all-start.2 = ((f32[8,32,256]{2,1,0:T(8,128)}), f32[8,32,256]{2,1,0:T(8,128)}, u32[]{:S(2)}, u32[]{:S(2)}) async-start(f32[8,32,256]{2,1,0:T(8,128)} %sum_copies.6), calls=%async_computation.2 | async-start | bytes 524288 | tf_op jit(solution)/shard_map/all_to_all | solution.py:442
  119.1 28.9 %copy-start.3 = (f32[384,256]{1,0:T(8,128)}, f32[384,256]{1,0:T(8,128)S(1)}, u32[]{:S(2)}) copy-start(f32[384,256]{1,0:T(8,128)S(1)} %merge_pieces.1.mine_ref) | copy-start | bytes 1179652
  119.1 28.9 %collective-permute-start.21 = (f32[384,256]{1,0:T(8,128)S(1)}, f32[384,256]{1,0:T(8,128)}, u32[]{:S(2)}, u32[]{:S(2)}) collective-permute-start(f32[384,256]{1,0:T(8,128)S(1)} %merge_pieces.1.mine_ref), channel_id=1, source_target_pairs={{0,1},{1,0},{2,3},{3,2},{4,5},{5,4},{6,7},{7,6},{8,9},{9,8},{10,11... | collective-permute-start | bytes 1179656 | tf_op jit(solution)/shard_map/ppermute | solution.py:602
  120.7 27.3 %copy-start.5 = (f32[256,384]{1,0:T(8,128)}, f32[256,384]{1,0:T(8,128)S(1)}, u32[]{:S(2)}) copy-start(f32[256,384]{1,0:T(8,128)S(1)} %add.24.top_ref) | copy-start | bytes 1179652
  120.7 27.3 %collective-permute-start.23 = (f32[256,384]{1,0:T(8,128)S(1)}, f32[256,384]{1,0:T(8,128)}, u32[]{:S(2)}, u32[]{:S(2)}) collective-permute-start(f32[256,384]{1,0:T(8,128)S(1)} %add.24.top_ref), channel_id=1, source_target_pairs={{0,8},{16,24},{1,9},{17,25},{2,10},{18,26},{3,11},{19,27},{4,12},{... | collective-permute-start | bytes 1179656 | tf_op jit(solution)/shard_map/ppermute | solution.py:544
  125.2 9.3 %collective-permute-start.26 = (f32[32,256]{1,0:T(8,128)S(1)}, f32[32,256]{1,0:T(8,128)S(1)}, u32[]{:S(2)}, u32[]{:S(2)}) collective-permute-start(f32[32,256]{1,0:T(8,128)S(1)} %get-tuple-element.116.refs_0_), channel_id=1, source_target_pairs={{0,24},{8,16},{16,8},{24,0},{1,25},{9,17},{17,9},{25,1},{2,26},{10... | collective-permute-start | bytes 98312 | tf_op jit(solution)/shard_map/ppermute | solution.py:529
  126.8 8.1 %collective-permute-start.25 = (f32[32,256]{1,0:T(8,128)S(1)}, f32[32,256]{1,0:T(8,128)S(1)}, u32[]{:S(2)}, u32[]{:S(2)}) collective-permute-start(f32[32,256]{1,0:T(8,128)S(1)} %get-tuple-element.116.refs_0_), channel_id=1, source_target_pairs={{0,16},{8,24},{16,0},{24,8},{1,17},{9,25},{17,1},{25,9},{2,18},{10... | collective-permute-start | bytes 98312 | tf_op jit(solution)/shard_map/ppermute | solution.py:529
  128.6 6.6 %collective-permute-start.24 = (f32[32,256]{1,0:T(8,128)S(1)}, f32[32,256]{1,0:T(8,128)S(1)}, u32[]{:S(2)}, u32[]{:S(2)}) collective-permute-start(f32[32,256]{1,0:T(8,128)S(1)} %get-tuple-element.116.refs_0_), channel_id=1, source_target_pairs={{0,8},{8,0},{16,24},{24,16},{1,9},{9,1},{17,25},{25,17},{2,10},{10... | collective-permute-start | bytes 98312 | tf_op jit(solution)/shard_map/ppermute | solution.py:529
  136.0 20.6 %all-to-all-start.3 = ((f32[8,32,256]{2,1,0:T(8,128)}), f32[8,32,256]{2,1,0:T(8,128)}, u32[]{:S(2)}, u32[]{:S(2)}) async-start(f32[8,32,256]{2,1,0:T(8,128)} %copy-done.14), calls=%async_computation.3 | async-start | bytes 524288 | tf_op jit(solution)/shard_map/all_to_all | solution.py:442
  140.2 7.8 %copy-start.8 = (f32[384,256]{1,0:T(8,128)S(1)}, f32[384,256]{1,0:T(8,128)}, u32[]{:S(2)}) copy-start(f32[384,256]{1,0:T(8,128)} %copy-done.7) | copy-start | bytes 1179652
  140.2 1.0 copy-start.13
  (13 other events, 11.3 us)

commit v7 on v6

--- a/solution.py
+++ b/solution.py
@@ -122,7 +122,7 @@
 
 
 def estimate(micros):
-    return pl.CostEstimate(flops=int(micros * 1e7), bytes_accessed=int(micros * 3e4), transcendentals=0)
+    return pl.CostEstimate(flops=int(micros * 1e9), bytes_accessed=int(micros * 3e6), transcendentals=0)
 
 
 def square(size):
@@ -170,7 +170,7 @@
 
     def more(state):
         count, _, _, _, worst = state
-        return jnp.logical_not(worst < 1e-5) & (count < 8)
+        return jnp.logical_not(worst < 1e-8) & (count < 10)
 
     def step(state):
         count, inv, _, low, _ = state
@@ -187,7 +187,7 @@
     upper = upper + mult3(split(low), split(upper), TURNED)
     upper_ref[...] = jnp.where(row <= col, upper, 0.0)
 
-    @pl.when(jnp.logical_not(worst < 1e-5))
+    @pl.when(jnp.logical_not(worst < 1e-8))
     def _():
         chol_kernel(gram_ref, upper_ref, inv_ref, work_ref)
 
@@ -214,13 +214,6 @@
     mat = gram_ref[...].reshape(size, size) + mult3(split(half_top), split(upper_ref[...]), TURNED)
     halves = split(mat)
 
-    def rough(left, right):
-        return jnp.dot(
-            left.astype(jnp.bfloat16),
-            right.astype(jnp.bfloat16),
-            preferred_element_type=jnp.float32,
-        )
-
     def residual(guess):
         return ident - mult3(halves, split(guess))
 
@@ -237,9 +230,10 @@
     guess = 0.5 * ident
     rest = ident - 0.5 * mat
     for _ in range(4):
-        guess = guess + rough(guess, rest)
-        rest = rough(rest, rest)
-    guess = guess + rough(guess, rest)
+        parts = split(rest)
+        guess = guess + mult3(split(guess), parts)
+        rest = mult3(parts, parts)
+    guess = guess + mult3(split(guess), split(rest))
     rest = residual(guess)
     state = (jnp.int32(0), guess, rest, jnp.max(jnp.abs(rest)))
     out_ref[...] = lax.while_loop(more, step, state)[1]
@@ -308,29 +302,54 @@
     )(place, panel, slab, got, inv)
 
 
-def near_rows_kernel(place_ref, ham_ref, half_ref, top_ref, *rest_refs):
-    piece_refs, near_ref = rest_refs[:-1], rest_refs[-1]
+def store_pieces(place_ref, whole_ref, piece_refs):
     share = piece_refs[0].shape[0]
-    row_place = place_ref[0]
+    for hop, ref in enumerate(piece_refs):
+        start = pl.multiple_of((place_ref[0] ^ hop) * share, share)
+        ref[...] = whole_ref[pl.ds(start, share), :]
+
+
+def top_rows_kernel(place_ref, ham_ref, *rest_refs):
+    top_ref = rest_refs[-1]
+    lead = jnp.where(place_ref[0] == 0, 1.0, 0.0)
+    top_ref[...] = ham_ref[: top_ref.shape[1], :].T * lead
+    store_pieces(place_ref, top_ref, rest_refs[:-1])
+
+
+def near_rows_kernel(place_ref, ham_ref, half_ref, *rest_refs):
+    near_ref = rest_refs[-1]
     near_ref[...] = mult3(split(ham_ref[...]), split(half_ref[...]), TURNED)
-    for hop, ref in enumerate(piece_refs):
-        start = pl.multiple_of((row_place ^ hop) * share, share)
-        ref[...] = near_ref[pl.ds(start, share), :]
-    top_ref[...] = ham_ref[: top_ref.shape[0], :] * jnp.where(row_place == 0, 1.0, 0.0)
-
-
-def near_rows(place, hamiltonian, half, rows):
-    cols_dev, width = hamiltonian.shape[1], half.shape[1]
-    out = pl.pallas_call(
-        near_rows_kernel,
-        in_specs=[SMEM, VMEM, VMEM],
-        out_shape=(array(width, cols_dev),) + (array(cols_dev // rows, width),) * rows,
+    store_pieces(place_ref, near_ref, rest_refs[:-1])
+
+
+def row_pieces(kernel, name, cols_dev, width, rows, place, *operands):
+    return pl.pallas_call(
+        kernel,
+        in_specs=[SMEM] + [VMEM] * len(operands),
+        out_shape=(array(cols_dev // rows, width),) * rows,
         scratch_shapes=[scratch(cols_dev, width)],
         compiler_params=LARGE,
-        cost_estimate=estimate(3),
-        name="near_rows",
-    )(place, hamiltonian, half)
-    return out[0], out[1:]
+        cost_estimate=estimate(1 if len(operands) == 1 else 2),
+        name=name,
+    )(place, *operands)
+
+
+def near_sum_kernel(upper_ref, *refs):
+    terms, out_ref = refs[:-1], refs[-1]
+    count = len(terms) // 2
+    total = tree_sum([ref[...] for ref in terms[:count]])
+    top = tree_sum([ref[...] for ref in terms[count:]])
+    out_ref[...] = total + mult3(split(top), split(upper_ref[...]))
+
+
+def near_sum(upper, terms, tops):
+    return pl.pallas_call(
+        near_sum_kernel,
+        out_shape=array(*terms[0].shape),
+        compiler_params=LARGE,
+        cost_estimate=estimate(1),
+        name="near_sum",
+    )(upper, *terms, *tops)
 
 
 def products_kernel(place_ref, ham_ref, half_ref, cols_ref, upper_ref,
@@ -462,64 +481,45 @@
     )(place, *pieces)
 
 
-def base_kernel(
+def update_kernel(
     place_ref, ham_ref, left_ref, mine_ref, other_ref, right_ref, factor_ref,
-    upper_ref, top_ref, got_ref, *rest_refs
+    parts_ref, *rest_refs
 ):
-    piece_refs, out_ref, near_ref = rest_refs[:-2], rest_refs[-2], rest_refs[-1]
+    piece_refs, (out_ref, near_ref, sum_ref) = rest_refs[:-3], rest_refs[-3:]
     deep = mine_ref.shape[0]
     share = piece_refs[0].shape[0]
     row_place, core = place_ref[0], place_ref[1] & 1
     for hop, ref in enumerate(piece_refs):
         start = pl.multiple_of((row_place ^ hop) * share, share)
         near_ref[pl.ds(start, share), :] = ref[...]
-    factor = split(factor_ref[...])
-    top = split(top_ref[...] + got_ref[...])
-    near = near_ref[...] + mult3(top, split(upper_ref[...]), TURNED)
-    near = split(mult3(split(near), factor))
-    far = split(mult3(split(right_ref[...]), factor, ACROSS))
-    for place, prod_ref in ((core, mine_ref), (1 - core, other_ref)):
-        block = pl.ds(pl.multiple_of(place * deep, deep), deep)
-        change = mult3(split(left_ref[block, :]), near, ACROSS)
-        change = change + mult3(split(prod_ref[...]), far, ACROSS)
-        out_ref[block, :] = ham_ref[block, :] - change
-
-
-def base_update(place, hamiltonian, left, mine, other, right, factor, upper, top, got, pieces):
-    return pl.pallas_call(
-        base_kernel,
-        in_specs=[SMEM] + [VMEM] * (9 + len(pieces)),
-        out_shape=array(*hamiltonian.shape),
-        scratch_shapes=[scratch(*right.shape)],
-        compiler_params=LARGE,
-        cost_estimate=estimate(4),
-        name="base_update",
-    )(place, hamiltonian, left, mine, other, right, factor, upper, top, got, *pieces)
-
-
-def coupling_kernel(base_ref, left_ref, right_ref, factor_ref, parts_ref, out_ref, sum_ref):
     strip = parts_ref.shape[1]
     chips = parts_ref.shape[0] // 2
     for c in range(parts_ref.shape[0]):
         start = ((c % 2) * chips + c // 2) * strip
         sum_ref[start : start + strip, :] = parts_ref[c]
     factor = split(factor_ref[...])
+    right = split(right_ref[...])
     turn = mult3(split(sum_ref[...]), factor)
     middle = mult3(factor, split(turn), TURNED)
-    near = split(mult3(split(right_ref[...]), split(middle)))
-    out_ref[...] = base_ref[...] + mult3(split(left_ref[...]), near, ACROSS)
-
-
-def coupling_update(base, left, right, factor, parts):
-    return pl.pallas_call(
-        coupling_kernel,
-        in_specs=[VMEM] * 5,
-        out_shape=array(*base.shape),
-        scratch_shapes=[scratch(*factor.shape)],
-        compiler_params=LARGE,
-        cost_estimate=estimate(3),
-        name="coupling_update",
-    )(base, left, right, factor, parts)
+    near = split(mult3(split(near_ref[...]), factor) - mult3(right, split(middle)))
+    far = split(mult3(right, factor, ACROSS))
+    for place, prod_ref in ((core, mine_ref), (1 - core, other_ref)):
+        block = pl.ds(pl.multiple_of(place * deep, deep), deep)
+        change = mult3(split(left_ref[block, :]), near, ACROSS)
+        change = change + mult3(split(prod_ref[...]), far, ACROSS)
+        out_ref[block, :] = ham_ref[block, :] - change
+
+
+def update(place, hamiltonian, left, mine, other, right, factor, parts, pieces):
+    return pl.pallas_call(
+        update_kernel,
+        in_specs=[SMEM] + [VMEM] * (7 + len(pieces)),
+        out_shape=array(*hamiltonian.shape),
+        scratch_shapes=[scratch(*right.shape), scratch(*factor.shape)],
+        compiler_params=LARGE,
+        cost_estimate=estimate(4),
+        name="two_sided_update",
+    )(place, hamiltonian, left, mine, other, right, factor, parts, *pieces)
 
 
 def hops(values, axis, size, scale=1):
@@ -569,15 +569,24 @@
     strips, slab = lax.optimization_barrier((strips, slab))
     slab, got = pass_on(slab, owners, rows, cols)
 
+    block, _ = lax.optimization_barrier((hamiltonian, slab))
+    near_tops = row_pieces(
+        top_rows_kernel, "top_rows", cols_dev, width, rows, place, block
+    )
+    near_tops = hops(near_tops, "row", rows)
+
     gram = trade(sum_copies(cols, strips, 0, strip))
     first_upper, first_inv = cholesky(gram)
+    first_inv, near_tops = lax.optimization_barrier((first_inv, near_tops))
     half, half_cols, gram2_strip = half_stage(place, panel, slab, got, first_inv, cols)
     gram2_strips = hops([gram2_strip] * rows, "row", rows)
     gram2 = trade(sum_copies(cols, gram2_strips, 0, strip))
 
     half, _ = lax.optimization_barrier((half, gram2_strips[-1]))
-    ham_top, near_pieces = near_rows(place, hamiltonian, half, rows)
-    gram2, near_pieces = lax.optimization_barrier((gram2, near_pieces))
+    near_pieces = row_pieces(
+        near_rows_kernel, "near_rows", cols_dev, width, rows, place, hamiltonian, half
+    )
+    gram2, _ = lax.optimization_barrier((gram2, near_pieces[0]))
     near_pieces = hops(near_pieces, "row", rows)
     second_upper = near_cholesky(gram2.reshape(width, width))
     second_upper, near_pieces = lax.optimization_barrier((second_upper, near_pieces))
@@ -585,12 +594,10 @@
     left, right, keep, send = products(place, hamiltonian, half, half_cols, second_upper, cols)
     got = lax.ppermute(send, "col", pair)
     near_pieces, _ = lax.optimization_barrier((near_pieces, left))
-    near_piece = tree_sum(near_pieces)
+    near_piece = near_sum(second_upper, near_pieces, near_tops)
     got, near_piece = lax.optimization_barrier((got, near_piece))
     near_pieces = hops([near_piece] * rows, "row", rows)
     totals = pair_add(keep, got)
-    ham_top, _ = lax.optimization_barrier((ham_top, totals[0]))
-    ham_top, top_got = pass_on(ham_top, [0] * cols, rows, cols)
     totals = hops(totals, "col", cols, 2)
     late = lax.optimization_barrier(tuple(strips) + (totals[0],))
     top = sum_copies(cols, late[:-1], strip, 2 * strip)
@@ -598,13 +605,16 @@
     top = trade(top)
     mine, coupling_strip = sum_pieces(totals, piece)
     coupling_strips = hops([coupling_strip] * rows, "row", rows)
-    mine = merge(place, hops([mine] * chips, "col", cols, 2))
+    mine = hops([mine] * chips, "col", cols, 2)
+    coupling = sum_copies(cols, coupling_strips, 0, strip)
+    mine, _ = lax.optimization_barrier((mine, coupling))
+    coupling = trade(coupling)
+    mine = merge(place, mine)
+    top, mine = lax.optimization_barrier((top, mine))
     other = lax.ppermute(mine, "col", pair)
     factor, band_block = compact_factor(gram2, top, first_inv, second_upper, first_upper)
-    coupling = trade(sum_copies(cols, coupling_strips, 0, strip))
-    base = base_update(place, hamiltonian, left, mine, other, right, factor, second_upper,
-                       ham_top, top_got, near_pieces)
-    updated = coupling_update(base, left, right, factor, coupling)
+    updated = update(place, hamiltonian, left, mine, other, right, factor, coupling,
+                     near_pieces)
     return (updated, band_block)
 
 

time: 164 us -> 129 us (0.79)
  waiting for transfers between devices: 41.2 us -> 24 us
  blocking collectives: 12.1 us -> 0 us
  local copies, waits for them, and re-layouts: 13.5 us -> 11.2 us
  other arithmetic: 2.33 us -> 0.15 us
  Pallas kernels: 36.2 us -> 34.4 us
    all_to_all x1 -> x0, blocking collectives: 12.1 us -> none  [trade(): return lax.all_to_all(copies, 'col', 0, 0, tiled=True)]
    ppermute x4 -> x2, starting transfers between devices: 14.5 us -> 4.81 us  [pass_on(): got = lax.ppermute(value, ('row', 'col'), pairs)]
    ppermute x21 -> x24, waiting for transfers between devices: 27.6 us -> 19.2 us  [hops(): got.append(lax.ppermute(values[hop], axis, pairs))]
    ppermute x21 -> x24, starting transfers between devices: 29.2 us -> 36.5 us  [hops(): got.append(lax.ppermute(values[hop], axis, pairs))]
    ppermute x4 -> x2, waiting for transfers between devices: 7.63 us -> 2.6 us  [pass_on(): got = lax.ppermute(value, ('row', 'col'), pairs)]
    all_to_all x3 -> x4, starting transfers between devices: 11.9 us -> 16 us  [trade(): return lax.all_to_all(copies, 'col', 0, 0, tiled=True)]
    all_to_all x3 -> x4, waiting for transfers between devices: 4.1 us -> 1.24 us  [trade(): return lax.all_to_all(copies, 'col', 0, 0, tiled=True)]
    unnamed x62 -> x60, local copies, waits for them, and re-layouts: 13.5 us -> 11.2 us
  transfers between devices with their start and end apart: 30 -> 32, of which waited for: 14 -> 12; matrix products, arithmetic and copies ran while one was open for 1% -> 0% of each run, Pallas kernels for 15% -> 18%
where the time goes in v7:
time: 129 us; the launch traced here: 128 us
  starting transfers between devices  57.4 us (44%)
  Pallas kernels  34.4 us (27%)
  waiting for transfers between devices  24 us (19%)
  local copies, waits for them, and re-layouts  11.2 us (9%)
    ppermute x24, starting transfers between devices, hops(): got.append(lax.ppermute(values[hop], axis, pairs))  36.5 us
    ppermute x24, waiting for transfers between devices, hops(): got.append(lax.ppermute(values[hop], axis, pairs))  19.2 us
    all_to_all x4, starting transfers between devices, trade(): return lax.all_to_all(copies, 'col', 0, 0, tiled=True)  16 us
    unnamed x60, local copies, waits for them, and re-layouts  11.2 us
    pallas_call x1, Pallas kernels, cholesky(): pl.pallas_call(first_kernel, in_specs=[VMEM], out_shape=(square(size), sq...  9.68 us
    ppermute x2, starting transfers between devices, pass_on(): got = lax.ppermute(value, ('row', 'col'), pairs)  4.81 us
    pallas_call x1, Pallas kernels, compact_factor(): pl.pallas_call(factor_kernel, out_shape=(square(inv.shape[0]), square(inv...  4.72 us
    pallas_call x1, Pallas kernels, update(): pl.pallas_call(update_kernel, in_specs=[SMEM] + [VMEM] * (7 + len(pieces)...  4.03 us
  transfers between devices with their start and end apart: 32, of which 12 were waited for; matrix products, arithmetic and copies ran while one was open for 0% of the time, Pallas kernels for 18%

profile of v7, /device:TPU:0, one launch (start us, length us, event | category | flops | bytes accessed | tf_op | source)
XLA Modules:
  0.0 128.2 jit_solution(17183474521134860148)
XLA Ops:
  0.7 1.1 copy-done
  1.8 1.5 %gram_strips.1.refs_0_ = f32[64,256]{1,0:T(8,128)S(1)} custom-call(s32[2]{0:T(128)S(1)} %pad_add_fusion.place_ref, f32[768,256]{1,0:T(8,128)S(1)} %copy-done), custom_call_target="tpu_custom_call" | custom-call | flops 2000000000 | bytes 6000000 | tf_op jit(solution)/shard_map/gram_strips/pallas_call | solution.py:270
  3.3 5.1 %collective-permute-start.2 = (f32[64,256]{1,0:T(8,128)S(1)}, f32[64,256]{1,0:T(8,128)S(1)}, u32[]{:S(2)}, u32[]{:S(2)}) collective-permute-start(f32[64,256]{1,0:T(8,128)S(1)} %gram_strips.1.refs_0_), channel_id=1, source_target_pairs={{0,24},{8,16},{16,8},{24,0},{1,25},{9,17},{17,9},{25,1},{2,26},{10... | collective-permute-start | bytes 196616 | tf_op jit(solution)/shard_map/ppermute | solution.py:529
  9.1 1.9 %collective-permute-done.2.refs_3_ = f32[64,256]{1,0:T(8,128)S(1)} collective-permute-done((f32[64,256]{1,0:T(8,128)S(1)}, f32[64,256]{1,0:T(8,128)S(1)}, u32[]{:S(2)}, u32[]{:S(2)}) %collective-permute-start.2) | collective-permute-done | bytes 65568 | tf_op jit(solution)/shard_map/ppermute | solution.py:529
  11.0 3.0 %collective-permute-done.1.refs_2_ = f32[64,256]{1,0:T(8,128)S(1)} collective-permute-done((f32[64,256]{1,0:T(8,128)S(1)}, f32[64,256]{1,0:T(8,128)S(1)}, u32[]{:S(2)}, u32[]{:S(2)}) %collective-permute-start.1) | collective-permute-done | bytes 65568 | tf_op jit(solution)/shard_map/ppermute | solution.py:529
  14.0 3.5 %collective-permute-start.3 = (f32[384,256]{1,0:T(8,128)S(1)}, f32[384,256]{1,0:T(8,128)S(1)}, u32[]{:S(2)}, u32[]{:S(2)}) collective-permute-start(f32[384,256]{1,0:T(8,128)S(1)} %dynamic-slice_select_fusion), channel_id=1, source_target_pairs={{0,16},{1,17},{10,26},{11,27},{20,4},{21,5},{30,14},{31,15}} | collective-permute-start | bytes 1179656 | tf_op jit(solution)/shard_map/ppermute | solution.py:544
  18.3 3.6 %all-to-all-start = ((f32[8,32,256]{2,1,0:T(8,128)}), f32[8,32,256]{2,1,0:T(8,128)S(1)}, u32[]{:S(2)}, u32[]{:S(2)}) async-start(f32[8,32,256]{2,1,0:T(8,128)} %sum_copies.4), calls=%async_computation | async-start | bytes 524288 | tf_op jit(solution)/shard_map/all_to_all | solution.py:461
  21.9 2.6 %collective-permute-done.3 = f32[384,256]{1,0:T(8,128)S(1)} collective-permute-done((f32[384,256]{1,0:T(8,128)S(1)}, f32[384,256]{1,0:T(8,128)S(1)}, u32[]{:S(2)}, u32[]{:S(2)}) %collective-permute-start.3) | collective-permute-done | bytes 393248 | tf_op jit(solution)/shard_map/ppermute | solution.py:544
  24.5 1.3 %collective-permute-start.4 = (f32[384,256]{1,0:T(8,128)S(1)}, f32[384,256]{1,0:T(8,128)S(1)}, u32[]{:S(2)}, u32[]{:S(2)}) collective-permute-start(f32[384,256]{1,0:T(8,128)S(1)} %add.8.slab_ref), channel_id=1, source_target_pairs={{0,8},{16,24},{1,9},{17,25},{10,2},{26,18},{11,3},{27,19},{20,28},... | collective-permute-start | bytes 1179656 | tf_op jit(solution)/shard_map/ppermute | solution.py:544
  25.9 1.4 %top_rows.1 = (f32[96,256]{1,0:T(8,128)S(1)}, f32[96,256]{1,0:T(8,128)}, f32[96,256]{1,0:T(8,128)S(1)}, f32[96,256]{1,0:T(8,128)S(1)}) custom-call(s32[2]{0:T(128)S(1)} %pad_add_fusion.place_ref, f32[768,384]{1,0:T(8,128)S(1)} %copy-done.2), custom_call_target="tpu_custom_call" | custom-call | flops 1000000000 | bytes 3000000 | tf_op jit(solution)/shard_map/top_rows/pallas_call | solution.py:326
  27.9 3.4 %collective-permute-start.6 = (f32[96,256]{1,0:T(8,128)S(1)}, f32[96,256]{1,0:T(8,128)S(1)}, u32[]{:S(2)}, u32[]{:S(2)}) collective-permute-start(f32[96,256]{1,0:T(8,128)S(1)} %get-tuple-element.79), channel_id=1, source_target_pairs={{0,16},{8,24},{16,0},{24,8},{1,17},{9,25},{17,1},{25,9},{2,18},{10... | collective-permute-start | bytes 294920 | tf_op jit(solution)/shard_map/ppermute | solution.py:529
  31.3 1.5 %collective-permute-start.7 = (f32[96,256]{1,0:T(8,128)S(1)}, f32[96,256]{1,0:T(8,128)S(1)}, u32[]{:S(2)}, u32[]{:S(2)}) collective-permute-start(f32[96,256]{1,0:T(8,128)S(1)} %get-tuple-element.80), channel_id=1, source_target_pairs={{0,24},{8,16},{16,8},{24,0},{1,25},{9,17},{17,9},{25,1},{2,26},{10... | collective-permute-start | bytes 294920 | tf_op jit(solution)/shard_map/ppermute | solution.py:529
  32.7 9.7 %cholesky_inverse.1 = (f32[256,256]{1,0:T(8,128)S(1)}, f32[256,256]{1,0:T(8,128)S(1)}) custom-call(f32[8,32,256]{2,1,0:T(8,128)S(1)} %all-to-all-done.parts_ref), custom_call_target="tpu_custom_call" | custom-call | flops 10000000000 | bytes 30000000 | tf_op jit(solution)/shard_map/cholesky_inverse/pallas_call | solution.py:141
  43.1 3.2 %half_stage.1 = (f32[768,256]{1,0:T(8,128)S(1)}, f32[384,256]{1,0:T(8,128)S(1)}, f32[32,256]{1,0:T(8,128)S(1)}) custom-call(s32[2]{0:T(128)S(1)} %pad_add_fusion.place_ref, f32[768,256]{1,0:T(8,128)S(1)} %copy-done.1, f32[384,256]{1,0:T(8,128)S(1)} %add.8.slab_ref, f32[384,256]{1,0:T(8,128)S(1)} %collective-permute-done.4.got_ref, ...), custom_call_target="tpu_custom_call" | custom-call | flops 3000000000 | bytes 9000000 | tf_op jit(solution)/shard_map/half_stage/pallas_call | solution.py:294
  46.3 0.9 copy-done.13
  48.0 2.0 %collective-permute-start.10 = (f32[32,256]{1,0:T(8,128)S(1)}, f32[32,256]{1,0:T(8,128)S(1)}, u32[]{:S(2)}, u32[]{:S(2)}) collective-permute-start(f32[32,256]{1,0:T(8,128)S(1)} %get-tuple-element.83.refs_0_), channel_id=1, source_target_pairs={{0,16},{8,24},{16,0},{24,8},{1,17},{9,25},{17,1},{25,9},{2,18},{10... | collective-permute-start | bytes 98312 | tf_op jit(solution)/shard_map/ppermute | solution.py:529
  50.0 0.9 collective-permute-start.9
  50.9 1.5 %collective-permute-start.8 = (f32[32,256]{1,0:T(8,128)S(1)}, f32[32,256]{1,0:T(8,128)S(1)}, u32[]{:S(2)}, u32[]{:S(2)}) collective-permute-start(f32[32,256]{1,0:T(8,128)S(1)} %get-tuple-element.83.refs_0_), channel_id=1, source_target_pairs={{0,24},{8,16},{16,8},{24,0},{1,25},{9,17},{17,9},{25,1},{2,26},{10... | collective-permute-start | bytes 98312 | tf_op jit(solution)/shard_map/ppermute | solution.py:529
  52.4 0.8 collective-permute-done.10.refs_2_
  53.9 2.7 %collective-permute-done.8.refs_3_ = f32[32,256]{1,0:T(8,128)S(1)} collective-permute-done((f32[32,256]{1,0:T(8,128)S(1)}, f32[32,256]{1,0:T(8,128)S(1)}, u32[]{:S(2)}, u32[]{:S(2)}) %collective-permute-start.8) | collective-permute-done | bytes 32800 | tf_op jit(solution)/shard_map/ppermute | solution.py:529
  57.3 4.7 %all-to-all-start.1 = ((f32[8,32,256]{2,1,0:T(8,128)}), f32[8,32,256]{2,1,0:T(8,128)S(1)}, u32[]{:S(2)}, u32[]{:S(2)}) async-start(f32[8,32,256]{2,1,0:T(8,128)} %sum_copies.5), calls=%async_computation.1 | async-start | bytes 524288 | tf_op jit(solution)/shard_map/all_to_all | solution.py:461
  62.1 1.2 near_rows.1
  63.4 2.9 %collective-permute-start.12 = (f32[96,256]{1,0:T(8,128)S(1)}, f32[96,256]{1,0:T(8,128)S(1)}, u32[]{:S(2)}, u32[]{:S(2)}) collective-permute-start(f32[96,256]{1,0:T(8,128)S(1)} %get-tuple-element.89), channel_id=1, source_target_pairs={{0,16},{8,24},{16,0},{24,8},{1,17},{9,25},{17,1},{25,9},{2,18},{10... | collective-permute-start | bytes 294920 | tf_op jit(solution)/shard_map/ppermute | solution.py:529
  66.3 1.5 %collective-permute-start.13 = (f32[96,256]{1,0:T(8,128)S(1)}, f32[96,256]{1,0:T(8,128)S(1)}, u32[]{:S(2)}, u32[]{:S(2)}) collective-permute-start(f32[96,256]{1,0:T(8,128)S(1)} %get-tuple-element.90), channel_id=1, source_target_pairs={{0,24},{8,16},{16,8},{24,0},{1,25},{9,17},{17,9},{25,1},{2,26},{10... | collective-permute-start | bytes 294920 | tf_op jit(solution)/shard_map/ppermute | solution.py:529
  67.8 1.2 all-to-all-done.1.gram_ref
  69.0 2.7 %near_cholesky.1.upper_ref = f32[256,256]{1,0:T(8,128)S(1)} custom-call(f32[256,256]{1,0:T(8,128)S(1)} %bitcast.3), custom_call_target="tpu_custom_call" | custom-call | flops 3000000000 | bytes 9000000 | tf_op jit(solution)/shard_map/near_cholesky/pallas_call | solution.py:197
  71.7 2.5 %collective-permute-done.12.refs_2_ = f32[96,256]{1,0:T(8,128)S(1)} collective-permute-done((f32[96,256]{1,0:T(8,128)S(1)}, f32[96,256]{1,0:T(8,128)S(1)}, u32[]{:S(2)}, u32[]{:S(2)}) %collective-permute-start.12) | collective-permute-done | bytes 98336 | tf_op jit(solution)/shard_map/ppermute | solution.py:529
  74.2 2.2 %products.1 = (f32[768,256]{1,0:T(8,128)S(1)}, f32[384,256]{1,0:T(8,128)S(1)}, f32[4,128,256]{2,1,0:T(8,128)S(1)}, f32[4,128,256]{2,1,0:T(8,128)S(1)}) custom-call(s32[2]{0:T(128)S(1)} %pad_add_fusion.place_ref, f32[768,384]{1,0:T(8,128)S(1)} %copy-done.2, f32[768,256]{1,0:T(8,128)S(1)} %copy-done.15, f32[384,256]{1,0:T(8,128)S(1)} %copy-done.21, ...), custom_call_target="tpu_custom_call" | custom-call | flops 4000000000 | bytes 12000000 | tf_op jit(solution)/shard_map/products/pallas_call | solution.py:385
  78.1 1.0 collective-permute-done.14.got_ref
  79.1 2.3 %collective-permute-start.20 = (f32[96,256]{1,0:T(8,128)S(1)}, f32[96,256]{1,0:T(8,128)S(1)}, u32[]{:S(2)}, u32[]{:S(2)}) collective-permute-start(f32[96,256]{1,0:T(8,128)S(1)} %near_sum.1.rest_refs_0_), channel_id=1, source_target_pairs={{0,24},{8,16},{16,8},{24,0},{1,25},{9,17},{17,9},{25,1},{2,26},{10... | collective-permute-start | bytes 294920 | tf_op jit(solution)/shard_map/ppermute | solution.py:529
  81.5 2.1 %collective-permute-start.15 = (f32[128,256]{1,0:T(8,128)S(1)}, f32[128,256]{1,0:T(8,128)S(1)}, u32[]{:S(2)}, u32[]{:S(2)}) collective-permute-start(f32[128,256]{1,0:T(8,128)S(1)} %get-tuple-element.109), channel_id=1, source_target_pairs={{0,2},{1,3},{2,0},{3,1},{4,6},{5,7},{6,4},{7,5},{8,10},{9,11},{10,... | collective-permute-start | bytes 393224 | tf_op jit(solution)/shard_map/ppermute | solution.py:529
  83.6 1.5 %collective-permute-start.16 = (f32[128,256]{1,0:T(8,128)S(1)}, f32[128,256]{1,0:T(8,128)S(1)}, u32[]{:S(2)}, u32[]{:S(2)}) collective-permute-start(f32[128,256]{1,0:T(8,128)S(1)} %get-tuple-element.110), channel_id=1, source_target_pairs={{0,4},{1,5},{2,6},{3,7},{4,0},{5,1},{6,2},{7,3},{8,12},{9,13},{10,... | collective-permute-start | bytes 393224 | tf_op jit(solution)/shard_map/ppermute | solution.py:529
  85.3 1.1 collective-permute-start.19
  86.5 1.9 %collective-permute-start.18 = (f32[96,256]{1,0:T(8,128)S(1)}, f32[96,256]{1,0:T(8,128)S(1)}, u32[]{:S(2)}, u32[]{:S(2)}) collective-permute-start(f32[96,256]{1,0:T(8,128)S(1)} %near_sum.1.rest_refs_0_), channel_id=1, source_target_pairs={{0,8},{8,0},{16,24},{24,16},{1,9},{9,1},{17,25},{25,17},{2,10},{10... | collective-permute-start | bytes 294920 | tf_op jit(solution)/shard_map/ppermute | solution.py:529
  89.1 3.4 %collective-permute-done.19.rest_refs_2_ = f32[96,256]{1,0:T(8,128)S(1)} collective-permute-done((f32[96,256]{1,0:T(8,128)S(1)}, f32[96,256]{1,0:T(8,128)S(1)}, u32[]{:S(2)}, u32[]{:S(2)}) %collective-permute-start.19) | collective-permute-done | bytes 98336 | tf_op jit(solution)/shard_map/ppermute | solution.py:529
  93.0 3.4 %all-to-all-start.2 = ((f32[8,32,256]{2,1,0:T(8,128)}), f32[8,32,256]{2,1,0:T(8,128)S(1)}, u32[]{:S(2)}, u32[]{:S(2)}) async-start(f32[8,32,256]{2,1,0:T(8,128)} %sum_copies.6), calls=%async_computation.2 | async-start | bytes 524288 | tf_op jit(solution)/shard_map/all_to_all | solution.py:461
  96.5 2.8 %collective-permute-start.26 = (f32[32,256]{1,0:T(8,128)S(1)}, f32[32,256]{1,0:T(8,128)S(1)}, u32[]{:S(2)}, u32[]{:S(2)}) collective-permute-start(f32[32,256]{1,0:T(8,128)S(1)} %get-tuple-element.123.refs_0_), channel_id=1, source_target_pairs={{0,24},{8,16},{16,8},{24,0},{1,25},{9,17},{17,9},{25,1},{2,26},{10... | collective-permute-start | bytes 98312 | tf_op jit(solution)/shard_map/ppermute | solution.py:529
  99.3 2.9 %collective-permute-start.23 = (f32[96,256]{1,0:T(8,128)S(1)}, f32[96,256]{1,0:T(8,128)S(1)}, u32[]{:S(2)}, u32[]{:S(2)}) collective-permute-start(f32[96,256]{1,0:T(8,128)S(1)} %get-tuple-element.124.refs_0_), channel_id=1, source_target_pairs={{0,6},{1,7},{2,4},{3,5},{4,2},{5,3},{6,0},{7,1},{8,14},{9,15},{10,... | collective-permute-start | bytes 294920 | tf_op jit(solution)/shard_map/ppermute | solution.py:529
  103.0 1.4 %collective-permute-start.24 = (f32[32,256]{1,0:T(8,128)S(1)}, f32[32,256]{1,0:T(8,128)S(1)}, u32[]{:S(2)}, u32[]{:S(2)}) collective-permute-start(f32[32,256]{1,0:T(8,128)S(1)} %get-tuple-element.123.refs_0_), channel_id=1, source_target_pairs={{0,8},{8,0},{16,24},{24,16},{1,9},{9,1},{17,25},{25,17},{2,10},{10... | collective-permute-start | bytes 98312 | tf_op jit(solution)/shard_map/ppermute | solution.py:529
  104.4 3.5 %collective-permute-done.25.refs_2_ = f32[32,256]{1,0:T(8,128)S(1)} collective-permute-done((f32[32,256]{1,0:T(8,128)S(1)}, f32[32,256]{1,0:T(8,128)S(1)}, u32[]{:S(2)}, u32[]{:S(2)}) %collective-permute-start.25) | collective-permute-done | bytes 32800 | tf_op jit(solution)/shard_map/ppermute | solution.py:529
  109.4 4.3 %all-to-all-start.3 = ((f32[8,32,256]{2,1,0:T(8,128)}), f32[8,32,256]{2,1,0:T(8,128)S(1)}, u32[]{:S(2)}, u32[]{:S(2)}) async-start(f32[8,32,256]{2,1,0:T(8,128)} %sum_copies.7), calls=%async_computation.3 | async-start | bytes 524288 | tf_op jit(solution)/shard_map/all_to_all | solution.py:461
  113.7 0.9 copy-done.25
  114.7 0.9 copy-done.29
  115.6 4.7 %compact_factor.1 = (f32[256,256]{1,0:T(8,128)S(1)}, f32[256,256]{1,0:T(8,128)}) custom-call(f32[8,32,256]{2,1,0:T(8,128)S(1)} %all-to-all-done.1.gram_ref, f32[8,32,256]{2,1,0:T(8,128)S(1)} %all-to-all-done.2.top_ref, f32[256,256]{1,0:T(8,128)S(1)} %copy-done.25, f32[256,256]{1,0:T(8,128)S(1)} %copy-done.12, f32[256,256]{1,0:T(8,128)S(1)} %copy-done.29), custom_call_target="tpu_custom_call" | custom-call | flops 4000000000 | bytes 12000000 | tf_op jit(solution)/shard_map/compact_factor/pallas_call | solution.py:243
  121.1 1.1 copy-done.19
  122.2 1.0 copy-done.23
  123.2 0.9 copy-done.27
  124.1 4.0 %two_sided_update.1 = f32[768,384]{1,0:T(8,128)} custom-call(s32[2]{0:T(128)S(1)} %pad_add_fusion.place_ref, f32[768,384]{1,0:T(8,128)S(1)} %copy-done.2, f32[768,256]{1,0:T(8,128)S(1)} %copy-done.19, f32[384,256]{1,0:T(8,128)S(1)} %merge_pieces.1.mine_ref, f32[384,256]{1,0:T(8,128)S(1)} %collective-permute-done.27.other_ref, f32[384,256]{1,0:T(8,128)S(1)} %copy-done.23, ...), custom_call_target="tpu_custom_call" | custom-call | flops 4000000000 | bytes 12000000 | tf_op jit(solution)/shard_map/two_sided_update/pallas_call | solution.py:514
  (96 shorter events, 11.4 us)
Async XLA Ops:
  1.8 7.2 %copy-start.1 = (f32[768,256]{1,0:T(8,128)S(1)}, f32[768,256]{1,0:T(8,128)}, u32[]{:S(2)}) copy-start(f32[768,256]{1,0:T(8,128)} %panel_ref.3) | copy-start | bytes 2359300
  3.3 15.0 %copy-start.3 = (f32[64,256]{1,0:T(8,128)}, f32[64,256]{1,0:T(8,128)S(1)}, u32[]{:S(2)}) copy-start(f32[64,256]{1,0:T(8,128)S(1)} %gram_strips.1.refs_0_) | copy-start | bytes 196612
  3.3 7.7 %collective-permute-start.2 = (f32[64,256]{1,0:T(8,128)S(1)}, f32[64,256]{1,0:T(8,128)S(1)}, u32[]{:S(2)}, u32[]{:S(2)}) collective-permute-start(f32[64,256]{1,0:T(8,128)S(1)} %gram_strips.1.refs_0_), channel_id=1, source_target_pairs={{0,24},{8,16},{16,8},{24,0},{1,25},{9,17},{17,9},{25,1},{2,26},{10... | collective-permute-start | bytes 196616 | tf_op jit(solution)/shard_map/ppermute | solution.py:529
  8.4 5.6 %collective-permute-start.1 = (f32[64,256]{1,0:T(8,128)S(1)}, f32[64,256]{1,0:T(8,128)S(1)}, u32[]{:S(2)}, u32[]{:S(2)}) collective-permute-start(f32[64,256]{1,0:T(8,128)S(1)} %gram_strips.1.refs_0_), channel_id=1, source_target_pairs={{0,16},{8,24},{16,0},{24,8},{1,17},{9,25},{17,1},{25,9},{2,18},{10... | collective-permute-start | bytes 196616 | tf_op jit(solution)/shard_map/ppermute | solution.py:529
  8.4 5.6 %collective-permute-start = (f32[64,256]{1,0:T(8,128)S(1)}, f32[64,256]{1,0:T(8,128)S(1)}, u32[]{:S(2)}, u32[]{:S(2)}) collective-permute-start(f32[64,256]{1,0:T(8,128)S(1)} %gram_strips.1.refs_0_), channel_id=1, source_target_pairs={{0,8},{8,0},{16,24},{24,16},{1,9},{9,1},{17,25},{25,17},{2,10},{10... | collective-permute-start | bytes 196616 | tf_op jit(solution)/shard_map/ppermute | solution.py:529
  11.0 7.3 %copy-start.5 = (f32[64,256]{1,0:T(8,128)}, f32[64,256]{1,0:T(8,128)S(1)}, u32[]{:S(2)}) copy-start(f32[64,256]{1,0:T(8,128)S(1)} %collective-permute-done.2.refs_3_) | copy-start | bytes 196612
  14.0 4.3 %copy-start.7 = (f32[64,256]{1,0:T(8,128)}, f32[64,256]{1,0:T(8,128)S(1)}, u32[]{:S(2)}) copy-start(f32[64,256]{1,0:T(8,128)S(1)} %collective-permute-done.1.refs_2_) | copy-start | bytes 196612
  14.0 4.3 %copy-start.9 = (f32[64,256]{1,0:T(8,128)}, f32[64,256]{1,0:T(8,128)S(1)}, u32[]{:S(2)}) copy-start(f32[64,256]{1,0:T(8,128)S(1)} %collective-permute-done.refs_1_) | copy-start | bytes 196612
  14.0 10.4 %collective-permute-start.3 = (f32[384,256]{1,0:T(8,128)S(1)}, f32[384,256]{1,0:T(8,128)S(1)}, u32[]{:S(2)}, u32[]{:S(2)}) collective-permute-start(f32[384,256]{1,0:T(8,128)S(1)} %dynamic-slice_select_fusion), channel_id=1, source_target_pairs={{0,16},{1,17},{10,26},{11,27},{20,4},{21,5},{30,14},{31,15}} | collective-permute-start | bytes 1179656 | tf_op jit(solution)/shard_map/ppermute | solution.py:544
  18.3 7.6 %copy-start.2 = (f32[768,384]{1,0:T(8,128)S(1)}, f32[768,384]{1,0:T(8,128)}, u32[]{:S(2)}) copy-start(f32[768,384]{1,0:T(8,128)} %ham_ref.6) | copy-start | bytes 3538948
  18.3 14.4 %all-to-all-start = ((f32[8,32,256]{2,1,0:T(8,128)}), f32[8,32,256]{2,1,0:T(8,128)S(1)}, u32[]{:S(2)}, u32[]{:S(2)}) async-start(f32[8,32,256]{2,1,0:T(8,128)} %sum_copies.4), calls=%async_computation | async-start | bytes 524288 | tf_op jit(solution)/shard_map/all_to_all | solution.py:461
  24.5 18.6 %collective-permute-start.4 = (f32[384,256]{1,0:T(8,128)S(1)}, f32[384,256]{1,0:T(8,128)S(1)}, u32[]{:S(2)}, u32[]{:S(2)}) collective-permute-start(f32[384,256]{1,0:T(8,128)S(1)} %add.8.slab_ref), channel_id=1, source_target_pairs={{0,8},{16,24},{1,9},{17,25},{10,2},{26,18},{11,3},{27,19},{20,28},... | collective-permute-start | bytes 1179656 | tf_op jit(solution)/shard_map/ppermute | solution.py:544
  27.9 15.2 %collective-permute-start.5 = (f32[96,256]{1,0:T(8,128)}, f32[96,256]{1,0:T(8,128)S(1)}, u32[]{:S(2)}, u32[]{:S(2)}) collective-permute-start(f32[96,256]{1,0:T(8,128)} %get-tuple-element.78), channel_id=1, source_target_pairs={{0,8},{8,0},{16,24},{24,16},{1,9},{9,1},{17,25},{25,17},{2,10},{10... | collective-permute-start | bytes 294920 | tf_op jit(solution)/shard_map/ppermute | solution.py:529
  27.9 15.2 %collective-permute-start.6 = (f32[96,256]{1,0:T(8,128)S(1)}, f32[96,256]{1,0:T(8,128)S(1)}, u32[]{:S(2)}, u32[]{:S(2)}) collective-permute-start(f32[96,256]{1,0:T(8,128)S(1)} %get-tuple-element.79), channel_id=1, source_target_pairs={{0,16},{8,24},{16,0},{24,8},{1,17},{9,25},{17,1},{25,9},{2,18},{10... | collective-permute-start | bytes 294920 | tf_op jit(solution)/shard_map/ppermute | solution.py:529
  31.3 11.9 %collective-permute-start.7 = (f32[96,256]{1,0:T(8,128)S(1)}, f32[96,256]{1,0:T(8,128)S(1)}, u32[]{:S(2)}, u32[]{:S(2)}) collective-permute-start(f32[96,256]{1,0:T(8,128)S(1)} %get-tuple-element.80), channel_id=1, source_target_pairs={{0,24},{8,16},{16,8},{24,0},{1,25},{9,17},{17,9},{25,1},{2,26},{10... | collective-permute-start | bytes 294920 | tf_op jit(solution)/shard_map/ppermute | solution.py:529
  43.1 3.2 %copy-start.24 = (f32[256,256]{1,0:T(8,128)}, f32[256,256]{1,0:T(8,128)S(1)}, u32[]{:S(2)}) copy-start(f32[256,256]{1,0:T(8,128)S(1)} %get-tuple-element.81.inv_ref) | copy-start | bytes 786436
  48.0 14.1 %copy-start.14 = (f32[768,256]{1,0:T(8,128)S(1)}, f32[768,256]{1,0:T(8,128)}, u32[]{:S(2)}) copy-start(f32[768,256]{1,0:T(8,128)} %copy-done.13) | copy-start | bytes 2359300
  48.0 5.2 %collective-permute-start.10 = (f32[32,256]{1,0:T(8,128)S(1)}, f32[32,256]{1,0:T(8,128)S(1)}, u32[]{:S(2)}, u32[]{:S(2)}) collective-permute-start(f32[32,256]{1,0:T(8,128)S(1)} %get-tuple-element.83.refs_0_), channel_id=1, source_target_pairs={{0,16},{8,24},{16,0},{24,8},{1,17},{9,25},{17,1},{25,9},{2,18},{10... | collective-permute-start | bytes 98312 | tf_op jit(solution)/shard_map/ppermute | solution.py:529
  50.0 3.9 %collective-permute-start.9 = (f32[32,256]{1,0:T(8,128)S(1)}, f32[32,256]{1,0:T(8,128)S(1)}, u32[]{:S(2)}, u32[]{:S(2)}) collective-permute-start(f32[32,256]{1,0:T(8,128)S(1)} %get-tuple-element.83.refs_0_), channel_id=1, source_target_pairs={{0,8},{8,0},{16,24},{24,16},{1,9},{9,1},{17,25},{25,17},{2,10},{10... | collective-permute-start | bytes 98312 | tf_op jit(solution)/shard_map/ppermute | solution.py:529
  50.9 5.7 %collective-permute-start.8 = (f32[32,256]{1,0:T(8,128)S(1)}, f32[32,256]{1,0:T(8,128)S(1)}, u32[]{:S(2)}, u32[]{:S(2)}) collective-permute-start(f32[32,256]{1,0:T(8,128)S(1)} %get-tuple-element.83.refs_0_), channel_id=1, source_target_pairs={{0,24},{8,16},{16,8},{24,0},{1,25},{9,17},{17,9},{25,1},{2,26},{10... | collective-permute-start | bytes 98312 | tf_op jit(solution)/shard_map/ppermute | solution.py:529
  57.3 11.7 %all-to-all-start.1 = ((f32[8,32,256]{2,1,0:T(8,128)}), f32[8,32,256]{2,1,0:T(8,128)S(1)}, u32[]{:S(2)}, u32[]{:S(2)}) async-start(f32[8,32,256]{2,1,0:T(8,128)} %sum_copies.5), calls=%async_computation.1 | async-start | bytes 524288 | tf_op jit(solution)/shard_map/all_to_all | solution.py:461
  63.3 8.4 %collective-permute-start.11 = (f32[96,256]{1,0:T(8,128)S(1)}, f32[96,256]{1,0:T(8,128)S(1)}, u32[]{:S(2)}, u32[]{:S(2)}) collective-permute-start(f32[96,256]{1,0:T(8,128)S(1)} %get-tuple-element.88), channel_id=1, source_target_pairs={{0,8},{8,0},{16,24},{24,16},{1,9},{9,1},{17,25},{25,17},{2,10},{10... | collective-permute-start | bytes 294920 | tf_op jit(solution)/shard_map/ppermute | solution.py:529
  63.4 10.8 %collective-permute-start.12 = (f32[96,256]{1,0:T(8,128)S(1)}, f32[96,256]{1,0:T(8,128)S(1)}, u32[]{:S(2)}, u32[]{:S(2)}) collective-permute-start(f32[96,256]{1,0:T(8,128)S(1)} %get-tuple-element.89), channel_id=1, source_target_pairs={{0,16},{8,24},{16,0},{24,8},{1,17},{9,25},{17,1},{25,9},{2,18},{10... | collective-permute-start | bytes 294920 | tf_op jit(solution)/shard_map/ppermute | solution.py:529
  66.3 8.0 %collective-permute-start.13 = (f32[96,256]{1,0:T(8,128)S(1)}, f32[96,256]{1,0:T(8,128)S(1)}, u32[]{:S(2)}, u32[]{:S(2)}) collective-permute-start(f32[96,256]{1,0:T(8,128)S(1)} %get-tuple-element.90), channel_id=1, source_target_pairs={{0,24},{8,16},{16,8},{24,0},{1,25},{9,17},{17,9},{25,1},{2,26},{10... | collective-permute-start | bytes 294920 | tf_op jit(solution)/shard_map/ppermute | solution.py:529
  69.0 5.2 %copy-start.15 = (f32[768,256]{1,0:T(8,128)S(1)}, f32[768,256]{1,0:T(8,128)}, u32[]{:S(2)}) copy-start(f32[768,256]{1,0:T(8,128)} %copy-done.13) | copy-start | bytes 2359300
  69.0 5.2 %copy-start.21 = (f32[384,256]{1,0:T(8,128)S(1)}, f32[384,256]{1,0:T(8,128)}, u32[]{:S(2)}) copy-start(f32[384,256]{1,0:T(8,128)} %copy-done.20) | copy-start | bytes 1179652
  71.7 5.5 %copy-start.11 = (f32[256,256]{1,0:T(8,128)}, f32[256,256]{1,0:T(8,128)S(1)}, u32[]{:S(2)}) copy-start(f32[256,256]{1,0:T(8,128)S(1)} %near_cholesky.1.upper_ref) | copy-start | bytes 786436
  77.2 1.9 %collective-permute-start.14 = (f32[4,128,256]{2,1,0:T(8,128)S(1)}, f32[4,128,256]{2,1,0:T(8,128)S(1)}, u32[]{:S(2)}, u32[]{:S(2)}) collective-permute-start(f32[4,128,256]{2,1,0:T(8,128)S(1)} %get-tuple-element.94), channel_id=1, source_target_pairs={{0,1},{1,0},{2,3},{3,2},{4,5},{5,4},{6,7},{7,6},{8,9},{9,8},{10,11... | collective-permute-start | bytes 1572872 | tf_op jit(solution)/shard_map/ppermute | solution.py:595
  78.1 10.2 %copy-start.4 = (f32[64,256]{1,0:T(8,128)S(1)}, f32[64,256]{1,0:T(8,128)}, u32[]{:S(2)}) copy-start(f32[64,256]{1,0:T(8,128)} %copy-done.3) | copy-start | bytes 196612
  78.1 10.2 %copy-start.6 = (f32[64,256]{1,0:T(8,128)S(1)}, f32[64,256]{1,0:T(8,128)}, u32[]{:S(2)}) copy-start(f32[64,256]{1,0:T(8,128)} %copy-done.5) | copy-start | bytes 196612
  78.1 10.2 %copy-start.8 = (f32[64,256]{1,0:T(8,128)S(1)}, f32[64,256]{1,0:T(8,128)}, u32[]{:S(2)}) copy-start(f32[64,256]{1,0:T(8,128)} %copy-done.7) | copy-start | bytes 196612
  78.1 10.2 %copy-start.10 = (f32[64,256]{1,0:T(8,128)S(1)}, f32[64,256]{1,0:T(8,128)}, u32[]{:S(2)}) copy-start(f32[64,256]{1,0:T(8,128)} %copy-done.9) | copy-start | bytes 196612
  79.1 7.3 %collective-permute-start.20 = (f32[96,256]{1,0:T(8,128)S(1)}, f32[96,256]{1,0:T(8,128)S(1)}, u32[]{:S(2)}, u32[]{:S(2)}) collective-permute-start(f32[96,256]{1,0:T(8,128)S(1)} %near_sum.1.rest_refs_0_), channel_id=1, source_target_pairs={{0,24},{8,16},{16,8},{24,0},{1,25},{9,17},{17,9},{25,1},{2,26},{10... | collective-permute-start | bytes 294920 | tf_op jit(solution)/shard_map/ppermute | solution.py:529
  81.5 11.5 %collective-permute-start.15 = (f32[128,256]{1,0:T(8,128)S(1)}, f32[128,256]{1,0:T(8,128)S(1)}, u32[]{:S(2)}, u32[]{:S(2)}) collective-permute-start(f32[128,256]{1,0:T(8,128)S(1)} %get-tuple-element.109), channel_id=1, source_target_pairs={{0,2},{1,3},{2,0},{3,1},{4,6},{5,7},{6,4},{7,5},{8,10},{9,11},{10,... | collective-permute-start | bytes 393224 | tf_op jit(solution)/shard_map/ppermute | solution.py:529
  83.6 9.4 %collective-permute-start.16 = (f32[128,256]{1,0:T(8,128)S(1)}, f32[128,256]{1,0:T(8,128)S(1)}, u32[]{:S(2)}, u32[]{:S(2)}) collective-permute-start(f32[128,256]{1,0:T(8,128)S(1)} %get-tuple-element.110), channel_id=1, source_target_pairs={{0,4},{1,5},{2,6},{3,7},{4,0},{5,1},{6,2},{7,3},{8,12},{9,13},{10,... | collective-permute-start | bytes 393224 | tf_op jit(solution)/shard_map/ppermute | solution.py:529
  85.1 7.9 %collective-permute-start.17 = (f32[128,256]{1,0:T(8,128)S(1)}, f32[128,256]{1,0:T(8,128)S(1)}, u32[]{:S(2)}, u32[]{:S(2)}) collective-permute-start(f32[128,256]{1,0:T(8,128)S(1)} %get-tuple-element.111), channel_id=1, source_target_pairs={{0,6},{1,7},{2,4},{3,5},{4,2},{5,3},{6,0},{7,1},{8,14},{9,15},{10,... | collective-permute-start | bytes 393224 | tf_op jit(solution)/shard_map/ppermute | solution.py:529
  85.3 7.1 %collective-permute-start.19 = (f32[96,256]{1,0:T(8,128)S(1)}, f32[96,256]{1,0:T(8,128)S(1)}, u32[]{:S(2)}, u32[]{:S(2)}) collective-permute-start(f32[96,256]{1,0:T(8,128)S(1)} %near_sum.1.rest_refs_0_), channel_id=1, source_target_pairs={{0,16},{8,24},{16,0},{24,8},{1,17},{9,25},{17,1},{25,9},{2,18},{10... | collective-permute-start | bytes 294920 | tf_op jit(solution)/shard_map/ppermute | solution.py:529
  86.5 6.5 %collective-permute-start.18 = (f32[96,256]{1,0:T(8,128)S(1)}, f32[96,256]{1,0:T(8,128)S(1)}, u32[]{:S(2)}, u32[]{:S(2)}) collective-permute-start(f32[96,256]{1,0:T(8,128)S(1)} %near_sum.1.rest_refs_0_), channel_id=1, source_target_pairs={{0,8},{8,0},{16,24},{24,16},{1,9},{9,1},{17,25},{25,17},{2,10},{10... | collective-permute-start | bytes 294920 | tf_op jit(solution)/shard_map/ppermute | solution.py:529
  93.0 16.3 %all-to-all-start.2 = ((f32[8,32,256]{2,1,0:T(8,128)}), f32[8,32,256]{2,1,0:T(8,128)S(1)}, u32[]{:S(2)}, u32[]{:S(2)}) async-start(f32[8,32,256]{2,1,0:T(8,128)} %sum_copies.6), calls=%async_computation.2 | async-start | bytes 524288 | tf_op jit(solution)/shard_map/all_to_all | solution.py:461
  96.5 6.6 %collective-permute-start.26 = (f32[32,256]{1,0:T(8,128)S(1)}, f32[32,256]{1,0:T(8,128)S(1)}, u32[]{:S(2)}, u32[]{:S(2)}) collective-permute-start(f32[32,256]{1,0:T(8,128)S(1)} %get-tuple-element.123.refs_0_), channel_id=1, source_target_pairs={{0,24},{8,16},{16,8},{24,0},{1,25},{9,17},{17,9},{25,1},{2,26},{10... | collective-permute-start | bytes 98312 | tf_op jit(solution)/shard_map/ppermute | solution.py:529
  99.3 9.4 %collective-permute-start.23 = (f32[96,256]{1,0:T(8,128)S(1)}, f32[96,256]{1,0:T(8,128)S(1)}, u32[]{:S(2)}, u32[]{:S(2)}) collective-permute-start(f32[96,256]{1,0:T(8,128)S(1)} %get-tuple-element.124.refs_0_), channel_id=1, source_target_pairs={{0,6},{1,7},{2,4},{3,5},{4,2},{5,3},{6,0},{7,1},{8,14},{9,15},{10,... | collective-permute-start | bytes 294920 | tf_op jit(solution)/shard_map/ppermute | solution.py:529
  102.2 6.5 %collective-permute-start.22 = (f32[96,256]{1,0:T(8,128)S(1)}, f32[96,256]{1,0:T(8,128)S(1)}, u32[]{:S(2)}, u32[]{:S(2)}) collective-permute-start(f32[96,256]{1,0:T(8,128)S(1)} %get-tuple-element.124.refs_0_), channel_id=1, source_target_pairs={{0,4},{1,5},{2,6},{3,7},{4,0},{5,1},{6,2},{7,3},{8,12},{9,13},{10,... | collective-permute-start | bytes 294920 | tf_op jit(solution)/shard_map/ppermute | solution.py:529
  102.8 5.9 %collective-permute-start.21 = (f32[96,256]{1,0:T(8,128)S(1)}, f32[96,256]{1,0:T(8,128)S(1)}, u32[]{:S(2)}, u32[]{:S(2)}) collective-permute-start(f32[96,256]{1,0:T(8,128)S(1)} %get-tuple-element.124.refs_0_), channel_id=1, source_target_pairs={{0,2},{1,3},{2,0},{3,1},{4,6},{5,7},{6,4},{7,5},{8,10},{9,11},{10,... | collective-permute-start | bytes 294920 | tf_op jit(solution)/shard_map/ppermute | solution.py:529
  102.8 5.2 %collective-permute-start.25 = (f32[32,256]{1,0:T(8,128)S(1)}, f32[32,256]{1,0:T(8,128)S(1)}, u32[]{:S(2)}, u32[]{:S(2)}) collective-permute-start(f32[32,256]{1,0:T(8,128)S(1)} %get-tuple-element.123.refs_0_), channel_id=1, source_target_pairs={{0,16},{8,24},{16,0},{24,8},{1,17},{9,25},{17,1},{25,9},{2,18},{10... | collective-permute-start | bytes 98312 | tf_op jit(solution)/shard_map/ppermute | solution.py:529
  103.0 4.9 %collective-permute-start.24 = (f32[32,256]{1,0:T(8,128)S(1)}, f32[32,256]{1,0:T(8,128)S(1)}, u32[]{:S(2)}, u32[]{:S(2)}) collective-permute-start(f32[32,256]{1,0:T(8,128)S(1)} %get-tuple-element.123.refs_0_), channel_id=1, source_target_pairs={{0,8},{8,0},{16,24},{24,16},{1,9},{9,1},{17,25},{25,17},{2,10},{10... | collective-permute-start | bytes 98312 | tf_op jit(solution)/shard_map/ppermute | solution.py:529
  108.7 5.0 %copy-start.12 = (f32[256,256]{1,0:T(8,128)S(1)}, f32[256,256]{1,0:T(8,128)}, u32[]{:S(2)}) copy-start(f32[256,256]{1,0:T(8,128)} %copy-done.11) | copy-start | bytes 786436
  109.3 11.7 %collective-permute-start.27 = (f32[384,256]{1,0:T(8,128)S(1)}, f32[384,256]{1,0:T(8,128)S(1)}, u32[]{:S(2)}, u32[]{:S(2)}) collective-permute-start(f32[384,256]{1,0:T(8,128)S(1)} %merge_pieces.1.mine_ref), channel_id=1, source_target_pairs={{0,1},{1,0},{2,3},{3,2},{4,5},{5,4},{6,7},{7,6},{8,9},{9,8},{10,11... | collective-permute-start | bytes 1179656 | tf_op jit(solution)/shard_map/ppermute | solution.py:614
  109.4 11.6 %all-to-all-start.3 = ((f32[8,32,256]{2,1,0:T(8,128)}), f32[8,32,256]{2,1,0:T(8,128)S(1)}, u32[]{:S(2)}, u32[]{:S(2)}) async-start(f32[8,32,256]{2,1,0:T(8,128)} %sum_copies.7), calls=%async_computation.3 | async-start | bytes 524288 | tf_op jit(solution)/shard_map/all_to_all | solution.py:461
  (14 other events, 14.4 us)

commit v8 on v5

--- a/solution.py
+++ b/solution.py
@@ -142,12 +142,11 @@
     return jax.ShapeDtypeStruct((size, size), jnp.float32)
 
 
-def first_kernel(parts_ref, upper_out, inv_ref, gram_ref, upper_ref, work_ref, sems):
+def first_kernel(parts_ref, upper_ref, inv_ref, gram_ref, work_ref):
     strip = parts_ref.shape[1]
     for c in range(parts_ref.shape[0]):
         gram_ref[c * strip : (c + 1) * strip, :] = parts_ref[c]
     chol_kernel(gram_ref, upper_ref, inv_ref, work_ref)
-    wait(move([(upper_ref, upper_out)], sems))
 
 
 def cholesky(parts):
@@ -155,9 +154,8 @@
     return pl.pallas_call(
         first_kernel,
         in_specs=[VMEM],
-        out_specs=(HBM, VMEM),
         out_shape=(square(size), square(size)),
-        scratch_shapes=[pltpu.VMEM((size, size), jnp.float32)] * 3 + [pltpu.SemaphoreType.DMA((1,))],
+        scratch_shapes=[pltpu.VMEM((size, size), jnp.float32)] * 2,
         compiler_params=SMALL,
         cost_estimate=estimate(10),
         name="cholesky_inverse",
@@ -185,7 +183,7 @@
 
     def more(state):
         count, _, _, _, worst = state
-        return jnp.logical_not(worst < 1e-5) & (count < 8)
+        return jnp.logical_not(worst < 1e-8) & (count < 10)
 
     def step(state):
         count, inv, _, low, _ = state
@@ -202,7 +200,7 @@
     upper = upper + mult3(split(low), split(upper), TURNED)
     upper_ref[...] = jnp.where(row <= col, upper, 0.0)
 
-    @pl.when(jnp.logical_not(worst < 1e-5))
+    @pl.when(jnp.logical_not(worst < 1e-8))
     def _():
         chol_kernel(gram_ref, upper_ref, inv_ref, work_ref)
 
@@ -219,22 +217,15 @@
     )(gram)
 
 
-def factor_kernel(parts_ref, inv_ref, upper_ref, first_ref, out_ref, band_ref,
-                  first, out, band, sems):
-    fetch = move([(first_ref, first)], sems)
+def factor_kernel(gram_ref, top_ref, inv_ref, upper_ref, first_ref, out_ref, band_ref):
     size = inv_ref.shape[0]
-    strip = size // parts_ref.shape[0]
     row, col = grids(size)
     ident = jnp.where(row == col, 1.0, 0.0)
-    pieces = range(parts_ref.shape[0])
-    gram = jnp.concatenate([parts_ref[c, :strip, :] for c in pieces], axis=0)
-    top = jnp.concatenate([parts_ref[c, strip:, :] for c in pieces], axis=0)
+    band_ref[...] = -mult(upper_ref[...], first_ref[...])
+    top = top_ref[...].reshape(size, size)
     half_top = mult(top, inv_ref[...], ACROSS)
-    mat = gram + mult(half_top, upper_ref[...], TURNED)
+    mat = gram_ref[...].reshape(size, size) + mult3(split(half_top), split(upper_ref[...]), TURNED)
     halves = split(mat)
-    wait(fetch)
-    band[...] = -mult(upper_ref[...], first[...])
-    store = move([(band, band_ref)], sems)
 
     def residual(guess):
         return ident - mult3(halves, split(guess))
@@ -258,22 +249,17 @@
     guess = guess + mult3(split(guess), split(rest))
     rest = residual(guess)
     state = (jnp.int32(0), guess, rest, jnp.max(jnp.abs(rest)))
-    out[...] = lax.while_loop(more, step, state)[1]
-    wait(store + move([(out, out_ref)], sems.at[pl.ds(1, 1)]))
-
-
-def compact_factor(parts, inv, upper, first):
-    size = inv.shape[0]
+    out_ref[...] = lax.while_loop(more, step, state)[1]
+
+
+def compact_factor(gram, top, inv, upper, first):
     return pl.pallas_call(
         factor_kernel,
-        in_specs=[VMEM] * 3 + [HBM],
-        out_specs=(HBM, HBM),
-        out_shape=(square(size), square(size)),
-        scratch_shapes=[pltpu.VMEM((size, size), jnp.float32)] * 3 + [pltpu.SemaphoreType.DMA((2,))],
+        out_shape=(square(inv.shape[0]), square(inv.shape[0])),
         compiler_params=SMALL,
         cost_estimate=estimate(4),
         name="compact_factor",
-    )(parts, inv, upper, first)
+    )(gram, top, inv, upper, first)
 
 
 def array(*dims):
@@ -451,29 +437,25 @@
     )(*totals, *pieces)
 
 
-def spread_kernel(groups, *refs):
+def spread_kernel(first, last, *refs):
     out_ref = refs[-1]
-    start = 0
-    for count, first, last in groups:
-        total = tree_sum([ref[first:last, :] for ref in refs[:count]])
-        refs = refs[count:]
-        for c in range(out_ref.shape[0]):
-            out_ref[c, start : start + last - first, :] = total
-        start += last - first
-
-
-def sum_gather(cols, *groups):
-    terms = [term for group in groups for term in group[0]]
-    bounds = [(len(group[0]), group[1], group[2]) for group in groups]
-    height = sum(last - first for _, first, last in bounds)
-    copies = pl.pallas_call(
-        functools.partial(spread_kernel, bounds),
+    total = tree_sum([ref[first:last, :] for ref in refs[:-1]])
+    for c in range(out_ref.shape[0]):
+        out_ref[c] = total
+
+
+def sum_copies(cols, terms, first, last):
+    return pl.pallas_call(
+        functools.partial(spread_kernel, first, last),
         in_specs=[VMEM] * len(terms),
-        out_shape=array(cols, height, terms[0].shape[1]),
+        out_shape=array(cols, last - first, terms[0].shape[1]),
         compiler_params=LARGE,
         cost_estimate=estimate(0.5),
         name="sum_copies",
     )(*terms)
+
+
+def trade(copies):
     return lax.all_to_all(copies, "col", 0, 0, tiled=True)
 
 
@@ -497,98 +479,45 @@
     )(place, *pieces)
 
 
-def base_kernel(place_ref, ham_ref, left_in, mine_ref, other_ref, right_in, factor_in, *rest_refs):
-    piece_refs, out_hbm = rest_refs[:-7], rest_refs[-7]
-    left_ref, right_ref, factor_ref, near_ref, out_ref, sems = rest_refs[-6:]
-    fetch = move([(factor_in, factor_ref), (right_in, right_ref), (left_in, left_ref)], sems)
+def update_kernel(
+    place_ref, ham_ref, left_ref, mine_ref, other_ref, right_ref, factor_ref,
+    parts_ref, *rest_refs
+):
+    piece_refs, (out_ref, near_ref, sum_ref) = rest_refs[:-3], rest_refs[-3:]
     deep = mine_ref.shape[0]
     share = near_ref.shape[0] // len(piece_refs)
     row_place, core = place_ref[0], place_ref[1] & 1
     for hop, ref in enumerate(piece_refs):
         start = pl.multiple_of((row_place ^ hop) * share, share)
         near_ref[pl.ds(start, share), :] = ref[:share, :]
-    fetch[0].wait()
+    strip = parts_ref.shape[1]
+    chips = parts_ref.shape[0] // 2
+    for c in range(parts_ref.shape[0]):
+        start = ((c % 2) * chips + c // 2) * strip
+        sum_ref[start : start + strip, :] = parts_ref[c]
     factor = split(factor_ref[...])
-    near = split(mult3(split(near_ref[...]), factor))
-    fetch[1].wait()
-    far = split(mult3(split(right_ref[...]), factor, ACROSS))
-    fetch[2].wait()
+    right = split(right_ref[...])
+    turn = mult3(split(sum_ref[...]), factor)
+    middle = mult3(factor, split(turn), TURNED)
+    near = split(mult3(split(near_ref[...]), factor) - mult3(right, split(middle)))
+    far = split(mult3(right, factor, ACROSS))
     for place, prod_ref in ((core, mine_ref), (1 - core, other_ref)):
         block = pl.ds(pl.multiple_of(place * deep, deep), deep)
         change = mult3(split(left_ref[block, :]), near, ACROSS)
         change = change + mult3(split(prod_ref[...]), far, ACROSS)
         out_ref[block, :] = ham_ref[block, :] - change
-    wait(move([(out_ref, out_hbm)], sems))
-
-
-def base_update(place, hamiltonian, left, mine, other, right, factor, pieces):
-    return pl.pallas_call(
-        base_kernel,
-        in_specs=[SMEM, VMEM, HBM, VMEM, VMEM, HBM, HBM] + [VMEM] * len(pieces),
-        out_specs=HBM,
+
+
+def update(place, hamiltonian, left, mine, other, right, factor, parts, pieces):
+    return pl.pallas_call(
+        update_kernel,
+        in_specs=[SMEM] + [VMEM] * (7 + len(pieces)),
         out_shape=array(*hamiltonian.shape),
-        scratch_shapes=[
-            scratch(*left.shape),
-            scratch(*right.shape),
-            scratch(*factor.shape),
-            scratch(*right.shape),
-            scratch(*hamiltonian.shape),
-            pltpu.SemaphoreType.DMA((3,)),
-        ],
+        scratch_shapes=[scratch(*right.shape), scratch(*factor.shape)],
         compiler_params=LARGE,
         cost_estimate=estimate(4),
-        name="base_update",
-    )(place, hamiltonian, left, mine, other, right, factor, *pieces)
-
-
-def coupling_kernel(base_in, left_in, right_in, factor_in, parts_ref, out_hbm,
-                    base_ref, left_ref, right_ref, factor_ref, sum_ref, sems):
-    fetch = move(
-        [(factor_in, factor_ref), (right_in, right_ref), (left_in, left_ref), (base_in, base_ref)],
-        sems,
-    )
-    strip = parts_ref.shape[1]
-    chips = parts_ref.shape[0] // 2
-    for c in range(parts_ref.shape[0]):
-        start = ((c % 2) * chips + c // 2) * strip
-        sum_ref[start : start + strip, :] = parts_ref[c]
-    fetch[0].wait()
-    factor = split(factor_ref[...])
-    turn = mult3(split(sum_ref[...]), factor)
-    middle = mult3(factor, split(turn), TURNED)
-    fetch[1].wait()
-    near = split(mult3(split(right_ref[...]), split(middle)))
-    fetch[2].wait()
-    fetch[3].wait()
-    deep = base_ref.shape[0] // 2
-    stores = []
-    for half in range(2):
-        block = pl.ds(half * deep, deep)
-        base_ref[block, :] += mult3(split(left_ref[block, :]), near, ACROSS)
-        copy = pltpu.make_async_copy(base_ref.at[block], out_hbm.at[block], sems.at[half])
-        copy.start()
-        stores.append(copy)
-    wait(stores)
-
-
-def coupling_update(base, left, right, factor, parts):
-    return pl.pallas_call(
-        coupling_kernel,
-        in_specs=[HBM] * 4 + [VMEM],
-        out_specs=HBM,
-        out_shape=array(*base.shape),
-        scratch_shapes=[
-            scratch(*base.shape),
-            scratch(*left.shape),
-            scratch(*right.shape),
-            scratch(*factor.shape),
-            scratch(*factor.shape),
-            pltpu.SemaphoreType.DMA((4,)),
-        ],
-        compiler_params=LARGE,
-        cost_estimate=estimate(3),
-        name="coupling_update",
-    )(base, left, right, factor, parts)
+        name="two_sided_update",
+    )(place, hamiltonian, left, mine, other, right, factor, parts, *pieces)
 
 
 def hops(values, axis, size, scale=1):
@@ -633,30 +562,37 @@
         having = having + [d ^ hop for d in having]
         hop //= 2
 
-    gram = sum_gather(cols, (strips, 0, strip))
+    gram = trade(sum_copies(cols, strips, 0, strip))
     first_upper, first_inv = cholesky(gram)
     half, half_cols, gram2_strip = half_stage(place, panel, slab, got, first_inv, cols)
     gram2_strips = hops([gram2_strip] * rows, "row", rows)
-    parts = sum_gather(cols, (gram2_strips, 0, strip), (strips, strip, 2 * strip))
-    gram2 = parts[:, :strip].reshape(width, width)
-    second_upper = near_cholesky(gram2)
+    gram2 = trade(sum_copies(cols, gram2_strips, 0, strip))
+    second_upper = near_cholesky(gram2.reshape(width, width))
 
     left, right, keep, send, pieces = products(
         place, hamiltonian, half, half_cols, second_upper, rows, cols
     )
-    parts, send = lax.optimization_barrier((parts, send))
-    factor, band_block = compact_factor(parts, first_inv, second_upper, first_upper)
-    totals = pair_add(keep, lax.ppermute(send, "col", pair))
-    totals = hops(totals, "col", cols, 2)
+    got = lax.ppermute(send, "col", pair)
     pieces = hops(pieces, "row", rows)
+    got, pieces[:3] = lax.optimization_barrier((got, pieces[:3]))
+    totals = hops(pair_add(keep, got), "col", cols, 2)
+
+    late = lax.optimization_barrier(tuple(strips) + (totals[0],))
+    top = sum_copies(cols, late[:-1], strip, 2 * strip)
+    totals, top = lax.optimization_barrier((totals, top))
+    top = trade(top)
     mine, both = sum_pieces(totals, pieces, piece)
     both = hops([both] * rows, "row", rows)
-    mine = merge(place, hops([mine] * chips, "col", cols, 2))
+    mine, both[1] = lax.optimization_barrier((mine, both[1]))
+    factor, band_block = compact_factor(gram2, top, first_inv, second_upper, first_upper)
+    both, factor = lax.optimization_barrier((both, factor))
+    coupling = sum_copies(cols, both, share, share + strip)
+    mine = hops([mine] * chips, "col", cols, 2)
+    mine, _ = lax.optimization_barrier((mine, coupling))
+    coupling = trade(coupling)
+    mine = merge(place, mine)
     other = lax.ppermute(mine, "col", pair)
-    both, factor = lax.optimization_barrier((both, factor))
-    coupling = sum_gather(cols, (both, share, share + strip))
-    base = base_update(place, hamiltonian, left, mine, other, right, factor, both)
-    updated = coupling_update(base, left, right, factor, coupling)
+    updated = update(place, hamiltonian, left, mine, other, right, factor, coupling, both)
     return (updated, band_block)
 
 

time: 118 us -> 120 us (1.017)
  blocking collectives: 12.2 us -> 20.1 us
  local copies, waits for them, and re-layouts: 8.76 us -> 3.75 us
  waiting for transfers between devices: 21.6 us -> 25.2 us
  starting transfers between devices: 39.6 us -> 37.3 us
  Pallas kernels: 34.4 us -> 32.3 us
    all_to_all x1 -> x2, blocking collectives: 12.2 us -> 20.1 us  [trade(): return lax.all_to_all(copies, 'col', 0, 0, tiled=True)]
    unnamed x22, local copies, waits for them, and re-layouts: 8.74 us -> 3.75 us
    ppermute x18, waiting for transfers between devices: 15.7 us -> 19.7 us  [hops(): got.append(lax.ppermute(values[hop], axis, pairs))]
    ppermute x18, starting transfers between devices: 27.9 us -> 25.3 us  [hops(): got.append(lax.ppermute(values[hop], axis, pairs))]
    pallas_call x7, Pallas kernels: 21.8 us -> 19.9 us  [the longest x1 9.68 us: cholesky(): pl.pallas_call(first_kernel, in_specs=[VMEM], out_shape=(square(size), sq...]
  transfers between devices with their start and end apart: 24 -> 24, of which waited for: 9 -> 11; matrix products, arithmetic and copies ran while one was open for 0% -> 0% of each run, Pallas kernels for 16% -> 13%
where the time goes in v8:
time: 120 us
  starting transfers between devices  37.3 us (31%)
  Pallas kernels  32.3 us (27%)
  waiting for transfers between devices  25.2 us (21%)
  blocking collectives  20.1 us (17%)
  local copies, waits for them, and re-layouts  3.75 us (3%)
    ppermute x18, starting transfers between devices, hops(): got.append(lax.ppermute(values[hop], axis, pairs))  25.3 us
    all_to_all x2, blocking collectives, trade(): return lax.all_to_all(copies, 'col', 0, 0, tiled=True)  20.1 us
    ppermute x18, waiting for transfers between devices, hops(): got.append(lax.ppermute(values[hop], axis, pairs))  19.7 us
    pallas_call x1, Pallas kernels, cholesky(): pl.pallas_call(first_kernel, in_specs=[VMEM], out_shape=(square(size), sq...  9.68 us
    all_to_all x2, starting transfers between devices, trade(): return lax.all_to_all(copies, 'col', 0, 0, tiled=True)  7.05 us
    ppermute x2, starting transfers between devices, shards(): got = lax.ppermute(slab, ('row', 'col'), pairs)  4.82 us
    pallas_call x1, Pallas kernels, compact_factor(): pl.pallas_call(factor_kernel, out_shape=(square(inv.shape[0]), square(inv...  4.72 us
    pallas_call x1, Pallas kernels, products(): pl.pallas_call(products_kernel, in_specs=[SMEM, VMEM, HBM, HBM, VMEM], ou...  4.29 us
  transfers between devices with their start and end apart: 24, of which 11 were waited for; matrix products, arithmetic and copies ran while one was open for 0% of the time, Pallas kernels for 13%

profile of v8, /device:TPU:0, one launch (start us, length us, event | category | flops | bytes accessed | tf_op | source)
XLA Modules:
  0.0 119.6 jit_solution(2567488166282113366)
XLA Ops:
  0.6 0.1 pad_add_fusion.place_ref
  0.7 1.1 copy-done
  1.8 1.5 %gram_strips.1.refs_0_ = f32[64,256]{1,0:T(8,128)S(1)} custom-call(s32[2]{0:T(128)S(1)} %pad_add_fusion.place_ref, f32[768,256]{1,0:T(8,128)S(1)} %copy-done), custom_call_target="tpu_custom_call" | custom-call | flops 2000000000 | bytes 6000000 | tf_op jit(solution)/shard_map/gram_strips/pallas_call | solution.py:283
  3.3 5.1 %collective-permute-start.2 = (f32[64,256]{1,0:T(8,128)S(1)}, f32[64,256]{1,0:T(8,128)S(1)}, u32[]{:S(2)}, u32[]{:S(2)}) collective-permute-start(f32[64,256]{1,0:T(8,128)S(1)} %gram_strips.1.refs_0_), channel_id=1, source_target_pairs={{0,24},{8,16},{16,8},{24,0},{1,25},{9,17},{17,9},{25,1},{2,26},{10... | collective-permute-start | bytes 196616 | tf_op jit(solution)/shard_map/ppermute | solution.py:527
  8.4 0.6 collective-permute-start
  9.1 1.9 %collective-permute-done.2.refs_3_ = f32[64,256]{1,0:T(8,128)S(1)} collective-permute-done((f32[64,256]{1,0:T(8,128)S(1)}, f32[64,256]{1,0:T(8,128)S(1)}, u32[]{:S(2)}, u32[]{:S(2)}) %collective-permute-start.2) | collective-permute-done | bytes 65568 | tf_op jit(solution)/shard_map/ppermute | solution.py:527
  11.0 3.0 %collective-permute-done.1.refs_2_ = f32[64,256]{1,0:T(8,128)S(1)} collective-permute-done((f32[64,256]{1,0:T(8,128)S(1)}, f32[64,256]{1,0:T(8,128)S(1)}, u32[]{:S(2)}, u32[]{:S(2)}) %collective-permute-start.1) | collective-permute-done | bytes 65568 | tf_op jit(solution)/shard_map/ppermute | solution.py:527
  14.0 3.5 %collective-permute-start.3 = (f32[384,256]{1,0:T(8,128)S(1)}, f32[384,256]{1,0:T(8,128)S(1)}, u32[]{:S(2)}, u32[]{:S(2)}) collective-permute-start(f32[384,256]{1,0:T(8,128)S(1)} %dynamic-slice_select_fusion), channel_id=1, source_target_pairs={{0,16},{1,17},{10,26},{11,27},{20,4},{21,5},{30,14},{31,15}} | collective-permute-start | bytes 1179656 | tf_op jit(solution)/shard_map/ppermute | solution.py:561
  17.5 0.7 sum_copies.4
  18.3 3.4 %all-to-all-start = ((f32[8,32,256]{2,1,0:T(8,128)}), f32[8,32,256]{2,1,0:T(8,128)S(1)}, u32[]{:S(2)}, u32[]{:S(2)}) async-start(f32[8,32,256]{2,1,0:T(8,128)} %sum_copies.4), calls=%async_computation | async-start | bytes 524288 | tf_op jit(solution)/shard_map/all_to_all | solution.py:459
  21.7 2.8 %collective-permute-done.3 = f32[384,256]{1,0:T(8,128)S(1)} collective-permute-done((f32[384,256]{1,0:T(8,128)S(1)}, f32[384,256]{1,0:T(8,128)S(1)}, u32[]{:S(2)}, u32[]{:S(2)}) %collective-permute-start.3) | collective-permute-done | bytes 393248 | tf_op jit(solution)/shard_map/ppermute | solution.py:561
  24.5 1.3 %collective-permute-start.4 = (f32[384,256]{1,0:T(8,128)S(1)}, f32[384,256]{1,0:T(8,128)S(1)}, u32[]{:S(2)}, u32[]{:S(2)}) collective-permute-start(f32[384,256]{1,0:T(8,128)S(1)} %add.8.slab_ref), channel_id=1, source_target_pairs={{0,8},{16,24},{1,9},{17,25},{10,2},{26,18},{11,3},{27,19},{20,28},... | collective-permute-start | bytes 1179656 | tf_op jit(solution)/shard_map/ppermute | solution.py:561
  25.8 2.7 %all-to-all-done.parts_ref = f32[8,32,256]{2,1,0:T(8,128)S(1)} async-done(((f32[8,32,256]{2,1,0:T(8,128)}), f32[8,32,256]{2,1,0:T(8,128)S(1)}, u32[]{:S(2)}, u32[]{:S(2)}) %all-to-all-start) | async-done | bytes 262176 | tf_op jit(solution)/shard_map/all_to_all | solution.py:459
  28.6 9.7 %cholesky_inverse.1 = (f32[256,256]{1,0:T(8,128)S(1)}, f32[256,256]{1,0:T(8,128)S(1)}) custom-call(f32[8,32,256]{2,1,0:T(8,128)S(1)} %all-to-all-done.parts_ref), custom_call_target="tpu_custom_call" | custom-call | flops 10000000000 | bytes 30000000 | tf_op jit(solution)/shard_map/cholesky_inverse/pallas_call | solution.py:154
  38.3 0.7 copy-done.9
  38.9 3.0 %half_stage.1 = (f32[768,256]{1,0:T(8,128)S(1)}, f32[384,256]{1,0:T(8,128)S(1)}, f32[32,256]{1,0:T(8,128)S(1)}) custom-call(s32[2]{0:T(128)S(1)} %pad_add_fusion.place_ref, f32[768,256]{1,0:T(8,128)S(1)} %copy-done.1, f32[384,256]{1,0:T(8,128)S(1)} %add.8.slab_ref, f32[384,256]{1,0:T(8,128)S(1)} %collective-permute-done.4.got_ref, ...), custom_call_target="tpu_custom_call" | custom-call | flops 3000000000 | bytes 9000000 | tf_op jit(solution)/shard_map/half_stage/pallas_call | solution.py:310
  42.0 2.3 %collective-permute-start.7 = (f32[32,256]{1,0:T(8,128)S(1)}, f32[32,256]{1,0:T(8,128)S(1)}, u32[]{:S(2)}, u32[]{:S(2)}) collective-permute-start(f32[32,256]{1,0:T(8,128)S(1)} %get-tuple-element.60.refs_0_), channel_id=1, source_target_pairs={{0,24},{8,16},{16,8},{24,0},{1,25},{9,17},{17,9},{25,1},{2,26},{10... | collective-permute-start | bytes 98312 | tf_op jit(solution)/shard_map/ppermute | solution.py:527
  44.3 0.3 collective-permute-start.6
  44.6 1.8 %collective-permute-start.5 = (f32[32,256]{1,0:T(8,128)S(1)}, f32[32,256]{1,0:T(8,128)S(1)}, u32[]{:S(2)}, u32[]{:S(2)}) collective-permute-start(f32[32,256]{1,0:T(8,128)S(1)} %get-tuple-element.60.refs_0_), channel_id=1, source_target_pairs={{0,8},{8,0},{16,24},{24,16},{1,9},{9,1},{17,25},{25,17},{2,10},{10... | collective-permute-start | bytes 98312 | tf_op jit(solution)/shard_map/ppermute | solution.py:527
  46.4 1.3 %collective-permute-done.7.refs_3_ = f32[32,256]{1,0:T(8,128)S(1)} collective-permute-done((f32[32,256]{1,0:T(8,128)S(1)}, f32[32,256]{1,0:T(8,128)S(1)}, u32[]{:S(2)}, u32[]{:S(2)}) %collective-permute-start.7) | collective-permute-done | bytes 32800 | tf_op jit(solution)/shard_map/ppermute | solution.py:527
  47.8 1.3 %collective-permute-done.6.refs_2_ = f32[32,256]{1,0:T(8,128)S(1)} collective-permute-done((f32[32,256]{1,0:T(8,128)S(1)}, f32[32,256]{1,0:T(8,128)S(1)}, u32[]{:S(2)}, u32[]{:S(2)}) %collective-permute-start.6) | collective-permute-done | bytes 32800 | tf_op jit(solution)/shard_map/ppermute | solution.py:527
  49.1 9.4 %all_to_all.20.gram_ref = f32[8,32,256]{2,1,0:T(8,128)S(1)} all-to-all(f32[8,32,256]{2,1,0:T(8,128)S(1)} %sum_copies.5), channel_id=1, replica_groups=mesh['row'=4,'col'=8] {'col'}, dimensions={0} | all-to-all | bytes 524288 | tf_op jit(solution)/shard_map/all_to_all | solution.py:459
  58.5 2.9 %near_cholesky.1.upper_ref = f32[256,256]{1,0:T(8,128)S(1)} custom-call(f32[256,256]{1,0:T(8,128)S(1)} %bitcast.3), custom_call_target="tpu_custom_call" | custom-call | flops 3000000000 | bytes 9000000 | tf_op jit(solution)/shard_map/near_cholesky/pallas_call | solution.py:210
  61.4 4.3 %products.1 = (f32[768,256]{1,0:T(8,128)S(1)}, f32[384,256]{1,0:T(8,128)S(1)}, f32[4,128,256]{2,1,0:T(8,128)S(1)}, f32[4,128,256]{2,1,0:T(8,128)S(1)}, f32[96,25...) custom-call(s32[2]{0:T(128)S(1)} %pad_add_fusion.place_ref, ...), custom_call_target="tpu_custom_call" | custom-call | flops 4000000000 | bytes 12000000 | tf_op jit(solution)/shard_map/products/pallas_call | solution.py:369
  65.8 2.0 %collective-permute-start.9 = (f32[96,256]{1,0:T(8,128)S(1)}, f32[96,256]{1,0:T(8,128)S(1)}, u32[]{:S(2)}, u32[]{:S(2)}) collective-permute-start(f32[96,256]{1,0:T(8,128)S(1)} %get-tuple-element.65), channel_id=1, source_target_pairs={{0,8},{8,0},{16,24},{24,16},{1,9},{9,1},{17,25},{25,17},{2,10},{10... | collective-permute-start | bytes 294920 | tf_op jit(solution)/shard_map/ppermute | solution.py:527
  67.8 0.9 collective-permute-start.10
  68.7 2.5 %collective-permute-done.9.refs_5_ = f32[96,256]{1,0:T(8,128)S(1)} collective-permute-done((f32[96,256]{1,0:T(8,128)S(1)}, f32[96,256]{1,0:T(8,128)S(1)}, u32[]{:S(2)}, u32[]{:S(2)}) %collective-permute-start.9) | collective-permute-done | bytes 98336 | tf_op jit(solution)/shard_map/ppermute | solution.py:527
  71.2 4.5 %collective-permute-done.10.refs_6_ = f32[96,256]{1,0:T(8,128)S(1)} collective-permute-done((f32[96,256]{1,0:T(8,128)S(1)}, f32[96,256]{1,0:T(8,128)S(1)}, u32[]{:S(2)}, u32[]{:S(2)}) %collective-permute-start.10) | collective-permute-done | bytes 98336 | tf_op jit(solution)/shard_map/ppermute | solution.py:527
  75.7 0.6 collective-permute-start.11
  76.4 0.6 collective-permute-start.12
  76.9 2.4 %collective-permute-start.13 = (f32[128,256]{1,0:T(8,128)S(1)}, f32[128,256]{1,0:T(8,128)S(1)}, u32[]{:S(2)}, u32[]{:S(2)}) collective-permute-start(f32[128,256]{1,0:T(8,128)S(1)} %get-tuple-element.71), channel_id=1, source_target_pairs={{0,6},{1,7},{2,4},{3,5},{4,2},{5,3},{6,0},{7,1},{8,14},{9,15},{10,... | collective-permute-start | bytes 393224 | tf_op jit(solution)/shard_map/ppermute | solution.py:527
  79.3 1.6 %collective-permute-start.14 = (f32[96,256]{1,0:T(8,128)S(1)}, f32[96,256]{1,0:T(8,128)S(1)}, u32[]{:S(2)}, u32[]{:S(2)}) collective-permute-start(f32[96,256]{1,0:T(8,128)S(1)} %get-tuple-element.83), channel_id=1, source_target_pairs={{0,24},{8,16},{16,8},{24,0},{1,25},{9,17},{17,9},{25,1},{2,26},{10... | collective-permute-start | bytes 294920 | tf_op jit(solution)/shard_map/ppermute | solution.py:527
  80.9 0.7 sum_copies.6
  81.6 0.5 collective-permute-done.11.refs_1_
  82.1 1.7 %collective-permute-done.12.refs_2_ = f32[128,256]{1,0:T(8,128)S(1)} collective-permute-done((f32[128,256]{1,0:T(8,128)S(1)}, f32[128,256]{1,0:T(8,128)S(1)}, u32[]{:S(2)}, u32[]{:S(2)}) %collective-permute-start.12) | collective-permute-done | bytes 131104 | tf_op jit(solution)/shard_map/ppermute | solution.py:527
  83.8 3.6 %all-to-all-start.2 = ((f32[8,32,256]{2,1,0:T(8,128)}), f32[8,32,256]{2,1,0:T(8,128)S(1)}, u32[]{:S(2)}, u32[]{:S(2)}) async-start(f32[8,32,256]{2,1,0:T(8,128)} %sum_copies.6), calls=%async_computation.2 | async-start | bytes 524288 | tf_op jit(solution)/shard_map/all_to_all | solution.py:459
  87.6 1.9 %collective-permute-start.20 = (f32[128,256]{1,0:T(8,128)S(1)}, f32[128,256]{1,0:T(8,128)S(1)}, u32[]{:S(2)}, u32[]{:S(2)}) collective-permute-start(f32[128,256]{1,0:T(8,128)S(1)} %get-tuple-element.91.refs_0_.rest_refs_0_), channel_id=1, source_target_pairs={{0,24},{8,16},{16,8},{24,0},{1,25},{9,17},{17,9},{25,1},{2,26},{10... | collective-permute-start | bytes 393224 | tf_op jit(solution)/shard_map/ppermute | solution.py:527
  89.5 1.6 %collective-permute-start.19 = (f32[128,256]{1,0:T(8,128)S(1)}, f32[128,256]{1,0:T(8,128)S(1)}, u32[]{:S(2)}, u32[]{:S(2)}) collective-permute-start(f32[128,256]{1,0:T(8,128)S(1)} %get-tuple-element.91.refs_0_.rest_refs_0_), channel_id=1, source_target_pairs={{0,16},{8,24},{16,0},{24,8},{1,17},{9,25},{17,1},{25,9},{2,18},{10... | collective-permute-start | bytes 393224 | tf_op jit(solution)/shard_map/ppermute | solution.py:527
  91.1 2.9 %collective-permute-done.15.refs_1_.rest_refs_1_ = f32[128,256]{1,0:T(8,128)S(1)} collective-permute-done((f32[128,256]{1,0:T(8,128)S(1)}, f32[128,256]{1,0:T(8,128)S(1)}, u32[]{:S(2)}, u32[]{:S(2)}) %collective-permute-start.15) | collective-permute-done | bytes 131104 | tf_op jit(solution)/shard_map/ppermute | solution.py:527
  94.0 2.6 %collective-permute-start.18 = (f32[96,256]{1,0:T(8,128)S(1)}, f32[96,256]{1,0:T(8,128)S(1)}, u32[]{:S(2)}, u32[]{:S(2)}) collective-permute-start(f32[96,256]{1,0:T(8,128)S(1)} %get-tuple-element.95.refs_0_), channel_id=1, source_target_pairs={{0,6},{1,7},{2,4},{3,5},{4,2},{5,3},{6,0},{7,1},{8,14},{9,15},{10,... | collective-permute-start | bytes 294920 | tf_op jit(solution)/shard_map/ppermute | solution.py:527
  96.6 0.5 collective-permute-start.17
  97.1 0.3 collective-permute-start.16
  97.4 0.9 copy-done.8
  98.4 0.9 copy-done.10
  99.3 4.7 %compact_factor.1 = (f32[256,256]{1,0:T(8,128)S(1)}, f32[256,256]{1,0:T(8,128)}) custom-call(f32[8,32,256]{2,1,0:T(8,128)S(1)} %all_to_all.20.gram_ref, f32[8,32,256]{2,1,0:T(8,128)S(1)} %all-to-all-done.2.top_ref, f32[256,256]{1,0:T(8,128)S(1)} %copy-done.6, f32[256,256]{1,0:T(8,128)S(1)} %copy-done.8, f32[256,256]{1,0:T(8,128)S(1)} %copy-done.10), custom_call_target="tpu_custom_call" | custom-call | flops 4000000000 | bytes 12000000 | tf_op jit(solution)/shard_map/compact_factor/pallas_call | solution.py:256
  104.1 0.6 merge_pieces.1.mine_ref
  104.8 10.7 %all_to_all.21.parts_ref = f32[8,32,256]{2,1,0:T(8,128)S(1)} all-to-all(f32[8,32,256]{2,1,0:T(8,128)S(1)} %sum_copies.7), channel_id=1, replica_groups=mesh['row'=4,'col'=8] {'col'}, dimensions={0} | all-to-all | bytes 524288 | tf_op jit(solution)/shard_map/all_to_all | solution.py:459
  115.5 4.0 %two_sided_update.1 = f32[768,384]{1,0:T(8,128)} custom-call(s32[2]{0:T(128)S(1)} %pad_add_fusion.place_ref, f32[768,384]{1,0:T(8,128)S(1)} %copy-done.2, f32[768,256]{1,0:T(8,128)S(1)} %copy-done.4, f32[384,256]{1,0:T(8,128)S(1)} %merge_pieces.1.mine_ref, f32[384,256]{1,0:T(8,128)S(1)} %collective-permute-done.21.other_ref, ...), custom_call_target="tpu_custom_call" | custom-call | flops 4000000000 | bytes 12000000 | tf_op jit(solution)/shard_map/two_sided_update/pallas_call | solution.py:512
  (41 shorter events, 0.5 us)
Async XLA Ops:
  0.7 1.1 copy-start
  1.8 7.2 %copy-start.1 = (f32[768,256]{1,0:T(8,128)S(1)}, f32[768,256]{1,0:T(8,128)}, u32[]{:S(2)}) copy-start(f32[768,256]{1,0:T(8,128)} %panel_ref.3) | copy-start | bytes 2359300
  3.3 7.7 %collective-permute-start.2 = (f32[64,256]{1,0:T(8,128)S(1)}, f32[64,256]{1,0:T(8,128)S(1)}, u32[]{:S(2)}, u32[]{:S(2)}) collective-permute-start(f32[64,256]{1,0:T(8,128)S(1)} %gram_strips.1.refs_0_), channel_id=1, source_target_pairs={{0,24},{8,16},{16,8},{24,0},{1,25},{9,17},{17,9},{25,1},{2,26},{10... | collective-permute-start | bytes 196616 | tf_op jit(solution)/shard_map/ppermute | solution.py:527
  8.4 5.6 %collective-permute-start.1 = (f32[64,256]{1,0:T(8,128)S(1)}, f32[64,256]{1,0:T(8,128)S(1)}, u32[]{:S(2)}, u32[]{:S(2)}) collective-permute-start(f32[64,256]{1,0:T(8,128)S(1)} %gram_strips.1.refs_0_), channel_id=1, source_target_pairs={{0,16},{8,24},{16,0},{24,8},{1,17},{9,25},{17,1},{25,9},{2,18},{10... | collective-permute-start | bytes 196616 | tf_op jit(solution)/shard_map/ppermute | solution.py:527
  8.4 5.6 %collective-permute-start = (f32[64,256]{1,0:T(8,128)S(1)}, f32[64,256]{1,0:T(8,128)S(1)}, u32[]{:S(2)}, u32[]{:S(2)}) collective-permute-start(f32[64,256]{1,0:T(8,128)S(1)} %gram_strips.1.refs_0_), channel_id=1, source_target_pairs={{0,8},{8,0},{16,24},{24,16},{1,9},{9,1},{17,25},{25,17},{2,10},{10... | collective-permute-start | bytes 196616 | tf_op jit(solution)/shard_map/ppermute | solution.py:527
  14.0 10.4 %collective-permute-start.3 = (f32[384,256]{1,0:T(8,128)S(1)}, f32[384,256]{1,0:T(8,128)S(1)}, u32[]{:S(2)}, u32[]{:S(2)}) collective-permute-start(f32[384,256]{1,0:T(8,128)S(1)} %dynamic-slice_select_fusion), channel_id=1, source_target_pairs={{0,16},{1,17},{10,26},{11,27},{20,4},{21,5},{30,14},{31,15}} | collective-permute-start | bytes 1179656 | tf_op jit(solution)/shard_map/ppermute | solution.py:561
  18.3 10.3 %all-to-all-start = ((f32[8,32,256]{2,1,0:T(8,128)}), f32[8,32,256]{2,1,0:T(8,128)S(1)}, u32[]{:S(2)}, u32[]{:S(2)}) async-start(f32[8,32,256]{2,1,0:T(8,128)} %sum_copies.4), calls=%async_computation | async-start | bytes 524288 | tf_op jit(solution)/shard_map/all_to_all | solution.py:459
  24.5 14.4 %collective-permute-start.4 = (f32[384,256]{1,0:T(8,128)S(1)}, f32[384,256]{1,0:T(8,128)S(1)}, u32[]{:S(2)}, u32[]{:S(2)}) collective-permute-start(f32[384,256]{1,0:T(8,128)S(1)} %add.8.slab_ref), channel_id=1, source_target_pairs={{0,8},{16,24},{1,9},{17,25},{10,2},{26,18},{11,3},{27,19},{20,28},... | collective-permute-start | bytes 1179656 | tf_op jit(solution)/shard_map/ppermute | solution.py:561
  38.2 0.7 copy-start.9
  38.9 3.0 %copy-start.5 = (f32[256,256]{1,0:T(8,128)}, f32[256,256]{1,0:T(8,128)S(1)}, u32[]{:S(2)}) copy-start(f32[256,256]{1,0:T(8,128)S(1)} %get-tuple-element.57.inv_ref) | copy-start | bytes 786436
  42.0 5.8 %collective-permute-start.7 = (f32[32,256]{1,0:T(8,128)S(1)}, f32[32,256]{1,0:T(8,128)S(1)}, u32[]{:S(2)}, u32[]{:S(2)}) collective-permute-start(f32[32,256]{1,0:T(8,128)S(1)} %get-tuple-element.60.refs_0_), channel_id=1, source_target_pairs={{0,24},{8,16},{16,8},{24,0},{1,25},{9,17},{17,9},{25,1},{2,26},{10... | collective-permute-start | bytes 98312 | tf_op jit(solution)/shard_map/ppermute | solution.py:527
  44.3 4.8 %collective-permute-start.6 = (f32[32,256]{1,0:T(8,128)S(1)}, f32[32,256]{1,0:T(8,128)S(1)}, u32[]{:S(2)}, u32[]{:S(2)}) collective-permute-start(f32[32,256]{1,0:T(8,128)S(1)} %get-tuple-element.60.refs_0_), channel_id=1, source_target_pairs={{0,16},{8,24},{16,0},{24,8},{1,17},{9,25},{17,1},{25,9},{2,18},{10... | collective-permute-start | bytes 98312 | tf_op jit(solution)/shard_map/ppermute | solution.py:527
  44.6 4.5 %collective-permute-start.5 = (f32[32,256]{1,0:T(8,128)S(1)}, f32[32,256]{1,0:T(8,128)S(1)}, u32[]{:S(2)}, u32[]{:S(2)}) collective-permute-start(f32[32,256]{1,0:T(8,128)S(1)} %get-tuple-element.60.refs_0_), channel_id=1, source_target_pairs={{0,8},{8,0},{16,24},{24,16},{1,9},{9,1},{17,25},{25,17},{2,10},{10... | collective-permute-start | bytes 98312 | tf_op jit(solution)/shard_map/ppermute | solution.py:527
  58.5 2.9 %copy-start.2 = (f32[768,384]{1,0:T(8,128)S(1)}, f32[768,384]{1,0:T(8,128)}, u32[]{:S(2)}) copy-start(f32[768,384]{1,0:T(8,128)} %ham_ref.3) | copy-start | bytes 3538948
  61.4 4.3 %copy-start.7 = (f32[256,256]{1,0:T(8,128)}, f32[256,256]{1,0:T(8,128)S(1)}, u32[]{:S(2)}) copy-start(f32[256,256]{1,0:T(8,128)S(1)} %near_cholesky.1.upper_ref) | copy-start | bytes 786436
  65.7 15.1 %copy-start.3 = (f32[768,256]{1,0:T(8,128)}, f32[768,256]{1,0:T(8,128)S(1)}, u32[]{:S(2)}) copy-start(f32[768,256]{1,0:T(8,128)S(1)} %get-tuple-element.61.left_ref) | copy-start | bytes 2359300
  65.7 9.9 %collective-permute-start.8 = (f32[4,128,256]{2,1,0:T(8,128)S(1)}, f32[4,128,256]{2,1,0:T(8,128)S(1)}, u32[]{:S(2)}, u32[]{:S(2)}) collective-permute-start(f32[4,128,256]{2,1,0:T(8,128)S(1)} %get-tuple-element.63), channel_id=1, source_target_pairs={{0,1},{1,0},{2,3},{3,2},{4,5},{5,4},{6,7},{7,6},{8,9},{9,8},{10,11... | collective-permute-start | bytes 1572872 | tf_op jit(solution)/shard_map/ppermute | solution.py:575
  65.8 5.4 %collective-permute-start.9 = (f32[96,256]{1,0:T(8,128)S(1)}, f32[96,256]{1,0:T(8,128)S(1)}, u32[]{:S(2)}, u32[]{:S(2)}) collective-permute-start(f32[96,256]{1,0:T(8,128)S(1)} %get-tuple-element.65), channel_id=1, source_target_pairs={{0,8},{8,0},{16,24},{24,16},{1,9},{9,1},{17,25},{25,17},{2,10},{10... | collective-permute-start | bytes 294920 | tf_op jit(solution)/shard_map/ppermute | solution.py:527
  67.8 7.9 %collective-permute-start.10 = (f32[96,256]{1,0:T(8,128)S(1)}, f32[96,256]{1,0:T(8,128)S(1)}, u32[]{:S(2)}, u32[]{:S(2)}) collective-permute-start(f32[96,256]{1,0:T(8,128)S(1)} %get-tuple-element.66), channel_id=1, source_target_pairs={{0,16},{8,24},{16,0},{24,8},{1,17},{9,25},{17,1},{25,9},{2,18},{10... | collective-permute-start | bytes 294920 | tf_op jit(solution)/shard_map/ppermute | solution.py:527
  75.7 6.4 %collective-permute-start.11 = (f32[128,256]{1,0:T(8,128)S(1)}, f32[128,256]{1,0:T(8,128)S(1)}, u32[]{:S(2)}, u32[]{:S(2)}) collective-permute-start(f32[128,256]{1,0:T(8,128)S(1)} %get-tuple-element.69), channel_id=1, source_target_pairs={{0,2},{1,3},{2,0},{3,1},{4,6},{5,7},{6,4},{7,5},{8,10},{9,11},{10,... | collective-permute-start | bytes 393224 | tf_op jit(solution)/shard_map/ppermute | solution.py:527
  76.4 7.5 %collective-permute-start.12 = (f32[128,256]{1,0:T(8,128)S(1)}, f32[128,256]{1,0:T(8,128)S(1)}, u32[]{:S(2)}, u32[]{:S(2)}) collective-permute-start(f32[128,256]{1,0:T(8,128)S(1)} %get-tuple-element.70), channel_id=1, source_target_pairs={{0,4},{1,5},{2,6},{3,7},{4,0},{5,1},{6,2},{7,3},{8,12},{9,13},{10,... | collective-permute-start | bytes 393224 | tf_op jit(solution)/shard_map/ppermute | solution.py:527
  76.9 6.9 %collective-permute-start.13 = (f32[128,256]{1,0:T(8,128)S(1)}, f32[128,256]{1,0:T(8,128)S(1)}, u32[]{:S(2)}, u32[]{:S(2)}) collective-permute-start(f32[128,256]{1,0:T(8,128)S(1)} %get-tuple-element.71), channel_id=1, source_target_pairs={{0,6},{1,7},{2,4},{3,5},{4,2},{5,3},{6,0},{7,1},{8,14},{9,15},{10,... | collective-permute-start | bytes 393224 | tf_op jit(solution)/shard_map/ppermute | solution.py:527
  79.3 8.2 %collective-permute-start.14 = (f32[96,256]{1,0:T(8,128)S(1)}, f32[96,256]{1,0:T(8,128)S(1)}, u32[]{:S(2)}, u32[]{:S(2)}) collective-permute-start(f32[96,256]{1,0:T(8,128)S(1)} %get-tuple-element.83), channel_id=1, source_target_pairs={{0,24},{8,16},{16,8},{24,0},{1,25},{9,17},{17,9},{25,1},{2,26},{10... | collective-permute-start | bytes 294920 | tf_op jit(solution)/shard_map/ppermute | solution.py:527
  81.6 15.8 %copy-start.6 = (f32[256,256]{1,0:T(8,128)S(1)}, f32[256,256]{1,0:T(8,128)}, u32[]{:S(2)}) copy-start(f32[256,256]{1,0:T(8,128)} %copy-done.5) | copy-start | bytes 786436
  83.8 13.6 %all-to-all-start.2 = ((f32[8,32,256]{2,1,0:T(8,128)}), f32[8,32,256]{2,1,0:T(8,128)S(1)}, u32[]{:S(2)}, u32[]{:S(2)}) async-start(f32[8,32,256]{2,1,0:T(8,128)} %sum_copies.6), calls=%async_computation.2 | async-start | bytes 524288 | tf_op jit(solution)/shard_map/all_to_all | solution.py:459
  87.5 6.4 %collective-permute-start.15 = (f32[128,256]{1,0:T(8,128)S(1)}, f32[128,256]{1,0:T(8,128)S(1)}, u32[]{:S(2)}, u32[]{:S(2)}) collective-permute-start(f32[128,256]{1,0:T(8,128)S(1)} %get-tuple-element.91.refs_0_.rest_refs_0_), channel_id=1, source_target_pairs={{0,8},{8,0},{16,24},{24,16},{1,9},{9,1},{17,25},{25,17},{2,10},{10... | collective-permute-start | bytes 393224 | tf_op jit(solution)/shard_map/ppermute | solution.py:527
  87.6 16.5 %collective-permute-start.20 = (f32[128,256]{1,0:T(8,128)S(1)}, f32[128,256]{1,0:T(8,128)S(1)}, u32[]{:S(2)}, u32[]{:S(2)}) collective-permute-start(f32[128,256]{1,0:T(8,128)S(1)} %get-tuple-element.91.refs_0_.rest_refs_0_), channel_id=1, source_target_pairs={{0,24},{8,16},{16,8},{24,0},{1,25},{9,17},{17,9},{25,1},{2,26},{10... | collective-permute-start | bytes 393224 | tf_op jit(solution)/shard_map/ppermute | solution.py:527
  89.5 14.5 %collective-permute-start.19 = (f32[128,256]{1,0:T(8,128)S(1)}, f32[128,256]{1,0:T(8,128)S(1)}, u32[]{:S(2)}, u32[]{:S(2)}) collective-permute-start(f32[128,256]{1,0:T(8,128)S(1)} %get-tuple-element.91.refs_0_.rest_refs_0_), channel_id=1, source_target_pairs={{0,16},{8,24},{16,0},{24,8},{1,17},{9,25},{17,1},{25,9},{2,18},{10... | collective-permute-start | bytes 393224 | tf_op jit(solution)/shard_map/ppermute | solution.py:527
  94.0 10.2 %collective-permute-start.18 = (f32[96,256]{1,0:T(8,128)S(1)}, f32[96,256]{1,0:T(8,128)S(1)}, u32[]{:S(2)}, u32[]{:S(2)}) collective-permute-start(f32[96,256]{1,0:T(8,128)S(1)} %get-tuple-element.95.refs_0_), channel_id=1, source_target_pairs={{0,6},{1,7},{2,4},{3,5},{4,2},{5,3},{6,0},{7,1},{8,14},{9,15},{10,... | collective-permute-start | bytes 294920 | tf_op jit(solution)/shard_map/ppermute | solution.py:527
  96.6 7.5 %collective-permute-start.17 = (f32[96,256]{1,0:T(8,128)S(1)}, f32[96,256]{1,0:T(8,128)S(1)}, u32[]{:S(2)}, u32[]{:S(2)}) collective-permute-start(f32[96,256]{1,0:T(8,128)S(1)} %get-tuple-element.95.refs_0_), channel_id=1, source_target_pairs={{0,4},{1,5},{2,6},{3,7},{4,0},{5,1},{6,2},{7,3},{8,12},{9,13},{10,... | collective-permute-start | bytes 294920 | tf_op jit(solution)/shard_map/ppermute | solution.py:527
  97.1 7.0 %collective-permute-start.16 = (f32[96,256]{1,0:T(8,128)S(1)}, f32[96,256]{1,0:T(8,128)S(1)}, u32[]{:S(2)}, u32[]{:S(2)}) collective-permute-start(f32[96,256]{1,0:T(8,128)S(1)} %get-tuple-element.95.refs_0_), channel_id=1, source_target_pairs={{0,2},{1,3},{2,0},{3,1},{4,6},{5,7},{6,4},{7,5},{8,10},{9,11},{10,... | collective-permute-start | bytes 294920 | tf_op jit(solution)/shard_map/ppermute | solution.py:527
  97.4 1.0 copy-start.8
  98.4 0.9 copy-start.10
  104.1 11.4 %copy-start.4 = (f32[768,256]{1,0:T(8,128)S(1)}, f32[768,256]{1,0:T(8,128)}, u32[]{:S(2)}) copy-start(f32[768,256]{1,0:T(8,128)} %copy-done.3) | copy-start | bytes 2359300
  104.7 10.8 %collective-permute-start.21 = (f32[384,256]{1,0:T(8,128)S(1)}, f32[384,256]{1,0:T(8,128)S(1)}, u32[]{:S(2)}, u32[]{:S(2)}) collective-permute-start(f32[384,256]{1,0:T(8,128)S(1)} %merge_pieces.1.mine_ref), channel_id=1, source_target_pairs={{0,1},{1,0},{2,3},{3,2},{4,5},{5,4},{6,7},{7,6},{8,9},{9,8},{10,11... | collective-permute-start | bytes 1179656 | tf_op jit(solution)/shard_map/ppermute | solution.py:594

commit v9 on v8

--- a/solution.py
+++ b/solution.py
@@ -142,11 +142,12 @@
     return jax.ShapeDtypeStruct((size, size), jnp.float32)
 
 
-def first_kernel(parts_ref, upper_ref, inv_ref, gram_ref, work_ref):
+def first_kernel(parts_ref, upper_out, inv_ref, gram_ref, upper_ref, work_ref, sems):
     strip = parts_ref.shape[1]
     for c in range(parts_ref.shape[0]):
         gram_ref[c * strip : (c + 1) * strip, :] = parts_ref[c]
     chol_kernel(gram_ref, upper_ref, inv_ref, work_ref)
+    wait(move([(upper_ref, upper_out)], sems))
 
 
 def cholesky(parts):
@@ -154,8 +155,9 @@
     return pl.pallas_call(
         first_kernel,
         in_specs=[VMEM],
+        out_specs=(HBM, VMEM),
         out_shape=(square(size), square(size)),
-        scratch_shapes=[pltpu.VMEM((size, size), jnp.float32)] * 2,
+        scratch_shapes=[pltpu.VMEM((size, size), jnp.float32)] * 3 + [pltpu.SemaphoreType.DMA((1,))],
         compiler_params=SMALL,
         cost_estimate=estimate(10),
         name="cholesky_inverse",
@@ -217,15 +219,22 @@
     )(gram)
 
 
-def factor_kernel(gram_ref, top_ref, inv_ref, upper_ref, first_ref, out_ref, band_ref):
+def factor_kernel(parts_ref, inv_ref, upper_ref, first_ref, out_ref, band_ref,
+                  first, out, band, sems):
+    fetch = move([(first_ref, first)], sems)
     size = inv_ref.shape[0]
+    strip = size // parts_ref.shape[0]
     row, col = grids(size)
     ident = jnp.where(row == col, 1.0, 0.0)
-    band_ref[...] = -mult(upper_ref[...], first_ref[...])
-    top = top_ref[...].reshape(size, size)
+    pieces = range(parts_ref.shape[0])
+    gram = jnp.concatenate([parts_ref[c, :strip, :] for c in pieces], axis=0)
+    top = jnp.concatenate([parts_ref[c, strip:, :] for c in pieces], axis=0)
     half_top = mult(top, inv_ref[...], ACROSS)
-    mat = gram_ref[...].reshape(size, size) + mult3(split(half_top), split(upper_ref[...]), TURNED)
+    mat = gram + mult(half_top, upper_ref[...], TURNED)
     halves = split(mat)
+    wait(fetch)
+    band[...] = -mult(upper_ref[...], first[...])
+    store = move([(band, band_ref)], sems)
 
     def residual(guess):
         return ident - mult3(halves, split(guess))
@@ -249,17 +258,22 @@
     guess = guess + mult3(split(guess), split(rest))
     rest = residual(guess)
     state = (jnp.int32(0), guess, rest, jnp.max(jnp.abs(rest)))
-    out_ref[...] = lax.while_loop(more, step, state)[1]
-
-
-def compact_factor(gram, top, inv, upper, first):
+    out[...] = lax.while_loop(more, step, state)[1]
+    wait(store + move([(out, out_ref)], sems.at[pl.ds(1, 1)]))
+
+
+def compact_factor(parts, inv, upper, first):
+    size = inv.shape[0]
     return pl.pallas_call(
         factor_kernel,
-        out_shape=(square(inv.shape[0]), square(inv.shape[0])),
+        in_specs=[VMEM] * 3 + [HBM],
+        out_specs=(HBM, HBM),
+        out_shape=(square(size), square(size)),
+        scratch_shapes=[pltpu.VMEM((size, size), jnp.float32)] * 3 + [pltpu.SemaphoreType.DMA((2,))],
         compiler_params=SMALL,
         cost_estimate=estimate(4),
         name="compact_factor",
-    )(gram, top, inv, upper, first)
+    )(parts, inv, upper, first)
 
 
 def array(*dims):
@@ -437,25 +451,29 @@
     )(*totals, *pieces)
 
 
-def spread_kernel(first, last, *refs):
+def spread_kernel(groups, *refs):
     out_ref = refs[-1]
-    total = tree_sum([ref[first:last, :] for ref in refs[:-1]])
-    for c in range(out_ref.shape[0]):
-        out_ref[c] = total
-
-
-def sum_copies(cols, terms, first, last):
-    return pl.pallas_call(
-        functools.partial(spread_kernel, first, last),
+    start = 0
+    for count, first, last in groups:
+        total = tree_sum([ref[first:last, :] for ref in refs[:count]])
+        refs = refs[count:]
+        for c in range(out_ref.shape[0]):
+            out_ref[c, start : start + last - first, :] = total
+        start += last - first
+
+
+def sum_gather(cols, *groups):
+    terms = [term for group in groups for term in group[0]]
+    bounds = [(len(group[0]), group[1], group[2]) for group in groups]
+    height = sum(last - first for _, first, last in bounds)
+    copies = pl.pallas_call(
+        functools.partial(spread_kernel, bounds),
         in_specs=[VMEM] * len(terms),
-        out_shape=array(cols, last - first, terms[0].shape[1]),
+        out_shape=array(cols, height, terms[0].shape[1]),
         compiler_params=LARGE,
         cost_estimate=estimate(0.5),
         name="sum_copies",
     )(*terms)
-
-
-def trade(copies):
     return lax.all_to_all(copies, "col", 0, 0, tiled=True)
 
 
@@ -562,36 +580,29 @@
         having = having + [d ^ hop for d in having]
         hop //= 2
 
-    gram = trade(sum_copies(cols, strips, 0, strip))
+    gram = sum_gather(cols, (strips, 0, strip))
     first_upper, first_inv = cholesky(gram)
     half, half_cols, gram2_strip = half_stage(place, panel, slab, got, first_inv, cols)
     gram2_strips = hops([gram2_strip] * rows, "row", rows)
-    gram2 = trade(sum_copies(cols, gram2_strips, 0, strip))
-    second_upper = near_cholesky(gram2.reshape(width, width))
+    parts = sum_gather(cols, (gram2_strips, 0, strip), (strips, strip, 2 * strip))
+    gram2 = parts[:, :strip].reshape(width, width)
+    second_upper = near_cholesky(gram2)
 
     left, right, keep, send, pieces = products(
         place, hamiltonian, half, half_cols, second_upper, rows, cols
     )
-    got = lax.ppermute(send, "col", pair)
+    parts, send = lax.optimization_barrier((parts, send))
+    factor, band_block = compact_factor(parts, first_inv, second_upper, first_upper)
+    totals = pair_add(keep, lax.ppermute(send, "col", pair))
+    totals = hops(totals, "col", cols, 2)
     pieces = hops(pieces, "row", rows)
-    got, pieces[:3] = lax.optimization_barrier((got, pieces[:3]))
-    totals = hops(pair_add(keep, got), "col", cols, 2)
-
-    late = lax.optimization_barrier(tuple(strips) + (totals[0],))
-    top = sum_copies(cols, late[:-1], strip, 2 * strip)
-    totals, top = lax.optimization_barrier((totals, top))
-    top = trade(top)
     mine, both = sum_pieces(totals, pieces, piece)
     both = hops([both] * rows, "row", rows)
     mine, both[1] = lax.optimization_barrier((mine, both[1]))
-    factor, band_block = compact_factor(gram2, top, first_inv, second_upper, first_upper)
+    mine = merge(place, hops([mine] * chips, "col", cols, 2))
+    other = lax.ppermute(mine, "col", pair)
     both, factor = lax.optimization_barrier((both, factor))
-    coupling = sum_copies(cols, both, share, share + strip)
-    mine = hops([mine] * chips, "col", cols, 2)
-    mine, _ = lax.optimization_barrier((mine, coupling))
-    coupling = trade(coupling)
-    mine = merge(place, mine)
-    other = lax.ppermute(mine, "col", pair)
+    coupling = sum_gather(cols, (both, share, share + strip))
     updated = update(place, hamiltonian, left, mine, other, right, factor, coupling, both)
     return (updated, band_block)
 

time: 120 us -> 118 us (0.983)
  local copies, waits for them, and re-layouts: 3.75 us -> 1.16 us
  blocking collectives: 20.1 us -> 21.5 us
    all_to_all x2 -> x1, starting transfers between devices: 7.05 us -> 3.41 us  [sum_gather(): return lax.all_to_all(copies, 'col', 0, 0, tiled=True)]
    ppermute x18, starting transfers between devices: 25.3 us -> 28.2 us  [hops(): got.append(lax.ppermute(values[hop], axis, pairs))]
    unnamed x22 -> x6, local copies, waits for them, and re-layouts: 3.75 us -> 1.14 us
    all_to_all x2, blocking collectives: 20.1 us -> 21.5 us  [sum_gather(): return lax.all_to_all(copies, 'col', 0, 0, tiled=True)]
    pallas_call x6 -> x5, Pallas kernels: 15.9 us -> 15 us  [the longest x1 9.72 us: cholesky(): pl.pallas_call(first_kernel, in_specs=[VMEM], out_specs=(HBM, VMEM), out_...]
    all_to_all x2 -> x1, waiting for transfers between devices: 2.73 us -> 2.72 us  [sum_gather(): return lax.all_to_all(copies, 'col', 0, 0, tiled=True)]
  transfers between devices with their start and end apart: 24 -> 23, of which waited for: 11 -> 10; matrix products, arithmetic and copies ran while one was open for 0% -> 0% of each run, Pallas kernels for 13% -> 13%
where the time goes in v9:
time: 118 us
  starting transfers between devices  36.5 us (31%)
  Pallas kernels  31.7 us (27%)
  waiting for transfers between devices  25.9 us (22%)
  blocking collectives  21.5 us (18%)
    ppermute x18, starting transfers between devices, hops(): got.append(lax.ppermute(values[hop], axis, pairs))  28.2 us
    all_to_all x2, blocking collectives, sum_gather(): return lax.all_to_all(copies, 'col', 0, 0, tiled=True)  21.5 us
    ppermute x18, waiting for transfers between devices, hops(): got.append(lax.ppermute(values[hop], axis, pairs))  20.4 us
    pallas_call x1, Pallas kernels, cholesky(): pl.pallas_call(first_kernel, in_specs=[VMEM], out_specs=(HBM, VMEM), out_...  9.72 us
    ppermute x2, starting transfers between devices, shards(): got = lax.ppermute(slab, ('row', 'col'), pairs)  4.82 us
    pallas_call x1, Pallas kernels, compact_factor(): pl.pallas_call(factor_kernel, in_specs=[VMEM] * 3 + [HBM], out_specs=(HBM...  4.53 us
    pallas_call x1, Pallas kernels, products(): pl.pallas_call(products_kernel, in_specs=[SMEM, VMEM, HBM, HBM, VMEM], ou...  4.32 us
    pallas_call x1, Pallas kernels, update(): pl.pallas_call(update_kernel, in_specs=[SMEM] + [VMEM] * (7 + len(pieces)...  4.05 us
  transfers between devices with their start and end apart: 23, of which 10 were waited for; matrix products, arithmetic and copies ran while one was open for 0% of the time, Pallas kernels for 13%

profile of v9, /device:TPU:0, one launch (start us, length us, event | category | flops | bytes accessed | tf_op | source)
XLA Modules:
  0.0 117.8 jit_solution(2290466239810763677)
XLA Ops:
  0.6 0.1 pad_add_fusion.place_ref
  0.7 1.1 copy-done
  1.8 1.5 %gram_strips.1.refs_0_.refs_4_ = f32[64,256]{1,0:T(8,128)S(1)} custom-call(s32[2]{0:T(128)S(1)} %pad_add_fusion.place_ref, f32[768,256]{1,0:T(8,128)S(1)} %copy-done), custom_call_target="tpu_custom_call" | custom-call | flops 2000000000 | bytes 6000000 | tf_op jit(solution)/shard_map/gram_strips/pallas_call | solution.py:297
  3.3 5.1 %collective-permute-start.2 = (f32[64,256]{1,0:T(8,128)S(1)}, f32[64,256]{1,0:T(8,128)S(1)}, u32[]{:S(2)}, u32[]{:S(2)}) collective-permute-start(f32[64,256]{1,0:T(8,128)S(1)} %gram_strips.1.refs_0_.refs_4_), channel_id=1, source_target_pairs={{0,24},{8,16},{16,8},{24,0},{1,25},{9,17},{17,9},{25,1},{2,26},{10... | collective-permute-start | bytes 196616 | tf_op jit(solution)/shard_map/ppermute | solution.py:545
  8.4 0.6 collective-permute-start
  9.1 1.9 %collective-permute-done.2.refs_3_.refs_7_ = f32[64,256]{1,0:T(8,128)S(1)} collective-permute-done((f32[64,256]{1,0:T(8,128)S(1)}, f32[64,256]{1,0:T(8,128)S(1)}, u32[]{:S(2)}, u32[]{:S(2)}) %collective-permute-start.2) | collective-permute-done | bytes 65568 | tf_op jit(solution)/shard_map/ppermute | solution.py:545
  11.0 3.0 %collective-permute-done.1.refs_2_.refs_6_ = f32[64,256]{1,0:T(8,128)S(1)} collective-permute-done((f32[64,256]{1,0:T(8,128)S(1)}, f32[64,256]{1,0:T(8,128)S(1)}, u32[]{:S(2)}, u32[]{:S(2)}) %collective-permute-start.1) | collective-permute-done | bytes 65568 | tf_op jit(solution)/shard_map/ppermute | solution.py:545
  14.0 3.5 %collective-permute-start.3 = (f32[384,256]{1,0:T(8,128)S(1)}, f32[384,256]{1,0:T(8,128)S(1)}, u32[]{:S(2)}, u32[]{:S(2)}) collective-permute-start(f32[384,256]{1,0:T(8,128)S(1)} %dynamic-slice_select_fusion), channel_id=1, source_target_pairs={{0,16},{1,17},{10,26},{11,27},{20,4},{21,5},{30,14},{31,15}} | collective-permute-start | bytes 1179656 | tf_op jit(solution)/shard_map/ppermute | solution.py:579
  17.5 0.7 sum_copies.3
  18.3 3.4 %all-to-all-start = ((f32[8,32,256]{2,1,0:T(8,128)}), f32[8,32,256]{2,1,0:T(8,128)S(1)}, u32[]{:S(2)}, u32[]{:S(2)}) async-start(f32[8,32,256]{2,1,0:T(8,128)} %sum_copies.3), calls=%async_computation | async-start | bytes 524288 | tf_op jit(solution)/shard_map/all_to_all | solution.py:477
  21.7 2.8 %collective-permute-done.3 = f32[384,256]{1,0:T(8,128)S(1)} collective-permute-done((f32[384,256]{1,0:T(8,128)S(1)}, f32[384,256]{1,0:T(8,128)S(1)}, u32[]{:S(2)}, u32[]{:S(2)}) %collective-permute-start.3) | collective-permute-done | bytes 393248 | tf_op jit(solution)/shard_map/ppermute | solution.py:579
  24.5 0.1 add.8.slab_ref
  24.5 1.3 %collective-permute-start.4 = (f32[384,256]{1,0:T(8,128)S(1)}, f32[384,256]{1,0:T(8,128)S(1)}, u32[]{:S(2)}, u32[]{:S(2)}) collective-permute-start(f32[384,256]{1,0:T(8,128)S(1)} %add.8.slab_ref), channel_id=1, source_target_pairs={{0,8},{16,24},{1,9},{17,25},{10,2},{26,18},{11,3},{27,19},{20,28},... | collective-permute-start | bytes 1179656 | tf_op jit(solution)/shard_map/ppermute | solution.py:579
  25.8 2.7 %all-to-all-done.parts_ref = f32[8,32,256]{2,1,0:T(8,128)S(1)} async-done(((f32[8,32,256]{2,1,0:T(8,128)}), f32[8,32,256]{2,1,0:T(8,128)S(1)}, u32[]{:S(2)}, u32[]{:S(2)}) %all-to-all-start) | async-done | bytes 262176 | tf_op jit(solution)/shard_map/all_to_all | solution.py:477
  28.6 9.7 %cholesky_inverse.1 = (f32[256,256]{1,0:T(8,128)S(1)}, f32[256,256]{1,0:T(8,128)S(1)}) custom-call(f32[8,32,256]{2,1,0:T(8,128)S(1)} %all-to-all-done.parts_ref), custom_call_target="tpu_custom_call" | custom-call | flops 10000000000 | bytes 30000000 | tf_op jit(solution)/shard_map/cholesky_inverse/pallas_call | solution.py:155
  38.3 3.0 %half_stage.1 = (f32[768,256]{1,0:T(8,128)S(1)}, f32[384,256]{1,0:T(8,128)S(1)}, f32[32,256]{1,0:T(8,128)S(1)}) custom-call(s32[2]{0:T(128)S(1)} %pad_add_fusion.place_ref, f32[768,256]{1,0:T(8,128)S(1)} %copy-done.1, f32[384,256]{1,0:T(8,128)S(1)} %add.8.slab_ref, f32[384,256]{1,0:T(8,128)S(1)} %collective-permute-done.4.got_ref, ...), custom_call_target="tpu_custom_call" | custom-call | flops 3000000000 | bytes 9000000 | tf_op jit(solution)/shard_map/half_stage/pallas_call | solution.py:324
  41.3 2.3 %collective-permute-start.7 = (f32[32,256]{1,0:T(8,128)S(1)}, f32[32,256]{1,0:T(8,128)S(1)}, u32[]{:S(2)}, u32[]{:S(2)}) collective-permute-start(f32[32,256]{1,0:T(8,128)S(1)} %get-tuple-element.45.refs_0_), channel_id=1, source_target_pairs={{0,24},{8,16},{16,8},{24,0},{1,25},{9,17},{17,9},{25,1},{2,26},{10... | collective-permute-start | bytes 98312 | tf_op jit(solution)/shard_map/ppermute | solution.py:545
  43.6 0.3 collective-permute-start.6
  44.0 1.8 %collective-permute-start.5 = (f32[32,256]{1,0:T(8,128)S(1)}, f32[32,256]{1,0:T(8,128)S(1)}, u32[]{:S(2)}, u32[]{:S(2)}) collective-permute-start(f32[32,256]{1,0:T(8,128)S(1)} %get-tuple-element.45.refs_0_), channel_id=1, source_target_pairs={{0,8},{8,0},{16,24},{24,16},{1,9},{9,1},{17,25},{25,17},{2,10},{10... | collective-permute-start | bytes 98312 | tf_op jit(solution)/shard_map/ppermute | solution.py:545
  45.8 1.3 %collective-permute-done.7.refs_3_ = f32[32,256]{1,0:T(8,128)S(1)} collective-permute-done((f32[32,256]{1,0:T(8,128)S(1)}, f32[32,256]{1,0:T(8,128)S(1)}, u32[]{:S(2)}, u32[]{:S(2)}) %collective-permute-start.7) | collective-permute-done | bytes 32800 | tf_op jit(solution)/shard_map/ppermute | solution.py:545
  47.1 1.3 %collective-permute-done.6.refs_2_ = f32[32,256]{1,0:T(8,128)S(1)} collective-permute-done((f32[32,256]{1,0:T(8,128)S(1)}, f32[32,256]{1,0:T(8,128)S(1)}, u32[]{:S(2)}, u32[]{:S(2)}) %collective-permute-start.6) | collective-permute-done | bytes 32800 | tf_op jit(solution)/shard_map/ppermute | solution.py:545
  48.5 12.2 %all_to_all.15.parts_ref = f32[8,64,256]{2,1,0:T(8,128)S(1)} all-to-all(f32[8,64,256]{2,1,0:T(8,128)S(1)} %sum_copies.4), channel_id=1, replica_groups=mesh['row'=4,'col'=8] {'col'}, dimensions={0} | all-to-all | bytes 1048576 | tf_op jit(solution)/shard_map/all_to_all | solution.py:477
  60.7 3.1 %near_cholesky.1.upper_ref = f32[256,256]{1,0:T(8,128)S(1)} custom-call(f32[256,256]{1,0:T(8,128)S(1)} %bitcast.3), custom_call_target="tpu_custom_call" | custom-call | flops 3000000000 | bytes 9000000 | tf_op jit(solution)/shard_map/near_cholesky/pallas_call | solution.py:212
  63.8 4.3 %products.1 = (f32[768,256]{1,0:T(8,128)S(1)}, f32[384,256]{1,0:T(8,128)S(1)}, f32[4,128,256]{2,1,0:T(8,128)S(1)}, f32[4,128,256]{2,1,0:T(8,128)S(1)}, f32[96,25...) custom-call(s32[2]{0:T(128)S(1)} %pad_add_fusion.place_ref, ...), custom_call_target="tpu_custom_call" | custom-call | flops 4000000000 | bytes 12000000 | tf_op jit(solution)/shard_map/products/pallas_call | solution.py:383
  68.2 0.1 collective-permute-start.8
  68.2 2.0 %collective-permute-start.12 = (f32[96,256]{1,0:T(8,128)S(1)}, f32[96,256]{1,0:T(8,128)S(1)}, u32[]{:S(2)}, u32[]{:S(2)}) collective-permute-start(f32[96,256]{1,0:T(8,128)S(1)} %get-tuple-element.55), channel_id=1, source_target_pairs={{0,8},{8,0},{16,24},{24,16},{1,9},{9,1},{17,25},{25,17},{2,10},{10... | collective-permute-start | bytes 294920 | tf_op jit(solution)/shard_map/ppermute | solution.py:545
  70.2 0.1 pair_add.1
  70.3 0.6 collective-permute-start.9
  70.9 0.6 collective-permute-start.10
  71.5 2.4 %collective-permute-start.11 = (f32[128,256]{1,0:T(8,128)S(1)}, f32[128,256]{1,0:T(8,128)S(1)}, u32[]{:S(2)}, u32[]{:S(2)}) collective-permute-start(f32[128,256]{1,0:T(8,128)S(1)} %get-tuple-element.53), channel_id=1, source_target_pairs={{0,6},{1,7},{2,4},{3,5},{4,2},{5,3},{6,0},{7,1},{8,14},{9,15},{10,... | collective-permute-start | bytes 393224 | tf_op jit(solution)/shard_map/ppermute | solution.py:545
  73.8 1.9 %collective-permute-start.13 = (f32[96,256]{1,0:T(8,128)S(1)}, f32[96,256]{1,0:T(8,128)S(1)}, u32[]{:S(2)}, u32[]{:S(2)}) collective-permute-start(f32[96,256]{1,0:T(8,128)S(1)} %get-tuple-element.56), channel_id=1, source_target_pairs={{0,16},{8,24},{16,0},{24,8},{1,17},{9,25},{17,1},{25,9},{2,18},{10... | collective-permute-start | bytes 294920 | tf_op jit(solution)/shard_map/ppermute | solution.py:545
  75.7 2.3 %collective-permute-start.14 = (f32[96,256]{1,0:T(8,128)S(1)}, f32[96,256]{1,0:T(8,128)S(1)}, u32[]{:S(2)}, u32[]{:S(2)}) collective-permute-start(f32[96,256]{1,0:T(8,128)S(1)} %get-tuple-element.57), channel_id=1, source_target_pairs={{0,24},{8,16},{16,8},{24,0},{1,25},{9,17},{17,9},{25,1},{2,26},{10... | collective-permute-start | bytes 294920 | tf_op jit(solution)/shard_map/ppermute | solution.py:545
  78.0 6.0 %collective-permute-done.13.refs_6_ = f32[96,256]{1,0:T(8,128)S(1)} collective-permute-done((f32[96,256]{1,0:T(8,128)S(1)}, f32[96,256]{1,0:T(8,128)S(1)}, u32[]{:S(2)}, u32[]{:S(2)}) %collective-permute-start.13) | collective-permute-done | bytes 98336 | tf_op jit(solution)/shard_map/ppermute | solution.py:545
  84.1 0.1 sum_pieces.1
  84.1 1.7 %collective-permute-start.15 = (f32[128,256]{1,0:T(8,128)S(1)}, f32[128,256]{1,0:T(8,128)S(1)}, u32[]{:S(2)}, u32[]{:S(2)}) collective-permute-start(f32[128,256]{1,0:T(8,128)S(1)} %get-tuple-element.67.refs_0_.rest_refs_0_), channel_id=1, source_target_pairs={{0,8},{8,0},{16,24},{24,16},{1,9},{9,1},{17,25},{25,17},{2,10},{10... | collective-permute-start | bytes 393224 | tf_op jit(solution)/shard_map/ppermute | solution.py:545
  85.8 3.4 %collective-permute-done.15.refs_1_.rest_refs_1_ = f32[128,256]{1,0:T(8,128)S(1)} collective-permute-done((f32[128,256]{1,0:T(8,128)S(1)}, f32[128,256]{1,0:T(8,128)S(1)}, u32[]{:S(2)}, u32[]{:S(2)}) %collective-permute-start.15) | collective-permute-done | bytes 131104 | tf_op jit(solution)/shard_map/ppermute | solution.py:545
  89.1 0.6 collective-permute-start.18
  89.7 1.5 %collective-permute-start.17 = (f32[96,256]{1,0:T(8,128)S(1)}, f32[96,256]{1,0:T(8,128)S(1)}, u32[]{:S(2)}, u32[]{:S(2)}) collective-permute-start(f32[96,256]{1,0:T(8,128)S(1)} %get-tuple-element.60.refs_0_), channel_id=1, source_target_pairs={{0,4},{1,5},{2,6},{3,7},{4,0},{5,1},{6,2},{7,3},{8,12},{9,13},{10,... | collective-permute-start | bytes 294920 | tf_op jit(solution)/shard_map/ppermute | solution.py:545
  91.2 1.5 %collective-permute-start.16 = (f32[96,256]{1,0:T(8,128)S(1)}, f32[96,256]{1,0:T(8,128)S(1)}, u32[]{:S(2)}, u32[]{:S(2)}) collective-permute-start(f32[96,256]{1,0:T(8,128)S(1)} %get-tuple-element.60.refs_0_), channel_id=1, source_target_pairs={{0,2},{1,3},{2,0},{3,1},{4,6},{5,7},{6,4},{7,5},{8,10},{9,11},{10,... | collective-permute-start | bytes 294920 | tf_op jit(solution)/shard_map/ppermute | solution.py:545
  92.6 1.9 %collective-permute-start.21 = (f32[128,256]{1,0:T(8,128)S(1)}, f32[128,256]{1,0:T(8,128)S(1)}, u32[]{:S(2)}, u32[]{:S(2)}) collective-permute-start(f32[128,256]{1,0:T(8,128)S(1)} %get-tuple-element.67.refs_0_.rest_refs_0_), channel_id=1, source_target_pairs={{0,24},{8,16},{16,8},{24,0},{1,25},{9,17},{17,9},{25,1},{2,26},{10... | collective-permute-start | bytes 393224 | tf_op jit(solution)/shard_map/ppermute | solution.py:545
  94.5 1.2 %collective-permute-start.20 = (f32[128,256]{1,0:T(8,128)S(1)}, f32[128,256]{1,0:T(8,128)S(1)}, u32[]{:S(2)}, u32[]{:S(2)}) collective-permute-start(f32[128,256]{1,0:T(8,128)S(1)} %get-tuple-element.67.refs_0_.rest_refs_0_), channel_id=1, source_target_pairs={{0,16},{8,24},{16,0},{24,8},{1,17},{9,25},{17,1},{25,9},{2,18},{10... | collective-permute-start | bytes 393224 | tf_op jit(solution)/shard_map/ppermute | solution.py:545
  95.7 0.1 collective-permute-done.16.refs_1_
  95.8 0.6 merge_pieces.1.mine_ref
  96.4 0.1 collective-permute-start.19
  96.5 4.5 %compact_factor.1 = (f32[256,256]{1,0:T(8,128)S(1)}, f32[256,256]{1,0:T(8,128)}) custom-call(f32[8,64,256]{2,1,0:T(8,128)S(1)} %all_to_all.15.parts_ref, f32[256,256]{1,0:T(8,128)S(1)} %get-tuple-element.42.inv_ref, f32[256,256]{1,0:T(8,128)S(1)} %near_cholesky.1.upper_ref, f32[256,256]{1,0:T(8,128)S(1)} %get-tuple-element.64.first_ref), custom_call_target="tpu_custom_call" | custom-call | flops 4000000000 | bytes 12000000 | tf_op jit(solution)/shard_map/compact_factor/pallas_call | solution.py:267
  101.0 3.3 %collective-permute-done.20.refs_2_.rest_refs_2_ = f32[128,256]{1,0:T(8,128)S(1)} collective-permute-done((f32[128,256]{1,0:T(8,128)S(1)}, f32[128,256]{1,0:T(8,128)S(1)}, u32[]{:S(2)}, u32[]{:S(2)}) %collective-permute-start.20) | collective-permute-done | bytes 131104 | tf_op jit(solution)/shard_map/ppermute | solution.py:545
  104.4 9.3 %all_to_all.16.parts_ref = f32[8,32,256]{2,1,0:T(8,128)S(1)} all-to-all(f32[8,32,256]{2,1,0:T(8,128)S(1)} %sum_copies.5), channel_id=1, replica_groups=mesh['row'=4,'col'=8] {'col'}, dimensions={0} | all-to-all | bytes 524288 | tf_op jit(solution)/shard_map/all_to_all | solution.py:477
  113.7 4.1 %two_sided_update.1 = f32[768,384]{1,0:T(8,128)} custom-call(s32[2]{0:T(128)S(1)} %pad_add_fusion.place_ref, f32[768,384]{1,0:T(8,128)S(1)} %copy-done.2, f32[768,256]{1,0:T(8,128)S(1)} %get-tuple-element.46.left_ref, f32[384,256]{1,0:T(8,128)S(1)} %merge_pieces.1.mine_ref, f32[384,256]{1,0:T(8,128)S(1)} %collective-permute-done.19.other_ref, ...), custom_call_target="tpu_custom_call" | custom-call | flops 4000000000 | bytes 12000000 | tf_op jit(solution)/shard_map/two_sided_update/pallas_call | solution.py:530
  (23 shorter events, 0.2 us)
Async XLA Ops:
  0.7 1.1 copy-start
  1.8 7.2 %copy-start.1 = (f32[768,256]{1,0:T(8,128)S(1)}, f32[768,256]{1,0:T(8,128)}, u32[]{:S(2)}) copy-start(f32[768,256]{1,0:T(8,128)} %panel_ref.3) | copy-start | bytes 2359300
  3.3 7.7 %collective-permute-start.2 = (f32[64,256]{1,0:T(8,128)S(1)}, f32[64,256]{1,0:T(8,128)S(1)}, u32[]{:S(2)}, u32[]{:S(2)}) collective-permute-start(f32[64,256]{1,0:T(8,128)S(1)} %gram_strips.1.refs_0_.refs_4_), channel_id=1, source_target_pairs={{0,24},{8,16},{16,8},{24,0},{1,25},{9,17},{17,9},{25,1},{2,26},{10... | collective-permute-start | bytes 196616 | tf_op jit(solution)/shard_map/ppermute | solution.py:545
  8.4 5.6 %collective-permute-start.1 = (f32[64,256]{1,0:T(8,128)S(1)}, f32[64,256]{1,0:T(8,128)S(1)}, u32[]{:S(2)}, u32[]{:S(2)}) collective-permute-start(f32[64,256]{1,0:T(8,128)S(1)} %gram_strips.1.refs_0_.refs_4_), channel_id=1, source_target_pairs={{0,16},{8,24},{16,0},{24,8},{1,17},{9,25},{17,1},{25,9},{2,18},{10... | collective-permute-start | bytes 196616 | tf_op jit(solution)/shard_map/ppermute | solution.py:545
  8.4 5.6 %collective-permute-start = (f32[64,256]{1,0:T(8,128)S(1)}, f32[64,256]{1,0:T(8,128)S(1)}, u32[]{:S(2)}, u32[]{:S(2)}) collective-permute-start(f32[64,256]{1,0:T(8,128)S(1)} %gram_strips.1.refs_0_.refs_4_), channel_id=1, source_target_pairs={{0,8},{8,0},{16,24},{24,16},{1,9},{9,1},{17,25},{25,17},{2,10},{10... | collective-permute-start | bytes 196616 | tf_op jit(solution)/shard_map/ppermute | solution.py:545
  14.0 10.4 %collective-permute-start.3 = (f32[384,256]{1,0:T(8,128)S(1)}, f32[384,256]{1,0:T(8,128)S(1)}, u32[]{:S(2)}, u32[]{:S(2)}) collective-permute-start(f32[384,256]{1,0:T(8,128)S(1)} %dynamic-slice_select_fusion), channel_id=1, source_target_pairs={{0,16},{1,17},{10,26},{11,27},{20,4},{21,5},{30,14},{31,15}} | collective-permute-start | bytes 1179656 | tf_op jit(solution)/shard_map/ppermute | solution.py:579
  18.3 10.3 %all-to-all-start = ((f32[8,32,256]{2,1,0:T(8,128)}), f32[8,32,256]{2,1,0:T(8,128)S(1)}, u32[]{:S(2)}, u32[]{:S(2)}) async-start(f32[8,32,256]{2,1,0:T(8,128)} %sum_copies.3), calls=%async_computation | async-start | bytes 524288 | tf_op jit(solution)/shard_map/all_to_all | solution.py:477
  24.5 13.8 %collective-permute-start.4 = (f32[384,256]{1,0:T(8,128)S(1)}, f32[384,256]{1,0:T(8,128)S(1)}, u32[]{:S(2)}, u32[]{:S(2)}) collective-permute-start(f32[384,256]{1,0:T(8,128)S(1)} %add.8.slab_ref), channel_id=1, source_target_pairs={{0,8},{16,24},{1,9},{17,25},{10,2},{26,18},{11,3},{27,19},{20,28},... | collective-permute-start | bytes 1179656 | tf_op jit(solution)/shard_map/ppermute | solution.py:579
  41.3 5.8 %collective-permute-start.7 = (f32[32,256]{1,0:T(8,128)S(1)}, f32[32,256]{1,0:T(8,128)S(1)}, u32[]{:S(2)}, u32[]{:S(2)}) collective-permute-start(f32[32,256]{1,0:T(8,128)S(1)} %get-tuple-element.45.refs_0_), channel_id=1, source_target_pairs={{0,24},{8,16},{16,8},{24,0},{1,25},{9,17},{17,9},{25,1},{2,26},{10... | collective-permute-start | bytes 98312 | tf_op jit(solution)/shard_map/ppermute | solution.py:545
  43.6 4.8 %collective-permute-start.6 = (f32[32,256]{1,0:T(8,128)S(1)}, f32[32,256]{1,0:T(8,128)S(1)}, u32[]{:S(2)}, u32[]{:S(2)}) collective-permute-start(f32[32,256]{1,0:T(8,128)S(1)} %get-tuple-element.45.refs_0_), channel_id=1, source_target_pairs={{0,16},{8,24},{16,0},{24,8},{1,17},{9,25},{17,1},{25,9},{2,18},{10... | collective-permute-start | bytes 98312 | tf_op jit(solution)/shard_map/ppermute | solution.py:545
  44.0 4.5 %collective-permute-start.5 = (f32[32,256]{1,0:T(8,128)S(1)}, f32[32,256]{1,0:T(8,128)S(1)}, u32[]{:S(2)}, u32[]{:S(2)}) collective-permute-start(f32[32,256]{1,0:T(8,128)S(1)} %get-tuple-element.45.refs_0_), channel_id=1, source_target_pairs={{0,8},{8,0},{16,24},{24,16},{1,9},{9,1},{17,25},{25,17},{2,10},{10... | collective-permute-start | bytes 98312 | tf_op jit(solution)/shard_map/ppermute | solution.py:545
  60.7 3.1 %copy-start.2 = (f32[768,384]{1,0:T(8,128)S(1)}, f32[768,384]{1,0:T(8,128)}, u32[]{:S(2)}) copy-start(f32[768,384]{1,0:T(8,128)} %ham_ref.3) | copy-start | bytes 3538948
  68.2 2.1 %collective-permute-start.8 = (f32[4,128,256]{2,1,0:T(8,128)S(1)}, f32[4,128,256]{2,1,0:T(8,128)S(1)}, u32[]{:S(2)}, u32[]{:S(2)}) collective-permute-start(f32[4,128,256]{2,1,0:T(8,128)S(1)} %get-tuple-element.49), channel_id=1, source_target_pairs={{0,1},{1,0},{2,3},{3,2},{4,5},{5,4},{6,7},{7,6},{8,9},{9,8},{10,11... | collective-permute-start | bytes 1572872 | tf_op jit(solution)/shard_map/ppermute | solution.py:596
  68.2 7.5 %collective-permute-start.12 = (f32[96,256]{1,0:T(8,128)S(1)}, f32[96,256]{1,0:T(8,128)S(1)}, u32[]{:S(2)}, u32[]{:S(2)}) collective-permute-start(f32[96,256]{1,0:T(8,128)S(1)} %get-tuple-element.55), channel_id=1, source_target_pairs={{0,8},{8,0},{16,24},{24,16},{1,9},{9,1},{17,25},{25,17},{2,10},{10... | collective-permute-start | bytes 294920 | tf_op jit(solution)/shard_map/ppermute | solution.py:545
  70.3 13.8 %collective-permute-start.9 = (f32[128,256]{1,0:T(8,128)S(1)}, f32[128,256]{1,0:T(8,128)S(1)}, u32[]{:S(2)}, u32[]{:S(2)}) collective-permute-start(f32[128,256]{1,0:T(8,128)S(1)} %get-tuple-element.51), channel_id=1, source_target_pairs={{0,2},{1,3},{2,0},{3,1},{4,6},{5,7},{6,4},{7,5},{8,10},{9,11},{10,... | collective-permute-start | bytes 393224 | tf_op jit(solution)/shard_map/ppermute | solution.py:545
  70.9 13.1 %collective-permute-start.10 = (f32[128,256]{1,0:T(8,128)S(1)}, f32[128,256]{1,0:T(8,128)S(1)}, u32[]{:S(2)}, u32[]{:S(2)}) collective-permute-start(f32[128,256]{1,0:T(8,128)S(1)} %get-tuple-element.52), channel_id=1, source_target_pairs={{0,4},{1,5},{2,6},{3,7},{4,0},{5,1},{6,2},{7,3},{8,12},{9,13},{10,... | collective-permute-start | bytes 393224 | tf_op jit(solution)/shard_map/ppermute | solution.py:545
  71.5 12.6 %collective-permute-start.11 = (f32[128,256]{1,0:T(8,128)S(1)}, f32[128,256]{1,0:T(8,128)S(1)}, u32[]{:S(2)}, u32[]{:S(2)}) collective-permute-start(f32[128,256]{1,0:T(8,128)S(1)} %get-tuple-element.53), channel_id=1, source_target_pairs={{0,6},{1,7},{2,4},{3,5},{4,2},{5,3},{6,0},{7,1},{8,14},{9,15},{10,... | collective-permute-start | bytes 393224 | tf_op jit(solution)/shard_map/ppermute | solution.py:545
  73.8 10.2 %collective-permute-start.13 = (f32[96,256]{1,0:T(8,128)S(1)}, f32[96,256]{1,0:T(8,128)S(1)}, u32[]{:S(2)}, u32[]{:S(2)}) collective-permute-start(f32[96,256]{1,0:T(8,128)S(1)} %get-tuple-element.56), channel_id=1, source_target_pairs={{0,16},{8,24},{16,0},{24,8},{1,17},{9,25},{17,1},{25,9},{2,18},{10... | collective-permute-start | bytes 294920 | tf_op jit(solution)/shard_map/ppermute | solution.py:545
  75.7 8.3 %collective-permute-start.14 = (f32[96,256]{1,0:T(8,128)S(1)}, f32[96,256]{1,0:T(8,128)S(1)}, u32[]{:S(2)}, u32[]{:S(2)}) collective-permute-start(f32[96,256]{1,0:T(8,128)S(1)} %get-tuple-element.57), channel_id=1, source_target_pairs={{0,24},{8,16},{16,8},{24,0},{1,25},{9,17},{17,9},{25,1},{2,26},{10... | collective-permute-start | bytes 294920 | tf_op jit(solution)/shard_map/ppermute | solution.py:545
  84.1 5.0 %collective-permute-start.15 = (f32[128,256]{1,0:T(8,128)S(1)}, f32[128,256]{1,0:T(8,128)S(1)}, u32[]{:S(2)}, u32[]{:S(2)}) collective-permute-start(f32[128,256]{1,0:T(8,128)S(1)} %get-tuple-element.67.refs_0_.rest_refs_0_), channel_id=1, source_target_pairs={{0,8},{8,0},{16,24},{24,16},{1,9},{9,1},{17,25},{25,17},{2,10},{10... | collective-permute-start | bytes 393224 | tf_op jit(solution)/shard_map/ppermute | solution.py:545
  89.1 6.6 %collective-permute-start.18 = (f32[96,256]{1,0:T(8,128)S(1)}, f32[96,256]{1,0:T(8,128)S(1)}, u32[]{:S(2)}, u32[]{:S(2)}) collective-permute-start(f32[96,256]{1,0:T(8,128)S(1)} %get-tuple-element.60.refs_0_), channel_id=1, source_target_pairs={{0,6},{1,7},{2,4},{3,5},{4,2},{5,3},{6,0},{7,1},{8,14},{9,15},{10,... | collective-permute-start | bytes 294920 | tf_op jit(solution)/shard_map/ppermute | solution.py:545
  89.7 6.0 %collective-permute-start.17 = (f32[96,256]{1,0:T(8,128)S(1)}, f32[96,256]{1,0:T(8,128)S(1)}, u32[]{:S(2)}, u32[]{:S(2)}) collective-permute-start(f32[96,256]{1,0:T(8,128)S(1)} %get-tuple-element.60.refs_0_), channel_id=1, source_target_pairs={{0,4},{1,5},{2,6},{3,7},{4,0},{5,1},{6,2},{7,3},{8,12},{9,13},{10,... | collective-permute-start | bytes 294920 | tf_op jit(solution)/shard_map/ppermute | solution.py:545
  91.2 4.6 %collective-permute-start.16 = (f32[96,256]{1,0:T(8,128)S(1)}, f32[96,256]{1,0:T(8,128)S(1)}, u32[]{:S(2)}, u32[]{:S(2)}) collective-permute-start(f32[96,256]{1,0:T(8,128)S(1)} %get-tuple-element.60.refs_0_), channel_id=1, source_target_pairs={{0,2},{1,3},{2,0},{3,1},{4,6},{5,7},{6,4},{7,5},{8,10},{9,11},{10,... | collective-permute-start | bytes 294920 | tf_op jit(solution)/shard_map/ppermute | solution.py:545
  92.6 8.4 %collective-permute-start.21 = (f32[128,256]{1,0:T(8,128)S(1)}, f32[128,256]{1,0:T(8,128)S(1)}, u32[]{:S(2)}, u32[]{:S(2)}) collective-permute-start(f32[128,256]{1,0:T(8,128)S(1)} %get-tuple-element.67.refs_0_.rest_refs_0_), channel_id=1, source_target_pairs={{0,24},{8,16},{16,8},{24,0},{1,25},{9,17},{17,9},{25,1},{2,26},{10... | collective-permute-start | bytes 393224 | tf_op jit(solution)/shard_map/ppermute | solution.py:545
  94.5 9.8 %collective-permute-start.20 = (f32[128,256]{1,0:T(8,128)S(1)}, f32[128,256]{1,0:T(8,128)S(1)}, u32[]{:S(2)}, u32[]{:S(2)}) collective-permute-start(f32[128,256]{1,0:T(8,128)S(1)} %get-tuple-element.67.refs_0_.rest_refs_0_), channel_id=1, source_target_pairs={{0,16},{8,24},{16,0},{24,8},{1,17},{9,25},{17,1},{25,9},{2,18},{10... | collective-permute-start | bytes 393224 | tf_op jit(solution)/shard_map/ppermute | solution.py:545
  96.4 17.3 %collective-permute-start.19 = (f32[384,256]{1,0:T(8,128)S(1)}, f32[384,256]{1,0:T(8,128)S(1)}, u32[]{:S(2)}, u32[]{:S(2)}) collective-permute-start(f32[384,256]{1,0:T(8,128)S(1)} %merge_pieces.1.mine_ref), channel_id=1, source_target_pairs={{0,1},{1,0},{2,3},{3,2},{4,5},{5,4},{6,7},{7,6},{8,9},{9,8},{10,11... | collective-permute-start | bytes 1179656 | tf_op jit(solution)/shard_map/ppermute | solution.py:603

commit v10 on v9

--- a/solution.py
+++ b/solution.py
@@ -591,17 +591,16 @@
     left, right, keep, send, pieces = products(
         place, hamiltonian, half, half_cols, second_upper, rows, cols
     )
-    parts, send = lax.optimization_barrier((parts, send))
+    totals = pair_add(keep, lax.ppermute(send, "col", pair))
+    pieces = hops(pieces, "row", rows)
+    parts, _ = lax.optimization_barrier((parts, totals[0]))
+    totals = hops(totals, "col", cols, 2)
     factor, band_block = compact_factor(parts, first_inv, second_upper, first_upper)
-    totals = pair_add(keep, lax.ppermute(send, "col", pair))
-    totals = hops(totals, "col", cols, 2)
-    pieces = hops(pieces, "row", rows)
+    totals, factor = lax.optimization_barrier((totals, factor))
     mine, both = sum_pieces(totals, pieces, piece)
     both = hops([both] * rows, "row", rows)
-    mine, both[1] = lax.optimization_barrier((mine, both[1]))
     mine = merge(place, hops([mine] * chips, "col", cols, 2))
     other = lax.ppermute(mine, "col", pair)
-    both, factor = lax.optimization_barrier((both, factor))
     coupling = sum_gather(cols, (both, share, share + strip))
     updated = update(place, hamiltonian, left, mine, other, right, factor, coupling, both)
     return (updated, band_block)

time: 118 us -> 114 us (0.966)
  waiting for transfers between devices: 25.9 us -> 22.9 us
  starting transfers between devices: 36.5 us -> 34.9 us
    ppermute x18, waiting for transfers between devices: 20.4 us -> 15.5 us  [hops(): got.append(lax.ppermute(values[hop], axis, pairs))]
    ppermute x1, waiting for transfers between devices: 0.01 us -> 1.9 us  [shards(): totals = pair_add(keep, lax.ppermute(send, 'col', pair))]
    ppermute x18, starting transfers between devices: 28.2 us -> 26.5 us  [hops(): got.append(lax.ppermute(values[hop], axis, pairs))]
  transfers between devices with their start and end apart: 23 -> 23, of which waited for: 10 -> 9; matrix products, arithmetic and copies ran while one was open for 0% -> 0% of each run, Pallas kernels for 13% -> 14%
where the time goes in v10:
time: 114 us; the launch traced here: 113 us
  starting transfers between devices  34.9 us (31%)
  Pallas kernels  31.7 us (28%)
  waiting for transfers between devices  22.9 us (20%)
  blocking collectives  21.5 us (19%)
  local copies, waits for them, and re-layouts  1.16 us (1%)
    ppermute x18, starting transfers between devices, hops(): got.append(lax.ppermute(values[hop], axis, pairs))  26.5 us
    all_to_all x2, blocking collectives, sum_gather(): return lax.all_to_all(copies, 'col', 0, 0, tiled=True)  21.5 us
    ppermute x18, waiting for transfers between devices, hops(): got.append(lax.ppermute(values[hop], axis, pairs))  15.5 us
    pallas_call x1, Pallas kernels, cholesky(): pl.pallas_call(first_kernel, in_specs=[VMEM], out_specs=(HBM, VMEM), out_...  9.71 us
    ppermute x2, starting transfers between devices, shards(): got = lax.ppermute(slab, ('row', 'col'), pairs)  4.82 us
    pallas_call x1, Pallas kernels, compact_factor(): pl.pallas_call(factor_kernel, in_specs=[VMEM] * 3 + [HBM], out_specs=(HBM...  4.74 us
    pallas_call x1, Pallas kernels, products(): pl.pallas_call(products_kernel, in_specs=[SMEM, VMEM, HBM, HBM, VMEM], ou...  4.32 us
    pallas_call x1, Pallas kernels, update(): pl.pallas_call(update_kernel, in_specs=[SMEM] + [VMEM] * (7 + len(pieces)...  4.05 us
  transfers between devices with their start and end apart: 23, of which 9 were waited for; matrix products, arithmetic and copies ran while one was open for 0% of the time, Pallas kernels for 14%

profile of v10, /device:TPU:0, one launch (start us, length us, event | category | flops | bytes accessed | tf_op | source)
XLA Modules:
  0.0 113.2 jit_solution(2137789445317855264)
XLA Ops:
  0.6 0.1 pad_add_fusion.place_ref
  0.7 1.1 copy-done
  1.8 1.5 %gram_strips.1.refs_0_.refs_4_ = f32[64,256]{1,0:T(8,128)S(1)} custom-call(s32[2]{0:T(128)S(1)} %pad_add_fusion.place_ref, f32[768,256]{1,0:T(8,128)S(1)} %copy-done), custom_call_target="tpu_custom_call" | custom-call | flops 2000000000 | bytes 6000000 | tf_op jit(solution)/shard_map/gram_strips/pallas_call | solution.py:297
  3.3 5.1 %collective-permute-start.2 = (f32[64,256]{1,0:T(8,128)S(1)}, f32[64,256]{1,0:T(8,128)S(1)}, u32[]{:S(2)}, u32[]{:S(2)}) collective-permute-start(f32[64,256]{1,0:T(8,128)S(1)} %gram_strips.1.refs_0_.refs_4_), channel_id=1, source_target_pairs={{0,24},{8,16},{16,8},{24,0},{1,25},{9,17},{17,9},{25,1},{2,26},{10... | collective-permute-start | bytes 196616 | tf_op jit(solution)/shard_map/ppermute | solution.py:545
  8.4 0.6 collective-permute-start
  9.1 1.9 %collective-permute-done.2.refs_3_.refs_7_ = f32[64,256]{1,0:T(8,128)S(1)} collective-permute-done((f32[64,256]{1,0:T(8,128)S(1)}, f32[64,256]{1,0:T(8,128)S(1)}, u32[]{:S(2)}, u32[]{:S(2)}) %collective-permute-start.2) | collective-permute-done | bytes 65568 | tf_op jit(solution)/shard_map/ppermute | solution.py:545
  11.0 3.0 %collective-permute-done.1.refs_2_.refs_6_ = f32[64,256]{1,0:T(8,128)S(1)} collective-permute-done((f32[64,256]{1,0:T(8,128)S(1)}, f32[64,256]{1,0:T(8,128)S(1)}, u32[]{:S(2)}, u32[]{:S(2)}) %collective-permute-start.1) | collective-permute-done | bytes 65568 | tf_op jit(solution)/shard_map/ppermute | solution.py:545
  14.0 3.5 %collective-permute-start.3 = (f32[384,256]{1,0:T(8,128)S(1)}, f32[384,256]{1,0:T(8,128)S(1)}, u32[]{:S(2)}, u32[]{:S(2)}) collective-permute-start(f32[384,256]{1,0:T(8,128)S(1)} %dynamic-slice_select_fusion), channel_id=1, source_target_pairs={{0,16},{1,17},{10,26},{11,27},{20,4},{21,5},{30,14},{31,15}} | collective-permute-start | bytes 1179656 | tf_op jit(solution)/shard_map/ppermute | solution.py:579
  17.5 0.7 sum_copies.3
  18.3 3.4 %all-to-all-start = ((f32[8,32,256]{2,1,0:T(8,128)}), f32[8,32,256]{2,1,0:T(8,128)S(1)}, u32[]{:S(2)}, u32[]{:S(2)}) async-start(f32[8,32,256]{2,1,0:T(8,128)} %sum_copies.3), calls=%async_computation | async-start | bytes 524288 | tf_op jit(solution)/shard_map/all_to_all | solution.py:477
  21.7 2.8 %collective-permute-done.3 = f32[384,256]{1,0:T(8,128)S(1)} collective-permute-done((f32[384,256]{1,0:T(8,128)S(1)}, f32[384,256]{1,0:T(8,128)S(1)}, u32[]{:S(2)}, u32[]{:S(2)}) %collective-permute-start.3) | collective-permute-done | bytes 393248 | tf_op jit(solution)/shard_map/ppermute | solution.py:579
  24.5 0.1 add.8.slab_ref
  24.5 1.3 %collective-permute-start.4 = (f32[384,256]{1,0:T(8,128)S(1)}, f32[384,256]{1,0:T(8,128)S(1)}, u32[]{:S(2)}, u32[]{:S(2)}) collective-permute-start(f32[384,256]{1,0:T(8,128)S(1)} %add.8.slab_ref), channel_id=1, source_target_pairs={{0,8},{16,24},{1,9},{17,25},{10,2},{26,18},{11,3},{27,19},{20,28},... | collective-permute-start | bytes 1179656 | tf_op jit(solution)/shard_map/ppermute | solution.py:579
  25.8 2.7 %all-to-all-done.parts_ref = f32[8,32,256]{2,1,0:T(8,128)S(1)} async-done(((f32[8,32,256]{2,1,0:T(8,128)}), f32[8,32,256]{2,1,0:T(8,128)S(1)}, u32[]{:S(2)}, u32[]{:S(2)}) %all-to-all-start) | async-done | bytes 262176 | tf_op jit(solution)/shard_map/all_to_all | solution.py:477
  28.6 9.7 %cholesky_inverse.1 = (f32[256,256]{1,0:T(8,128)S(1)}, f32[256,256]{1,0:T(8,128)S(1)}) custom-call(f32[8,32,256]{2,1,0:T(8,128)S(1)} %all-to-all-done.parts_ref), custom_call_target="tpu_custom_call" | custom-call | flops 10000000000 | bytes 30000000 | tf_op jit(solution)/shard_map/cholesky_inverse/pallas_call | solution.py:155
  38.3 3.0 %half_stage.1 = (f32[768,256]{1,0:T(8,128)S(1)}, f32[384,256]{1,0:T(8,128)S(1)}, f32[32,256]{1,0:T(8,128)S(1)}) custom-call(s32[2]{0:T(128)S(1)} %pad_add_fusion.place_ref, f32[768,256]{1,0:T(8,128)S(1)} %copy-done.1, f32[384,256]{1,0:T(8,128)S(1)} %add.8.slab_ref, f32[384,256]{1,0:T(8,128)S(1)} %collective-permute-done.4.got_ref, ...), custom_call_target="tpu_custom_call" | custom-call | flops 3000000000 | bytes 9000000 | tf_op jit(solution)/shard_map/half_stage/pallas_call | solution.py:324
  41.3 2.3 %collective-permute-start.7 = (f32[32,256]{1,0:T(8,128)S(1)}, f32[32,256]{1,0:T(8,128)S(1)}, u32[]{:S(2)}, u32[]{:S(2)}) collective-permute-start(f32[32,256]{1,0:T(8,128)S(1)} %get-tuple-element.42.refs_0_), channel_id=1, source_target_pairs={{0,24},{8,16},{16,8},{24,0},{1,25},{9,17},{17,9},{25,1},{2,26},{10... | collective-permute-start | bytes 98312 | tf_op jit(solution)/shard_map/ppermute | solution.py:545
  43.6 0.3 collective-permute-start.6
  44.0 1.8 %collective-permute-start.5 = (f32[32,256]{1,0:T(8,128)S(1)}, f32[32,256]{1,0:T(8,128)S(1)}, u32[]{:S(2)}, u32[]{:S(2)}) collective-permute-start(f32[32,256]{1,0:T(8,128)S(1)} %get-tuple-element.42.refs_0_), channel_id=1, source_target_pairs={{0,8},{8,0},{16,24},{24,16},{1,9},{9,1},{17,25},{25,17},{2,10},{10... | collective-permute-start | bytes 98312 | tf_op jit(solution)/shard_map/ppermute | solution.py:545
  45.8 1.3 %collective-permute-done.7.refs_3_ = f32[32,256]{1,0:T(8,128)S(1)} collective-permute-done((f32[32,256]{1,0:T(8,128)S(1)}, f32[32,256]{1,0:T(8,128)S(1)}, u32[]{:S(2)}, u32[]{:S(2)}) %collective-permute-start.7) | collective-permute-done | bytes 32800 | tf_op jit(solution)/shard_map/ppermute | solution.py:545
  47.1 1.3 %collective-permute-done.6.refs_2_ = f32[32,256]{1,0:T(8,128)S(1)} collective-permute-done((f32[32,256]{1,0:T(8,128)S(1)}, f32[32,256]{1,0:T(8,128)S(1)}, u32[]{:S(2)}, u32[]{:S(2)}) %collective-permute-start.6) | collective-permute-done | bytes 32800 | tf_op jit(solution)/shard_map/ppermute | solution.py:545
  48.5 12.2 %all_to_all.15.parts_ref = f32[8,64,256]{2,1,0:T(8,128)S(1)} all-to-all(f32[8,64,256]{2,1,0:T(8,128)S(1)} %sum_copies.4), channel_id=1, replica_groups=mesh['row'=4,'col'=8] {'col'}, dimensions={0} | all-to-all | bytes 1048576 | tf_op jit(solution)/shard_map/all_to_all | solution.py:477
  60.7 2.9 %near_cholesky.1.upper_ref = f32[256,256]{1,0:T(8,128)S(1)} custom-call(f32[256,256]{1,0:T(8,128)S(1)} %bitcast.3), custom_call_target="tpu_custom_call" | custom-call | flops 3000000000 | bytes 9000000 | tf_op jit(solution)/shard_map/near_cholesky/pallas_call | solution.py:212
  63.6 4.3 %products.1 = (f32[768,256]{1,0:T(8,128)S(1)}, f32[384,256]{1,0:T(8,128)S(1)}, f32[4,128,256]{2,1,0:T(8,128)S(1)}, f32[4,128,256]{2,1,0:T(8,128)S(1)}, f32[96,25...) custom-call(s32[2]{0:T(128)S(1)} %pad_add_fusion.place_ref, ...), custom_call_target="tpu_custom_call" | custom-call | flops 4000000000 | bytes 12000000 | tf_op jit(solution)/shard_map/products/pallas_call | solution.py:383
  67.9 0.1 collective-permute-start.8
  68.0 1.9 %collective-permute-done.8.got_ref = f32[4,128,256]{2,1,0:T(8,128)S(1)} collective-permute-done((f32[4,128,256]{2,1,0:T(8,128)S(1)}, f32[4,128,256]{2,1,0:T(8,128)S(1)}, u32[]{:S(2)}, u32[]{:S(2)}) %collective-permute-start.8) | collective-permute-done | bytes 524320 | tf_op jit(solution)/shard_map/ppermute | solution.py:594
  69.9 0.1 pair_add.1
  70.0 0.6 collective-permute-start.9
  70.6 1.9 %collective-permute-start.12 = (f32[96,256]{1,0:T(8,128)S(1)}, f32[96,256]{1,0:T(8,128)S(1)}, u32[]{:S(2)}, u32[]{:S(2)}) collective-permute-start(f32[96,256]{1,0:T(8,128)S(1)} %get-tuple-element.58), channel_id=1, source_target_pairs={{0,8},{8,0},{16,24},{24,16},{1,9},{9,1},{17,25},{25,17},{2,10},{10... | collective-permute-start | bytes 294920 | tf_op jit(solution)/shard_map/ppermute | solution.py:545
  72.5 0.9 collective-permute-start.13
  73.4 1.6 %collective-permute-start.14 = (f32[96,256]{1,0:T(8,128)S(1)}, f32[96,256]{1,0:T(8,128)S(1)}, u32[]{:S(2)}, u32[]{:S(2)}) collective-permute-start(f32[96,256]{1,0:T(8,128)S(1)} %get-tuple-element.60), channel_id=1, source_target_pairs={{0,24},{8,16},{16,8},{24,0},{1,25},{9,17},{17,9},{25,1},{2,26},{10... | collective-permute-start | bytes 294920 | tf_op jit(solution)/shard_map/ppermute | solution.py:545
  75.0 0.6 collective-permute-start.10
  75.6 0.0 collective-permute-done.9.refs_1_
  75.6 2.3 %collective-permute-start.11 = (f32[128,256]{1,0:T(8,128)S(1)}, f32[128,256]{1,0:T(8,128)S(1)}, u32[]{:S(2)}, u32[]{:S(2)}) collective-permute-start(f32[128,256]{1,0:T(8,128)S(1)} %get-tuple-element.49), channel_id=1, source_target_pairs={{0,6},{1,7},{2,4},{3,5},{4,2},{5,3},{6,0},{7,1},{8,14},{9,15},{10,... | collective-permute-start | bytes 393224 | tf_op jit(solution)/shard_map/ppermute | solution.py:545
  77.9 4.7 %compact_factor.1 = (f32[256,256]{1,0:T(8,128)S(1)}, f32[256,256]{1,0:T(8,128)}) custom-call(f32[8,64,256]{2,1,0:T(8,128)S(1)} %all_to_all.15.parts_ref, f32[256,256]{1,0:T(8,128)S(1)} %get-tuple-element.39.inv_ref, f32[256,256]{1,0:T(8,128)S(1)} %near_cholesky.1.upper_ref, f32[256,256]{1,0:T(8,128)S(1)} %get-tuple-element.51.first_ref), custom_call_target="tpu_custom_call" | custom-call | flops 4000000000 | bytes 12000000 | tf_op jit(solution)/shard_map/compact_factor/pallas_call | solution.py:267
  82.7 0.1 sum_pieces.1
  82.8 1.6 %collective-permute-start.17 = (f32[96,256]{1,0:T(8,128)S(1)}, f32[96,256]{1,0:T(8,128)S(1)}, u32[]{:S(2)}, u32[]{:S(2)}) collective-permute-start(f32[96,256]{1,0:T(8,128)S(1)} %get-tuple-element.61.refs_0_), channel_id=1, source_target_pairs={{0,6},{1,7},{2,4},{3,5},{4,2},{5,3},{6,0},{7,1},{8,14},{9,15},{10,... | collective-permute-start | bytes 294920 | tf_op jit(solution)/shard_map/ppermute | solution.py:545
  84.4 1.3 %collective-permute-start.16 = (f32[96,256]{1,0:T(8,128)S(1)}, f32[96,256]{1,0:T(8,128)S(1)}, u32[]{:S(2)}, u32[]{:S(2)}) collective-permute-start(f32[96,256]{1,0:T(8,128)S(1)} %get-tuple-element.61.refs_0_), channel_id=1, source_target_pairs={{0,4},{1,5},{2,6},{3,7},{4,0},{5,1},{6,2},{7,3},{8,12},{9,13},{10,... | collective-permute-start | bytes 294920 | tf_op jit(solution)/shard_map/ppermute | solution.py:545
  85.6 0.7 collective-permute-start.15
  86.3 2.3 %collective-permute-start.21 = (f32[128,256]{1,0:T(8,128)S(1)}, f32[128,256]{1,0:T(8,128)S(1)}, u32[]{:S(2)}, u32[]{:S(2)}) collective-permute-start(f32[128,256]{1,0:T(8,128)S(1)} %get-tuple-element.64.refs_0_.rest_refs_0_), channel_id=1, source_target_pairs={{0,24},{8,16},{16,8},{24,0},{1,25},{9,17},{17,9},{25,1},{2,26},{10... | collective-permute-start | bytes 393224 | tf_op jit(solution)/shard_map/ppermute | solution.py:545
  88.6 1.0 collective-permute-start.20
  89.6 1.6 %collective-permute-start.19 = (f32[128,256]{1,0:T(8,128)S(1)}, f32[128,256]{1,0:T(8,128)S(1)}, u32[]{:S(2)}, u32[]{:S(2)}) collective-permute-start(f32[128,256]{1,0:T(8,128)S(1)} %get-tuple-element.64.refs_0_.rest_refs_0_), channel_id=1, source_target_pairs={{0,8},{8,0},{16,24},{24,16},{1,9},{9,1},{17,25},{25,17},{2,10},{10... | collective-permute-start | bytes 393224 | tf_op jit(solution)/shard_map/ppermute | solution.py:545
  91.2 0.6 merge_pieces.1.mine_ref
  91.8 0.1 collective-permute-start.18
  91.8 2.5 %collective-permute-done.21.refs_3_.rest_refs_3_ = f32[128,256]{1,0:T(8,128)S(1)} collective-permute-done((f32[128,256]{1,0:T(8,128)S(1)}, f32[128,256]{1,0:T(8,128)S(1)}, u32[]{:S(2)}, u32[]{:S(2)}) %collective-permute-start.21) | collective-permute-done | bytes 131104 | tf_op jit(solution)/shard_map/ppermute | solution.py:545
  94.3 5.5 %collective-permute-done.20.refs_2_.rest_refs_2_ = f32[128,256]{1,0:T(8,128)S(1)} collective-permute-done((f32[128,256]{1,0:T(8,128)S(1)}, f32[128,256]{1,0:T(8,128)S(1)}, u32[]{:S(2)}, u32[]{:S(2)}) %collective-permute-start.20) | collective-permute-done | bytes 131104 | tf_op jit(solution)/shard_map/ppermute | solution.py:545
  99.8 9.3 %all_to_all.16.parts_ref = f32[8,32,256]{2,1,0:T(8,128)S(1)} all-to-all(f32[8,32,256]{2,1,0:T(8,128)S(1)} %sum_copies.5), channel_id=1, replica_groups=mesh['row'=4,'col'=8] {'col'}, dimensions={0} | all-to-all | bytes 524288 | tf_op jit(solution)/shard_map/all_to_all | solution.py:477
  109.1 4.1 %two_sided_update.1 = f32[768,384]{1,0:T(8,128)} custom-call(s32[2]{0:T(128)S(1)} %pad_add_fusion.place_ref, f32[768,384]{1,0:T(8,128)S(1)} %copy-done.2, f32[768,256]{1,0:T(8,128)S(1)} %get-tuple-element.43.left_ref, f32[384,256]{1,0:T(8,128)S(1)} %merge_pieces.1.mine_ref, f32[384,256]{1,0:T(8,128)S(1)} %collective-permute-done.18.other_ref, ...), custom_call_target="tpu_custom_call" | custom-call | flops 4000000000 | bytes 12000000 | tf_op jit(solution)/shard_map/two_sided_update/pallas_call | solution.py:530
  (23 shorter events, 0.2 us)
Async XLA Ops:
  0.7 1.1 %copy-start = (f32[768,256]{1,0:T(8,128)S(1)}, f32[768,256]{1,0:T(8,128)}, u32[]{:S(2)}) copy-start(f32[768,256]{1,0:T(8,128)} %panel_ref.3) | copy-start | bytes 2359300
  1.8 7.2 %copy-start.1 = (f32[768,256]{1,0:T(8,128)S(1)}, f32[768,256]{1,0:T(8,128)}, u32[]{:S(2)}) copy-start(f32[768,256]{1,0:T(8,128)} %panel_ref.3) | copy-start | bytes 2359300
  3.3 7.7 %collective-permute-start.2 = (f32[64,256]{1,0:T(8,128)S(1)}, f32[64,256]{1,0:T(8,128)S(1)}, u32[]{:S(2)}, u32[]{:S(2)}) collective-permute-start(f32[64,256]{1,0:T(8,128)S(1)} %gram_strips.1.refs_0_.refs_4_), channel_id=1, source_target_pairs={{0,24},{8,16},{16,8},{24,0},{1,25},{9,17},{17,9},{25,1},{2,26},{10... | collective-permute-start | bytes 196616 | tf_op jit(solution)/shard_map/ppermute | solution.py:545
  8.4 5.6 %collective-permute-start.1 = (f32[64,256]{1,0:T(8,128)S(1)}, f32[64,256]{1,0:T(8,128)S(1)}, u32[]{:S(2)}, u32[]{:S(2)}) collective-permute-start(f32[64,256]{1,0:T(8,128)S(1)} %gram_strips.1.refs_0_.refs_4_), channel_id=1, source_target_pairs={{0,16},{8,24},{16,0},{24,8},{1,17},{9,25},{17,1},{25,9},{2,18},{10... | collective-permute-start | bytes 196616 | tf_op jit(solution)/shard_map/ppermute | solution.py:545
  8.4 5.6 %collective-permute-start = (f32[64,256]{1,0:T(8,128)S(1)}, f32[64,256]{1,0:T(8,128)S(1)}, u32[]{:S(2)}, u32[]{:S(2)}) collective-permute-start(f32[64,256]{1,0:T(8,128)S(1)} %gram_strips.1.refs_0_.refs_4_), channel_id=1, source_target_pairs={{0,8},{8,0},{16,24},{24,16},{1,9},{9,1},{17,25},{25,17},{2,10},{10... | collective-permute-start | bytes 196616 | tf_op jit(solution)/shard_map/ppermute | solution.py:545
  14.0 10.4 %collective-permute-start.3 = (f32[384,256]{1,0:T(8,128)S(1)}, f32[384,256]{1,0:T(8,128)S(1)}, u32[]{:S(2)}, u32[]{:S(2)}) collective-permute-start(f32[384,256]{1,0:T(8,128)S(1)} %dynamic-slice_select_fusion), channel_id=1, source_target_pairs={{0,16},{1,17},{10,26},{11,27},{20,4},{21,5},{30,14},{31,15}} | collective-permute-start | bytes 1179656 | tf_op jit(solution)/shard_map/ppermute | solution.py:579
  18.3 10.3 %all-to-all-start = ((f32[8,32,256]{2,1,0:T(8,128)}), f32[8,32,256]{2,1,0:T(8,128)S(1)}, u32[]{:S(2)}, u32[]{:S(2)}) async-start(f32[8,32,256]{2,1,0:T(8,128)} %sum_copies.3), calls=%async_computation | async-start | bytes 524288 | tf_op jit(solution)/shard_map/all_to_all | solution.py:477
  24.5 13.8 %collective-permute-start.4 = (f32[384,256]{1,0:T(8,128)S(1)}, f32[384,256]{1,0:T(8,128)S(1)}, u32[]{:S(2)}, u32[]{:S(2)}) collective-permute-start(f32[384,256]{1,0:T(8,128)S(1)} %add.8.slab_ref), channel_id=1, source_target_pairs={{0,8},{16,24},{1,9},{17,25},{10,2},{26,18},{11,3},{27,19},{20,28},... | collective-permute-start | bytes 1179656 | tf_op jit(solution)/shard_map/ppermute | solution.py:579
  41.3 5.8 %collective-permute-start.7 = (f32[32,256]{1,0:T(8,128)S(1)}, f32[32,256]{1,0:T(8,128)S(1)}, u32[]{:S(2)}, u32[]{:S(2)}) collective-permute-start(f32[32,256]{1,0:T(8,128)S(1)} %get-tuple-element.42.refs_0_), channel_id=1, source_target_pairs={{0,24},{8,16},{16,8},{24,0},{1,25},{9,17},{17,9},{25,1},{2,26},{10... | collective-permute-start | bytes 98312 | tf_op jit(solution)/shard_map/ppermute | solution.py:545
  43.6 4.8 %collective-permute-start.6 = (f32[32,256]{1,0:T(8,128)S(1)}, f32[32,256]{1,0:T(8,128)S(1)}, u32[]{:S(2)}, u32[]{:S(2)}) collective-permute-start(f32[32,256]{1,0:T(8,128)S(1)} %get-tuple-element.42.refs_0_), channel_id=1, source_target_pairs={{0,16},{8,24},{16,0},{24,8},{1,17},{9,25},{17,1},{25,9},{2,18},{10... | collective-permute-start | bytes 98312 | tf_op jit(solution)/shard_map/ppermute | solution.py:545
  44.0 4.5 %collective-permute-start.5 = (f32[32,256]{1,0:T(8,128)S(1)}, f32[32,256]{1,0:T(8,128)S(1)}, u32[]{:S(2)}, u32[]{:S(2)}) collective-permute-start(f32[32,256]{1,0:T(8,128)S(1)} %get-tuple-element.42.refs_0_), channel_id=1, source_target_pairs={{0,8},{8,0},{16,24},{24,16},{1,9},{9,1},{17,25},{25,17},{2,10},{10... | collective-permute-start | bytes 98312 | tf_op jit(solution)/shard_map/ppermute | solution.py:545
  60.7 2.9 %copy-start.2 = (f32[768,384]{1,0:T(8,128)S(1)}, f32[768,384]{1,0:T(8,128)}, u32[]{:S(2)}) copy-start(f32[768,384]{1,0:T(8,128)} %ham_ref.3) | copy-start | bytes 3538948
  67.9 2.0 %collective-permute-start.8 = (f32[4,128,256]{2,1,0:T(8,128)S(1)}, f32[4,128,256]{2,1,0:T(8,128)S(1)}, u32[]{:S(2)}, u32[]{:S(2)}) collective-permute-start(f32[4,128,256]{2,1,0:T(8,128)S(1)} %get-tuple-element.45), channel_id=1, source_target_pairs={{0,1},{1,0},{2,3},{3,2},{4,5},{5,4},{6,7},{7,6},{8,9},{9,8},{10,11... | collective-permute-start | bytes 1572872 | tf_op jit(solution)/shard_map/ppermute | solution.py:594
  70.0 5.6 %collective-permute-start.9 = (f32[128,256]{1,0:T(8,128)S(1)}, f32[128,256]{1,0:T(8,128)S(1)}, u32[]{:S(2)}, u32[]{:S(2)}) collective-permute-start(f32[128,256]{1,0:T(8,128)S(1)} %get-tuple-element.47), channel_id=1, source_target_pairs={{0,2},{1,3},{2,0},{3,1},{4,6},{5,7},{6,4},{7,5},{8,10},{9,11},{10,... | collective-permute-start | bytes 393224 | tf_op jit(solution)/shard_map/ppermute | solution.py:545
  70.6 12.1 %collective-permute-start.12 = (f32[96,256]{1,0:T(8,128)S(1)}, f32[96,256]{1,0:T(8,128)S(1)}, u32[]{:S(2)}, u32[]{:S(2)}) collective-permute-start(f32[96,256]{1,0:T(8,128)S(1)} %get-tuple-element.58), channel_id=1, source_target_pairs={{0,8},{8,0},{16,24},{24,16},{1,9},{9,1},{17,25},{25,17},{2,10},{10... | collective-permute-start | bytes 294920 | tf_op jit(solution)/shard_map/ppermute | solution.py:545
  72.5 10.2 %collective-permute-start.13 = (f32[96,256]{1,0:T(8,128)S(1)}, f32[96,256]{1,0:T(8,128)S(1)}, u32[]{:S(2)}, u32[]{:S(2)}) collective-permute-start(f32[96,256]{1,0:T(8,128)S(1)} %get-tuple-element.59), channel_id=1, source_target_pairs={{0,16},{8,24},{16,0},{24,8},{1,17},{9,25},{17,1},{25,9},{2,18},{10... | collective-permute-start | bytes 294920 | tf_op jit(solution)/shard_map/ppermute | solution.py:545
  73.4 9.3 %collective-permute-start.14 = (f32[96,256]{1,0:T(8,128)S(1)}, f32[96,256]{1,0:T(8,128)S(1)}, u32[]{:S(2)}, u32[]{:S(2)}) collective-permute-start(f32[96,256]{1,0:T(8,128)S(1)} %get-tuple-element.60), channel_id=1, source_target_pairs={{0,24},{8,16},{16,8},{24,0},{1,25},{9,17},{17,9},{25,1},{2,26},{10... | collective-permute-start | bytes 294920 | tf_op jit(solution)/shard_map/ppermute | solution.py:545
  75.0 7.7 %collective-permute-start.10 = (f32[128,256]{1,0:T(8,128)S(1)}, f32[128,256]{1,0:T(8,128)S(1)}, u32[]{:S(2)}, u32[]{:S(2)}) collective-permute-start(f32[128,256]{1,0:T(8,128)S(1)} %get-tuple-element.48), channel_id=1, source_target_pairs={{0,4},{1,5},{2,6},{3,7},{4,0},{5,1},{6,2},{7,3},{8,12},{9,13},{10,... | collective-permute-start | bytes 393224 | tf_op jit(solution)/shard_map/ppermute | solution.py:545
  75.6 7.1 %collective-permute-start.11 = (f32[128,256]{1,0:T(8,128)S(1)}, f32[128,256]{1,0:T(8,128)S(1)}, u32[]{:S(2)}, u32[]{:S(2)}) collective-permute-start(f32[128,256]{1,0:T(8,128)S(1)} %get-tuple-element.49), channel_id=1, source_target_pairs={{0,6},{1,7},{2,4},{3,5},{4,2},{5,3},{6,0},{7,1},{8,14},{9,15},{10,... | collective-permute-start | bytes 393224 | tf_op jit(solution)/shard_map/ppermute | solution.py:545
  82.8 6.8 %collective-permute-start.17 = (f32[96,256]{1,0:T(8,128)S(1)}, f32[96,256]{1,0:T(8,128)S(1)}, u32[]{:S(2)}, u32[]{:S(2)}) collective-permute-start(f32[96,256]{1,0:T(8,128)S(1)} %get-tuple-element.61.refs_0_), channel_id=1, source_target_pairs={{0,6},{1,7},{2,4},{3,5},{4,2},{5,3},{6,0},{7,1},{8,14},{9,15},{10,... | collective-permute-start | bytes 294920 | tf_op jit(solution)/shard_map/ppermute | solution.py:545
  84.4 6.8 %collective-permute-start.16 = (f32[96,256]{1,0:T(8,128)S(1)}, f32[96,256]{1,0:T(8,128)S(1)}, u32[]{:S(2)}, u32[]{:S(2)}) collective-permute-start(f32[96,256]{1,0:T(8,128)S(1)} %get-tuple-element.61.refs_0_), channel_id=1, source_target_pairs={{0,4},{1,5},{2,6},{3,7},{4,0},{5,1},{6,2},{7,3},{8,12},{9,13},{10,... | collective-permute-start | bytes 294920 | tf_op jit(solution)/shard_map/ppermute | solution.py:545
  85.6 5.5 %collective-permute-start.15 = (f32[96,256]{1,0:T(8,128)S(1)}, f32[96,256]{1,0:T(8,128)S(1)}, u32[]{:S(2)}, u32[]{:S(2)}) collective-permute-start(f32[96,256]{1,0:T(8,128)S(1)} %get-tuple-element.61.refs_0_), channel_id=1, source_target_pairs={{0,2},{1,3},{2,0},{3,1},{4,6},{5,7},{6,4},{7,5},{8,10},{9,11},{10,... | collective-permute-start | bytes 294920 | tf_op jit(solution)/shard_map/ppermute | solution.py:545
  86.3 7.9 %collective-permute-start.21 = (f32[128,256]{1,0:T(8,128)S(1)}, f32[128,256]{1,0:T(8,128)S(1)}, u32[]{:S(2)}, u32[]{:S(2)}) collective-permute-start(f32[128,256]{1,0:T(8,128)S(1)} %get-tuple-element.64.refs_0_.rest_refs_0_), channel_id=1, source_target_pairs={{0,24},{8,16},{16,8},{24,0},{1,25},{9,17},{17,9},{25,1},{2,26},{10... | collective-permute-start | bytes 393224 | tf_op jit(solution)/shard_map/ppermute | solution.py:545
  88.6 11.2 %collective-permute-start.20 = (f32[128,256]{1,0:T(8,128)S(1)}, f32[128,256]{1,0:T(8,128)S(1)}, u32[]{:S(2)}, u32[]{:S(2)}) collective-permute-start(f32[128,256]{1,0:T(8,128)S(1)} %get-tuple-element.64.refs_0_.rest_refs_0_), channel_id=1, source_target_pairs={{0,16},{8,24},{16,0},{24,8},{1,17},{9,25},{17,1},{25,9},{2,18},{10... | collective-permute-start | bytes 393224 | tf_op jit(solution)/shard_map/ppermute | solution.py:545
  89.6 10.2 %collective-permute-start.19 = (f32[128,256]{1,0:T(8,128)S(1)}, f32[128,256]{1,0:T(8,128)S(1)}, u32[]{:S(2)}, u32[]{:S(2)}) collective-permute-start(f32[128,256]{1,0:T(8,128)S(1)} %get-tuple-element.64.refs_0_.rest_refs_0_), channel_id=1, source_target_pairs={{0,8},{8,0},{16,24},{24,16},{1,9},{9,1},{17,25},{25,17},{2,10},{10... | collective-permute-start | bytes 393224 | tf_op jit(solution)/shard_map/ppermute | solution.py:545
  91.8 17.4 %collective-permute-start.18 = (f32[384,256]{1,0:T(8,128)S(1)}, f32[384,256]{1,0:T(8,128)S(1)}, u32[]{:S(2)}, u32[]{:S(2)}) collective-permute-start(f32[384,256]{1,0:T(8,128)S(1)} %merge_pieces.1.mine_ref), channel_id=1, source_target_pairs={{0,1},{1,0},{2,3},{3,2},{4,5},{5,4},{6,7},{7,6},{8,9},{9,8},{10,11... | collective-permute-start | bytes 1179656 | tf_op jit(solution)/shard_map/ppermute | solution.py:603
